TPU v7x, 32 devices: a whole 2x2x4 slice. The times are simulated.
32 devices in a mesh: dp: 4 (over z), ctx: 4 (over x, core), expert: 2 (over y).
Axes of the slice: x: 2, y: 2, z: 4, core: 2. Of those that a mesh axis runs over, the one named last changes fastest.
Arguments:
- hidden_in: bfloat16 [6144, 2048], P(('dp', 'ctx', 'expert')), may hold values from -6 to 6
- attn_gain: float32 [2048], replicated, may hold values from 0.5 to 1.5
- query_weight: bfloat16 [2048, 4096], P('expert'), may hold values from -0.125 to 0.125
- key_matrix: bfloat16 [2048, 512], P('expert'), may hold values from -0.125 to 0.125
- value_matrix: bfloat16 [2048, 512], P('expert'), may hold values from -0.125 to 0.125
- query_gain: float32 [128], replicated, may hold values from 0.5 to 1.5
- key_gain: float32 [128], replicated, may hold values from 0.5 to 1.5
- output_weight: bfloat16 [4096, 2048], P('expert'), may hold values from -1.5 to 1.5
- ffn_gain: float32 [2048], replicated, may hold values from 0.5 to 1.5
- router_weight: bfloat16 [2048, 16], replicated, may hold values from -0.0625 to 0.0625
- gate_up: bfloat16 [16, 2048, 1536], P(('ctx', 'expert')), may hold values from -0.125 to 0.125
- down_proj: bfloat16 [16, 768, 2048], P(('ctx', 'expert')), may hold values from -1.25 to 1.25
- routes: int32 [6144, 8], P(('dp', 'ctx', 'expert')), may hold values from 0 to 15, all different within a row; in each aligned block of 192 rows (0 to 191, 192 to 383, ...) at most 137 rows name the same one
- out_grad: bfloat16 [6144, 2048], P(('dp', 'ctx', 'expert')), may hold values from -6 to 6
Outputs:
- block_out: bfloat16 [6144, 2048], P(('dp', 'ctx', 'expert'))
- hidden_grad: float32 [6144, 2048], P(('dp', 'ctx', 'expert'))
- attn_gain_grad: float32 [2048], P(('dp', 'ctx', 'expert'))
- query_weight_grad: float32 [2048, 4096], P(('dp', 'ctx', 'expert'))
- key_weight_grad: float32 [2048, 512], P(('dp', 'ctx', 'expert'))
- value_weight_grad: float32 [2048, 512], P(('dp', 'ctx', 'expert'))
- query_gain_grad: float32 [128], P(('dp', 'ctx', 'expert'))
- key_gain_grad: float32 [128], P(('dp', 'ctx', 'expert'))
- output_weight_grad: float32 [4096, 2048], P(('dp', 'ctx', 'expert'))
- ffn_gain_grad: float32 [2048], P(('dp', 'ctx', 'expert'))
- router_grad: float32 [2048, 16], P(('dp', 'ctx', 'expert'))
- gate_up_grad: float32 [16, 2048, 1536], P(('ctx', 'expert'), 'dp')
- down_grad: float32 [16, 768, 2048], P(('ctx', 'expert'), 'dp')
Inputs may be any that keep to these rules, and one draw needn't show every extreme that they name: `routes`: among the rows of one device no expert is named by more than 137 rows, a bound that some block reaches.
All inputs are finite; a program needn't handle non-finite values.
Results may differ from a plain program's by a relative error of at most 0.02.
Values may be sent and summed in bfloat16 or wider, within the bound.
A program may use at most 384 MiB of HBM per device.

v0:
```python
import math

import jax
import jax.numpy as jnp
from jax import lax
from jax.sharding import PartitionSpec as P

MODEL_WIDTH = 2048
QUERY_HEADS = 32
KEY_VALUE_HEADS = 4
HEAD_SIZE = 128
TOP = 8
PROMPT_DEV = 128


highest = lax.Precision.HIGHEST
epsilon = 1e-06
rope_base = 1000000.0
masked = -1e30


def rms_scale(value_rows):
    return lax.rsqrt(jnp.mean(value_rows * value_rows, axis=-1, keepdims=True) + epsilon)


def norm_back(inputs, inv_rms, norm_gain, gradient):
    weighted = gradient * norm_gain
    return inv_rms * weighted - inputs * inv_rms**3 * jnp.mean(
        weighted * inputs, axis=-1, keepdims=True
    )


def angles(position, head_width):
    freq_index = jnp.arange(head_width // 2, dtype=jnp.float32)
    inverse = jnp.exp(-(2.0 * freq_index / head_width) * math.log(rope_base))
    rope_angle = position.astype(jnp.float32)[:, None] * inverse[None, :]
    rope_angle = jnp.concatenate([rope_angle, rope_angle], axis=-1)
    return (jnp.cos(rope_angle), jnp.sin(rope_angle))


def rotate(value_rows, cosine, rope_sine):
    half_width = value_rows.shape[-1] // 2
    turned = jnp.concatenate([-value_rows[..., half_width:], value_rows[..., :half_width]], axis=-1)
    return value_rows * cosine + turned * rope_sine


def rotate_back(gradient, cosine, rope_sine):
    shifted = gradient * rope_sine
    half_width = gradient.shape[-1] // 2
    return gradient * cosine + jnp.concatenate(
        [shifted[..., half_width:], -shifted[..., :half_width]], axis=-1
    )


def move_rows(slot_block):
    return lax.all_to_all(slot_block, ("ctx", "expert"), split_axis=1, concat_axis=1, tiled=True)


def body(
    hidden_in,
    attn_gain,
    query_weight,
    key_matrix,
    value_matrix,
    query_gain,
    key_gain,
    output_weight,
    ffn_gain,
    router_weight,
    gate_up,
    down_proj,
    routes,
    out_grad,
):
    ctx_count = lax.axis_size("ctx")
    spread_count = lax.axis_size(("ctx", "expert"))
    local_experts = gate_up.shape[0]
    count_of_rows = hidden_in.shape[0]
    prompt_all = PROMPT_DEV * ctx_count
    capacity = 10 * count_of_rows * TOP // (7 * local_experts * spread_count)
    slot_span = spread_count * capacity
    pair_count = count_of_rows * TOP
    heads_per_group = QUERY_HEADS // KEY_VALUE_HEADS
    score_scale = HEAD_SIZE ** (-0.5)
    hidden_ff = gate_up.shape[2] // 2
    full_query, full_key, full_value, full_output = (
        lax.all_gather(query_weight, "expert", axis=0, tiled=True),
        lax.all_gather(key_matrix, "expert", axis=0, tiled=True),
        lax.all_gather(value_matrix, "expert", axis=0, tiled=True),
        lax.all_gather(output_weight, "expert", axis=0, tiled=True),
    )
    inputs = hidden_in.astype(jnp.float32)
    scale_in = rms_scale(inputs)
    normalized_input = (inputs * scale_in * attn_gain).astype(jnp.bfloat16)
    query_pre = jnp.dot(normalized_input, full_query, preferred_element_type=jnp.float32).reshape(
        count_of_rows, QUERY_HEADS, HEAD_SIZE
    )
    key_before_norm = jnp.dot(
        normalized_input, full_key, preferred_element_type=jnp.float32
    ).reshape(count_of_rows, KEY_VALUE_HEADS, HEAD_SIZE)
    value_low = (
        jnp.dot(normalized_input, full_value, preferred_element_type=jnp.float32)
        .astype(jnp.bfloat16)
        .reshape(count_of_rows, KEY_VALUE_HEADS, HEAD_SIZE)
    )
    query_inv = rms_scale(query_pre)
    key_inv = rms_scale(key_before_norm)
    member = lax.axis_index("ctx")
    offsets = jnp.arange(count_of_rows, dtype=jnp.int32)
    position = jnp.where(
        offsets < PROMPT_DEV, member * PROMPT_DEV + offsets, prompt_all + offsets - PROMPT_DEV
    )
    cosine, rope_sine = angles(position, HEAD_SIZE)
    cosine = cosine[:, None, :]
    rope_sine = rope_sine[:, None, :]
    query_reduced = rotate(query_pre * query_inv * query_gain, cosine, rope_sine).astype(
        jnp.bfloat16
    )
    key_low = rotate(key_before_norm * key_inv * key_gain, cosine, rope_sine).astype(jnp.bfloat16)
    prompt_keys, prompt_values = (
        lax.all_gather(key_low[:PROMPT_DEV], "ctx", axis=0, tiled=True),
        lax.all_gather(value_low[:PROMPT_DEV], "ctx", axis=0, tiled=True),
    )
    keys_all = jnp.concatenate([prompt_keys, key_low[PROMPT_DEV:]], axis=0)
    values_all = jnp.concatenate([prompt_values, value_low[PROMPT_DEV:]], axis=0)
    key_position = jnp.concatenate(
        [
            jnp.arange(prompt_all, dtype=jnp.int32),
            prompt_all + jnp.arange(count_of_rows - PROMPT_DEV, dtype=jnp.int32),
        ]
    )
    visible = key_position[None, :] <= position[:, None]
    grouped_queries = query_reduced.reshape(
        count_of_rows, KEY_VALUE_HEADS, heads_per_group, HEAD_SIZE
    )

    def scores_of():
        raw_scores = (
            jnp.einsum(
                "rkgd,skd->kgrs", grouped_queries, keys_all, preferred_element_type=jnp.float32
            )
            * score_scale
        )
        return jnp.where(visible, raw_scores, masked)

    scores = scores_of()
    row_max = jnp.max(scores, axis=-1, keepdims=True)
    weights = jnp.exp(scores - row_max)
    row_total = jnp.sum(weights, axis=-1, keepdims=True)
    log_total = row_max + jnp.log(row_total)
    attention = (weights / row_total).astype(jnp.bfloat16)
    attended = (
        jnp.einsum("kgrs,skd->rkgd", attention, values_all, preferred_element_type=jnp.float32)
        .reshape(count_of_rows, QUERY_HEADS * HEAD_SIZE)
        .astype(jnp.bfloat16)
    )
    residual = inputs + jnp.dot(attended, full_output, preferred_element_type=jnp.float32)
    scale_ffn = rms_scale(residual)
    ffn_in = (residual * scale_ffn * ffn_gain).astype(jnp.bfloat16)
    logits = jnp.dot(ffn_in, router_weight, preferred_element_type=jnp.float32)
    gate_weights = jax.nn.softmax(jnp.take_along_axis(logits, routes, axis=1), axis=-1)
    flat_routes = routes.reshape(pair_count)
    expert_ids = jnp.arange(local_experts * spread_count, dtype=jnp.int32)
    onehot = (flat_routes[:, None] == expert_ids[None, :]).astype(jnp.int32)
    pair_rank = jnp.sum((jnp.cumsum(onehot, axis=0) - onehot) * onehot, axis=1)
    pair_slot = (
        flat_routes % local_experts * slot_span
        + flat_routes // local_experts * capacity
        + pair_rank
    )
    slot_pair = (
        jnp.full((local_experts * slot_span,), pair_count, dtype=jnp.int32)
        .at[pair_slot]
        .set(jnp.arange(pair_count, dtype=jnp.int32))
    )
    slot_token = slot_pair // TOP
    padded_in = jnp.concatenate([ffn_in, jnp.zeros((1, MODEL_WIDTH), jnp.bfloat16)], axis=0)
    send_rows = padded_in[slot_token].reshape(local_experts, spread_count, capacity, MODEL_WIDTH)
    expert_slot_rows = lax.all_to_all(
        send_rows, ("ctx", "expert"), split_axis=1, concat_axis=1, tiled=True
    )
    expert_projected = jnp.einsum(
        "encd,edf->encf", expert_slot_rows, gate_up, preferred_element_type=jnp.float32
    )
    expert_hidden_low = (
        jax.nn.silu(expert_projected[..., :hidden_ff]) * expert_projected[..., hidden_ff:]
    ).astype(jnp.bfloat16)
    expert_out = jnp.einsum(
        "encf,efd->encd", expert_hidden_low, down_proj, preferred_element_type=jnp.float32
    ).astype(jnp.bfloat16)
    slot_rows, projected, hidden_low, expert_out = (
        expert_slot_rows,
        expert_projected,
        expert_hidden_low,
        expert_out,
    )
    returned = move_rows(expert_out)
    pair_rows = returned.reshape(local_experts * slot_span, MODEL_WIDTH)[pair_slot].reshape(
        count_of_rows, TOP, MODEL_WIDTH
    )
    moe_sum = jnp.zeros((count_of_rows, MODEL_WIDTH), jnp.float32)
    for which in range(TOP):
        moe_sum = moe_sum + gate_weights[:, which : which + 1] * pair_rows[:, which].astype(
            jnp.float32
        )
    block_out = (residual + moe_sum).astype(jnp.bfloat16)
    grad_out = out_grad.astype(jnp.float32)
    gate_grad = jnp.stack(
        [
            jnp.sum(pair_rows[:, which].astype(jnp.float32) * grad_out, axis=-1)
            for which in range(TOP)
        ],
        axis=1,
    )
    chosen_grad = gate_weights * (
        gate_grad - jnp.sum(gate_weights * gate_grad, axis=-1, keepdims=True)
    )
    logit_grad = jnp.sum(
        jnp.where(routes[:, :, None] == expert_ids[None, None, :], chosen_grad[:, :, None], 0.0),
        axis=1,
    )
    router_local = jnp.dot(ffn_in.T, logit_grad, preferred_element_type=jnp.float32)
    ffn_in_grad = jnp.dot(logit_grad, router_weight.astype(jnp.float32).T, precision=highest)
    pair_low = (
        (gate_weights[:, :, None] * grad_out[:, None, :])
        .astype(jnp.bfloat16)
        .reshape(pair_count, MODEL_WIDTH)
    )
    send_back = jnp.concatenate([pair_low, jnp.zeros((1, MODEL_WIDTH), jnp.bfloat16)], axis=0)[
        slot_pair
    ].reshape(send_rows.shape)
    out_grads = move_rows(send_back)
    gate_part = projected[..., :hidden_ff]
    up_part = projected[..., hidden_ff:]
    sigmoid_gate = jax.nn.sigmoid(gate_part)
    down_local = jnp.einsum(
        "encf,encd->efd", hidden_low, out_grads, preferred_element_type=jnp.float32
    )
    hidden_back = jnp.einsum(
        "encd,efd->encf", out_grads, down_proj, preferred_element_type=jnp.float32
    )
    gate_back = hidden_back * up_part * sigmoid_gate * (1.0 + gate_part * (1.0 - sigmoid_gate))
    up_back = hidden_back * gate_part * sigmoid_gate
    projected_grad = jnp.concatenate([gate_back, up_back], axis=-1).astype(jnp.bfloat16)
    gate_up_local = jnp.einsum(
        "encd,encf->edf", slot_rows, projected_grad, preferred_element_type=jnp.float32
    )
    rows_grad = jnp.einsum(
        "encf,edf->encd", projected_grad, gate_up, preferred_element_type=jnp.float32
    ).astype(jnp.bfloat16)
    rows_grad, gate_up_local, down_local = (rows_grad, gate_up_local, down_local)
    returned_grads = move_rows(rows_grad)
    gate_up_grad, down_grad = (
        lax.psum_scatter(
            gate_up_local.astype(jnp.bfloat16), "dp", scatter_dimension=1, tiled=True
        ).astype(jnp.float32),
        lax.psum_scatter(
            down_local.astype(jnp.bfloat16), "dp", scatter_dimension=1, tiled=True
        ).astype(jnp.float32),
    )
    back_rows = returned_grads.reshape(local_experts * slot_span, MODEL_WIDTH)[pair_slot].reshape(
        count_of_rows, TOP, MODEL_WIDTH
    )
    for which in range(TOP):
        ffn_in_grad = ffn_in_grad + back_rows[:, which].astype(jnp.float32)
    residual_grad = grad_out + norm_back(residual, scale_ffn, ffn_gain, ffn_in_grad)
    ffn_gain_local = jnp.sum(ffn_in_grad * residual * scale_ffn, axis=0)
    branch_low = residual_grad.astype(jnp.bfloat16)
    output_local = jnp.dot(attended.T, branch_low, preferred_element_type=jnp.float32)
    attended_grad = (
        jnp.dot(branch_low, full_output.T, preferred_element_type=jnp.float32)
        .astype(jnp.bfloat16)
        .reshape(count_of_rows, KEY_VALUE_HEADS, heads_per_group, HEAD_SIZE)
    )
    attention_again = jnp.exp(scores_of() - log_total)
    prob_grad = jnp.einsum(
        "rkgd,skd->kgrs", attended_grad, values_all, preferred_element_type=jnp.float32
    )
    row_delta = jnp.sum(attention_again * prob_grad, axis=-1, keepdims=True)
    score_grad = (attention_again * (prob_grad - row_delta)).astype(jnp.bfloat16)
    query_grad = (
        jnp.einsum("kgrs,skd->rkgd", score_grad, keys_all, preferred_element_type=jnp.float32)
        * score_scale
    ).reshape(count_of_rows, QUERY_HEADS, HEAD_SIZE)
    key_grad_all = (
        jnp.einsum(
            "kgrs,rkgd->skd", score_grad, grouped_queries, preferred_element_type=jnp.float32
        )
        * score_scale
    )
    value_grad_all = jnp.einsum(
        "kgrs,rkgd->skd",
        attention_again.astype(jnp.bfloat16),
        attended_grad,
        preferred_element_type=jnp.float32,
    )
    prompt_key_grad, prompt_value_grad = (
        lax.psum_scatter(
            key_grad_all[:prompt_all].astype(jnp.bfloat16), "ctx", scatter_dimension=0, tiled=True
        ).astype(jnp.float32),
        lax.psum_scatter(
            value_grad_all[:prompt_all].astype(jnp.bfloat16), "ctx", scatter_dimension=0, tiled=True
        ).astype(jnp.float32),
    )
    key_grad = jnp.concatenate([prompt_key_grad, key_grad_all[prompt_all:]], axis=0)
    value_gradient = jnp.concatenate([prompt_value_grad, value_grad_all[prompt_all:]], axis=0)
    query_rot_grad = rotate_back(query_grad, cosine, rope_sine)
    key_rot_grad = rotate_back(key_grad, cosine, rope_sine)
    query_gain_local = jnp.sum(query_rot_grad * query_pre * query_inv, axis=(0, 1))
    key_gain_local = jnp.sum(key_rot_grad * key_before_norm * key_inv, axis=(0, 1))
    query_pre_grad = (
        norm_back(query_pre, query_inv, query_gain, query_rot_grad)
        .astype(jnp.bfloat16)
        .reshape(count_of_rows, QUERY_HEADS * HEAD_SIZE)
    )
    key_pre_grad = (
        norm_back(key_before_norm, key_inv, key_gain, key_rot_grad)
        .astype(jnp.bfloat16)
        .reshape(count_of_rows, KEY_VALUE_HEADS * HEAD_SIZE)
    )
    value_before_norm_gradient = value_gradient.astype(jnp.bfloat16).reshape(
        count_of_rows, KEY_VALUE_HEADS * HEAD_SIZE
    )
    query_local = jnp.dot(normalized_input.T, query_pre_grad, preferred_element_type=jnp.float32)
    key_local = jnp.dot(normalized_input.T, key_pre_grad, preferred_element_type=jnp.float32)
    value_local = jnp.dot(
        normalized_input.T, value_before_norm_gradient, preferred_element_type=jnp.float32
    )
    normed_grad = jnp.dot(query_pre_grad, full_query.T, preferred_element_type=jnp.float32)
    normed_grad = normed_grad + jnp.dot(
        key_pre_grad, full_key.T, preferred_element_type=jnp.float32
    )
    normed_grad = normed_grad + jnp.dot(
        value_before_norm_gradient, full_value.T, preferred_element_type=jnp.float32
    )
    attn_gain_local = jnp.sum(normed_grad * inputs * scale_in, axis=0)
    hidden_grad = residual_grad + norm_back(inputs, scale_in, attn_gain, normed_grad)
    summed = (
        lax.psum_scatter(attn_gain_local, ("dp", "ctx", "expert"), scatter_dimension=0, tiled=True),
        lax.psum_scatter(query_local, ("dp", "ctx", "expert"), scatter_dimension=0, tiled=True),
        lax.psum_scatter(key_local, ("dp", "ctx", "expert"), scatter_dimension=0, tiled=True),
        lax.psum_scatter(value_local, ("dp", "ctx", "expert"), scatter_dimension=0, tiled=True),
        lax.psum_scatter(
            query_gain_local, ("dp", "ctx", "expert"), scatter_dimension=0, tiled=True
        ),
        lax.psum_scatter(key_gain_local, ("dp", "ctx", "expert"), scatter_dimension=0, tiled=True),
        lax.psum_scatter(output_local, ("dp", "ctx", "expert"), scatter_dimension=0, tiled=True),
        lax.psum_scatter(ffn_gain_local, ("dp", "ctx", "expert"), scatter_dimension=0, tiled=True),
        lax.psum_scatter(router_local, ("dp", "ctx", "expert"), scatter_dimension=0, tiled=True),
    )
    return (
        block_out,
        hidden_grad,
        summed[0],
        summed[1],
        summed[2],
        summed[3],
        summed[4],
        summed[5],
        summed[6],
        summed[7],
        summed[8],
        gate_up_grad,
        down_grad,
    )


def solution(mesh):
    placed = (
        P(("dp", "ctx", "expert"), None),
        P(),
        P("expert", None),
        P("expert", None),
        P("expert", None),
        P(),
        P(),
        P("expert", None),
        P(),
        P(),
        P(("ctx", "expert"), None, None),
        P(("ctx", "expert"), None, None),
        P(("dp", "ctx", "expert"), None),
        P(("dp", "ctx", "expert"), None),
    )
    return jax.shard_map(
        body,
        mesh=mesh,
        in_specs=placed,
        out_specs=(
            P(("dp", "ctx", "expert"), None),
            P(("dp", "ctx", "expert"), None),
            P(("dp", "ctx", "expert")),
            P(("dp", "ctx", "expert"), None),
            P(("dp", "ctx", "expert"), None),
            P(("dp", "ctx", "expert"), None),
            P(("dp", "ctx", "expert")),
            P(("dp", "ctx", "expert")),
            P(("dp", "ctx", "expert"), None),
            P(("dp", "ctx", "expert")),
            P(("dp", "ctx", "expert"), None),
            P(("ctx", "expert"), "dp", None),
            P(("ctx", "expert"), "dp", None),
        ),
        check_vma=False,
    )
```

profile of v0, /device:TPU:0, one launch (start us, length us, event | category | flops | bytes accessed | tf_op | source)
XLA Modules:
  0.0 3545.4 jit_solution(13999207431892546945)
XLA Ops:
  16.8 6.2 scatter_custom_fusion
  25.3 20.1 all-gather.7.cloned.1.call-done
  49.5 7.1 all_gather.21
  56.7 23.5 all-gather.5.cloned.1.call-done
  82.4 7.6 all_gather.19
  90.7 189.9 %all-gather.9.cloned.1.call-done = bf16[2048,4096]{1,0:T(8,128)(2,1)} async-done(((bf16[1024,4096]{1,0:T(8,128)(2,1)}), bf16[2048,4096]{1,0:T(8,128)(2,1)}) %all-gather.9.cloned.1.call-update) | async-done | bytes 16777232 | tf_op jit(solution)/shard_map/all_gather | solution.py:87
  280.6 11.6 fusion.140
  292.2 6.0 copy.348
  333.1 147.9 %all-gather.11.cloned.1.call-done = bf16[4096,2048]{1,0:T(8,128)(2,1)} async-done(((bf16[2048,2048]{1,0:T(8,128)(2,1)}), bf16[4096,2048]{1,0:T(8,128)(2,1)}) %all-gather.11.cloned.1.call-update) | async-done | bytes 16777232 | tf_op jit(solution)/shard_map/all_gather | solution.py:90
  480.9 7.9 multiply_reduce_fusion.4
  490.3 9.8 gather_fusion
  500.1 11.4 reshape.531
  511.5 16.8 copy.360
  528.4 112.2 %all_to_all.20 = bf16[2,8,137,2048]{3,0,2,1:T(2,128)(2,1)} all-to-all(bf16[2,8,137,2048]{3,0,2,1:T(2,128)(2,1)S(1)} %copy.360), channel_id=1, replica_groups=mesh['dp'=4,'ctx'=4,'expert'=2] {'ctx','expert'}, dimensions={1} | all-to-all | bytes 17956864 | tf_op jit(solution)/shard_map/all_to_all | solution.py:179
  640.5 33.2 fusion.6
  673.7 6.1 multiply_convert_fusion.2
  679.9 8.0 fusion.22
  687.8 8.5 copy.362
  696.4 5.1 all-to-all-start.1
  703.4 12.7 gather_fusion.4
  716.4 84.6 %all-to-all-done.1 = bf16[2,8,137,2048]{3,0,2,1:T(2,128)(2,1)} async-done(((bf16[2,8,137,2048]{3,0,2,1:T(2,128)(2,1)}), bf16[2,8,137,2048]{3,0,2,1:T(2,128)(2,1)}, u32[]{:S(2)}, u32[]{:S(2)}) %all-to-all-start.1) | async-done | bytes 8978464 | tf_op jit(solution)/shard_map/all_to_all | solution.py:56
  801.0 11.5 copy.363
  812.5 11.6 reshape.532
  824.1 17.4 gather_fusion.1
  841.5 31.8 fusion.147
  883.0 21.7 gather_fusion.2
  904.8 11.5 reshape.534
  916.3 16.8 copy.373
  933.1 103.8 %all_to_all.21 = bf16[2,8,137,2048]{3,0,2,1:T(2,128)(2,1)} all-to-all(bf16[2,8,137,2048]{3,0,2,1:T(2,128)(2,1)S(1)} %copy.373), channel_id=1, replica_groups=mesh['dp'=4,'ctx'=4,'expert'=2] {'ctx','expert'}, dimensions={1} | all-to-all | bytes 17956864 | tf_op jit(solution)/shard_map/all_to_all | solution.py:56
  1036.8 21.6 multiply_convert_fusion.1
  1058.4 22.3 fusion.25
  1080.7 16.5 copy.375
  1097.2 5.1 all-to-all-start.3
  1102.7 99.2 %all-to-all-done.3 = bf16[2,8,137,2048]{3,0,2,1:T(2,128)(2,1)} async-done(((bf16[2,8,137,2048]{3,0,2,1:T(2,128)(2,1)}), bf16[2,8,137,2048]{3,0,2,1:T(2,128)(2,1)}, u32[]{:S(2)}, u32[]{:S(2)}) %all-to-all-start.3) | async-done | bytes 8978464 | tf_op jit(solution)/shard_map/all_to_all | solution.py:56
  1201.8 11.4 copy.376
  1213.3 11.6 reshape.535
  1224.9 17.4 gather_fusion.3
  1242.3 31.9 fusion.146
  1274.2 6.2 multiply_reduce_fusion.2
  1280.9 13.1 fusion.81
  1295.9 11.5 fusion
  1307.3 14.5 fusion.9
  1327.1 8.2 fusion.92
  1338.4 19.8 bitcast_convert_fusion.1
  1358.3 26.4 bitcast_convert_fusion
  1402.8 5.3 copy.387
  1411.0 5.4 copy.390
  1417.1 7.1 multiply_bitcast_fusion
  1429.2 5.5 copy.386
  1438.3 5.8 pad_maximum_fusion.3
  1444.0 5.3 copy.389
  1452.5 11.3 multiply_reduce_fusion.1
  1464.9 13.3 fusion.138
  1479.7 15.0 fusion.75
  1495.4 11.4 fusion.57
  1511.6 14.2 fusion.153
  1531.2 46.2 %all-reduce.6 = (f32[2048]{0:T(1024)S(1)}, f32[128]{0:T(128)S(1)}, f32[128]{0:T(128)S(1)}, f32[2048]{0:T(1024)S(1)}) all-reduce(f32[2048]{0:T(1024)S(1)} %get-tuple-element.15, f32[128]{0:T(128)S(1)} %bitcast_reduce_fusion, f32[128]{0:T(128)S(1)} %bitcast_reduce_fusion.1, ...), channel_id=4, replica_groups=mesh['dp'=4,'ctx'=4,'expert'=2] {'dp','ctx','expert'}, use_global_device_ids=true, to_apply=%region_30.31.clone | all-reduce | flops 4352 | bytes 34816
  1582.7 38.2 %reduce-scatter.26.cloned.1.call-done = bf16[2,192,2048]{2,1,0:T(8,128)(2,1)} async-done(((bf16[2,768,2048]{2,1,0:T(8,128)(2,1)}), bf16[2,192,2048]{2,1,0:T(8,128)(2,1)}) %reduce-scatter.26.cloned.1.call-update) | async-done | bytes 1572880 | tf_op jit(solution)/shard_map/reduce_scatter | solution.py:257
  1624.4 211.4 %reduce-scatter.24.cloned.1.call-done = bf16[2,512,1536]{2,1,0:T(8,128)(2,1)} async-done(((bf16[2,2048,1536]{2,1,0:T(8,128)(2,1)}), bf16[2,512,1536]{2,1,0:T(8,128)(2,1)}) %reduce-scatter.24.cloned.1.call-update) | async-done | bytes 3145744 | tf_op jit(solution)/shard_map/reduce_scatter | solution.py:254
  1835.8 5.5 convert_element_type.269
  1841.3 139.9 %reduce-scatter.18.cloned.1.call-done = f32[64,512]{1,0:T(8,128)} async-done(((f32[2048,512]{1,0:T(8,128)}), f32[64,512]{1,0:T(8,128)}) %reduce-scatter.18.cloned.1.call-update) | async-done | bytes 131088 | tf_op jit(solution)/shard_map/reduce_scatter | solution.py:341
  1981.2 141.1 %reduce-scatter.20.cloned.1.call-done = f32[64,512]{1,0:T(8,128)} async-done(((f32[2048,512]{1,0:T(8,128)}), f32[64,512]{1,0:T(8,128)}) %reduce-scatter.20.cloned.1.call-update) | async-done | bytes 131088 | tf_op jit(solution)/shard_map/reduce_scatter | solution.py:342
  2122.3 705.8 %reduce-scatter.16.cloned.1.call-done = f32[64,4096]{1,0:T(8,128)} async-done(((f32[2048,4096]{1,0:T(8,128)}), f32[64,4096]{1,0:T(8,128)}) %reduce-scatter.16.cloned.1.call-update) | async-done | bytes 1048592 | tf_op jit(solution)/shard_map/reduce_scatter | solution.py:340
  2828.1 710.3 %reduce-scatter.22.cloned.1.call-done = f32[128,2048]{1,0:T(8,128)} async-done(((f32[4096,2048]{1,0:T(8,128)}), f32[128,2048]{1,0:T(8,128)}) %reduce-scatter.22.cloned.1.call-update) | async-done | bytes 1048592 | tf_op jit(solution)/shard_map/reduce_scatter | solution.py:347
  (345 shorter events, 132.6 us)
Async XLA Ops:
  7.2 695.9 %copy-start = (bf16[2048,16]{0,1:T(8,128)(2,1)S(1)}, bf16[2048,16]{0,1:T(8,128)(2,1)}, u32[]{:S(2)}) copy-start(bf16[2048,16]{0,1:T(8,128)(2,1)} %param.23) | copy-start | bytes 196612
  7.2 38.2 %all-gather.7.cloned.1.call-start = ((), (), s32[]{:S(2)}) async-start(), calls=%async_computation.14 | async-start | bytes 3145728 | tf_op jit(solution)/shard_map/all_gather | solution.py:88
  7.9 72.2 %all-gather.5.cloned.1.call-start = ((), (), s32[]{:S(2)}) async-start(), calls=%async_computation.13 | async-start | bytes 3145728 | tf_op jit(solution)/shard_map/all_gather | solution.py:89
  8.7 271.9 %all-gather.9.cloned.1.call-start = ((), (), s32[]{:S(2)}) async-start(), calls=%async_computation.15 | async-start | bytes 25165824 | tf_op jit(solution)/shard_map/all_gather | solution.py:87
  9.4 471.5 %all-gather.11.cloned.1.call-start = ((), (), s32[]{:S(2)}) async-start(), calls=%async_computation.16 | async-start | bytes 25165824 | tf_op jit(solution)/shard_map/all_gather | solution.py:90
  10.0 13.7 copy-start.6
  10.0 35.4 copy-start.53
  11.1 34.3 copy-start.42
  11.1 34.3 copy-start.47
  11.2 37.9 %copy-start.45 = (f32[192,128]{1,0:T(8,128)}, f32[192,128]{1,0:T(8,128)S(1)}, u32[]{:S(2)}) copy-start(f32[192,128]{1,0:T(8,128)S(1)} %copy.347) | copy-start | bytes 294916
  11.4 37.8 %copy-start.38 = (f32[192,128]{1,0:T(8,128)}, f32[192,128]{1,0:T(8,128)S(1)}, u32[]{:S(2)}) copy-start(f32[192,128]{1,0:T(8,128)S(1)} %copy.346) | copy-start | bytes 294916
  16.8 6.3 copy-start.78
  24.5 256.1 %copy-start.73 = (f32[192]{0:T(256)}, f32[192]{0:T(256)S(1)}, u32[]{:S(2)}) copy-start(f32[192]{0:T(256)S(1)} %get-tuple-element.89) | copy-start | bytes 2308
  49.5 269.0 %copy-start.50 = (bf16[64,4,128]{2,0,1:T(8,128)(2,1)}, bf16[64,4,128]{2,0,1:T(8,128)(2,1)S(1)}, u32[]{:S(2)}) copy-start(bf16[64,4,128]{2,0,1:T(8,128)(2,1)S(1)} %slice.212) | copy-start | bytes 196612
  56.7 261.8 %copy-start.34 = (bf16[512,4,128]{2,0,1:T(8,128)(2,1)}, bf16[512,4,128]{2,0,1:T(8,128)(2,1)S(1)}, u32[]{:S(2)}) copy-start(bf16[512,4,128]{2,0,1:T(8,128)(2,1)S(1)} %all_gather.21) | copy-start | bytes 1572868
  321.8 5.5 copy-start.1
  321.9 5.8 copy-start.56
  321.9 5.8 copy-start.40
  321.9 5.8 copy-start.62
  333.0 155.8 %copy-start.30 = (bf16[192,4,8,128]{3,2,1,0:T(8,128)(2,1)}, bf16[192,4,8,128]{3,2,1,0:T(8,128)(2,1)S(1)}, u32[]{:S(2)}) copy-start(bf16[192,4,8,128]{3,2,1,0:T(8,128)(2,1)S(1)} %copy.354) | copy-start | bytes 4718596
  480.9 9.1 copy-start.76
  489.6 10.5 copy-start.81
  490.2 212.9 %copy-start.23 = (bf16[192,2048]{1,0:T(8,128)(2,1)}, bf16[192,2048]{1,0:T(8,128)(2,1)S(1)}, u32[]{:S(2)}) copy-start(bf16[192,2048]{1,0:T(8,128)(2,1)S(1)} %multiply_convert_fusion.3) | copy-start | bytes 2359300
  528.3 151.5 %slice-start.1 = ((s8[6291456]{0:T(1024)(128)(4,1)}), s8[4194304]{0:T(1024)(128)(4,1)S(1)}, s32[]{:S(2)}) async-start(s8[6291456]{0:T(1024)(128)(4,1)} %bitcast.427), calls=%async_computation.27 | async-start | bytes 8388608
  640.5 39.3 %slice-start.2 = ((s8[6291456]{0:T(1024)(128)(4,1)}), s8[2097152]{0:T(1024)(128)(4,1)S(1)}, s32[]{:S(2)}) async-start(s8[6291456]{0:T(1024)(128)(4,1)} %bitcast.427), calls=%async_computation.28 | async-start | bytes 4194304
  679.8 8.0 copy-start.36
  696.4 5.2 copy-start.61
  696.4 5.4 copy-start.31
  696.4 104.7 %all-to-all-start.1 = ((bf16[2,8,137,2048]{3,0,2,1:T(2,128)(2,1)}), bf16[2,8,137,2048]{3,0,2,1:T(2,128)(2,1)}, u32[]{:S(2)}, u32[]{:S(2)}) async-start(bf16[2,8,137,2048]{3,0,2,1:T(2,128)(2,1)} %copy.362), calls=%async_computation.1 | async-start | bytes 17956864 | tf_op jit(solution)/shard_map/all_to_all | solution.py:56
  873.3 4.8 copy-start.15
  873.3 4.8 copy-start.16
  873.3 4.8 copy-start.17
  873.4 4.8 copy-start.18
  873.4 4.8 copy-start.19
  873.4 5.0 copy-start.33
  878.2 224.4 %copy-start.68 = (f32[192,8]{0,1:T(8,128)}, f32[192,8]{0,1:T(8,128)S(1)}, u32[]{:S(2)}) copy-start(f32[192,8]{0,1:T(8,128)S(1)} %get-tuple-element.30) | copy-start | bytes 18436
  1097.2 5.4 copy-start.57
  1097.2 5.4 copy-start.65
  1097.2 104.7 %all-to-all-start.3 = ((bf16[2,8,137,2048]{3,0,2,1:T(2,128)(2,1)}), bf16[2,8,137,2048]{3,0,2,1:T(2,128)(2,1)}, u32[]{:S(2)}, u32[]{:S(2)}) async-start(bf16[2,8,137,2048]{3,0,2,1:T(2,128)(2,1)} %copy.375), calls=%async_computation.3 | async-start | bytes 17956864 | tf_op jit(solution)/shard_map/all_to_all | solution.py:56
  1102.3 284.3 %reduce-scatter.12.cloned.1.call-start = ((), (), s32[]{:S(2)}) async-start(), calls=%async_computation.17 | async-start | bytes 655360 | tf_op jit(solution)/shard_map/reduce_scatter | solution.py:298
  1242.3 31.9 copy-start.14
  1242.3 31.9 copy-start.77
  1242.3 31.9 copy-start.82
  1274.2 6.2 copy-start.90
  1280.9 13.1 copy-start.11
  1307.3 14.5 copy-start.10
  1327.1 68.5 %reduce-scatter.14.cloned.1.call-start = ((), (), s32[]{:S(2)}) async-start(), calls=%async_computation.18 | async-start | bytes 655360 | tf_op jit(solution)/shard_map/reduce_scatter | solution.py:301
  1336.2 173.9 %reduce-scatter.28.cloned.1.call-start = ((), (), s32[]{:S(2)}) async-start(), calls=%async_computation.25 | async-start | bytes 1081344
  1338.4 282.6 %reduce-scatter.26.cloned.1.call-start = ((), (), s32[]{:S(2)}) async-start(), calls=%async_computation.24 | async-start | bytes 7864320 | tf_op jit(solution)/shard_map/reduce_scatter | solution.py:257
  1358.2 477.6 %reduce-scatter.24.cloned.1.call-start = ((), (), s32[]{:S(2)}) async-start(), calls=%async_computation.23 | async-start | bytes 15728640 | tf_op jit(solution)/shard_map/reduce_scatter | solution.py:254
  1384.7 596.5 %reduce-scatter.18.cloned.1.call-start = ((), (), s32[]{:S(2)}) async-start(), calls=%async_computation.20 | async-start | bytes 4325376 | tf_op jit(solution)/shard_map/reduce_scatter | solution.py:341
  1394.6 727.8 %reduce-scatter.20.cloned.1.call-start = ((), (), s32[]{:S(2)}) async-start(), calls=%async_computation.21 | async-start | bytes 4325376 | tf_op jit(solution)/shard_map/reduce_scatter | solution.py:342
  1399.4 1428.7 %reduce-scatter.16.cloned.1.call-start = ((), (), s32[]{:S(2)}) async-start(), calls=%async_computation.19 | async-start | bytes 34603008 | tf_op jit(solution)/shard_map/reduce_scatter | solution.py:340
  1402.8 5.3 copy-start.84
  1402.8 5.9 copy-start.59
  1411.0 5.4 copy-start.67
  1411.0 6.1 copy-start.35
  1411.0 6.1 copy-start.51
  1429.2 5.5 copy-start.5
  1429.2 5.6 copy-start.48
  1444.0 5.3 copy-start.66
  1478.3 2060.1 %reduce-scatter.22.cloned.1.call-start = ((), (), s32[]{:S(2)}) async-start(), calls=%async_computation.22 | async-start | bytes 34603008 | tf_op jit(solution)/shard_map/reduce_scatter | solution.py:347
  1511.6 14.2 copy-start.88
  1529.0 50.8 %copy-start.89 = (f32[192]{0:T(256)S(1)}, f32[192]{0:T(256)}, u32[]{:S(2)}) copy-start(f32[192]{0:T(256)} %get-tuple-element.88) | copy-start | bytes 2308
  (45 other events, 104.5 us)
Sparse Core Ops, SparseCore 0:
  9.6 35.8 all-gather.6
  47.0 33.1 all-gather.4
  81.7 198.8 all-gather.8
  282.0 198.8 all-gather.10
  1327.2 21.6 reduce-scatter.11
  1351.3 21.6 reduce-scatter.13
  1375.3 134.7 reduce-scatter.27
  1513.1 107.8 reduce-scatter.25
  1623.4 212.3 reduce-scatter.23
  1838.6 142.5 reduce-scatter.17
  1984.2 138.1 reduce-scatter.19
  2125.2 702.8 reduce-scatter.15
  2831.1 707.2 reduce-scatter.21
where the time goes:
time: 3550 us
  waiting for transfers between devices  2520 us (71%)
  local copies, waits for them, and re-layouts  359 us (10%)
  blocking collectives  277 us (8%)
  matrix products  267 us (8%)
  other arithmetic  97.4 us (3%)
    reduce_scatter x1, waiting for transfers between devices, body(): lax.psum_scatter(output_local, ('dp', 'ctx', 'expert'), scatter_dimension...  710 us
    reduce_scatter x1, waiting for transfers between devices, body(): lax.psum_scatter(query_local, ('dp', 'ctx', 'expert'), scatter_dimension=...  706 us
    reduce_scatter x1, waiting for transfers between devices, body(): lax.psum_scatter(gate_up_local.astype(jnp.bfloat16), 'dp', scatter_dimens...  211 us
    all_gather x1, waiting for transfers between devices, body(): lax.all_gather(query_weight, 'expert', axis=0, tiled=True)  190 us
    all_to_all x2, waiting for transfers between devices, move_rows(): lax.all_to_all(slot_block, ('ctx', 'expert'), split_axis=1, concat_axis=1...  184 us
    all_gather x1, waiting for transfers between devices, body(): lax.all_gather(output_weight, 'expert', axis=0, tiled=True)  148 us
    reduce_scatter x1, waiting for transfers between devices, body(): lax.psum_scatter(value_local, ('dp', 'ctx', 'expert'), scatter_dimension=...  141 us
    reduce_scatter x1, waiting for transfers between devices, body(): lax.psum_scatter(key_local, ('dp', 'ctx', 'expert'), scatter_dimension=0,...  140 us
  transfers between devices with their start and end apart: 15, of which 13 were waited for; matrix products, arithmetic and copies ran while one was open for 8% of the time, Pallas kernels for 0%

commit v1 on v0

v1 whole, which is shorter than its diff:
```python
import math

import jax
import jax.numpy as jnp
from jax import lax
from jax.sharding import PartitionSpec as P

MODEL_WIDTH = 2048
QUERY_HEADS = 32
KEY_VALUE_HEADS = 4
HEAD_SIZE = 128
TOP = 8
PROMPT_DEV = 128


highest = lax.Precision.HIGHEST
epsilon = 1e-06
rope_base = 1000000.0
masked = -1e30
every = ("dp", "ctx", "expert")
plane = ("ctx", "expert")
bf16 = jnp.bfloat16
f32 = jnp.float32


def rms_scale(value_rows):
    return lax.rsqrt(jnp.mean(value_rows * value_rows, axis=-1, keepdims=True) + epsilon)


def norm_back(inputs, inv_rms, norm_gain, gradient):
    weighted = gradient * norm_gain
    return inv_rms * weighted - inputs * inv_rms**3 * jnp.mean(
        weighted * inputs, axis=-1, keepdims=True
    )


def angles(position, head_width):
    freq_index = jnp.arange(head_width // 2, dtype=f32)
    inverse = jnp.exp(-(2.0 * freq_index / head_width) * math.log(rope_base))
    rope_angle = position.astype(f32)[:, None] * inverse[None, :]
    rope_angle = jnp.concatenate([rope_angle, rope_angle], axis=-1)
    return (jnp.cos(rope_angle), jnp.sin(rope_angle))


def rotate(value_rows, cosine, rope_sine):
    half_width = value_rows.shape[-1] // 2
    turned = jnp.concatenate([-value_rows[..., half_width:], value_rows[..., :half_width]], axis=-1)
    return value_rows * cosine + turned * rope_sine


def rotate_back(gradient, cosine, rope_sine):
    shifted = gradient * rope_sine
    half_width = gradient.shape[-1] // 2
    return gradient * cosine + jnp.concatenate(
        [shifted[..., half_width:], -shifted[..., :half_width]], axis=-1
    )


def small_plane():
    return lax.axis_size("ctx") == 4 and lax.axis_size("expert") == 2


def swap(v, axis, bit):
    return lax.ppermute(v, axis, [(i, i ^ bit) for i in range(lax.axis_size(axis))])


def core(v):
    return swap(v, "ctx", 1)


def over_x(v):
    return swap(v, "ctx", 2)


def over_y(v):
    return swap(v, "expert", 1)


def relative():
    count = lax.axis_size(plane)
    me = lax.axis_index(plane)
    if small_plane():
        return [me ^ r for r in range(count)]
    return list(range(count))


def gather_plane(v):
    if not small_plane():
        out = lax.all_gather(v, plane, axis=0, tiled=False)
        return [out[i] for i in range(out.shape[0])]
    half = v.shape[0] // 2
    vy, vx, vc = over_y(v), over_x(v), core(v)
    top, low = over_x(vy[:half]), over_y(vx[half:])
    vyc, vxc = core(vy), core(vx)
    vxy = jnp.concatenate([top, low], axis=0)
    vxyc = jnp.concatenate([core(top), core(low)], axis=0)
    return [v, vy, vc, vyc, vx, vxy, vxc, vxyc]


def scatter_plane(blocks):
    if not small_plane():
        return lax.psum_scatter(
            jnp.concatenate(blocks, axis=0), plane, scatter_dimension=0, tiled=True
        )
    half = blocks[0].shape[0] // 2

    def add(a, b):
        return (a.astype(f32) + b.astype(f32)).astype(bf16)

    here = {}
    for r in (5, 4, 1, 0):
        here[r] = add(blocks[r], core(blocks[r ^ 2]))
    from_x = over_x(here[5][:half])
    from_y = over_y(here[5][half:])
    y_part = jnp.concatenate([add(here[1][:half], from_x), here[1][half:]], axis=0)
    x_part = jnp.concatenate([here[4][:half], add(here[4][half:], from_y)], axis=0)
    return here[0].astype(f32) + over_x(x_part).astype(f32) + over_y(y_part).astype(f32)


def exchange_plane(blocks):
    if not small_plane():
        out = lax.all_to_all(jnp.stack(blocks), plane, split_axis=0, concat_axis=0, tiled=True)
        return [out[i] for i in range(out.shape[0])]
    out = [blocks[0]]
    for r in range(1, 8):
        pairs = [(i, i ^ r) for i in range(8)]
        out.append(lax.ppermute(blocks[r], plane, pairs))
    return out


def piece_starts(total):
    if not small_plane():
        return [(0, total)]
    half, quarter = total // 2, total // 8
    mine = lax.axis_index("expert") * half
    other = half - mine
    member = lax.axis_index("ctx")
    return [(mine, half)] + [(other + (member ^ j) * quarter, quarter) for j in range(4)]


def fetch(weight):
    if not small_plane():
        return lax.all_gather(weight, "expert", axis=0, tiled=True)
    quarter = weight.shape[0] // 4
    member = lax.axis_index("ctx")
    mine = lax.dynamic_slice_in_dim(weight, member * quarter, quarter, axis=0)
    first = over_y(mine)
    second = core(first)
    third = over_x(first)
    fourth = core(third)
    return jnp.concatenate([weight, first, second, third, fourth], axis=0)


def reorder(v, axis):
    total = v.shape[axis]
    return jnp.concatenate(
        [
            lax.dynamic_slice_in_dim(v, start, size, axis=axis)
            for start, size in piece_starts(total)
        ],
        axis=axis,
    )


def restore(v, axis):
    total = v.shape[axis]
    out = jnp.zeros_like(v)
    at = 0
    for start, size in piece_starts(total):
        piece = lax.slice_in_dim(v, at, at + size, axis=axis)
        out = lax.dynamic_update_slice_in_dim(out, piece, start, axis=axis)
        at += size
    return out


def ctx_blocks(v):
    count = lax.axis_size("ctx")
    member = lax.axis_index("ctx")
    if count != 4:
        out = lax.all_gather(v, "ctx", axis=0, tiled=False)
        return [out[i] for i in range(count)], [jnp.int32(i) for i in range(count)]
    vc, vx = core(v), over_x(v)
    return [v, vc, vx, core(vx)], [member ^ j for j in range(4)]


def ctx_sum(blocks):
    count = lax.axis_size("ctx")
    if count != 4:
        return lax.psum_scatter(
            jnp.concatenate(blocks, axis=0), "ctx", scatter_dimension=0, tiled=True
        ).astype(f32)
    near = blocks[0].astype(f32) + core(blocks[1]).astype(f32)
    far = (blocks[2].astype(f32) + core(blocks[3]).astype(f32)).astype(bf16)
    return near + over_x(far).astype(f32)


def body(
    hidden_in,
    attn_gain,
    query_weight,
    key_matrix,
    value_matrix,
    query_gain,
    key_gain,
    output_weight,
    ffn_gain,
    router_weight,
    gate_up,
    down_proj,
    routes,
    out_grad,
):
    ctx_count = lax.axis_size("ctx")
    spread_count = lax.axis_size(plane)
    dp_count = lax.axis_size("dp")
    device_count = dp_count * spread_count
    local_experts = gate_up.shape[0]
    count_of_rows = hidden_in.shape[0]
    prompt_all = PROMPT_DEV * ctx_count
    heads_per_group = QUERY_HEADS // KEY_VALUE_HEADS
    score_scale = HEAD_SIZE ** (-0.5)
    hidden_ff = gate_up.shape[2] // 2
    full_query, full_key, full_value, full_output = (
        fetch(query_weight),
        fetch(key_matrix),
        fetch(value_matrix),
        fetch(output_weight),
    )
    order = relative()
    g_rows = jnp.concatenate(gather_plane(out_grad), axis=0)
    route_rows = jnp.concatenate(gather_plane(routes), axis=0)

    inputs = hidden_in.astype(f32)
    scale_in = rms_scale(inputs)
    normalized_input = (inputs * scale_in * attn_gain).astype(bf16)
    normed_reordered = reorder(normalized_input, 1)
    query_pre = jnp.dot(normed_reordered, full_query, preferred_element_type=f32).reshape(
        count_of_rows, QUERY_HEADS, HEAD_SIZE
    )
    key_before_norm = jnp.dot(normed_reordered, full_key, preferred_element_type=f32).reshape(
        count_of_rows, KEY_VALUE_HEADS, HEAD_SIZE
    )
    value_low = (
        jnp.dot(normed_reordered, full_value, preferred_element_type=f32)
        .astype(bf16)
        .reshape(count_of_rows, KEY_VALUE_HEADS, HEAD_SIZE)
    )
    query_inv = rms_scale(query_pre)
    key_inv = rms_scale(key_before_norm)
    member = lax.axis_index("ctx")
    offsets = jnp.arange(count_of_rows, dtype=jnp.int32)
    position = jnp.where(
        offsets < PROMPT_DEV, member * PROMPT_DEV + offsets, prompt_all + offsets - PROMPT_DEV
    )
    cosine, rope_sine = angles(position, HEAD_SIZE)
    cosine = cosine[:, None, :]
    rope_sine = rope_sine[:, None, :]
    query_reduced = rotate(query_pre * query_inv * query_gain, cosine, rope_sine).astype(bf16)
    key_low = rotate(key_before_norm * key_inv * key_gain, cosine, rope_sine).astype(bf16)
    pair_blocks, members = ctx_blocks(
        jnp.stack([key_low[:PROMPT_DEV], value_low[:PROMPT_DEV]])
    )
    keys_all = jnp.concatenate([b[0] for b in pair_blocks] + [key_low[PROMPT_DEV:]], axis=0)
    values_all = jnp.concatenate([b[1] for b in pair_blocks] + [value_low[PROMPT_DEV:]], axis=0)
    prompt_offsets = jnp.arange(PROMPT_DEV, dtype=jnp.int32)
    key_position = jnp.concatenate(
        [m * PROMPT_DEV + prompt_offsets for m in members]
        + [prompt_all + jnp.arange(count_of_rows - PROMPT_DEV, dtype=jnp.int32)]
    )
    visible = key_position[None, :] <= position[:, None]
    grouped_queries = query_reduced.reshape(
        count_of_rows, KEY_VALUE_HEADS, heads_per_group, HEAD_SIZE
    )

    def scores_of():
        raw_scores = (
            jnp.einsum("rkgd,skd->kgrs", grouped_queries, keys_all, preferred_element_type=f32)
            * score_scale
        )
        return jnp.where(visible, raw_scores, masked)

    scores = scores_of()
    row_max = jnp.max(scores, axis=-1, keepdims=True)
    weights = jnp.exp(scores - row_max)
    row_total = jnp.sum(weights, axis=-1, keepdims=True)
    log_total = row_max + jnp.log(row_total)
    attention = (weights / row_total).astype(bf16)
    attended = (
        jnp.einsum("kgrs,skd->rkgd", attention, values_all, preferred_element_type=f32)
        .reshape(count_of_rows, QUERY_HEADS * HEAD_SIZE)
        .astype(bf16)
    )
    residual = inputs + jnp.dot(reorder(attended, 1), full_output, preferred_element_type=f32)
    scale_ffn = rms_scale(residual)
    ffn_in = (residual * scale_ffn * ffn_gain).astype(bf16)

    rows = jnp.concatenate(gather_plane(ffn_in), axis=0)
    expert_count = local_experts * spread_count
    expert_ids = jnp.arange(expert_count, dtype=jnp.int32)

    def gates_of(some_rows, some_routes):
        logits = jnp.dot(some_rows, router_weight, preferred_element_type=f32)
        chosen = jnp.any(some_routes[:, :, None] == expert_ids[None, None, :], axis=1)
        logits = jnp.where(chosen, logits, masked)
        raised = jnp.where(
            chosen, jnp.exp(logits - jnp.max(logits, axis=-1, keepdims=True)), 0.0
        )
        return raised / jnp.sum(raised, axis=-1, keepdims=True)

    gates_all = gates_of(rows, route_rows)
    first_expert = lax.axis_index(plane) * local_experts
    gates_mine = lax.dynamic_slice_in_dim(gates_all, first_expert, local_experts, axis=1)
    moe_part = 0.0
    row_part = 0.0
    gate_grads = []
    gate_up_local = []
    down_local = []
    for which in range(local_experts):
        gate = gates_mine[:, which : which + 1]
        projected = jnp.dot(rows, gate_up[which], preferred_element_type=f32)
        back = jnp.dot(g_rows, down_proj[which].T, preferred_element_type=f32)
        gate_part = projected[:, :hidden_ff]
        up_part = projected[:, hidden_ff:]
        sigmoid_gate = jax.nn.sigmoid(gate_part)
        hidden = gate_part * sigmoid_gate * up_part
        gate_grads.append(jnp.sum(hidden * back, axis=-1))
        hidden_low = (gate * hidden).astype(bf16)
        hidden_back = gate * back
        gate_back = hidden_back * up_part * sigmoid_gate * (1.0 + gate_part * (1.0 - sigmoid_gate))
        up_back = hidden_back * gate_part * sigmoid_gate
        projected_grad = jnp.concatenate([gate_back, up_back], axis=-1).astype(bf16)
        moe_part = moe_part + jnp.dot(hidden_low, down_proj[which], preferred_element_type=f32)
        row_part = row_part + jnp.dot(
            projected_grad, gate_up[which].T, preferred_element_type=f32
        )
        gate_up_local.append(jnp.dot(rows.T, projected_grad, preferred_element_type=f32))
        down_local.append(jnp.dot(hidden_low.T, g_rows, preferred_element_type=f32))
    gate_up_grad, down_grad = (
        lax.psum_scatter(
            jnp.stack(gate_up_local).astype(bf16), "dp", scatter_dimension=1, tiled=True
        ).astype(f32),
        lax.psum_scatter(
            jnp.stack(down_local).astype(bf16), "dp", scatter_dimension=1, tiled=True
        ).astype(f32),
    )

    def blocks_of(v):
        return [
            v[i * count_of_rows : (i + 1) * count_of_rows] for i in range(spread_count)
        ]

    moe_sum = scatter_plane(blocks_of(moe_part.astype(bf16)))
    block_out = (residual + moe_sum).astype(bf16)
    back_sum = scatter_plane(blocks_of(row_part.astype(bf16)))
    gate_grad_blocks = exchange_plane(blocks_of(jnp.stack(gate_grads, axis=1)))
    gate_grad = jnp.zeros((count_of_rows, expert_count), f32)
    for r in range(spread_count):
        gate_grad = lax.dynamic_update_slice_in_dim(
            gate_grad, gate_grad_blocks[r], order[r] * local_experts, axis=1
        )
    gates = gates_of(ffn_in, routes)
    logit_grad = gates * (gate_grad - jnp.sum(gates * gate_grad, axis=-1, keepdims=True))

    grad_out = out_grad.astype(f32)
    router_local = jnp.dot(ffn_in.T, logit_grad, preferred_element_type=f32)
    ffn_in_grad = back_sum + jnp.dot(
        logit_grad, router_weight.astype(f32).T, precision=highest
    )
    residual_grad = grad_out + norm_back(residual, scale_ffn, ffn_gain, ffn_in_grad)
    ffn_gain_local = jnp.sum(ffn_in_grad * residual * scale_ffn, axis=0)
    branch_low = residual_grad.astype(bf16)
    branch_rows = jnp.concatenate(gather_plane(branch_low), axis=0)
    attended_grad = restore(
        jnp.dot(branch_low, full_output.T, preferred_element_type=f32).astype(bf16), 1
    ).reshape(count_of_rows, KEY_VALUE_HEADS, heads_per_group, HEAD_SIZE)
    attention_again = jnp.exp(scores_of() - log_total)
    prob_grad = jnp.einsum(
        "rkgd,skd->kgrs", attended_grad, values_all, preferred_element_type=f32
    )
    row_delta = jnp.sum(attention_again * prob_grad, axis=-1, keepdims=True)
    score_grad = (attention_again * (prob_grad - row_delta)).astype(bf16)
    query_grad = (
        jnp.einsum("kgrs,skd->rkgd", score_grad, keys_all, preferred_element_type=f32)
        * score_scale
    ).reshape(count_of_rows, QUERY_HEADS, HEAD_SIZE)
    key_grad_all = (
        jnp.einsum("kgrs,rkgd->skd", score_grad, grouped_queries, preferred_element_type=f32)
        * score_scale
    )
    value_grad_all = jnp.einsum(
        "kgrs,rkgd->skd",
        attention_again.astype(bf16),
        attended_grad,
        preferred_element_type=f32,
    )
    pair_grads = jnp.stack([key_grad_all[:prompt_all], value_grad_all[:prompt_all]]).astype(bf16)
    prompt_grads = ctx_sum(
        [pair_grads[:, i * PROMPT_DEV : (i + 1) * PROMPT_DEV] for i in range(ctx_count)]
        if ctx_count == 4
        else [pair_grads]
    )
    key_grad = jnp.concatenate([prompt_grads[0], key_grad_all[prompt_all:]], axis=0)
    value_gradient = jnp.concatenate([prompt_grads[1], value_grad_all[prompt_all:]], axis=0)
    query_rot_grad = rotate_back(query_grad, cosine, rope_sine)
    key_rot_grad = rotate_back(key_grad, cosine, rope_sine)
    query_gain_local = jnp.sum(query_rot_grad * query_pre * query_inv, axis=(0, 1))
    key_gain_local = jnp.sum(key_rot_grad * key_before_norm * key_inv, axis=(0, 1))
    query_pre_grad = (
        norm_back(query_pre, query_inv, query_gain, query_rot_grad)
        .astype(bf16)
        .reshape(count_of_rows, QUERY_HEADS * HEAD_SIZE)
    )
    key_pre_grad = (
        norm_back(key_before_norm, key_inv, key_gain, key_rot_grad)
        .astype(bf16)
        .reshape(count_of_rows, KEY_VALUE_HEADS * HEAD_SIZE)
    )
    value_before_norm_gradient = value_gradient.astype(bf16).reshape(
        count_of_rows, KEY_VALUE_HEADS * HEAD_SIZE
    )
    normed_grad = jnp.dot(query_pre_grad, full_query.T, preferred_element_type=f32)
    normed_grad = normed_grad + jnp.dot(key_pre_grad, full_key.T, preferred_element_type=f32)
    normed_grad = normed_grad + jnp.dot(
        value_before_norm_gradient, full_value.T, preferred_element_type=f32
    )
    normed_grad = restore(normed_grad, 1)
    attn_gain_local = jnp.sum(normed_grad * inputs * scale_in, axis=0)
    hidden_grad = residual_grad + norm_back(inputs, scale_in, attn_gain, normed_grad)

    pre_rows = jnp.concatenate(
        gather_plane(
            jnp.concatenate([query_pre_grad, key_pre_grad, value_before_norm_gradient], axis=1)
        ),
        axis=0,
    )

    def owned(v):
        width = v.shape[1] // device_count
        split = v.reshape(count_of_rows, dp_count, spread_count, width)
        parts = [
            lax.dynamic_index_in_dim(split, o, axis=2, keepdims=False).reshape(
                count_of_rows, dp_count * width
            )
            for o in order
        ]
        return jnp.concatenate(exchange_plane(parts), axis=0)

    normed_owned = owned(normalized_input)
    attended_owned = owned(attended)
    pre_local = jnp.dot(normed_owned.T, pre_rows, preferred_element_type=f32)
    output_local = jnp.dot(attended_owned.T, branch_rows, preferred_element_type=f32)
    pre_sum = lax.psum_scatter(pre_local.astype(bf16), "dp", scatter_dimension=0, tiled=True).astype(
        f32
    )
    output_sum = lax.psum_scatter(
        output_local.astype(bf16), "dp", scatter_dimension=0, tiled=True
    ).astype(f32)
    wide = QUERY_HEADS * HEAD_SIZE
    narrow = KEY_VALUE_HEADS * HEAD_SIZE

    small = jnp.concatenate(
        [
            v.reshape(device_count, -1)
            for v in (
                attn_gain_local,
                ffn_gain_local,
                query_gain_local,
                key_gain_local,
                router_local,
            )
        ],
        axis=1,
    )
    small = lax.all_to_all(small[:, None], every, split_axis=0, concat_axis=0, tiled=True)
    small = jnp.sum(small[:, 0], axis=0)
    share = MODEL_WIDTH // device_count
    head_share = HEAD_SIZE // device_count
    cuts = [share, share, head_share, head_share, share * expert_count]
    ends = [sum(cuts[: i + 1]) for i in range(5)]
    a_grad, f_grad, q_grad, k_grad, r_grad = [
        small[end - cut : end] for end, cut in zip(ends, cuts)
    ]
    return (
        block_out,
        hidden_grad,
        a_grad,
        pre_sum[:, :wide],
        pre_sum[:, wide : wide + narrow],
        pre_sum[:, wide + narrow :],
        q_grad,
        k_grad,
        output_sum,
        f_grad,
        r_grad.reshape(share, expert_count),
        gate_up_grad,
        down_grad,
    )


def solution(mesh):
    placed = (
        P(("dp", "ctx", "expert"), None),
        P(),
        P("expert", None),
        P("expert", None),
        P("expert", None),
        P(),
        P(),
        P("expert", None),
        P(),
        P(),
        P(("ctx", "expert"), None, None),
        P(("ctx", "expert"), None, None),
        P(("dp", "ctx", "expert"), None),
        P(("dp", "ctx", "expert"), None),
    )
    return jax.shard_map(
        body,
        mesh=mesh,
        in_specs=placed,
        out_specs=(
            P(("dp", "ctx", "expert"), None),
            P(("dp", "ctx", "expert"), None),
            P(("dp", "ctx", "expert")),
            P(("dp", "ctx", "expert"), None),
            P(("dp", "ctx", "expert"), None),
            P(("dp", "ctx", "expert"), None),
            P(("dp", "ctx", "expert")),
            P(("dp", "ctx", "expert")),
            P(("dp", "ctx", "expert"), None),
            P(("dp", "ctx", "expert")),
            P(("dp", "ctx", "expert"), None),
            P(("ctx", "expert"), "dp", None),
            P(("ctx", "expert"), "dp", None),
        ),
        check_vma=False,
    )
```

time: 3550 us -> 1200 us (0.34)
  waiting for transfers between devices: 2520 us -> 526 us
  blocking collectives: 277 us -> 0 us
  local copies, waits for them, and re-layouts: 359 us -> 212 us
  starting transfers between devices: 11.2 us -> 83.5 us
    reduce_scatter x8 -> x4, waiting for transfers between devices: 1950 us -> 270 us  [the longest x1 211 us: body(): lax.psum_scatter(jnp.stack(gate_up_local).astype(bf16), 'dp', scatter_dim...]
    all_gather x4 -> x0, waiting for transfers between devices: 381 us -> none  [the longest x1 190 us: body(): lax.all_gather(query_weight, 'expert', axis=0, tiled=True)]
    ppermute x0 -> x104, waiting for transfers between devices: none -> 247 us  [the longest x83 217 us: swap(): lax.ppermute(v, axis, [(i, i ^ bit) for i in range(lax.axis_size(axis))])]
    all_to_all x2 -> x0, blocking collectives: 216 us -> none  [the longest x1 112 us: body(): lax.all_to_all(send_rows, ('ctx', 'expert'), split_axis=1, concat_axis=1,...]
    all_to_all x2 -> x1, waiting for transfers between devices: 184 us -> 8.93 us  [body(): lax.all_to_all(small[:, None], every, split_axis=0, concat_axis=0, tiled=...]
    unnamed x196 -> x324, local copies, waits for them, and re-layouts: 23.5 us -> 106 us
    gather x9 -> x0, local copies, waits for them, and re-layouts: 79.4 us -> none  [the longest x1 21.7 us: body(): jnp.concatenate([pair_low, jnp.zeros((1, MODEL_WIDTH), jnp.bfloat16)], ax...]
    ppermute x0 -> x104, starting transfers between devices: none -> 78 us  [the longest x83 59.4 us: swap(): lax.ppermute(v, axis, [(i, i ^ bit) for i in range(lax.axis_size(axis))])]
  transfers between devices with their start and end apart: 15 -> 109, of which waited for: 13 -> 38; matrix products, arithmetic and copies ran while one was open for 8% -> 39% of each run, Pallas kernels for 0% -> 0%
where the time goes in v1:
time: 1200 us; the launch traced here: 1190 us
  waiting for transfers between devices  526 us (44%)
  matrix products  251 us (21%)
  local copies, waits for them, and re-layouts  212 us (18%)
  other arithmetic  96.9 us (8%)
  starting transfers between devices  83.5 us (7%)
  between operations  16.6 us (1%)
    ppermute x83, waiting for transfers between devices, swap(): lax.ppermute(v, axis, [(i, i ^ bit) for i in range(lax.axis_size(axis))])  217 us
    reduce_scatter x1, waiting for transfers between devices, body(): lax.psum_scatter(jnp.stack(gate_up_local).astype(bf16), 'dp', scatter_dim...  211 us
    unnamed x324, local copies, waits for them, and re-layouts  106 us
    ppermute x83, starting transfers between devices, swap(): lax.ppermute(v, axis, [(i, i ^ bit) for i in range(lax.axis_size(axis))])  59.4 us
    reduce_scatter x1, waiting for transfers between devices, body(): lax.psum_scatter(jnp.stack(down_local).astype(bf16), 'dp', scatter_dimens...  58.5 us
    dot_general x2, matrix products, body(): jnp.dot(projected_grad, gate_up[which].T, preferred_element_type=f32)  31.3 us
    dot_general x2, matrix products, body(): projected = jnp.dot(rows, gate_up[which], preferred_element_type=f32)  30.4 us
    ppermute x21, waiting for transfers between devices, exchange_plane(): out.append(lax.ppermute(blocks[r], plane, pairs))  30.2 us
  transfers between devices with their start and end apart: 109, of which 38 were waited for; matrix products, arithmetic and copies ran while one was open for 39% of the time, Pallas kernels for 0%

profile of v1, /device:TPU:0, one launch (start us, length us, event | category | flops | bytes accessed | tf_op | source)
XLA Modules:
  0.0 1185.1 jit_solution(13814053817021564196)
XLA Ops:
  22.4 8.0 constant_dynamic-update-slice_fusion.29
  36.9 8.5 constant_dynamic-update-slice_fusion.34
  45.4 3.3 constant_dynamic-slice_fusion.9
  65.6 5.3 copy.216
  96.9 4.8 collective-permute-done.2
  130.0 20.6 %collective-permute-done.11 = bf16[256,4096]{1,0:T(8,128)(2,1)} collective-permute-done((bf16[256,4096]{1,0:T(8,128)(2,1)}, bf16[256,4096]{1,0:T(8,128)(2,1)}, u32[]{:S(2)}, u32[]{:S(2)}) %collective-permute-start.11) | collective-permute-done | bytes 2097184 | tf_op jit(solution)/shard_map/ppermute | solution.py:64
  155.8 39.7 %collective-permute-done.15 = bf16[512,2048]{1,0:T(8,128)(2,1)} collective-permute-done((bf16[512,2048]{1,0:T(8,128)(2,1)}, bf16[512,2048]{1,0:T(8,128)(2,1)}, u32[]{:S(2)}, u32[]{:S(2)}) %collective-permute-start.15) | collective-permute-done | bytes 2097184 | tf_op jit(solution)/shard_map/ppermute | solution.py:64
  199.1 3.7 collective-permute-done.50
  216.3 27.6 %collective-permute-done.17 = bf16[512,2048]{1,0:T(8,128)(2,1)} collective-permute-done((bf16[512,2048]{1,0:T(8,128)(2,1)}, bf16[512,2048]{1,0:T(8,128)(2,1)}, u32[]{:S(2)}, u32[]{:S(2)}) %collective-permute-start.17) | collective-permute-done | bytes 2097184 | tf_op jit(solution)/shard_map/ppermute | solution.py:64
  252.9 7.8 fusion.126
  260.6 3.7 copy.207
  270.9 3.4 copy.210
  274.3 3.4 copy.211
  283.0 3.3 fusion.122
  286.4 3.8 fusion.3
  291.8 5.4 fusion.46
  302.4 7.8 multiply_reduce_fusion.6
  325.4 5.3 copy.219
  332.0 4.2 collective-permute-done.88
  348.3 4.0 collective-permute-done.92
  356.5 3.7 collective-permute-done.94
  365.8 6.3 collective-permute-done.32
  378.9 16.1 %fusion.11 = f32[1536,1536]{0,1:T(8,128)} fusion(bf16[1536,2048]{1,0:T(8,128)(2,1)} %constant_dynamic-update-slice_fusion.35, bf16[2,2048,1536]{2,1,0:T(8,128)(2,1)} %param.24), kind=kOutput, calls=%fused_computation.24 | convolution fusion | flops 9663676416 | bytes 22020096 | tf_op jit(solution)/shard_map/dot_general | solution.py:320
  395.1 14.3 %fusion.15 = f32[1536,1536]{0,1:T(8,128)} fusion(bf16[1536,2048]{1,0:T(8,128)(2,1)S(1)} %copy-done.27, bf16[2,2048,1536]{2,1,0:T(8,128)(2,1)} %param.24), kind=kOutput, calls=%fused_computation.28 | convolution fusion | flops 9663676416 | bytes 22020096 | tf_op jit(solution)/shard_map/dot_general | solution.py:320
  411.3 10.9 multiply_convert_fusion.3
  422.2 8.1 fusion.35
  430.4 12.1 %multiply_convert_fusion.1 = (bf16[1536,768]{0,1:T(8,128)(2,1)}, bf16[1536,768]{0,1:T(8,128)(2,1)}, f32[1536]{0:T(1024)S(1)}, f32[1536,768]{0,1:T(8,128)}) fusion(f32[1536,1536]{0,1:T(8,128)} %fusion.11, f32[1536]{0:T(1024)S(1)} %get-tuple-element.82, bf16[1536,2048]{1,0:T(8,128)(2,1)S(1)} %bitcast.420, bf16[2,768,2048]{2,1,0:T(8,128)(2,1)S(1)} %bitcast.422), kind=kOutput, calls=%fused_computation.40 | convolution fusion | flops 4853070336 | bytes 28325888 | tf_op jit(solution)/shard_map/dot_general | solution.py:321
  443.8 15.7 %fusion.13 = f32[1536,2048]{1,0:T(8,128)} fusion(bf16[2,2048,1536]{2,1,0:T(8,128)(2,1)} %param.24, bf16[1536,768]{0,1:T(8,128)(2,1)} %get-tuple-element.102, bf16[1536,768]{0,1:T(8,128)(2,1)S(1)} %get-tuple-element.101), kind=kOutput, calls=%fused_computation.26 | convolution fusion | flops 9673113600 | bytes 23592960 | tf_op jit(solution)/shard_map/dot_general | solution.py:333
  459.5 15.7 %add_convert_fusion = bf16[1536,2048]{1,0:T(8,128)(2,1)S(1)} fusion(f32[1536,2048]{1,0:T(8,128)} %fusion.13, bf16[2,2048,1536]{2,1,0:T(8,128)(2,1)} %param.24, bf16[1536,768]{0,1:T(8,128)(2,1)} %get-tuple-element.100, bf16[1536,768]{0,1:T(8,128)(2,1)} %get-tuple-element.99), kind=kOutput, calls=%fused_computation.11 | convolution fusion | flops 9679405056 | bytes 29884416 | tf_op jit(solution)/shard_map/dot_general | solution.py:333
  477.3 10.4 add_convert_fusion.1
  506.1 8.7 collective-permute-done.57
  515.9 8.3 collective-permute-done.60
  526.8 9.6 collective-permute-done.43
  539.3 8.8 collective-permute-done.68
  551.7 15.9 %collective-permute-done.41 = bf16[192,2048]{1,0:T(8,128)(2,1)S(1)} collective-permute-done((bf16[192,2048]{1,0:T(8,128)(2,1)S(1)}, bf16[192,2048]{1,0:T(8,128)(2,1)S(1)}, u32[]{:S(2)}, u32[]{:S(2)}) %collective-permute-start.41) | collective-permute-done | bytes 786464 | tf_op jit(solution)/shard_map/ppermute | solution.py:64
  575.6 11.7 convolution_convert_fusion.3
  588.4 11.5 fusion
  599.9 14.4 %fusion.2 = (bf16[4,8,192,576]{3,2,1,0:T(8,128)(2,1)S(1)}, bf16[4,8,192,576]{3,2,1,0:T(8,128)(2,1)}) fusion(f32[4,576,192,8]{1,2,3,0:T(8,128)} %get-tuple-element.208, f32[4,8,192,576]{3,2,1,0:T(8,128)} %copy-done.2, f32[4,8,192]{2,1,0:T(8,128)S(1)} %get-tuple-element.207, f32[4,8,192]{2,1,0:T(8,128)S(1)} %copy-done.64), kind=kLoop, calls=%fused_computation.4 | loop fusion | flops 17694720 | bytes 42516480 | tf_op jit(solution)/shard_map/convert_element_type | solution.py:381
  616.5 3.6 fusion.62
  620.1 3.5 copy.217
  627.7 8.3 fusion.66
  639.4 3.8 pad_maximum_fusion.4
  643.1 3.5 copy.215
  646.7 5.5 copy.218
  657.5 11.9 %multiply_reduce_fusion.3 = (f32[4096]{0:T(1024)S(1)}, bf16[192,4096]{1,0:T(8,128)(2,1)}) fusion(f32[192,4096]{1,0:T(8,128)S(1)} %copy-done.19, f32[192,4096]{1,0:T(8,128)S(1)} %copy-done.7, f32[192,4096]{1,0:T(8,128)} %copy.218, f32[192,4096]{1,0:T(8,128)S(1)} %copy-done.18, f32[24,8,32,128]{3,2,1,0:T(8,128)} %bitcast.374, ...), kind=kLoop, calls=%fused_computation.85 | loop fusion | flops 8646656 | bytes 23625728 | tf_op jit(solution)/shard_map/reduce_sum | solution.py:406
  687.8 5.9 collective-permute-done.99
  694.6 38.2 %collective-permute-done.100 = bf16[96,2048]{1,0:T(8,128)(2,1)S(1)} collective-permute-done((bf16[96,2048]{1,0:T(8,128)(2,1)S(1)}, bf16[96,2048]{1,0:T(8,128)(2,1)S(1)}, u32[]{:S(2)}, u32[]{:S(2)}) %collective-permute-start.100) | collective-permute-done | bytes 393248 | tf_op jit(solution)/shard_map/ppermute | solution.py:64
  735.3 4.6 convolution_convert_fusion.6
  747.9 16.3 %collective-permute-done.83 = bf16[96,5120]{1,0:T(8,128)(2,1)S(1)} collective-permute-done((bf16[96,5120]{1,0:T(8,128)(2,1)S(1)}, bf16[96,5120]{1,0:T(8,128)(2,1)S(1)}, u32[]{:S(2)}, u32[]{:S(2)}) %collective-permute-start.83) | collective-permute-done | bytes 983072 | tf_op jit(solution)/shard_map/ppermute | solution.py:64
  777.4 11.8 convolution_convert_fusion.2
  789.3 8.7 fusion.40
  798.1 8.8 fusion.39
  806.9 3.3 pad_maximum_fusion.1
  811.8 13.2 %fusion.8 = bf16[1,2048,1536]{2,1,0:T(8,128)(2,1)S(1)} fusion(bf16[1536,2048]{1,0:T(8,128)(2,1)} %constant_dynamic-update-slice_fusion.35, bf16[1536,768]{0,1:T(8,128)(2,1)} %get-tuple-element.102, bf16[1536,768]{0,1:T(8,128)(2,1)S(1)} %copy-done.111), kind=kOutput, calls=%fused_computation.19 | convolution fusion | flops 9676259328 | bytes 17301504 | tf_op jit(solution)/shard_map/dot_general | solution.py:336
  825.0 12.1 %fusion.9 = bf16[1,2048,1536]{2,1,0:T(8,128)(2,1)S(1)} fusion(bf16[1536,2048]{1,0:T(8,128)(2,1)} %constant_dynamic-update-slice_fusion.35, bf16[1536,768]{0,1:T(8,128)(2,1)S(1)} %copy-done.113, bf16[1536,768]{0,1:T(8,128)(2,1)S(1)} %copy-done.112), kind=kOutput, calls=%fused_computation.20 | convolution fusion | flops 9676259328 | bytes 17301504 | tf_op jit(solution)/shard_map/dot_general | solution.py:336
  837.2 5.8 pad_maximum_fusion
  847.7 3.6 fusion.127
  853.3 13.9 %fusion.45 = f32[192,2048]{1,0:T(8,128)} fusion(f32[192,2048]{1,0:T(8,128)} %fusion.128, f32[192,2048]{1,0:T(8,128)} %fusion.127, bf16[192,4096]{1,0:T(8,128)(2,1)} %get-tuple-element.98, bf16[2048,4096]{1,0:T(8,128)(2,1)} %constant_dynamic-update-slice_fusion.25), kind=kOutput, calls=%fused_computation.95 | convolution fusion | flops 3222011904 | bytes 23068672 | tf_op jit(solution)/shard_map/dot_general | solution.py:421
  874.1 5.4 all-to-all-start
  882.6 8.9 all-to-all-done
  899.4 58.5 %reduce-scatter.11.cloned.1.call-done = bf16[2,192,2048]{2,1,0:T(8,128)(2,1)} async-done(((bf16[2,768,2048]{2,1,0:T(8,128)(2,1)}), bf16[2,192,2048]{2,1,0:T(8,128)(2,1)}) %reduce-scatter.11.cloned.1.call-update) | async-done | bytes 1572880 | tf_op jit(solution)/shard_map/reduce_scatter | solution.py:342
  957.9 3.5 convert_element_type.324
  961.4 211.2 %reduce-scatter.9.cloned.1.call-done = bf16[2,512,1536]{2,1,0:T(8,128)(2,1)} async-done(((bf16[2,2048,1536]{2,1,0:T(8,128)(2,1)}), bf16[2,512,1536]{2,1,0:T(8,128)(2,1)}) %reduce-scatter.9.cloned.1.call-update) | async-done | bytes 3145744 | tf_op jit(solution)/shard_map/reduce_scatter | solution.py:339
  1172.7 5.5 convert_element_type.323
  (714 shorter events, 313.5 us)
Async XLA Ops:
  7.2 886.4 %reduce-scatter.7.cloned.1.call-start = ((), (), s32[]{:S(2)}) async-start(), calls=%async_computation.6 | async-start | bytes 2621440 | tf_op jit(solution)/shard_map/reduce_scatter | solution.py:455
  7.2 47.2 %collective-permute-start.19 = (s32[192,8]{0,1:T(8,128)}, s32[192,8]{0,1:T(8,128)S(1)}, u32[]{:S(2)}, u32[]{:S(2)}) collective-permute-start(s32[192,8]{0,1:T(8,128)} %param.26), channel_id=1, source_target_pairs={{0,1},{1,0},{2,3},{3,2},{4,5},{5,4},{6,7},{7,6},{8,9},{9,8},{10,11... | collective-permute-start | bytes 18440 | tf_op jit(solution)/shard_map/ppermute | solution.py:64
  10.3 44.3 %collective-permute-start.22 = (s32[192,8]{0,1:T(8,128)}, s32[192,8]{0,1:T(8,128)}, u32[]{:S(2)}, u32[]{:S(2)}) collective-permute-start(s32[192,8]{0,1:T(8,128)} %param.26), channel_id=1, source_target_pairs={{0,4},{2,6},{4,0},{6,2},{1,5},{3,7},{5,1},{7,3},{8,12},{10,14},{12... | collective-permute-start | bytes 18440 | tf_op jit(solution)/shard_map/ppermute | solution.py:64
  11.8 47.8 %collective-permute-start.20 = (s32[192,8]{0,1:T(8,128)}, s32[192,8]{0,1:T(8,128)S(1)}, u32[]{:S(2)}, u32[]{:S(2)}) collective-permute-start(s32[192,8]{0,1:T(8,128)} %param.26), channel_id=1, source_target_pairs={{0,2},{2,0},{4,6},{6,4},{1,3},{3,1},{5,7},{7,5},{8,10},{10,8},{12,... | collective-permute-start | bytes 18440 | tf_op jit(solution)/shard_map/ppermute | solution.py:64
  13.4 66.4 %collective-permute-start.4 = (bf16[256,512]{1,0:T(8,128)(2,1)}, bf16[256,512]{1,0:T(8,128)(2,1)}, u32[]{:S(2)}, u32[]{:S(2)}) collective-permute-start(bf16[256,512]{1,0:T(8,128)(2,1)} %constant_dynamic-slice_fusion.11), channel_id=1, source_target_pairs={{0,1},{1,0},{2,3},{3,2},{4,5},{5,4},{6,7},{7,6},{8,9},{9,8},{10,11... | collective-permute-start | bytes 786440 | tf_op jit(solution)/shard_map/ppermute | solution.py:64
  59.6 29.9 %collective-permute-start = (bf16[256,512]{1,0:T(8,128)(2,1)}, bf16[256,512]{1,0:T(8,128)(2,1)}, u32[]{:S(2)}, u32[]{:S(2)}) collective-permute-start(bf16[256,512]{1,0:T(8,128)(2,1)} %constant_dynamic-slice_fusion.12), channel_id=1, source_target_pairs={{0,1},{1,0},{2,3},{3,2},{4,5},{5,4},{6,7},{7,6},{8,9},{9,8},{10,11... | collective-permute-start | bytes 786440 | tf_op jit(solution)/shard_map/ppermute | solution.py:64
  61.7 12.4 %collective-permute-start.73 = (bf16[192,256]{0,1:T(8,128)(2,1)}, bf16[192,256]{0,1:T(8,128)(2,1)}, u32[]{:S(2)}, u32[]{:S(2)}) collective-permute-start(bf16[192,256]{0,1:T(8,128)(2,1)} %bitcast.45), channel_id=1, source_target_pairs={{0,2},{1,3},{2,0},{3,1},{4,6},{5,7},{6,4},{7,5},{8,10},{9,11},{10,... | collective-permute-start | bytes 294920 | tf_op jit(solution)/shard_map/ppermute | solution.py:127
  79.8 12.4 %collective-permute-start.5 = (bf16[256,512]{1,0:T(8,128)(2,1)}, bf16[256,512]{1,0:T(8,128)(2,1)}, u32[]{:S(2)}, u32[]{:S(2)}) collective-permute-start(bf16[256,512]{1,0:T(8,128)(2,1)} %collective-permute-done.4), channel_id=1, source_target_pairs={{0,2},{2,0},{4,6},{6,4},{1,3},{3,1},{5,7},{7,5},{8,10},{10,8},{12,... | collective-permute-start | bytes 786440 | tf_op jit(solution)/shard_map/ppermute | solution.py:64
  81.2 12.6 %collective-permute-start.6 = (bf16[256,512]{1,0:T(8,128)(2,1)}, bf16[256,512]{1,0:T(8,128)(2,1)S(1)}, u32[]{:S(2)}, u32[]{:S(2)}) collective-permute-start(bf16[256,512]{1,0:T(8,128)(2,1)} %collective-permute-done.4), channel_id=1, source_target_pairs={{0,4},{2,6},{4,0},{6,2},{1,5},{3,7},{5,1},{7,3},{8,12},{10,14},{12... | collective-permute-start | bytes 786440 | tf_op jit(solution)/shard_map/ppermute | solution.py:64
  84.5 34.0 %collective-permute-start.45 = (bf16[192,2048]{1,0:T(8,128)(2,1)}, bf16[192,2048]{1,0:T(8,128)(2,1)}, u32[]{:S(2)}, u32[]{:S(2)}) collective-permute-start(bf16[192,2048]{1,0:T(8,128)(2,1)} %param.27), channel_id=1, source_target_pairs={{0,1},{1,0},{2,3},{3,2},{4,5},{5,4},{6,7},{7,6},{8,9},{9,8},{10,11... | collective-permute-start | bytes 2359304 | tf_op jit(solution)/shard_map/ppermute | solution.py:64
  86.6 37.8 %collective-permute-start.46 = (bf16[192,2048]{1,0:T(8,128)(2,1)}, bf16[192,2048]{1,0:T(8,128)(2,1)}, u32[]{:S(2)}, u32[]{:S(2)}) collective-permute-start(bf16[192,2048]{1,0:T(8,128)(2,1)} %param.27), channel_id=1, source_target_pairs={{0,2},{2,0},{4,6},{6,4},{1,3},{3,1},{5,7},{7,5},{8,10},{10,8},{12,... | collective-permute-start | bytes 2359304 | tf_op jit(solution)/shard_map/ppermute | solution.py:64
  96.4 22.4 %collective-permute-start.48 = (bf16[192,2048]{1,0:T(8,128)(2,1)}, bf16[192,2048]{1,0:T(8,128)(2,1)}, u32[]{:S(2)}, u32[]{:S(2)}) collective-permute-start(bf16[192,2048]{1,0:T(8,128)(2,1)} %param.27), channel_id=1, source_target_pairs={{0,4},{2,6},{4,0},{6,2},{1,5},{3,7},{5,1},{7,3},{8,12},{10,14},{12... | collective-permute-start | bytes 2359304 | tf_op jit(solution)/shard_map/ppermute | solution.py:64
  101.7 48.9 %collective-permute-start.11 = (bf16[256,4096]{1,0:T(8,128)(2,1)}, bf16[256,4096]{1,0:T(8,128)(2,1)}, u32[]{:S(2)}, u32[]{:S(2)}) collective-permute-start(bf16[256,4096]{1,0:T(8,128)(2,1)} %constant_dynamic-slice_fusion.10), channel_id=1, source_target_pairs={{0,1},{1,0},{2,3},{3,2},{4,5},{5,4},{6,7},{7,6},{8,9},{9,8},{10,11... | collective-permute-start | bytes 6291464 | tf_op jit(solution)/shard_map/ppermute | solution.py:64
  113.0 82.5 %collective-permute-start.15 = (bf16[512,2048]{1,0:T(8,128)(2,1)}, bf16[512,2048]{1,0:T(8,128)(2,1)}, u32[]{:S(2)}, u32[]{:S(2)}) collective-permute-start(bf16[512,2048]{1,0:T(8,128)(2,1)} %constant_dynamic-slice_fusion.9), channel_id=1, source_target_pairs={{0,1},{1,0},{2,3},{3,2},{4,5},{5,4},{6,7},{7,6},{8,9},{9,8},{10,11... | collective-permute-start | bytes 6291464 | tf_op jit(solution)/shard_map/ppermute | solution.py:64
  124.4 71.1 %collective-permute-start.49 = (bf16[96,2048]{1,0:T(8,128)(2,1)S(1)}, bf16[96,2048]{1,0:T(8,128)(2,1)S(1)}, u32[]{:S(2)}, u32[]{:S(2)}) collective-permute-start(bf16[96,2048]{1,0:T(8,128)(2,1)S(1)} %slice.462), channel_id=1, source_target_pairs={{0,4},{2,6},{4,0},{6,2},{1,5},{3,7},{5,1},{7,3},{8,12},{10,14},{12... | collective-permute-start | bytes 1179656 | tf_op jit(solution)/shard_map/ppermute | solution.py:64
  127.2 25.9 %collective-permute-start.47 = (bf16[192,2048]{1,0:T(8,128)(2,1)}, bf16[192,2048]{1,0:T(8,128)(2,1)S(1)}, u32[]{:S(2)}, u32[]{:S(2)}) collective-permute-start(bf16[192,2048]{1,0:T(8,128)(2,1)} %collective-permute-done.45), channel_id=1, source_target_pairs={{0,2},{2,0},{4,6},{6,4},{1,3},{3,1},{5,7},{7,5},{8,10},{10,8},{12,... | collective-permute-start | bytes 2359304 | tf_op jit(solution)/shard_map/ppermute | solution.py:64
  129.8 73.8 %collective-permute-start.51 = (bf16[192,2048]{1,0:T(8,128)(2,1)}, bf16[192,2048]{1,0:T(8,128)(2,1)S(1)}, u32[]{:S(2)}, u32[]{:S(2)}) collective-permute-start(bf16[192,2048]{1,0:T(8,128)(2,1)} %collective-permute-done.48), channel_id=1, source_target_pairs={{0,2},{2,0},{4,6},{6,4},{1,3},{3,1},{5,7},{7,5},{8,10},{10,8},{12,... | collective-permute-start | bytes 2359304 | tf_op jit(solution)/shard_map/ppermute | solution.py:64
  150.6 58.8 %collective-permute-start.13 = (bf16[256,4096]{1,0:T(8,128)(2,1)}, bf16[256,4096]{1,0:T(8,128)(2,1)S(1)}, u32[]{:S(2)}, u32[]{:S(2)}) collective-permute-start(bf16[256,4096]{1,0:T(8,128)(2,1)} %collective-permute-done.11), channel_id=1, source_target_pairs={{0,4},{2,6},{4,0},{6,2},{1,5},{3,7},{5,1},{7,3},{8,12},{10,14},{12... | collective-permute-start | bytes 6291464 | tf_op jit(solution)/shard_map/ppermute | solution.py:64
  153.0 49.8 %collective-permute-start.50 = (bf16[96,2048]{1,0:T(8,128)(2,1)S(1)}, bf16[96,2048]{1,0:T(8,128)(2,1)S(1)}, u32[]{:S(2)}, u32[]{:S(2)}) collective-permute-start(bf16[96,2048]{1,0:T(8,128)(2,1)S(1)} %slice.463), channel_id=1, source_target_pairs={{0,1},{1,0},{2,3},{3,2},{4,5},{5,4},{6,7},{7,6},{8,9},{9,8},{10,11... | collective-permute-start | bytes 1179656 | tf_op jit(solution)/shard_map/ppermute | solution.py:64
  195.5 48.4 %collective-permute-start.16 = (bf16[512,2048]{1,0:T(8,128)(2,1)}, bf16[512,2048]{1,0:T(8,128)(2,1)S(1)}, u32[]{:S(2)}, u32[]{:S(2)}) collective-permute-start(bf16[512,2048]{1,0:T(8,128)(2,1)} %collective-permute-done.15), channel_id=1, source_target_pairs={{0,2},{2,0},{4,6},{6,4},{1,3},{3,1},{5,7},{7,5},{8,10},{10,8},{12,... | collective-permute-start | bytes 6291464 | tf_op jit(solution)/shard_map/ppermute | solution.py:64
  195.5 48.4 %collective-permute-start.17 = (bf16[512,2048]{1,0:T(8,128)(2,1)}, bf16[512,2048]{1,0:T(8,128)(2,1)}, u32[]{:S(2)}, u32[]{:S(2)}) collective-permute-start(bf16[512,2048]{1,0:T(8,128)(2,1)} %collective-permute-done.15), channel_id=1, source_target_pairs={{0,4},{2,6},{4,0},{6,2},{1,5},{3,7},{5,1},{7,3},{8,12},{10,14},{12... | collective-permute-start | bytes 6291464 | tf_op jit(solution)/shard_map/ppermute | solution.py:64
  203.7 44.8 %collective-permute-start.12 = (bf16[256,4096]{1,0:T(8,128)(2,1)}, bf16[256,4096]{1,0:T(8,128)(2,1)S(1)}, u32[]{:S(2)}, u32[]{:S(2)}) collective-permute-start(bf16[256,4096]{1,0:T(8,128)(2,1)} %collective-permute-done.11), channel_id=1, source_target_pairs={{0,2},{2,0},{4,6},{6,4},{1,3},{3,1},{5,7},{7,5},{8,10},{10,8},{12,... | collective-permute-start | bytes 6291464 | tf_op jit(solution)/shard_map/ppermute | solution.py:64
  209.4 42.0 %collective-permute-start.14 = (bf16[256,4096]{1,0:T(8,128)(2,1)S(1)}, bf16[256,4096]{1,0:T(8,128)(2,1)S(1)}, u32[]{:S(2)}, u32[]{:S(2)}) collective-permute-start(bf16[256,4096]{1,0:T(8,128)(2,1)S(1)} %collective-permute-done.13), channel_id=1, source_target_pairs={{0,2},{2,0},{4,6},{6,4},{1,3},{3,1},{5,7},{7,5},{8,10},{10,8},{12,... | collective-permute-start | bytes 6291464 | tf_op jit(solution)/shard_map/ppermute | solution.py:64
  243.9 55.3 %collective-permute-start.18 = (bf16[512,2048]{1,0:T(8,128)(2,1)}, bf16[512,2048]{1,0:T(8,128)(2,1)}, u32[]{:S(2)}, u32[]{:S(2)}) collective-permute-start(bf16[512,2048]{1,0:T(8,128)(2,1)} %collective-permute-done.17), channel_id=1, source_target_pairs={{0,2},{2,0},{4,6},{6,4},{1,3},{3,1},{5,7},{7,5},{8,10},{10,8},{12,... | collective-permute-start | bytes 6291464 | tf_op jit(solution)/shard_map/ppermute | solution.py:64
  312.0 40.9 %collective-permute-start.28 = (bf16[192,2048]{1,0:T(8,128)(2,1)S(1)}, bf16[192,2048]{1,0:T(8,128)(2,1)S(1)}, u32[]{:S(2)}, u32[]{:S(2)}) collective-permute-start(bf16[192,2048]{1,0:T(8,128)(2,1)S(1)} %get-tuple-element.94), channel_id=1, source_target_pairs={{0,1},{1,0},{2,3},{3,2},{4,5},{5,4},{6,7},{7,6},{8,9},{9,8},{10,11... | collective-permute-start | bytes 2359304 | tf_op jit(solution)/shard_map/ppermute | solution.py:64
  313.6 51.3 %collective-permute-start.29 = (bf16[192,2048]{1,0:T(8,128)(2,1)S(1)}, bf16[192,2048]{1,0:T(8,128)(2,1)S(1)}, u32[]{:S(2)}, u32[]{:S(2)}) collective-permute-start(bf16[192,2048]{1,0:T(8,128)(2,1)S(1)} %get-tuple-element.94), channel_id=1, source_target_pairs={{0,2},{2,0},{4,6},{6,4},{1,3},{3,1},{5,7},{7,5},{8,10},{10,8},{12,... | collective-permute-start | bytes 2359304 | tf_op jit(solution)/shard_map/ppermute | solution.py:64
  313.8 48.6 %collective-permute-start.31 = (bf16[192,2048]{1,0:T(8,128)(2,1)S(1)}, bf16[192,2048]{1,0:T(8,128)(2,1)S(1)}, u32[]{:S(2)}, u32[]{:S(2)}) collective-permute-start(bf16[192,2048]{1,0:T(8,128)(2,1)S(1)} %get-tuple-element.94), channel_id=1, source_target_pairs={{0,4},{2,6},{4,0},{6,2},{1,5},{3,7},{5,1},{7,3},{8,12},{10,14},{12... | collective-permute-start | bytes 2359304 | tf_op jit(solution)/shard_map/ppermute | solution.py:64
  317.1 19.1 %collective-permute-start.88 = (bf16[192,512]{1,0:T(8,128)(2,1)}, bf16[192,512]{1,0:T(8,128)(2,1)}, u32[]{:S(2)}, u32[]{:S(2)}) collective-permute-start(bf16[192,512]{1,0:T(8,128)(2,1)} %bitcast.367), channel_id=1, source_target_pairs={{0,1},{1,0},{2,3},{3,2},{4,5},{5,4},{6,7},{7,6},{8,9},{9,8},{10,11... | collective-permute-start | bytes 589832 | tf_op jit(solution)/shard_map/ppermute | solution.py:127
  319.4 19.4 %collective-permute-start.89 = (bf16[192,512]{1,0:T(8,128)(2,1)}, bf16[192,512]{1,0:T(8,128)(2,1)}, u32[]{:S(2)}, u32[]{:S(2)}) collective-permute-start(bf16[192,512]{1,0:T(8,128)(2,1)} %bitcast.366), channel_id=1, source_target_pairs={{0,2},{1,3},{2,0},{3,1},{4,6},{5,7},{6,4},{7,5},{8,10},{9,11},{10,... | collective-permute-start | bytes 589832 | tf_op jit(solution)/shard_map/ppermute | solution.py:127
  352.8 20.2 %collective-permute-start.30 = (bf16[192,2048]{1,0:T(8,128)(2,1)S(1)}, bf16[192,2048]{1,0:T(8,128)(2,1)S(1)}, u32[]{:S(2)}, u32[]{:S(2)}) collective-permute-start(bf16[192,2048]{1,0:T(8,128)(2,1)S(1)} %collective-permute-done.28), channel_id=1, source_target_pairs={{0,2},{2,0},{4,6},{6,4},{1,3},{3,1},{5,7},{7,5},{8,10},{10,8},{12,... | collective-permute-start | bytes 2359304 | tf_op jit(solution)/shard_map/ppermute | solution.py:64
  363.9 12.5 %collective-permute-start.34 = (bf16[192,2048]{1,0:T(8,128)(2,1)S(1)}, bf16[192,2048]{1,0:T(8,128)(2,1)S(1)}, u32[]{:S(2)}, u32[]{:S(2)}) collective-permute-start(bf16[192,2048]{1,0:T(8,128)(2,1)S(1)} %collective-permute-done.31), channel_id=1, source_target_pairs={{0,2},{2,0},{4,6},{6,4},{1,3},{3,1},{5,7},{7,5},{8,10},{10,8},{12,... | collective-permute-start | bytes 2359304 | tf_op jit(solution)/shard_map/ppermute | solution.py:64
  442.6 45.9 %collective-permute-start.62 = (f32[192,2]{0,1:T(2,128)S(1)}, f32[192,2]{0,1:T(2,128)S(1)}, u32[]{:S(2)}, u32[]{:S(2)}) collective-permute-start(f32[192,2]{0,1:T(2,128)S(1)} %get-tuple-element.183), channel_id=1, source_target_pairs={{0,1},{1,0},{2,3},{3,2},{4,5},{5,4},{6,7},{7,6},{8,9},{9,8},{10,11... | collective-permute-start | bytes 4616 | tf_op jit(solution)/shard_map/ppermute | solution.py:127
  476.6 20.5 %collective-permute-start.55 = (bf16[192,2048]{1,0:T(8,128)(2,1)}, bf16[192,2048]{1,0:T(8,128)(2,1)S(1)}, u32[]{:S(2)}, u32[]{:S(2)}) collective-permute-start(bf16[192,2048]{1,0:T(8,128)(2,1)} %get-tuple-element.110), channel_id=1, source_target_pairs={{0,2},{2,0},{4,6},{6,4},{1,3},{3,1},{5,7},{7,5},{8,10},{10,8},{12,... | collective-permute-start | bytes 2359304 | tf_op jit(solution)/shard_map/ppermute | solution.py:64
  476.8 20.9 %collective-permute-start.56 = (bf16[192,2048]{1,0:T(8,128)(2,1)}, bf16[192,2048]{1,0:T(8,128)(2,1)S(1)}, u32[]{:S(2)}, u32[]{:S(2)}) collective-permute-start(bf16[192,2048]{1,0:T(8,128)(2,1)} %get-tuple-element.109), channel_id=1, source_target_pairs={{0,2},{2,0},{4,6},{6,4},{1,3},{3,1},{5,7},{7,5},{8,10},{10,8},{12,... | collective-permute-start | bytes 2359304 | tf_op jit(solution)/shard_map/ppermute | solution.py:64
  477.1 21.9 %collective-permute-start.59 = (bf16[192,2048]{1,0:T(8,128)(2,1)S(1)}, bf16[192,2048]{1,0:T(8,128)(2,1)}, u32[]{:S(2)}, u32[]{:S(2)}) collective-permute-start(bf16[192,2048]{1,0:T(8,128)(2,1)S(1)} %get-tuple-element.108), channel_id=1, source_target_pairs={{0,2},{2,0},{4,6},{6,4},{1,3},{3,1},{5,7},{7,5},{8,10},{10,8},{12,... | collective-permute-start | bytes 2359304 | tf_op jit(solution)/shard_map/ppermute | solution.py:64
  488.1 14.0 %collective-permute-start.38 = (bf16[192,2048]{1,0:T(8,128)(2,1)S(1)}, bf16[192,2048]{1,0:T(8,128)(2,1)S(1)}, u32[]{:S(2)}, u32[]{:S(2)}) collective-permute-start(bf16[192,2048]{1,0:T(8,128)(2,1)S(1)} %get-tuple-element.117), channel_id=1, source_target_pairs={{0,2},{2,0},{4,6},{6,4},{1,3},{3,1},{5,7},{7,5},{8,10},{10,8},{12,... | collective-permute-start | bytes 2359304 | tf_op jit(solution)/shard_map/ppermute | solution.py:64
  497.7 40.0 %collective-permute-start.66 = (f32[192,2]{0,1:T(2,128)S(1)}, f32[192,2]{0,1:T(2,128)S(1)}, u32[]{:S(2)}, u32[]{:S(2)}) collective-permute-start(f32[192,2]{0,1:T(2,128)S(1)} %get-tuple-element.187), channel_id=1, source_target_pairs={{0,5},{1,4},{2,7},{3,6},{4,1},{5,0},{6,3},{7,2},{8,13},{9,12},{10,... | collective-permute-start | bytes 4616 | tf_op jit(solution)/shard_map/ppermute | solution.py:127
  499.0 38.9 %collective-permute-start.67 = (f32[192,2]{0,1:T(2,128)S(1)}, f32[192,2]{0,1:T(2,128)S(1)}, u32[]{:S(2)}, u32[]{:S(2)}) collective-permute-start(f32[192,2]{0,1:T(2,128)S(1)} %get-tuple-element.188), channel_id=1, source_target_pairs={{0,6},{1,7},{2,4},{3,5},{4,2},{5,3},{6,0},{7,1},{8,14},{9,15},{10,... | collective-permute-start | bytes 4616 | tf_op jit(solution)/shard_map/ppermute | solution.py:127
  502.1 47.1 %collective-permute-start.54 = (bf16[192,2048]{1,0:T(8,128)(2,1)}, bf16[192,2048]{1,0:T(8,128)(2,1)S(1)}, u32[]{:S(2)}, u32[]{:S(2)}) collective-permute-start(bf16[192,2048]{1,0:T(8,128)(2,1)} %get-tuple-element.107), channel_id=1, source_target_pairs={{0,2},{2,0},{4,6},{6,4},{1,3},{3,1},{5,7},{7,5},{8,10},{10,8},{12,... | collective-permute-start | bytes 2359304 | tf_op jit(solution)/shard_map/ppermute | solution.py:64
  505.0 20.5 %collective-permute-start.40 = (bf16[96,2048]{1,0:T(8,128)(2,1)S(1)}, bf16[96,2048]{1,0:T(8,128)(2,1)S(1)}, u32[]{:S(2)}, u32[]{:S(2)}) collective-permute-start(bf16[96,2048]{1,0:T(8,128)(2,1)S(1)} %get-tuple-element.156), channel_id=1, source_target_pairs={{0,1},{1,0},{2,3},{3,2},{4,5},{5,4},{6,7},{7,6},{8,9},{9,8},{10,11... | collective-permute-start | bytes 1179656 | tf_op jit(solution)/shard_map/ppermute | solution.py:64
  525.5 24.9 %collective-permute-start.58 = (bf16[192,2048]{1,0:T(8,128)(2,1)S(1)}, bf16[192,2048]{1,0:T(8,128)(2,1)S(1)}, u32[]{:S(2)}, u32[]{:S(2)}) collective-permute-start(bf16[192,2048]{1,0:T(8,128)(2,1)S(1)} %pad_maximum_fusion.12), channel_id=1, source_target_pairs={{0,4},{2,6},{4,0},{6,2},{1,5},{3,7},{5,1},{7,3},{8,12},{10,14},{12... | collective-permute-start | bytes 2359304 | tf_op jit(solution)/shard_map/ppermute | solution.py:64
  536.3 14.1 %collective-permute-start.61 = (bf16[192,2048]{1,0:T(8,128)(2,1)S(1)}, bf16[192,2048]{1,0:T(8,128)(2,1)S(1)}, u32[]{:S(2)}, u32[]{:S(2)}) collective-permute-start(bf16[192,2048]{1,0:T(8,128)(2,1)S(1)} %pad_maximum_fusion.13), channel_id=1, source_target_pairs={{0,1},{1,0},{2,3},{3,2},{4,5},{5,4},{6,7},{7,6},{8,9},{9,8},{10,11... | collective-permute-start | bytes 2359304 | tf_op jit(solution)/shard_map/ppermute | solution.py:64
  537.8 13.8 %collective-permute-start.37 = (bf16[192,2048]{1,0:T(8,128)(2,1)S(1)}, bf16[192,2048]{1,0:T(8,128)(2,1)S(1)}, u32[]{:S(2)}, u32[]{:S(2)}) collective-permute-start(bf16[192,2048]{1,0:T(8,128)(2,1)S(1)} %get-tuple-element.114), channel_id=1, source_target_pairs={{0,2},{2,0},{4,6},{6,4},{1,3},{3,1},{5,7},{7,5},{8,10},{10,8},{12,... | collective-permute-start | bytes 2359304 | tf_op jit(solution)/shard_map/ppermute | solution.py:64
  548.1 19.5 %collective-permute-start.41 = (bf16[192,2048]{1,0:T(8,128)(2,1)S(1)}, bf16[192,2048]{1,0:T(8,128)(2,1)S(1)}, u32[]{:S(2)}, u32[]{:S(2)}) collective-permute-start(bf16[192,2048]{1,0:T(8,128)(2,1)S(1)} %pad_maximum_fusion.10), channel_id=1, source_target_pairs={{0,4},{2,6},{4,0},{6,2},{1,5},{3,7},{5,1},{7,3},{8,12},{10,14},{12... | collective-permute-start | bytes 2359304 | tf_op jit(solution)/shard_map/ppermute | solution.py:64
  549.2 20.2 %collective-permute-start.44 = (bf16[192,2048]{1,0:T(8,128)(2,1)S(1)}, bf16[192,2048]{1,0:T(8,128)(2,1)S(1)}, u32[]{:S(2)}, u32[]{:S(2)}) collective-permute-start(bf16[192,2048]{1,0:T(8,128)(2,1)S(1)} %pad_maximum_fusion.11), channel_id=1, source_target_pairs={{0,1},{1,0},{2,3},{3,2},{4,5},{5,4},{6,7},{7,6},{8,9},{9,8},{10,11... | collective-permute-start | bytes 2359304 | tf_op jit(solution)/shard_map/ppermute | solution.py:64
  574.1 102.4 %collective-permute-start.95 = (bf16[192,2048]{1,0:T(8,128)(2,1)}, bf16[192,2048]{1,0:T(8,128)(2,1)}, u32[]{:S(2)}, u32[]{:S(2)}) collective-permute-start(bf16[192,2048]{1,0:T(8,128)(2,1)} %get-tuple-element.85), channel_id=1, source_target_pairs={{0,1},{1,0},{2,3},{3,2},{4,5},{5,4},{6,7},{7,6},{8,9},{9,8},{10,11... | collective-permute-start | bytes 2359304 | tf_op jit(solution)/shard_map/ppermute | solution.py:64
  575.1 109.1 %collective-permute-start.96 = (bf16[192,2048]{1,0:T(8,128)(2,1)}, bf16[192,2048]{1,0:T(8,128)(2,1)}, u32[]{:S(2)}, u32[]{:S(2)}) collective-permute-start(bf16[192,2048]{1,0:T(8,128)(2,1)} %get-tuple-element.85), channel_id=1, source_target_pairs={{0,2},{2,0},{4,6},{6,4},{1,3},{3,1},{5,7},{7,5},{8,10},{10,8},{12,... | collective-permute-start | bytes 2359304 | tf_op jit(solution)/shard_map/ppermute | solution.py:64
  575.1 107.2 %collective-permute-start.98 = (bf16[192,2048]{1,0:T(8,128)(2,1)}, bf16[192,2048]{1,0:T(8,128)(2,1)}, u32[]{:S(2)}, u32[]{:S(2)}) collective-permute-start(bf16[192,2048]{1,0:T(8,128)(2,1)} %get-tuple-element.85), channel_id=1, source_target_pairs={{0,4},{2,6},{4,0},{6,2},{1,5},{3,7},{5,1},{7,3},{8,12},{10,14},{12... | collective-permute-start | bytes 2359304 | tf_op jit(solution)/shard_map/ppermute | solution.py:64
  639.3 13.5 %collective-permute-start.70 = (bf16[2,128,4,128]{3,1,2,0:T(8,128)(2,1)}, bf16[2,128,4,128]{3,1,2,0:T(8,128)(2,1)}, u32[]{:S(2)}, u32[]{:S(2)}) collective-permute-start(bf16[2,128,4,128]{3,1,2,0:T(8,128)(2,1)} %get-tuple-element.151), channel_id=1, source_target_pairs={{0,2},{2,0},{4,6},{6,4},{1,3},{3,1},{5,7},{7,5},{8,10},{10,8},{12,... | collective-permute-start | bytes 786440 | tf_op jit(solution)/shard_map/ppermute | solution.py:64
  652.2 18.2 %collective-permute-start.69 = (bf16[2,128,4,128]{3,1,2,0:T(8,128)(2,1)}, bf16[2,128,4,128]{3,1,2,0:T(8,128)(2,1)S(1)}, u32[]{:S(2)}, u32[]{:S(2)}) collective-permute-start(bf16[2,128,4,128]{3,1,2,0:T(8,128)(2,1)} %get-tuple-element.150), channel_id=1, source_target_pairs={{0,2},{2,0},{4,6},{6,4},{1,3},{3,1},{5,7},{7,5},{8,10},{10,8},{12,... | collective-permute-start | bytes 786440 | tf_op jit(solution)/shard_map/ppermute | solution.py:64
  654.2 16.2 %collective-permute-start.71 = (bf16[2,128,4,128]{3,1,2,0:T(8,128)(2,1)S(1)}, bf16[2,128,4,128]{3,1,2,0:T(8,128)(2,1)S(1)}, u32[]{:S(2)}, u32[]{:S(2)}) collective-permute-start(bf16[2,128,4,128]{3,1,2,0:T(8,128)(2,1)S(1)} %add_convert_fusion.15), channel_id=1, source_target_pairs={{0,4},{2,6},{4,0},{6,2},{1,5},{3,7},{5,1},{7,3},{8,12},{10,14},{12... | collective-permute-start | bytes 786440 | tf_op jit(solution)/shard_map/ppermute | solution.py:64
  679.0 56.2 %collective-permute-start.79 = (bf16[192,5120]{1,0:T(8,128)(2,1)}, bf16[192,5120]{1,0:T(8,128)(2,1)S(1)}, u32[]{:S(2)}, u32[]{:S(2)}) collective-permute-start(bf16[192,5120]{1,0:T(8,128)(2,1)} %get-tuple-element.127), channel_id=1, source_target_pairs={{0,1},{1,0},{2,3},{3,2},{4,5},{5,4},{6,7},{7,6},{8,9},{9,8},{10,11... | collective-permute-start | bytes 5898248 | tf_op jit(solution)/shard_map/ppermute | solution.py:64
  679.9 64.9 %collective-permute-start.80 = (bf16[192,5120]{1,0:T(8,128)(2,1)}, bf16[192,5120]{1,0:T(8,128)(2,1)}, u32[]{:S(2)}, u32[]{:S(2)}) collective-permute-start(bf16[192,5120]{1,0:T(8,128)(2,1)} %get-tuple-element.127), channel_id=1, source_target_pairs={{0,2},{2,0},{4,6},{6,4},{1,3},{3,1},{5,7},{7,5},{8,10},{10,8},{12,... | collective-permute-start | bytes 5898248 | tf_op jit(solution)/shard_map/ppermute | solution.py:64
  684.3 48.6 %collective-permute-start.100 = (bf16[96,2048]{1,0:T(8,128)(2,1)S(1)}, bf16[96,2048]{1,0:T(8,128)(2,1)S(1)}, u32[]{:S(2)}, u32[]{:S(2)}) collective-permute-start(bf16[96,2048]{1,0:T(8,128)(2,1)S(1)} %slice.527), channel_id=1, source_target_pairs={{0,1},{1,0},{2,3},{3,2},{4,5},{5,4},{6,7},{7,6},{8,9},{9,8},{10,11... | collective-permute-start | bytes 1179656 | tf_op jit(solution)/shard_map/ppermute | solution.py:64
  686.4 46.5 %collective-permute-start.101 = (bf16[192,2048]{1,0:T(8,128)(2,1)}, bf16[192,2048]{1,0:T(8,128)(2,1)S(1)}, u32[]{:S(2)}, u32[]{:S(2)}) collective-permute-start(bf16[192,2048]{1,0:T(8,128)(2,1)} %collective-permute-done.98), channel_id=1, source_target_pairs={{0,2},{2,0},{4,6},{6,4},{1,3},{3,1},{5,7},{7,5},{8,10},{10,8},{12,... | collective-permute-start | bytes 2359304 | tf_op jit(solution)/shard_map/ppermute | solution.py:64
  693.7 47.1 %collective-permute-start.82 = (bf16[192,5120]{1,0:T(8,128)(2,1)}, bf16[192,5120]{1,0:T(8,128)(2,1)}, u32[]{:S(2)}, u32[]{:S(2)}) collective-permute-start(bf16[192,5120]{1,0:T(8,128)(2,1)} %get-tuple-element.127), channel_id=1, source_target_pairs={{0,4},{2,6},{4,0},{6,2},{1,5},{3,7},{5,1},{7,3},{8,12},{10,14},{12... | collective-permute-start | bytes 5898248 | tf_op jit(solution)/shard_map/ppermute | solution.py:64
  735.1 30.7 %collective-permute-start.81 = (bf16[192,5120]{1,0:T(8,128)(2,1)S(1)}, bf16[192,5120]{1,0:T(8,128)(2,1)}, u32[]{:S(2)}, u32[]{:S(2)}) collective-permute-start(bf16[192,5120]{1,0:T(8,128)(2,1)S(1)} %collective-permute-done.79), channel_id=1, source_target_pairs={{0,2},{2,0},{4,6},{6,4},{1,3},{3,1},{5,7},{7,5},{8,10},{10,8},{12,... | collective-permute-start | bytes 5898248 | tf_op jit(solution)/shard_map/ppermute | solution.py:64
  740.0 155.7 %reduce-scatter.5.cloned.1.call-start = ((), (), s32[]{:S(2)}) async-start(), calls=%async_computation.5 | async-start | bytes 3276800 | tf_op jit(solution)/shard_map/reduce_scatter | solution.py:452
  740.1 24.1 %collective-permute-start.83 = (bf16[96,5120]{1,0:T(8,128)(2,1)S(1)}, bf16[96,5120]{1,0:T(8,128)(2,1)S(1)}, u32[]{:S(2)}, u32[]{:S(2)}) collective-permute-start(bf16[96,5120]{1,0:T(8,128)(2,1)S(1)} %slice.519), channel_id=1, source_target_pairs={{0,4},{2,6},{4,0},{6,2},{1,5},{3,7},{5,1},{7,3},{8,12},{10,14},{12... | collective-permute-start | bytes 2949128 | tf_op jit(solution)/shard_map/ppermute | solution.py:64
  742.1 23.8 %collective-permute-start.84 = (bf16[96,5120]{1,0:T(8,128)(2,1)S(1)}, bf16[96,5120]{1,0:T(8,128)(2,1)S(1)}, u32[]{:S(2)}, u32[]{:S(2)}) collective-permute-start(bf16[96,5120]{1,0:T(8,128)(2,1)S(1)} %slice.520), channel_id=1, source_target_pairs={{0,1},{1,0},{2,3},{3,2},{4,5},{5,4},{6,7},{7,6},{8,9},{9,8},{10,11... | collective-permute-start | bytes 2949128 | tf_op jit(solution)/shard_map/ppermute | solution.py:64
  743.3 30.6 %collective-permute-start.85 = (bf16[192,5120]{1,0:T(8,128)(2,1)}, bf16[192,5120]{1,0:T(8,128)(2,1)S(1)}, u32[]{:S(2)}, u32[]{:S(2)}) collective-permute-start(bf16[192,5120]{1,0:T(8,128)(2,1)} %collective-permute-done.82), channel_id=1, source_target_pairs={{0,2},{2,0},{4,6},{6,4},{1,3},{3,1},{5,7},{7,5},{8,10},{10,8},{12,... | collective-permute-start | bytes 5898248 | tf_op jit(solution)/shard_map/ppermute | solution.py:64
  789.3 168.7 %reduce-scatter.11.cloned.1.call-start = ((), (), s32[]{:S(2)}) async-start(), calls=%async_computation.8 | async-start | bytes 7864320 | tf_op jit(solution)/shard_map/reduce_scatter | solution.py:342
  810.2 362.5 %reduce-scatter.9.cloned.1.call-start = ((), (), s32[]{:S(2)}) async-start(), calls=%async_computation.7 | async-start | bytes 15728640 | tf_op jit(solution)/shard_map/reduce_scatter | solution.py:339
  874.1 17.4 %all-to-all-start = ((f32[32,1,1160]{2,1,0:T(1,128)}), f32[32,1,1160]{2,1,0:T(1,128)S(1)}, u32[]{:S(2)}, u32[]{:S(2)}) async-start(f32[32,1,1160]{2,1,0:T(1,128)} %copy.235), calls=%async_computation | async-start | bytes 327680 | tf_op jit(solution)/shard_map/all_to_all | solution.py:474
  (165 other events, 2733.3 us)
Sparse Core Ops, SparseCore 0:
  740.1 43.8 reduce-scatter.6
  789.4 52.9 reduce-scatter.4
  844.8 113.0 reduce-scatter.10
  960.3 212.3 reduce-scatter.8

commit v2 on v1

--- a/solution.py
+++ b/solution.py
@@ -3,6 +3,8 @@
 import jax
 import jax.numpy as jnp
 from jax import lax
+from jax.experimental import pallas as pl
+from jax.experimental.pallas import tpu as pltpu
 from jax.sharding import PartitionSpec as P
 
 MODEL_WIDTH = 2048
@@ -128,69 +130,419 @@
     return out
 
 
-def piece_starts(total):
+def over_z(v):
+    return swap(v, "dp", 1)
+
+
+def after(v, *earlier):
+    return lax.optimization_barrier((v, *earlier))[0]
+
+
+class Places:
+    def __init__(self):
+        self.dp = lax.axis_index("dp")
+        ctx = lax.axis_index("ctx")
+        self.ctx = ctx
+        self.z = lax.rem(self.dp, 2)
+        self.x = lax.div(ctx, 2)
+        self.c = lax.rem(ctx, 2)
+        self.y = lax.axis_index("expert")
+        self.to_x = {"ctx": (1 - self.x) * 2 + self.c}
+        self.to_c = {"ctx": self.x * 2 + 1 - self.c}
+        self.to_y = {"expert": 1 - self.y}
+        self.to_z = {"dp": self.dp + 1 - 2 * self.z}
+
+
+def plane_slot(x, c, y):
+    return x * 4 + c * 2 + y
+
+
+def greet(targets):
+    barrier = pltpu.get_barrier_semaphore()
+    for target in targets:
+        pl.semaphore_signal(barrier, inc=1, device_id=target, device_id_type=pl.DeviceIdType.MESH)
+    pl.semaphore_wait(barrier, len(targets))
+
+
+class Sender:
+    def __init__(self, send_sem, recv_sem):
+        self.send_sem = send_sem
+        self.recv_sem = recv_sem
+        self.copies = []
+
+    def __call__(self, source, target_ref, device):
+        i = len(self.copies)
+        copy = pltpu.make_async_remote_copy(
+            src_ref=source,
+            dst_ref=target_ref,
+            send_sem=self.send_sem.at[i],
+            recv_sem=self.recv_sem.at[i],
+            device_id=device,
+            device_id_type=pl.DeviceIdType.MESH,
+        )
+        copy.start()
+        self.copies.append(copy)
+        return copy
+
+    def finish(self):
+        for copy in self.copies:
+            copy.wait_send()
+
+
+def run_rounds(work, between):
+    turns = max(i + len(todo) for i, todo in enumerate(work))
+    for turn in range(turns):
+        for i, todo in enumerate(work):
+            if 0 <= turn - i < len(todo):
+                todo[turn - i]()
+        if turn in between:
+            between[turn]()
+
+
+def half_fetch(here, send, sources, other, columns, rows):
+    def at(piece, part=None):
+        first, size = piece * rows, rows
+        if part is not None:
+            size = rows // 2
+            first = first + part * size
+        return other.at[pl.ds(pl.multiple_of(first, size), size), columns]
+
+    def piece(z, x, c):
+        return z * 4 + x * 2 + c
+
+    z, x, c = here.z, here.x, here.c
+    got = {}
+
+    def first():
+        mine = piece(z, x, c)
+        got["y"] = [
+            send(
+                source.at[pl.ds(pl.multiple_of(mine * rows, rows), rows), source_columns],
+                other.at[pl.ds(pl.multiple_of(mine * rows, rows), rows), target_columns],
+                here.to_y,
+            )
+            for source, source_columns, target_columns in sources
+        ]
+
+    def second():
+        for copy in got["y"]:
+            copy.wait_recv()
+        mine = at(piece(z, x, c))
+        got["x"] = send(mine, mine, here.to_x)
+        got["z"] = send(mine, mine, here.to_z)
+        got["c"] = send(mine, mine, here.to_c)
+
+    def third():
+        got["x"].wait_recv()
+        from_x = piece(z, 1 - x, c)
+        got["low"] = send(at(from_x, 1), at(from_x, 1), here.to_z)
+        got["xc"] = send(at(from_x), at(from_x), here.to_c)
+        got["z"].wait_recv()
+        from_z = piece(1 - z, x, c)
+        got["top"] = send(at(from_z, 0), at(from_z, 0), here.to_x)
+        got["zc"] = send(at(from_z), at(from_z), here.to_c)
+
+    def fourth():
+        far = piece(1 - z, 1 - x, c)
+        got["low"].wait_recv()
+        got["lowc"] = send(at(far, 1), at(far, 1), here.to_c)
+        got["top"].wait_recv()
+        got["topc"] = send(at(far, 0), at(far, 0), here.to_c)
+
+    def fifth():
+        for name in ("c", "xc", "zc", "lowc", "topc"):
+            got[name].wait_recv()
+
+    return [first, second, third, fourth, fifth]
+
+
+def block_gather(here, send, mine, local_sem, blocks):
+    half = blocks.shape[1] // 2
+    x, c, y = here.x, here.c, here.y
+    got = {}
+
+    def at(slot, part=None):
+        if part is None:
+            return blocks.at[slot]
+        return blocks.at[slot, pl.ds(part * half, half)]
+
+    def first():
+        slot = plane_slot(x, c, y)
+        got["own"] = pltpu.make_async_copy(mine, at(slot), local_sem)
+        got["own"].start()
+        got["y"] = send(mine, at(slot), here.to_y)
+        got["x"] = send(mine, at(slot), here.to_x)
+        got["c"] = send(mine, at(slot), here.to_c)
+
+    def second():
+        got["y"].wait_recv()
+        from_y = plane_slot(x, c, 1 - y)
+        got["top"] = send(at(from_y, 0), at(from_y, 0), here.to_x)
+        got["yc"] = send(at(from_y), at(from_y), here.to_c)
+        got["x"].wait_recv()
+        from_x = plane_slot(1 - x, c, y)
+        got["low"] = send(at(from_x, 1), at(from_x, 1), here.to_y)
+        got["xc"] = send(at(from_x), at(from_x), here.to_c)
+
+    def third():
+        far = plane_slot(1 - x, c, 1 - y)
+        got["top"].wait_recv()
+        got["topc"] = send(at(far, 0), at(far, 0), here.to_c)
+        got["low"].wait_recv()
+        got["lowc"] = send(at(far, 1), at(far, 1), here.to_c)
+
+    def fourth():
+        for name in ("c", "yc", "xc", "topc", "lowc"):
+            got[name].wait_recv()
+        got["own"].wait()
+
+    return [first, second, third, fourth]
+
+
+def turn_half(v):
+    return pltpu.roll(v, v.shape[-1] // 2, axis=1)
+
+
+def head_norm(v):
+    return lax.rsqrt(jnp.mean(v * v, axis=-1, keepdims=True) + epsilon)
+
+
+def fetch_kernel(
+    hidden_ref,
+    attn_gain_ref,
+    key_gain_ref,
+    cosine_ref,
+    sine_ref,
+    key_ref,
+    value_ref,
+    query_ref,
+    output_ref,
+    grad_ref,
+    kv_out,
+    q_out,
+    o_other,
+    g_blocks,
+    normed_ref,
+    query_pre_ref,
+    kv_pre_ref,
+    kv_low_ref,
+    kv_blocks,
+    kv_own,
+    kv_other,
+    q_own,
+    q_other,
+    send_sem,
+    recv_sem,
+    local_sem,
+):
+    here = Places()
+    greet([here.to_y, here.to_z, here.to_c, here.to_x])
+    send = Sender(send_sem, recv_sem)
+    width = hidden_ref.shape[1]
+    half = width // 2
+    narrow = key_ref.shape[1]
+    wide = query_ref.shape[1]
+    tile = 512
+    loads = [
+        pltpu.make_async_copy(key_ref, kv_own.at[:, pl.ds(0, narrow)], local_sem.at[0]),
+        pltpu.make_async_copy(value_ref, kv_own.at[:, pl.ds(narrow, narrow)], local_sem.at[1]),
+        pltpu.make_async_copy(query_ref, q_own, local_sem.at[2]),
+    ]
+    stores = [
+        pltpu.make_async_copy(kv_other, kv_out, local_sem.at[3]),
+        pltpu.make_async_copy(q_other, q_out, local_sem.at[4]),
+    ]
+    mine = pl.ds(pl.multiple_of(here.y * half, half), half)
+    others = pl.ds(pl.multiple_of(half - here.y * half, half), half)
+
+    def project(weight, out, rows, first, count, add):
+        @pl.loop(first, first + count)
+        def _(i):
+            cols = pl.ds(pl.multiple_of(i * tile, tile), tile)
+            part = jnp.dot(normed_ref[:, rows], weight[:, cols], preferred_element_type=f32)
+            out[:, cols] = out[:, cols] + part if add else part
+
+    def start():
+        for load in loads:
+            load.start()
+        inputs = hidden_ref[...].astype(f32)
+        normed_ref[...] = (inputs * head_norm(inputs) * attn_gain_ref[...]).astype(bf16)
+
+    def own_part():
+        for load in loads:
+            load.wait()
+        project(kv_own, kv_pre_ref, mine, 0, 2 * narrow // tile, False)
+        project(q_own, query_pre_ref, mine, 0, wide // tile, False)
+
+    exchange = {}
+
+    def keys_part():
+        project(kv_other, kv_pre_ref, others, 0, 2 * narrow // tile, True)
+        stores[0].start()
+        for h in range(narrow // HEAD_SIZE):
+            cols = slice(h * HEAD_SIZE, (h + 1) * HEAD_SIZE)
+            v = kv_pre_ref[:, cols]
+            v = v * head_norm(v) * key_gain_ref[...]
+            kv_low_ref[:, cols] = (v * cosine_ref[...] + turn_half(v) * sine_ref[...]).astype(bf16)
+        kv_low_ref[:, narrow:] = kv_pre_ref[:, narrow:].astype(bf16)
+        source = kv_low_ref.at[pl.ds(0, PROMPT_DEV)]
+        slot = kv_blocks.at[here.ctx]
+        exchange["own"] = pltpu.make_async_copy(source, slot, local_sem.at[5])
+        exchange["own"].start()
+        exchange["c"] = send(source, slot, here.to_c)
+        exchange["x"] = send(source, slot, here.to_x)
+
+    def keys_forward():
+        exchange["x"].wait_recv()
+        slot = kv_blocks.at[(1 - here.x) * 2 + here.c]
+        exchange["xc"] = send(slot, slot, here.to_c)
+        project(q_other, query_pre_ref, others, 0, wide // tile // 2, True)
+
+    def queries_rest():
+        stores[1].start()
+        project(q_other, query_pre_ref, others, wide // tile // 2, wide // tile // 2, True)
+
+    low, high = pl.ds(0, wide // 2), pl.ds(wide // 2, wide // 2)
+    o_low, o_high = pl.ds(0, width // 2), pl.ds(width // 2, width // 2)
+    rows, o_rows = half // 8, output_ref.shape[0] // 8
+    work = [
+        half_fetch(
+            here,
+            send,
+            [
+                (key_ref, pl.ds(0, narrow), pl.ds(0, narrow)),
+                (value_ref, pl.ds(0, narrow), pl.ds(narrow, narrow)),
+            ],
+            kv_other,
+            pl.ds(0, 2 * narrow),
+            rows,
+        ),
+        half_fetch(here, send, [(query_ref, low, low)], q_other, low, rows),
+        half_fetch(here, send, [(query_ref, high, high)], q_other, high, rows),
+        half_fetch(here, send, [(output_ref, o_low, o_low)], o_other, o_low, o_rows),
+        half_fetch(here, send, [(output_ref, o_high, o_high)], o_other, o_high, o_rows),
+        block_gather(here, send, grad_ref, local_sem.at[6], g_blocks),
+    ]
+    run_rounds(
+        work, {0: start, 2: own_part, 4: keys_part, 5: keys_forward, 6: queries_rest}
+    )
+    for name in ("c", "xc"):
+        exchange[name].wait_recv()
+    exchange["own"].wait()
+    for store in stores:
+        store.wait()
+    send.finish()
+
+
+def fetch_and_project(
+    hidden_in, attn_gain, key_gain, cosine, sine, key_matrix, value_matrix, query_weight,
+    output_weight, out_grad,
+):
+    rows, width = hidden_in.shape
+    half, wide = query_weight.shape
+    narrow = key_matrix.shape[1]
+    spread = lax.axis_size(plane)
+    vmem = pl.BlockSpec(memory_space=pltpu.VMEM)
+    anywhere = pl.BlockSpec(memory_space=pl.ANY)
+    copies = 5 * 10 + 1 + 9 + 3
+    return pl.pallas_call(
+        fetch_kernel,
+        out_shape=[
+            jax.ShapeDtypeStruct((half, 2 * narrow), bf16),
+            jax.ShapeDtypeStruct((half, wide), bf16),
+            jax.ShapeDtypeStruct(output_weight.shape, bf16),
+            jax.ShapeDtypeStruct((spread, rows, width), bf16),
+            jax.ShapeDtypeStruct((rows, width), bf16),
+            jax.ShapeDtypeStruct((rows, wide), f32),
+            jax.ShapeDtypeStruct((rows, 2 * narrow), f32),
+            jax.ShapeDtypeStruct((rows, 2 * narrow), bf16),
+            jax.ShapeDtypeStruct((lax.axis_size("ctx"), PROMPT_DEV, 2 * narrow), bf16),
+        ],
+        in_specs=[vmem] * 5 + [anywhere] * 5,
+        out_specs=[anywhere] * 4 + [vmem] * 4 + [anywhere],
+        scratch_shapes=[
+            pltpu.VMEM((half, 2 * narrow), bf16),
+            pltpu.VMEM((half, 2 * narrow), bf16),
+            pltpu.VMEM((half, wide), bf16),
+            pltpu.VMEM((half, wide), bf16),
+            pltpu.SemaphoreType.DMA((copies,)),
+            pltpu.SemaphoreType.DMA((copies,)),
+            pltpu.SemaphoreType.DMA((7,)),
+        ],
+        compiler_params=pltpu.CompilerParams(
+            collective_id=1, has_side_effects=True, vmem_limit_bytes=48 * 2**20
+        ),
+    )(
+        hidden_in, attn_gain.reshape(1, width), key_gain.reshape(1, HEAD_SIZE), cosine, sine,
+        key_matrix, value_matrix, query_weight, output_weight, out_grad,
+    )
+
+
+def gather_kernel(mine_ref, blocks, send_sem, recv_sem, local_sem):
+    here = Places()
+    greet([here.to_y, here.to_c, here.to_x])
+    send = Sender(send_sem, recv_sem)
+    run_rounds([block_gather(here, send, mine_ref, local_sem.at[0], blocks)], {})
+    send.finish()
+
+
+def gather_blocks(v, collective_id):
+    anywhere = pl.BlockSpec(memory_space=pl.ANY)
+    return pl.pallas_call(
+        gather_kernel,
+        out_shape=jax.ShapeDtypeStruct((lax.axis_size(plane),) + v.shape, v.dtype),
+        in_specs=[anywhere],
+        out_specs=anywhere,
+        scratch_shapes=[
+            pltpu.SemaphoreType.DMA((9,)),
+            pltpu.SemaphoreType.DMA((9,)),
+            pltpu.SemaphoreType.DMA((1,)),
+        ],
+        compiler_params=pltpu.CompilerParams(collective_id=collective_id, has_side_effects=True),
+    )(v)
+
+
+def gather_small(v):
     if not small_plane():
-        return [(0, total)]
-    half, quarter = total // 2, total // 8
+        return lax.all_gather(v, plane, axis=0, tiled=True)
+    v = jnp.concatenate([v, over_y(v)], axis=0)
+    v = jnp.concatenate([v, core(v)], axis=0)
+    v = jnp.concatenate([v, over_x(v)], axis=0)
+    blocks = v.reshape(lax.axis_size(plane), -1, v.shape[1])
+    blocks = jnp.take(blocks, jnp.arange(blocks.shape[0]) ^ lax.axis_index(plane), axis=0)
+    return blocks.reshape(v.shape)
+
+
+def halves(v):
+    half = v.shape[1] // 2
     mine = lax.axis_index("expert") * half
-    other = half - mine
+    return (
+        lax.dynamic_slice_in_dim(v, mine, half, axis=1),
+        lax.dynamic_slice_in_dim(v, half - mine, half, axis=1),
+    )
+
+
+def join_halves(mine, other):
+    lower = lax.axis_index("expert") == 0
+    return jnp.concatenate(
+        [jnp.where(lower, mine, other), jnp.where(lower, other, mine)], axis=1
+    )
+
+
+def dot(a, b):
+    return jnp.dot(a, b, preferred_element_type=f32)
+
+
+def ctx_sum(v):
+    if not small_plane():
+        return lax.psum_scatter(v, "ctx", scatter_dimension=1, tiled=True).astype(f32)
     member = lax.axis_index("ctx")
-    return [(mine, half)] + [(other + (member ^ j) * quarter, quarter) for j in range(4)]
-
-
-def fetch(weight):
-    if not small_plane():
-        return lax.all_gather(weight, "expert", axis=0, tiled=True)
-    quarter = weight.shape[0] // 4
-    member = lax.axis_index("ctx")
-    mine = lax.dynamic_slice_in_dim(weight, member * quarter, quarter, axis=0)
-    first = over_y(mine)
-    second = core(first)
-    third = over_x(first)
-    fourth = core(third)
-    return jnp.concatenate([weight, first, second, third, fourth], axis=0)
-
-
-def reorder(v, axis):
-    total = v.shape[axis]
-    return jnp.concatenate(
-        [
-            lax.dynamic_slice_in_dim(v, start, size, axis=axis)
-            for start, size in piece_starts(total)
-        ],
-        axis=axis,
-    )
-
-
-def restore(v, axis):
-    total = v.shape[axis]
-    out = jnp.zeros_like(v)
-    at = 0
-    for start, size in piece_starts(total):
-        piece = lax.slice_in_dim(v, at, at + size, axis=axis)
-        out = lax.dynamic_update_slice_in_dim(out, piece, start, axis=axis)
-        at += size
-    return out
-
-
-def ctx_blocks(v):
-    count = lax.axis_size("ctx")
-    member = lax.axis_index("ctx")
-    if count != 4:
-        out = lax.all_gather(v, "ctx", axis=0, tiled=False)
-        return [out[i] for i in range(count)], [jnp.int32(i) for i in range(count)]
-    vc, vx = core(v), over_x(v)
-    return [v, vc, vx, core(vx)], [member ^ j for j in range(4)]
-
-
-def ctx_sum(blocks):
-    count = lax.axis_size("ctx")
-    if count != 4:
-        return lax.psum_scatter(
-            jnp.concatenate(blocks, axis=0), "ctx", scatter_dimension=0, tiled=True
-        ).astype(f32)
-    near = blocks[0].astype(f32) + core(blocks[1]).astype(f32)
-    far = (blocks[2].astype(f32) + core(blocks[3]).astype(f32)).astype(bf16)
+
+    def block(j):
+        return lax.dynamic_slice_in_dim(v, (member ^ j) * PROMPT_DEV, PROMPT_DEV, axis=1)
+
+    near = block(0).astype(f32) + core(block(1)).astype(f32)
+    far = (block(2).astype(f32) + core(block(3)).astype(f32)).astype(bf16)
     return near + over_x(far).astype(f32)
 
 
@@ -220,53 +572,88 @@
     heads_per_group = QUERY_HEADS // KEY_VALUE_HEADS
     score_scale = HEAD_SIZE ** (-0.5)
     hidden_ff = gate_up.shape[2] // 2
-    full_query, full_key, full_value, full_output = (
-        fetch(query_weight),
-        fetch(key_matrix),
-        fetch(value_matrix),
-        fetch(output_weight),
-    )
     order = relative()
-    g_rows = jnp.concatenate(gather_plane(out_grad), axis=0)
-    route_rows = jnp.concatenate(gather_plane(routes), axis=0)
-
-    inputs = hidden_in.astype(f32)
-    scale_in = rms_scale(inputs)
-    normalized_input = (inputs * scale_in * attn_gain).astype(bf16)
-    normed_reordered = reorder(normalized_input, 1)
-    query_pre = jnp.dot(normed_reordered, full_query, preferred_element_type=f32).reshape(
-        count_of_rows, QUERY_HEADS, HEAD_SIZE
-    )
-    key_before_norm = jnp.dot(normed_reordered, full_key, preferred_element_type=f32).reshape(
-        count_of_rows, KEY_VALUE_HEADS, HEAD_SIZE
-    )
-    value_low = (
-        jnp.dot(normed_reordered, full_value, preferred_element_type=f32)
-        .astype(bf16)
-        .reshape(count_of_rows, KEY_VALUE_HEADS, HEAD_SIZE)
-    )
-    query_inv = rms_scale(query_pre)
-    key_inv = rms_scale(key_before_norm)
     member = lax.axis_index("ctx")
     offsets = jnp.arange(count_of_rows, dtype=jnp.int32)
     position = jnp.where(
         offsets < PROMPT_DEV, member * PROMPT_DEV + offsets, prompt_all + offsets - PROMPT_DEV
     )
     cosine, rope_sine = angles(position, HEAD_SIZE)
+    narrow = KEY_VALUE_HEADS * HEAD_SIZE
+    wide = QUERY_HEADS * HEAD_SIZE
+    route_rows = gather_small(routes)
+    inputs = hidden_in.astype(f32)
+    scale_in = rms_scale(inputs)
+    if small_plane():
+        sign = jnp.where(jnp.arange(HEAD_SIZE) < HEAD_SIZE // 2, -1.0, 1.0)
+        (
+            kv_other,
+            q_other,
+            o_other,
+            g_blocks,
+            normalized_input,
+            query_pre,
+            key_value_pre,
+            kv_low,
+            kv_blocks,
+        ) = fetch_and_project(
+            hidden_in, attn_gain, key_gain, cosine, rope_sine * sign, key_matrix, value_matrix,
+            query_weight, output_weight, out_grad,
+        )
+        kv_weights = [jnp.concatenate([key_matrix, value_matrix], axis=1), kv_other]
+        q_weights = [query_weight, q_other]
+        o_weights = [output_weight, o_other]
+        g_rows = g_blocks.reshape(spread_count * count_of_rows, MODEL_WIDTH)
+        kv_blocks = kv_blocks.reshape(prompt_all, 2 * narrow)
+    else:
+        full = [
+            lax.all_gather(w, "expert", axis=0, tiled=True)
+            for w in (
+                jnp.concatenate([key_matrix, value_matrix], axis=1),
+                query_weight,
+                output_weight,
+            )
+        ]
+        kv_weights, q_weights, o_weights = [[w] for w in full]
+        g_rows = lax.all_gather(out_grad, plane, axis=0, tiled=True)
+        normalized_input = (inputs * scale_in * attn_gain).astype(bf16)
+        query_pre = dot(normalized_input, q_weights[0])
+        key_value_pre = dot(normalized_input, kv_weights[0])
+        key_pre = key_value_pre[:, :narrow].reshape(count_of_rows, KEY_VALUE_HEADS, HEAD_SIZE)
+        key_low = rotate(
+            key_pre * rms_scale(key_pre) * key_gain, cosine[:, None, :], rope_sine[:, None, :]
+        ).astype(bf16)
+        kv_low = jnp.concatenate(
+            [key_low.reshape(count_of_rows, narrow), key_value_pre[:, narrow:].astype(bf16)],
+            axis=1,
+        )
+        kv_blocks = lax.all_gather(kv_low[:PROMPT_DEV], "ctx", axis=0, tiled=True)
+
+    def forward_dot(v, weights):
+        if len(weights) == 1:
+            return dot(v, weights[0])
+        mine, other = halves(v)
+        return dot(mine, weights[0]) + dot(other, weights[1])
+
+    def backward_dot(v, weights):
+        parts = [dot(v, w.T) for w in weights]
+        return parts[0] if len(parts) == 1 else join_halves(*parts)
+
+    query_pre = query_pre.reshape(count_of_rows, QUERY_HEADS, HEAD_SIZE)
+    key_before_norm = key_value_pre[:, :narrow].reshape(
+        count_of_rows, KEY_VALUE_HEADS, HEAD_SIZE
+    )
+    query_inv = rms_scale(query_pre)
+    key_inv = rms_scale(key_before_norm)
     cosine = cosine[:, None, :]
     rope_sine = rope_sine[:, None, :]
     query_reduced = rotate(query_pre * query_inv * query_gain, cosine, rope_sine).astype(bf16)
-    key_low = rotate(key_before_norm * key_inv * key_gain, cosine, rope_sine).astype(bf16)
-    pair_blocks, members = ctx_blocks(
-        jnp.stack([key_low[:PROMPT_DEV], value_low[:PROMPT_DEV]])
-    )
-    keys_all = jnp.concatenate([b[0] for b in pair_blocks] + [key_low[PROMPT_DEV:]], axis=0)
-    values_all = jnp.concatenate([b[1] for b in pair_blocks] + [value_low[PROMPT_DEV:]], axis=0)
-    prompt_offsets = jnp.arange(PROMPT_DEV, dtype=jnp.int32)
-    key_position = jnp.concatenate(
-        [m * PROMPT_DEV + prompt_offsets for m in members]
-        + [prompt_all + jnp.arange(count_of_rows - PROMPT_DEV, dtype=jnp.int32)]
-    )
+    kv_all = jnp.concatenate([kv_blocks, kv_low[PROMPT_DEV:]], axis=0)
+    keys_all, values_all = [
+        v.reshape(kv_all.shape[0], KEY_VALUE_HEADS, HEAD_SIZE)
+        for v in (kv_all[:, :narrow], kv_all[:, narrow:])
+    ]
+    key_position = jnp.arange(kv_all.shape[0], dtype=jnp.int32)
     visible = key_position[None, :] <= position[:, None]
     grouped_queries = query_reduced.reshape(
         count_of_rows, KEY_VALUE_HEADS, heads_per_group, HEAD_SIZE
@@ -290,11 +677,14 @@
         .reshape(count_of_rows, QUERY_HEADS * HEAD_SIZE)
         .astype(bf16)
     )
-    residual = inputs + jnp.dot(reorder(attended, 1), full_output, preferred_element_type=f32)
+    residual = inputs + forward_dot(attended, o_weights)
     scale_ffn = rms_scale(residual)
     ffn_in = (residual * scale_ffn * ffn_gain).astype(bf16)
 
-    rows = jnp.concatenate(gather_plane(ffn_in), axis=0)
+    if small_plane():
+        rows = gather_blocks(ffn_in, 2).reshape(spread_count * count_of_rows, MODEL_WIDTH)
+    else:
+        rows = lax.all_gather(ffn_in, plane, axis=0, tiled=True)
     expert_count = local_experts * spread_count
     expert_ids = jnp.arange(expert_count, dtype=jnp.int32)
 
@@ -313,8 +703,8 @@
     moe_part = 0.0
     row_part = 0.0
     gate_grads = []
-    gate_up_local = []
-    down_local = []
+    hiddens = []
+    projected_grads = []
     for which in range(local_experts):
         gate = gates_mine[:, which : which + 1]
         projected = jnp.dot(rows, gate_up[which], preferred_element_type=f32)
@@ -329,24 +719,30 @@
         gate_back = hidden_back * up_part * sigmoid_gate * (1.0 + gate_part * (1.0 - sigmoid_gate))
         up_back = hidden_back * gate_part * sigmoid_gate
         projected_grad = jnp.concatenate([gate_back, up_back], axis=-1).astype(bf16)
-        moe_part = moe_part + jnp.dot(hidden_low, down_proj[which], preferred_element_type=f32)
+        hiddens.append(hidden_low)
+        projected_grads.append(projected_grad)
+    gate_up_local = jnp.stack(
+        [jnp.dot(rows.T, v, preferred_element_type=f32).astype(bf16) for v in projected_grads]
+    )
+    down_local = jnp.stack(
+        [jnp.dot(v.T, g_rows, preferred_element_type=f32).astype(bf16) for v in hiddens]
+    )
+    gate_up_low = lax.psum_scatter(gate_up_local, "dp", scatter_dimension=1, tiled=True)
+    down_low = lax.psum_scatter(down_local, "dp", scatter_dimension=1, tiled=True)
+    gate_up_grad = gate_up_low.astype(f32)
+    down_grad = down_low.astype(f32)
+    projected_grads, hiddens = lax.optimization_barrier(
+        ((projected_grads, hiddens), gate_up_local, down_local)
+    )[0]
+    for which in range(local_experts):
         row_part = row_part + jnp.dot(
-            projected_grad, gate_up[which].T, preferred_element_type=f32
+            projected_grads[which], gate_up[which].T, preferred_element_type=f32
         )
-        gate_up_local.append(jnp.dot(rows.T, projected_grad, preferred_element_type=f32))
-        down_local.append(jnp.dot(hidden_low.T, g_rows, preferred_element_type=f32))
-    gate_up_grad, down_grad = (
-        lax.psum_scatter(
-            jnp.stack(gate_up_local).astype(bf16), "dp", scatter_dimension=1, tiled=True
-        ).astype(f32),
-        lax.psum_scatter(
-            jnp.stack(down_local).astype(bf16), "dp", scatter_dimension=1, tiled=True
-        ).astype(f32),
-    )
+        moe_part = moe_part + jnp.dot(hiddens[which], down_proj[which], preferred_element_type=f32)
 
     def blocks_of(v):
         return [
-            v[i * count_of_rows : (i + 1) * count_of_rows] for i in range(spread_count)
+            lax.dynamic_slice_in_dim(v, i * count_of_rows, count_of_rows, axis=0) for i in order
         ]
 
     moe_sum = scatter_plane(blocks_of(moe_part.astype(bf16)))
@@ -370,9 +766,11 @@
     ffn_gain_local = jnp.sum(ffn_in_grad * residual * scale_ffn, axis=0)
     branch_low = residual_grad.astype(bf16)
     branch_rows = jnp.concatenate(gather_plane(branch_low), axis=0)
-    attended_grad = restore(
-        jnp.dot(branch_low, full_output.T, preferred_element_type=f32).astype(bf16), 1
-    ).reshape(count_of_rows, KEY_VALUE_HEADS, heads_per_group, HEAD_SIZE)
+    attended_grad = (
+        backward_dot(branch_low, o_weights)
+        .astype(bf16)
+        .reshape(count_of_rows, KEY_VALUE_HEADS, heads_per_group, HEAD_SIZE)
+    )
     attention_again = jnp.exp(scores_of() - log_total)
     prob_grad = jnp.einsum(
         "rkgd,skd->kgrs", attended_grad, values_all, preferred_element_type=f32
@@ -394,11 +792,7 @@
         preferred_element_type=f32,
     )
     pair_grads = jnp.stack([key_grad_all[:prompt_all], value_grad_all[:prompt_all]]).astype(bf16)
-    prompt_grads = ctx_sum(
-        [pair_grads[:, i * PROMPT_DEV : (i + 1) * PROMPT_DEV] for i in range(ctx_count)]
-        if ctx_count == 4
-        else [pair_grads]
-    )
+    prompt_grads = ctx_sum(pair_grads)
     key_grad = jnp.concatenate([prompt_grads[0], key_grad_all[prompt_all:]], axis=0)
     value_gradient = jnp.concatenate([prompt_grads[1], value_grad_all[prompt_all:]], axis=0)
     query_rot_grad = rotate_back(query_grad, cosine, rope_sine)
@@ -418,18 +812,16 @@
     value_before_norm_gradient = value_gradient.astype(bf16).reshape(
         count_of_rows, KEY_VALUE_HEADS * HEAD_SIZE
     )
-    normed_grad = jnp.dot(query_pre_grad, full_query.T, preferred_element_type=f32)
-    normed_grad = normed_grad + jnp.dot(key_pre_grad, full_key.T, preferred_element_type=f32)
-    normed_grad = normed_grad + jnp.dot(
-        value_before_norm_gradient, full_value.T, preferred_element_type=f32
-    )
-    normed_grad = restore(normed_grad, 1)
+    key_value_grad = jnp.concatenate([key_pre_grad, value_before_norm_gradient], axis=1)
+    normed_grad = backward_dot(query_pre_grad, q_weights) + backward_dot(
+        key_value_grad, kv_weights
+    )
     attn_gain_local = jnp.sum(normed_grad * inputs * scale_in, axis=0)
     hidden_grad = residual_grad + norm_back(inputs, scale_in, attn_gain, normed_grad)
 
     pre_rows = jnp.concatenate(
         gather_plane(
-            jnp.concatenate([query_pre_grad, key_pre_grad, value_before_norm_gradient], axis=1)
+            jnp.concatenate([query_pre_grad, key_value_grad], axis=1)
         ),
         axis=0,
     )
@@ -445,18 +837,15 @@
         ]
         return jnp.concatenate(exchange_plane(parts), axis=0)
 
-    normed_owned = owned(normalized_input)
-    attended_owned = owned(attended)
+    normed_owned = owned(after(normalized_input, rows))
+    attended_owned = owned(after(attended, rows))
     pre_local = jnp.dot(normed_owned.T, pre_rows, preferred_element_type=f32)
     output_local = jnp.dot(attended_owned.T, branch_rows, preferred_element_type=f32)
-    pre_sum = lax.psum_scatter(pre_local.astype(bf16), "dp", scatter_dimension=0, tiled=True).astype(
-        f32
-    )
-    output_sum = lax.psum_scatter(
-        output_local.astype(bf16), "dp", scatter_dimension=0, tiled=True
-    ).astype(f32)
-    wide = QUERY_HEADS * HEAD_SIZE
-    narrow = KEY_VALUE_HEADS * HEAD_SIZE
+    pre_local, output_local = lax.optimization_barrier(
+        ((pre_local.astype(bf16), output_local.astype(bf16)), gate_up_low, down_low)
+    )[0]
+    output_sum = lax.psum_scatter(output_local, "dp", scatter_dimension=0, tiled=True).astype(f32)
+    pre_sum = lax.psum_scatter(pre_local, "dp", scatter_dimension=0, tiled=True).astype(f32)
 
     small = jnp.concatenate(
         [

time: 1200 us -> 904 us (0.75)
  waiting for transfers between devices: 526 us -> 182 us
  Pallas kernels: 0 us -> 157 us
  local copies, waits for them, and re-layouts: 212 us -> 156 us
  starting transfers between devices: 83.5 us -> 50.2 us
  matrix products: 251 us -> 237 us
    reduce_scatter x4, waiting for transfers between devices: 270 us -> 48.1 us  [the longest x1 48.1 us: body(): lax.psum_scatter(pre_local, 'dp', scatter_dimension=0, tiled=True)]
    pallas_call x0 -> x2, Pallas kernels: none -> 157 us  [the longest x1 125 us: fetch_and_project(): pl.pallas_call(fetch_kernel, out_shape=[jax.ShapeDtypeStruct((half, 2 * n...]
    ppermute x83 -> x40, waiting for transfers between devices: 217 us -> 87.4 us  [swap(): lax.ppermute(v, axis, [(i, i ^ bit) for i in range(lax.axis_size(axis))])]
    unnamed x324 -> x280, local copies, waits for them, and re-layouts: 106 us -> 67.4 us
    ppermute x83 -> x40, starting transfers between devices: 59.4 us -> 26.9 us  [swap(): lax.ppermute(v, axis, [(i, i ^ bit) for i in range(lax.axis_size(axis))])]
    dot_general x16, matrix products: 142 us -> 124 us  [the longest x8 36.5 us: dot(): return jnp.dot(a, b, preferred_element_type=f32)]
  transfers between devices with their start and end apart: 109 -> 66, of which waited for: 38 -> 21; matrix products, arithmetic and copies ran while one was open for 39% -> 52% of each run, Pallas kernels for 0% -> 18%
where the time goes in v2:
time: 904 us; the launch traced here: 894 us
  matrix products  237 us (26%)
  waiting for transfers between devices  182 us (20%)
  Pallas kernels  157 us (17%)
  local copies, waits for them, and re-layouts  156 us (17%)
  other arithmetic  93.9 us (10%)
  starting transfers between devices  50.2 us (6%)
  between operations  16 us (2%)
    pallas_call x1, Pallas kernels, fetch_and_project(): pl.pallas_call(fetch_kernel, out_shape=[jax.ShapeDtypeStruct((half, 2 * n...  125 us
    ppermute x40, waiting for transfers between devices, swap(): lax.ppermute(v, axis, [(i, i ^ bit) for i in range(lax.axis_size(axis))])  87.4 us
    unnamed x280, local copies, waits for them, and re-layouts  67.4 us
    reduce_scatter x1, waiting for transfers between devices, body(): lax.psum_scatter(pre_local, 'dp', scatter_dimension=0, tiled=True)  48.1 us
    ppermute x21, waiting for transfers between devices, exchange_plane(): out.append(lax.ppermute(blocks[r], plane, pairs))  37.7 us
    dot_general x8, matrix products, dot(): return jnp.dot(a, b, preferred_element_type=f32)  36.5 us
    pallas_call x1, Pallas kernels, gather_blocks(): pl.pallas_call(gather_kernel, out_shape=jax.ShapeDtypeStruct((lax.axis_si...  32.3 us
    dot_general x2, matrix products, body(): jnp.dot(projected_grads[which], gate_up[which].T, preferred_element_type=...  31.4 us
  transfers between devices with their start and end apart: 66, of which 21 were waited for; matrix products, arithmetic and copies ran while one was open for 52% of the time, Pallas kernels for 18%

profile of v2, /device:TPU:0, one launch (start us, length us, event | category | flops | bytes accessed | tf_op | source)
XLA Modules:
  0.0 893.7 jit_solution(16508594704791466675)
XLA Ops:
  7.2 3.0 collective-permute-start
  15.8 125.1 %shard_map.237 = (bf16[1024,1024]{1,0:T(8,128)(2,1)}, bf16[1024,4096]{1,0:T(8,128)(2,1)}, bf16[2048,2048]{1,0:T(8,128)(2,1)}, bf16[8,192,2048]{2,1,0:T(8,128)(2,...) custom-call(bf16[192,2048]{1,0:T(8,128)(2,1)S(1)} %copy-done.1, ...), custom_call_target="tpu_custom_call" | custom-call | tf_op jit(solution)/shard_map/pallas_call | solution.py:448
  140.9 4.4 copy.447
  145.3 5.0 copy.371
  159.0 3.4 copy.373
  162.4 3.4 copy.372
  166.4 5.4 fusion.30
  171.8 3.4 fusion.129
  175.2 4.2 fusion.3
  180.7 4.3 fusion.58
  186.8 6.4 fusion.73
  193.2 5.8 multiply_reduce_fusion.6
  201.2 32.3 %shard_map.238 = bf16[8,192,2048]{2,1,0:T(8,128)(2,1)} custom-call(bf16[192,2048]{1,0:T(8,128)(2,1)} %multiply_convert_fusion.6.mine_ref), custom_call_target="tpu_custom_call" | custom-call | tf_op jit(solution)/shard_map/pallas_call | solution.py:491
  238.9 16.0 %fusion.16 = f32[1536,1536]{0,1:T(8,128)} fusion(bf16[1536,2048]{1,0:T(8,128)(2,1)} %bitcast.308, bf16[2,2048,1536]{2,1,0:T(8,128)(2,1)} %param.24), kind=kOutput, calls=%fused_computation.29 | convolution fusion | flops 9663676416 | bytes 22020096 | tf_op jit(solution)/shard_map/dot_general | solution.py:710
  254.9 14.0 %fusion.12 = f32[1536,1536]{0,1:T(8,128)} fusion(bf16[1536,2048]{1,0:T(8,128)(2,1)S(1)} %bitcast.312, bf16[2,2048,1536]{2,1,0:T(8,128)(2,1)} %param.24), kind=kOutput, calls=%fused_computation.25 | convolution fusion | flops 9663676416 | bytes 22020096 | tf_op jit(solution)/shard_map/dot_general | solution.py:710
  272.5 9.9 %dynamic-slice_reduce_fusion = (bf16[192,4,128]{2,1,0:T(4,128)(2,1)S(1)}, bf16[192,4,128]{2,1,0:T(4,128)(2,1)S(1)}, bf16[192,4,128]{2,1,0:T(4,128)(2,1)S(1)}, bf...) fusion(bf16[192,4,8,128]{3,2,1,0:T(8,128)(2,1)S(1)} %bitcast.32, ...), kind=kLoop, calls=%fused_computation.192 | loop fusion | bytes 3145760 | tf_op jit(solution)/shard_map/jit(dynamic_index_in_dim)/dynamic_slice | solution.py:833
  290.7 5.3 copy.426
  298.5 5.5 copy.431
  310.0 4.7 fusion.130
  314.8 14.0 %multiply_convert_fusion.3 = (bf16[1536,768]{0,1:T(8,128)(2,1)S(1)}, bf16[1536,768]{0,1:T(8,128)(2,1)}, f32[1536]{0:T(1024)S(1)}, bf16[1536,768]{0,1:T(8,128)(2,1)S(1)}) fusion(f32[1536,1536]{0,1:T(8,128)} %fusion.12, f32[1536]{0:T(1024)S(1)} %get-tuple-element.176, bf16[1536,2048]{1,0:T(8,128)(2,1)} %bitcast.376, bf16[2,768,2048]{2,1,0:T(8,128)(2,1)} %param.25), kind=kOutput, calls=%fused_computation.44 | convolution fusion | flops 4855429632 | bytes 25964544 | tf_op jit(solution)/shard_map/dot_general | solution.py:711
  328.9 5.3 fusion.41
  334.2 11.5 %multiply_convert_fusion.5 = (bf16[1536,768]{0,1:T(8,128)(2,1)}, bf16[1536,768]{0,1:T(8,128)(2,1)}, f32[1536]{0:T(1024)S(1)}, bf16[1536,768]{0,1:T(8,128)(2,1)S(1)}) fusion(f32[1536,1536]{0,1:T(8,128)} %fusion.16, f32[1536]{0:T(1024)S(1)} %get-tuple-element.177, bf16[1536,2048]{1,0:T(8,128)(2,1)S(1)} %bitcast.380, bf16[2,768,2048]{2,1,0:T(8,128)(2,1)S(1)} %bitcast.375), kind=kOutput, calls=%fused_computation.47 | convolution fusion | flops 4855429632 | bytes 25966592 | tf_op jit(solution)/shard_map/dot_general | solution.py:711
  347.1 5.7 fusion.40
  352.8 3.1 pad_maximum_fusion.1
  356.0 5.0 pad_maximum_fusion.2
  361.1 3.1 pad_maximum_fusion.3
  364.2 12.4 %fusion.10 = bf16[1,2048,1536]{2,1,0:T(8,128)(2,1)S(1)} fusion(bf16[1536,2048]{1,0:T(8,128)(2,1)S(1)} %bitcast.315, bf16[1536,768]{0,1:T(8,128)(2,1)S(1)} %copy-done.48, bf16[1536,768]{0,1:T(8,128)(2,1)S(1)} %get-tuple-element.185), kind=kOutput, calls=%fused_computation.21 | convolution fusion | flops 9676259328 | bytes 17301504 | tf_op jit(solution)/shard_map/dot_general | solution.py:725
  376.6 12.9 %fusion.9 = bf16[1,2048,1536]{2,1,0:T(8,128)(2,1)S(1)} fusion(bf16[1536,2048]{1,0:T(8,128)(2,1)S(1)} %bitcast.316, bf16[1536,768]{0,1:T(8,128)(2,1)} %get-tuple-element.188, bf16[1536,768]{0,1:T(8,128)(2,1)} %get-tuple-element.187), kind=kOutput, calls=%fused_computation.20 | convolution fusion | flops 9676259328 | bytes 17301504 | tf_op jit(solution)/shard_map/dot_general | solution.py:725
  389.5 5.5 pad_maximum_fusion
  397.4 16.7 %fusion.14 = f32[1536,2048]{1,0:T(8,128)} fusion(bf16[1536,1536]{0,1:T(8,128)(2,1)} %pad_maximum_fusion.2, bf16[2,2048,1536]{2,1,0:T(8,128)(2,1)} %param.24), kind=kOutput, calls=%fused_computation.27 | convolution fusion | flops 9663676416 | bytes 23592960 | tf_op jit(solution)/shard_map/dot_general | solution.py:738
  414.1 14.7 %add_convert_fusion = bf16[1536,2048]{1,0:T(8,128)(2,1)S(1)} fusion(f32[1536,2048]{1,0:T(8,128)} %fusion.14, bf16[1536,1536]{0,1:T(8,128)(2,1)S(1)} %bitcast.337, bf16[2,2048,1536]{2,1,0:T(8,128)(2,1)} %param.24), kind=kOutput, calls=%fused_computation.12 | convolution fusion | flops 9669967872 | bytes 29884416 | tf_op jit(solution)/shard_map/dot_general | solution.py:738
  432.2 10.4 %fusion.34 = f32[1536,2048]{1,0:T(8,128)} fusion(bf16[1536,768]{0,1:T(8,128)(2,1)S(1)} %copy-done.97, bf16[2,768,2048]{2,1,0:T(8,128)(2,1)} %param.25), kind=kOutput, calls=%fused_computation.71 | convolution fusion | flops 4831838208 | bytes 18087936 | tf_op jit(solution)/shard_map/dot_general | solution.py:741
  442.6 9.1 %add_convert_fusion.1 = bf16[1536,2048]{1,0:T(8,128)(2,1)S(1)} fusion(f32[1536,2048]{1,0:T(8,128)} %fusion.34, bf16[1536,768]{0,1:T(8,128)(2,1)S(1)} %copy-done.99, bf16[2,768,2048]{2,1,0:T(8,128)(2,1)} %param.25), kind=kOutput, calls=%fused_computation.13 | convolution fusion | flops 4838129664 | bytes 24379392 | tf_op jit(solution)/shard_map/dot_general | solution.py:741
  469.3 5.3 collective-permute-done.33
  476.0 4.5 collective-permute-done.35
  495.0 3.5 add_convert_fusion.4
  501.9 8.5 collective-permute-done.17
  512.4 8.3 collective-permute-done.9
  525.7 18.5 %collective-permute-done.50 = bf16[192,512]{1,0:T(8,128)(2,1)S(1)} collective-permute-done((bf16[192,512]{1,0:T(8,128)(2,1)S(1)}, bf16[192,512]{1,0:T(8,128)(2,1)S(1)}, u32[]{:S(2)}, u32[]{:S(2)}) %collective-permute-start.50) | collective-permute-done | bytes 196640 | tf_op jit(solution)/shard_map/ppermute | solution.py:129
  554.2 11.2 %collective-permute-done.10 = bf16[192,2048]{1,0:T(8,128)(2,1)S(1)} collective-permute-done((bf16[192,2048]{1,0:T(8,128)(2,1)S(1)}, bf16[192,2048]{1,0:T(8,128)(2,1)S(1)}, u32[]{:S(2)}, u32[]{:S(2)}) %collective-permute-start.10) | collective-permute-done | bytes 786464 | tf_op jit(solution)/shard_map/ppermute | solution.py:66
  574.3 6.6 fusion.71
  581.8 10.1 %fusion = (f32[4,8,192]{2,1,0:T(8,128)S(1)}, f32[4,576,192,8]{1,2,3,0:T(8,128)}) fusion(f32[4,8,192,576]{3,2,1,0:T(8,128)S(1)} %bitcast.302, f32[4,8,192]{2,1,0:T(8,128)S(1)} %copy-done.58, bf16[192,4,8,128]{3,0,2,1:T(8,128)(2,1)S(1)} %copy_dynamic-update-slice_fusion, bf16[576,4,128,1]{2,1,0,3:T(4,128)(2,1)} %bitcast.340), kind=kOutput, calls=%fused_computation.3 | convolution fusion | flops 916580352 | bytes 30523392 | tf_op jit(solution)/shard_map/rkgd,skd->kgrs/dot_general | solution.py:775
  591.9 7.5 fusion.2
  599.4 3.1 copy-done.19
  604.7 3.4 copy.387
  608.1 3.5 copy.384
  614.2 7.9 fusion.67
  630.2 3.8 pad_maximum_fusion.4
  634.0 5.4 copy.432
  643.1 12.1 %multiply_reduce_fusion.2 = (f32[4096]{0:T(1024)}, bf16[192,4096]{1,0:T(8,128)(2,1)S(1)}) fusion(f32[192,4096]{1,0:T(8,128)S(1)} %copy-done.30, f32[192,4096]{1,0:T(8,128)} %get-tuple-element.32, f32[192,4096]{1,0:T(8,128)} %copy.432, f32[192,4096]{1,0:T(8,128)S(1)} %copy-done.31, f32[24,8,32,128]{3,2,1,0:T(8,128)} %bitcast.322, ...), kind=kLoop, calls=%fused_computation.78 | loop fusion | flops 8646656 | bytes 23625728 | tf_op jit(solution)/shard_map/reduce_sum | solution.py:800
  684.2 36.1 %collective-permute-done.57 = bf16[96,2048]{1,0:T(8,128)(2,1)S(1)} collective-permute-done((bf16[96,2048]{1,0:T(8,128)(2,1)S(1)}, bf16[96,2048]{1,0:T(8,128)(2,1)S(1)}, u32[]{:S(2)}, u32[]{:S(2)}) %collective-permute-start.57) | collective-permute-done | bytes 393248 | tf_op jit(solution)/shard_map/ppermute | solution.py:66
  724.1 7.4 convolution_convert_fusion.5
  736.5 3.0 constant_dynamic-update-slice_fusion.8
  742.4 14.6 %collective-permute-done.40 = bf16[96,5120]{1,0:T(8,128)(2,1)S(1)} collective-permute-done((bf16[96,5120]{1,0:T(8,128)(2,1)S(1)}, bf16[96,5120]{1,0:T(8,128)(2,1)S(1)}, u32[]{:S(2)}, u32[]{:S(2)}) %collective-permute-start.40) | collective-permute-done | bytes 983072 | tf_op jit(solution)/shard_map/ppermute | solution.py:66
  762.5 3.0 constant_dynamic-update-slice_fusion.5
  771.0 11.0 %convolution_convert_fusion.2 = bf16[256,5120]{1,0:T(8,128)(2,1)} fusion(bf16[1536,256]{0,1:T(8,128)(2,1)S(1)} %copy-done.59, bf16[1536,5120]{1,0:T(8,128)(2,1)} %constant_dynamic-update-slice_fusion), kind=kOutput, calls=%fused_computation.22 | convolution fusion | flops 4027842560 | bytes 19136512 | tf_op jit(solution)/shard_map/dot_general | solution.py:842
  788.1 6.6 fusion.133
  794.8 6.5 broadcast_select_fusion.3
  806.3 5.4 all-to-all-start
  811.8 3.3 fusion.54
  815.1 8.9 all-to-all-done
  826.1 3.5 convert_element_type.322
  829.6 3.6 convert_element_type.321
  835.3 48.1 %reduce-scatter.9.cloned.1.call-done = bf16[64,5120]{1,0:T(8,128)(2,1)} async-done(((bf16[256,5120]{1,0:T(8,128)(2,1)}), bf16[64,5120]{1,0:T(8,128)(2,1)}) %reduce-scatter.9.cloned.1.call-update) | async-done | bytes 655376 | tf_op jit(solution)/shard_map/reduce_scatter | solution.py:848
  (562 shorter events, 202.5 us)
Async XLA Ops:
  7.2 774.8 %reduce-scatter.7.cloned.1.call-start = ((), (), s32[]{:S(2)}) async-start(), calls=%async_computation.6 | async-start | bytes 7864320 | tf_op jit(solution)/shard_map/reduce_scatter | solution.py:731
  7.2 276.9 %collective-permute-start = (s32[192,8]{0,1:T(8,128)}, s32[192,8]{0,1:T(8,128)S(1)}, u32[]{:S(2)}, u32[]{:S(2)}) collective-permute-start(s32[192,8]{0,1:T(8,128)} %param.26), channel_id=1, source_target_pairs={{0,1},{1,0},{2,3},{3,2},{4,5},{5,4},{6,7},{7,6},{8,9},{9,8},{10,11... | collective-permute-start | bytes 18440 | tf_op jit(solution)/shard_map/ppermute | solution.py:66
  237.1 226.8 %collective-permute-start.29 = (bf16[192,256]{0,1:T(8,128)(2,1)}, bf16[192,256]{0,1:T(8,128)(2,1)}, u32[]{:S(2)}, u32[]{:S(2)}) collective-permute-start(bf16[192,256]{0,1:T(8,128)(2,1)} %bitcast.45), channel_id=1, source_target_pairs={{0,1},{1,0},{2,3},{3,2},{4,5},{5,4},{6,7},{7,6},{8,9},{9,8},{10,11... | collective-permute-start | bytes 294920 | tf_op jit(solution)/shard_map/ppermute | solution.py:129
  238.8 225.1 %collective-permute-start.30 = (bf16[192,256]{0,1:T(8,128)(2,1)}, bf16[192,256]{0,1:T(8,128)(2,1)}, u32[]{:S(2)}, u32[]{:S(2)}) collective-permute-start(bf16[192,256]{0,1:T(8,128)(2,1)} %bitcast.46), channel_id=1, source_target_pairs={{0,2},{1,3},{2,0},{3,1},{4,6},{5,7},{6,4},{7,5},{8,10},{9,11},{10,... | collective-permute-start | bytes 294920 | tf_op jit(solution)/shard_map/ppermute | solution.py:129
  285.5 23.4 %collective-permute-start.2 = (s32[768,8]{0,1:T(8,128)S(1)}, s32[768,8]{0,1:T(8,128)S(1)}, u32[]{:S(2)}, u32[]{:S(2)}) collective-permute-start(s32[768,8]{0,1:T(8,128)S(1)} %pad_add_fusion), channel_id=1, source_target_pairs={{0,4},{2,6},{4,0},{6,2},{1,5},{3,7},{5,1},{7,3},{8,12},{10,14},{12... | collective-permute-start | bytes 73736 | tf_op jit(solution)/shard_map/ppermute | solution.py:66
  356.0 426.1 %reduce-scatter.5.cloned.1.call-start = ((), (), s32[]{:S(2)}) async-start(), calls=%async_computation.5 | async-start | bytes 15728640 | tf_op jit(solution)/shard_map/reduce_scatter | solution.py:730
  395.2 60.6 %collective-permute-start.19 = (f32[192,2]{0,1:T(2,128)S(1)}, f32[192,2]{0,1:T(2,128)S(1)}, u32[]{:S(2)}, u32[]{:S(2)}) collective-permute-start(f32[192,2]{0,1:T(2,128)S(1)} %get-tuple-element.259), channel_id=1, source_target_pairs={{0,1},{1,0},{2,3},{3,2},{4,5},{5,4},{6,7},{7,6},{8,9},{9,8},{10,11... | collective-permute-start | bytes 4616 | tf_op jit(solution)/shard_map/ppermute | solution.py:129
  397.1 60.4 %collective-permute-start.20 = (f32[192,2]{0,1:T(2,128)S(1)}, f32[192,2]{0,1:T(2,128)S(1)}, u32[]{:S(2)}, u32[]{:S(2)}) collective-permute-start(f32[192,2]{0,1:T(2,128)S(1)} %get-tuple-element.260), channel_id=1, source_target_pairs={{0,2},{1,3},{2,0},{3,1},{4,6},{5,7},{6,4},{7,5},{8,10},{9,11},{10,... | collective-permute-start | bytes 4616 | tf_op jit(solution)/shard_map/ppermute | solution.py:129
  397.1 61.9 %collective-permute-start.21 = (f32[192,2]{0,1:T(2,128)S(1)}, f32[192,2]{0,1:T(2,128)S(1)}, u32[]{:S(2)}, u32[]{:S(2)}) collective-permute-start(f32[192,2]{0,1:T(2,128)S(1)} %get-tuple-element.261), channel_id=1, source_target_pairs={{0,3},{1,2},{2,1},{3,0},{4,7},{5,6},{6,5},{7,4},{8,11},{9,10},{10,... | collective-permute-start | bytes 4616 | tf_op jit(solution)/shard_map/ppermute | solution.py:129
  455.6 377.6 %reduce-scatter.11.cloned.1.call-start = ((), (), s32[]{:S(2)}) async-start(), calls=%async_computation.8 | async-start | bytes 2621440 | tf_op jit(solution)/shard_map/reduce_scatter | solution.py:847
  455.7 3.7 collective-permute-start.22
  457.5 4.5 collective-permute-start.23
  459.0 3.3 collective-permute-start.24
  459.4 3.9 collective-permute-start.25
  462.0 5.3 collective-permute-start.31
  462.3 6.4 collective-permute-start.32
  463.3 31.0 %collective-permute-start.12 = (bf16[192,2048]{1,0:T(8,128)(2,1)}, bf16[192,2048]{1,0:T(8,128)(2,1)}, u32[]{:S(2)}, u32[]{:S(2)}) collective-permute-start(bf16[192,2048]{1,0:T(8,128)(2,1)} %get-tuple-element.196), channel_id=1, source_target_pairs={{0,2},{2,0},{4,6},{6,4},{1,3},{3,1},{5,7},{7,5},{8,10},{10,8},{12,... | collective-permute-start | bytes 2359304 | tf_op jit(solution)/shard_map/ppermute | solution.py:66
  463.9 30.6 %collective-permute-start.16 = (bf16[192,2048]{1,0:T(8,128)(2,1)}, bf16[192,2048]{1,0:T(8,128)(2,1)}, u32[]{:S(2)}, u32[]{:S(2)}) collective-permute-start(bf16[192,2048]{1,0:T(8,128)(2,1)} %get-tuple-element.194), channel_id=1, source_target_pairs={{0,2},{2,0},{4,6},{6,4},{1,3},{3,1},{5,7},{7,5},{8,10},{10,8},{12,... | collective-permute-start | bytes 2359304 | tf_op jit(solution)/shard_map/ppermute | solution.py:66
  463.9 30.9 %collective-permute-start.13 = (bf16[192,2048]{1,0:T(8,128)(2,1)}, bf16[192,2048]{1,0:T(8,128)(2,1)}, u32[]{:S(2)}, u32[]{:S(2)}) collective-permute-start(bf16[192,2048]{1,0:T(8,128)(2,1)} %get-tuple-element.195), channel_id=1, source_target_pairs={{0,2},{2,0},{4,6},{6,4},{1,3},{3,1},{5,7},{7,5},{8,10},{10,8},{12,... | collective-permute-start | bytes 2359304 | tf_op jit(solution)/shard_map/ppermute | solution.py:66
  467.2 7.4 collective-permute-start.33
  468.6 7.3 collective-permute-start.34
  474.7 5.8 collective-permute-start.35
  476.0 8.7 collective-permute-start.45
  480.5 7.2 collective-permute-start.46
  484.7 7.2 collective-permute-start.47
  487.7 35.2 %collective-permute-start.48 = (bf16[192,512]{1,0:T(8,128)(2,1)}, bf16[192,512]{1,0:T(8,128)(2,1)S(1)}, u32[]{:S(2)}, u32[]{:S(2)}) collective-permute-start(bf16[192,512]{1,0:T(8,128)(2,1)} %bitcast.365), channel_id=1, source_target_pairs={{0,4},{1,5},{2,6},{3,7},{4,0},{5,1},{6,2},{7,3},{8,12},{9,13},{10,... | collective-permute-start | bytes 589832 | tf_op jit(solution)/shard_map/ppermute | solution.py:129
  491.9 31.1 %collective-permute-start.49 = (bf16[192,512]{1,0:T(8,128)(2,1)}, bf16[192,512]{1,0:T(8,128)(2,1)S(1)}, u32[]{:S(2)}, u32[]{:S(2)}) collective-permute-start(bf16[192,512]{1,0:T(8,128)(2,1)} %bitcast.364), channel_id=1, source_target_pairs={{0,5},{1,4},{2,7},{3,6},{4,1},{5,0},{6,3},{7,2},{8,13},{9,12},{10,... | collective-permute-start | bytes 589832 | tf_op jit(solution)/shard_map/ppermute | solution.py:129
  494.3 4.3 collective-permute-start.4
  494.5 4.7 collective-permute-start.8
  494.9 5.4 collective-permute-start.5
  498.7 49.0 %collective-permute-start.11 = (bf16[192,2048]{1,0:T(8,128)(2,1)S(1)}, bf16[192,2048]{1,0:T(8,128)(2,1)S(1)}, u32[]{:S(2)}, u32[]{:S(2)}) collective-permute-start(bf16[192,2048]{1,0:T(8,128)(2,1)S(1)} %get-tuple-element.193), channel_id=1, source_target_pairs={{0,2},{2,0},{4,6},{6,4},{1,3},{3,1},{5,7},{7,5},{8,10},{10,8},{12,... | collective-permute-start | bytes 2359304 | tf_op jit(solution)/shard_map/ppermute | solution.py:66
  499.3 11.1 %collective-permute-start.17 = (bf16[96,2048]{1,0:T(8,128)(2,1)S(1)}, bf16[96,2048]{1,0:T(8,128)(2,1)S(1)}, u32[]{:S(2)}, u32[]{:S(2)}) collective-permute-start(bf16[96,2048]{1,0:T(8,128)(2,1)S(1)} %get-tuple-element.243), channel_id=1, source_target_pairs={{0,4},{2,6},{4,0},{6,2},{1,5},{3,7},{5,1},{7,3},{8,12},{10,14},{12... | collective-permute-start | bytes 1179656 | tf_op jit(solution)/shard_map/ppermute | solution.py:66
  500.2 11.3 %collective-permute-start.14 = (bf16[96,2048]{1,0:T(8,128)(2,1)S(1)}, bf16[96,2048]{1,0:T(8,128)(2,1)S(1)}, u32[]{:S(2)}, u32[]{:S(2)}) collective-permute-start(bf16[96,2048]{1,0:T(8,128)(2,1)S(1)} %get-tuple-element.242), channel_id=1, source_target_pairs={{0,1},{1,0},{2,3},{3,2},{4,5},{5,4},{6,7},{7,6},{8,9},{9,8},{10,11... | collective-permute-start | bytes 1179656 | tf_op jit(solution)/shard_map/ppermute | solution.py:66
  510.4 10.4 %collective-permute-start.9 = (bf16[96,2048]{1,0:T(8,128)(2,1)S(1)}, bf16[96,2048]{1,0:T(8,128)(2,1)S(1)}, u32[]{:S(2)}, u32[]{:S(2)}) collective-permute-start(bf16[96,2048]{1,0:T(8,128)(2,1)S(1)} %get-tuple-element.245), channel_id=1, source_target_pairs={{0,4},{2,6},{4,0},{6,2},{1,5},{3,7},{5,1},{7,3},{8,12},{10,14},{12... | collective-permute-start | bytes 1179656 | tf_op jit(solution)/shard_map/ppermute | solution.py:66
  511.5 10.5 %collective-permute-start.6 = (bf16[96,2048]{1,0:T(8,128)(2,1)S(1)}, bf16[96,2048]{1,0:T(8,128)(2,1)S(1)}, u32[]{:S(2)}, u32[]{:S(2)}) collective-permute-start(bf16[96,2048]{1,0:T(8,128)(2,1)S(1)} %get-tuple-element.244), channel_id=1, source_target_pairs={{0,1},{1,0},{2,3},{3,2},{4,5},{5,4},{6,7},{7,6},{8,9},{9,8},{10,11... | collective-permute-start | bytes 1179656 | tf_op jit(solution)/shard_map/ppermute | solution.py:66
  520.7 30.7 %collective-permute-start.18 = (bf16[192,2048]{1,0:T(8,128)(2,1)S(1)}, bf16[192,2048]{1,0:T(8,128)(2,1)S(1)}, u32[]{:S(2)}, u32[]{:S(2)}) collective-permute-start(bf16[192,2048]{1,0:T(8,128)(2,1)S(1)} %pad_maximum_fusion.9), channel_id=1, source_target_pairs={{0,1},{1,0},{2,3},{3,2},{4,5},{5,4},{6,7},{7,6},{8,9},{9,8},{10,11... | collective-permute-start | bytes 2359304 | tf_op jit(solution)/shard_map/ppermute | solution.py:66
  522.0 29.4 %collective-permute-start.15 = (bf16[192,2048]{1,0:T(8,128)(2,1)S(1)}, bf16[192,2048]{1,0:T(8,128)(2,1)S(1)}, u32[]{:S(2)}, u32[]{:S(2)}) collective-permute-start(bf16[192,2048]{1,0:T(8,128)(2,1)S(1)} %pad_maximum_fusion.8), channel_id=1, source_target_pairs={{0,4},{2,6},{4,0},{6,2},{1,5},{3,7},{5,1},{7,3},{8,12},{10,14},{12... | collective-permute-start | bytes 2359304 | tf_op jit(solution)/shard_map/ppermute | solution.py:66
  522.9 21.3 %collective-permute-start.50 = (bf16[192,512]{1,0:T(8,128)(2,1)S(1)}, bf16[192,512]{1,0:T(8,128)(2,1)S(1)}, u32[]{:S(2)}, u32[]{:S(2)}) collective-permute-start(bf16[192,512]{1,0:T(8,128)(2,1)S(1)} %bitcast.363), channel_id=1, source_target_pairs={{0,6},{1,7},{2,4},{3,5},{4,2},{5,3},{6,0},{7,1},{8,14},{9,15},{10,... | collective-permute-start | bytes 589832 | tf_op jit(solution)/shard_map/ppermute | solution.py:129
  523.0 23.4 %collective-permute-start.51 = (bf16[192,512]{1,0:T(8,128)(2,1)S(1)}, bf16[192,512]{1,0:T(8,128)(2,1)S(1)}, u32[]{:S(2)}, u32[]{:S(2)}) collective-permute-start(bf16[192,512]{1,0:T(8,128)(2,1)S(1)} %bitcast.362), channel_id=1, source_target_pairs={{0,7},{1,6},{2,5},{3,4},{4,3},{5,2},{6,1},{7,0},{8,15},{9,14},{10,... | collective-permute-start | bytes 589832 | tf_op jit(solution)/shard_map/ppermute | solution.py:129
  544.2 9.9 %collective-permute-start.3 = (bf16[192,2048]{1,0:T(8,128)(2,1)S(1)}, bf16[192,2048]{1,0:T(8,128)(2,1)S(1)}, u32[]{:S(2)}, u32[]{:S(2)}) collective-permute-start(bf16[192,2048]{1,0:T(8,128)(2,1)S(1)} %get-tuple-element.200), channel_id=1, source_target_pairs={{0,2},{2,0},{4,6},{6,4},{1,3},{3,1},{5,7},{7,5},{8,10},{10,8},{12,... | collective-permute-start | bytes 2359304 | tf_op jit(solution)/shard_map/ppermute | solution.py:66
  546.4 19.0 %collective-permute-start.10 = (bf16[192,2048]{1,0:T(8,128)(2,1)S(1)}, bf16[192,2048]{1,0:T(8,128)(2,1)S(1)}, u32[]{:S(2)}, u32[]{:S(2)}) collective-permute-start(bf16[192,2048]{1,0:T(8,128)(2,1)S(1)} %pad_maximum_fusion.7), channel_id=1, source_target_pairs={{0,1},{1,0},{2,3},{3,2},{4,5},{5,4},{6,7},{7,6},{8,9},{9,8},{10,11... | collective-permute-start | bytes 2359304 | tf_op jit(solution)/shard_map/ppermute | solution.py:66
  547.7 19.9 %collective-permute-start.7 = (bf16[192,2048]{1,0:T(8,128)(2,1)S(1)}, bf16[192,2048]{1,0:T(8,128)(2,1)S(1)}, u32[]{:S(2)}, u32[]{:S(2)}) collective-permute-start(bf16[192,2048]{1,0:T(8,128)(2,1)S(1)} %pad_maximum_fusion.6), channel_id=1, source_target_pairs={{0,4},{2,6},{4,0},{6,2},{1,5},{3,7},{5,1},{7,3},{8,12},{10,14},{12... | collective-permute-start | bytes 2359304 | tf_op jit(solution)/shard_map/ppermute | solution.py:66
  611.6 52.4 %collective-permute-start.52 = (bf16[192,2048]{1,0:T(8,128)(2,1)}, bf16[192,2048]{1,0:T(8,128)(2,1)}, u32[]{:S(2)}, u32[]{:S(2)}) collective-permute-start(bf16[192,2048]{1,0:T(8,128)(2,1)} %copy-done.60), channel_id=1, source_target_pairs={{0,1},{1,0},{2,3},{3,2},{4,5},{5,4},{6,7},{7,6},{8,9},{9,8},{10,11... | collective-permute-start | bytes 2359304 | tf_op jit(solution)/shard_map/ppermute | solution.py:66
  611.8 61.3 %collective-permute-start.53 = (bf16[192,2048]{1,0:T(8,128)(2,1)}, bf16[192,2048]{1,0:T(8,128)(2,1)}, u32[]{:S(2)}, u32[]{:S(2)}) collective-permute-start(bf16[192,2048]{1,0:T(8,128)(2,1)} %copy-done.60), channel_id=1, source_target_pairs={{0,2},{2,0},{4,6},{6,4},{1,3},{3,1},{5,7},{7,5},{8,10},{10,8},{12,... | collective-permute-start | bytes 2359304 | tf_op jit(solution)/shard_map/ppermute | solution.py:66
  612.7 58.4 %collective-permute-start.55 = (bf16[192,2048]{1,0:T(8,128)(2,1)}, bf16[192,2048]{1,0:T(8,128)(2,1)}, u32[]{:S(2)}, u32[]{:S(2)}) collective-permute-start(bf16[192,2048]{1,0:T(8,128)(2,1)} %copy-done.60), channel_id=1, source_target_pairs={{0,4},{2,6},{4,0},{6,2},{1,5},{3,7},{5,1},{7,3},{8,12},{10,14},{12... | collective-permute-start | bytes 2359304 | tf_op jit(solution)/shard_map/ppermute | solution.py:66
  626.8 12.7 %collective-permute-start.27 = (bf16[2,128,4,128]{3,1,2,0:T(8,128)(2,1)}, bf16[2,128,4,128]{3,1,2,0:T(8,128)(2,1)}, u32[]{:S(2)}, u32[]{:S(2)}) collective-permute-start(bf16[2,128,4,128]{3,1,2,0:T(8,128)(2,1)} %get-tuple-element.237), channel_id=1, source_target_pairs={{0,2},{2,0},{4,6},{6,4},{1,3},{3,1},{5,7},{7,5},{8,10},{10,8},{12,... | collective-permute-start | bytes 786440 | tf_op jit(solution)/shard_map/ppermute | solution.py:66
  626.9 30.0 %collective-permute-start.26 = (bf16[2,128,4,128]{3,1,2,0:T(8,128)(2,1)}, bf16[2,128,4,128]{3,1,2,0:T(8,128)(2,1)S(1)}, u32[]{:S(2)}, u32[]{:S(2)}) collective-permute-start(bf16[2,128,4,128]{3,1,2,0:T(8,128)(2,1)} %get-tuple-element.236), channel_id=1, source_target_pairs={{0,2},{2,0},{4,6},{6,4},{1,3},{3,1},{5,7},{7,5},{8,10},{10,8},{12,... | collective-permute-start | bytes 786440 | tf_op jit(solution)/shard_map/ppermute | solution.py:66
  640.7 16.2 %collective-permute-start.28 = (bf16[2,128,4,128]{3,1,2,0:T(8,128)(2,1)S(1)}, bf16[2,128,4,128]{3,1,2,0:T(8,128)(2,1)S(1)}, u32[]{:S(2)}, u32[]{:S(2)}) collective-permute-start(bf16[2,128,4,128]{3,1,2,0:T(8,128)(2,1)S(1)} %add_convert_fusion.15), channel_id=1, source_target_pairs={{0,4},{2,6},{4,0},{6,2},{1,5},{3,7},{5,1},{7,3},{8,12},{10,14},{12... | collective-permute-start | bytes 786440 | tf_op jit(solution)/shard_map/ppermute | solution.py:66
  664.0 12.5 %collective-permute-start.54 = (bf16[192,2048]{1,0:T(8,128)(2,1)}, bf16[192,2048]{1,0:T(8,128)(2,1)S(1)}, u32[]{:S(2)}, u32[]{:S(2)}) collective-permute-start(bf16[192,2048]{1,0:T(8,128)(2,1)} %collective-permute-done.52), channel_id=1, source_target_pairs={{0,2},{2,0},{4,6},{6,4},{1,3},{3,1},{5,7},{7,5},{8,10},{10,8},{12,... | collective-permute-start | bytes 2359304 | tf_op jit(solution)/shard_map/ppermute | solution.py:66
  666.4 57.7 %collective-permute-start.36 = (bf16[192,5120]{1,0:T(8,128)(2,1)}, bf16[192,5120]{1,0:T(8,128)(2,1)}, u32[]{:S(2)}, u32[]{:S(2)}) collective-permute-start(bf16[192,5120]{1,0:T(8,128)(2,1)} %get-tuple-element.215), channel_id=1, source_target_pairs={{0,1},{1,0},{2,3},{3,2},{4,5},{5,4},{6,7},{7,6},{8,9},{9,8},{10,11... | collective-permute-start | bytes 5898248 | tf_op jit(solution)/shard_map/ppermute | solution.py:66
  667.8 71.7 %collective-permute-start.37 = (bf16[192,5120]{1,0:T(8,128)(2,1)}, bf16[192,5120]{1,0:T(8,128)(2,1)}, u32[]{:S(2)}, u32[]{:S(2)}) collective-permute-start(bf16[192,5120]{1,0:T(8,128)(2,1)} %get-tuple-element.215), channel_id=1, source_target_pairs={{0,2},{2,0},{4,6},{6,4},{1,3},{3,1},{5,7},{7,5},{8,10},{10,8},{12,... | collective-permute-start | bytes 5898248 | tf_op jit(solution)/shard_map/ppermute | solution.py:66
  671.1 11.4 %collective-permute-start.56 = (bf16[96,2048]{1,0:T(8,128)(2,1)S(1)}, bf16[96,2048]{1,0:T(8,128)(2,1)S(1)}, u32[]{:S(2)}, u32[]{:S(2)}) collective-permute-start(bf16[96,2048]{1,0:T(8,128)(2,1)S(1)} %slice.245), channel_id=1, source_target_pairs={{0,4},{2,6},{4,0},{6,2},{1,5},{3,7},{5,1},{7,3},{8,12},{10,14},{12... | collective-permute-start | bytes 1179656 | tf_op jit(solution)/shard_map/ppermute | solution.py:66
  673.1 47.2 %collective-permute-start.57 = (bf16[96,2048]{1,0:T(8,128)(2,1)S(1)}, bf16[96,2048]{1,0:T(8,128)(2,1)S(1)}, u32[]{:S(2)}, u32[]{:S(2)}) collective-permute-start(bf16[96,2048]{1,0:T(8,128)(2,1)S(1)} %slice.246), channel_id=1, source_target_pairs={{0,1},{1,0},{2,3},{3,2},{4,5},{5,4},{6,7},{7,6},{8,9},{9,8},{10,11... | collective-permute-start | bytes 1179656 | tf_op jit(solution)/shard_map/ppermute | solution.py:66
  676.5 44.5 %collective-permute-start.58 = (bf16[192,2048]{1,0:T(8,128)(2,1)}, bf16[192,2048]{1,0:T(8,128)(2,1)S(1)}, u32[]{:S(2)}, u32[]{:S(2)}) collective-permute-start(bf16[192,2048]{1,0:T(8,128)(2,1)} %collective-permute-done.55), channel_id=1, source_target_pairs={{0,2},{2,0},{4,6},{6,4},{1,3},{3,1},{5,7},{7,5},{8,10},{10,8},{12,... | collective-permute-start | bytes 2359304 | tf_op jit(solution)/shard_map/ppermute | solution.py:66
  682.5 51.8 %collective-permute-start.39 = (bf16[192,5120]{1,0:T(8,128)(2,1)}, bf16[192,5120]{1,0:T(8,128)(2,1)}, u32[]{:S(2)}, u32[]{:S(2)}) collective-permute-start(bf16[192,5120]{1,0:T(8,128)(2,1)} %get-tuple-element.215), channel_id=1, source_target_pairs={{0,4},{2,6},{4,0},{6,2},{1,5},{3,7},{5,1},{7,3},{8,12},{10,14},{12... | collective-permute-start | bytes 5898248 | tf_op jit(solution)/shard_map/ppermute | solution.py:66
  720.3 2.2 collective-permute-start.59
  724.1 35.5 %collective-permute-start.38 = (bf16[192,5120]{1,0:T(8,128)(2,1)}, bf16[192,5120]{1,0:T(8,128)(2,1)}, u32[]{:S(2)}, u32[]{:S(2)}) collective-permute-start(bf16[192,5120]{1,0:T(8,128)(2,1)} %collective-permute-done.36), channel_id=1, source_target_pairs={{0,2},{2,0},{4,6},{6,4},{1,3},{3,1},{5,7},{7,5},{8,10},{10,8},{12,... | collective-permute-start | bytes 5898248 | tf_op jit(solution)/shard_map/ppermute | solution.py:66
  732.8 24.2 %collective-permute-start.40 = (bf16[96,5120]{1,0:T(8,128)(2,1)S(1)}, bf16[96,5120]{1,0:T(8,128)(2,1)S(1)}, u32[]{:S(2)}, u32[]{:S(2)}) collective-permute-start(bf16[96,5120]{1,0:T(8,128)(2,1)S(1)} %slice.243), channel_id=1, source_target_pairs={{0,4},{2,6},{4,0},{6,2},{1,5},{3,7},{5,1},{7,3},{8,12},{10,14},{12... | collective-permute-start | bytes 2949128 | tf_op jit(solution)/shard_map/ppermute | solution.py:66
  735.6 23.9 %collective-permute-start.41 = (bf16[96,5120]{1,0:T(8,128)(2,1)S(1)}, bf16[96,5120]{1,0:T(8,128)(2,1)S(1)}, u32[]{:S(2)}, u32[]{:S(2)}) collective-permute-start(bf16[96,5120]{1,0:T(8,128)(2,1)S(1)} %slice.244), channel_id=1, source_target_pairs={{0,1},{1,0},{2,3},{3,2},{4,5},{5,4},{6,7},{7,6},{8,9},{9,8},{10,11... | collective-permute-start | bytes 2949128 | tf_op jit(solution)/shard_map/ppermute | solution.py:66
  736.5 31.1 %collective-permute-start.42 = (bf16[192,5120]{1,0:T(8,128)(2,1)}, bf16[192,5120]{1,0:T(8,128)(2,1)S(1)}, u32[]{:S(2)}, u32[]{:S(2)}) collective-permute-start(bf16[192,5120]{1,0:T(8,128)(2,1)} %collective-permute-done.39), channel_id=1, source_target_pairs={{0,2},{2,0},{4,6},{6,4},{1,3},{3,1},{5,7},{7,5},{8,10},{10,8},{12,... | collective-permute-start | bytes 5898248 | tf_op jit(solution)/shard_map/ppermute | solution.py:66
  757.0 11.9 %collective-permute-start.43 = (bf16[96,5120]{1,0:T(8,128)(2,1)S(1)}, bf16[96,5120]{1,0:T(8,128)(2,1)S(1)}, u32[]{:S(2)}, u32[]{:S(2)}) collective-permute-start(bf16[96,5120]{1,0:T(8,128)(2,1)S(1)} %collective-permute-done.40), channel_id=1, source_target_pairs={{0,2},{2,0},{4,6},{6,4},{1,3},{3,1},{5,7},{7,5},{8,10},{10,8},{12,... | collective-permute-start | bytes 2949128 | tf_op jit(solution)/shard_map/ppermute | solution.py:66
  759.5 10.5 %collective-permute-start.44 = (bf16[96,5120]{1,0:T(8,128)(2,1)S(1)}, bf16[96,5120]{1,0:T(8,128)(2,1)S(1)}, u32[]{:S(2)}, u32[]{:S(2)}) collective-permute-start(bf16[96,5120]{1,0:T(8,128)(2,1)S(1)} %collective-permute-done.41), channel_id=1, source_target_pairs={{0,2},{2,0},{4,6},{6,4},{1,3},{3,1},{5,7},{7,5},{8,10},{10,8},{12,... | collective-permute-start | bytes 2949128 | tf_op jit(solution)/shard_map/ppermute | solution.py:66
  782.1 101.2 %reduce-scatter.9.cloned.1.call-start = ((), (), s32[]{:S(2)}) async-start(), calls=%async_computation.7 | async-start | bytes 3276800 | tf_op jit(solution)/shard_map/reduce_scatter | solution.py:848
  806.3 17.7 %all-to-all-start = ((f32[32,1,1160]{2,1,0:T(1,128)}), f32[32,1,1160]{2,1,0:T(1,128)S(1)}, u32[]{:S(2)}, u32[]{:S(2)}) async-start(f32[32,1,1160]{2,1,0:T(1,128)} %copy.404), calls=%async_computation | async-start | bytes 327680 | tf_op jit(solution)/shard_map/all_to_all | solution.py:863
  (122 other events, 1997.9 us)
Sparse Core Ops, SparseCore 0:
  356.1 111.5 reduce-scatter.6
  470.1 212.3 reduce-scatter.4
  782.2 47.2 reduce-scatter.10
  831.8 51.4 reduce-scatter.8

commit v3 on v2

--- a/solution.py
+++ b/solution.py
@@ -97,26 +97,6 @@
     vxy = jnp.concatenate([top, low], axis=0)
     vxyc = jnp.concatenate([core(top), core(low)], axis=0)
     return [v, vy, vc, vyc, vx, vxy, vxc, vxyc]
-
-
-def scatter_plane(blocks):
-    if not small_plane():
-        return lax.psum_scatter(
-            jnp.concatenate(blocks, axis=0), plane, scatter_dimension=0, tiled=True
-        )
-    half = blocks[0].shape[0] // 2
-
-    def add(a, b):
-        return (a.astype(f32) + b.astype(f32)).astype(bf16)
-
-    here = {}
-    for r in (5, 4, 1, 0):
-        here[r] = add(blocks[r], core(blocks[r ^ 2]))
-    from_x = over_x(here[5][:half])
-    from_y = over_y(here[5][half:])
-    y_part = jnp.concatenate([add(here[1][:half], from_x), here[1][half:]], axis=0)
-    x_part = jnp.concatenate([here[4][:half], add(here[4][half:], from_y)], axis=0)
-    return here[0].astype(f32) + over_x(x_part).astype(f32) + over_y(y_part).astype(f32)
 
 
 def exchange_plane(blocks):
@@ -154,7 +134,7 @@
 
 
 def plane_slot(x, c, y):
-    return x * 4 + c * 2 + y
+    return x * 4 + y * 2 + c
 
 
 def greet(targets):
@@ -257,14 +237,16 @@
 
 
 def block_gather(here, send, mine, local_sem, blocks):
-    half = blocks.shape[1] // 2
+    rows = blocks.shape[0] // lax.axis_size(plane)
+    half = rows // 2
     x, c, y = here.x, here.c, here.y
     got = {}
 
     def at(slot, part=None):
-        if part is None:
-            return blocks.at[slot]
-        return blocks.at[slot, pl.ds(part * half, half)]
+        first, size = slot * rows, rows
+        if part is not None:
+            first, size = first + part * half, half
+        return blocks.at[pl.ds(pl.multiple_of(first, size), size)]
 
     def first():
         slot = plane_slot(x, c, y)
@@ -296,7 +278,7 @@
             got[name].wait_recv()
         got["own"].wait()
 
-    return [first, second, third, fourth]
+    return [first, second, third, fourth], got
 
 
 def turn_half(v):
@@ -421,7 +403,7 @@
         half_fetch(here, send, [(query_ref, high, high)], q_other, high, rows),
         half_fetch(here, send, [(output_ref, o_low, o_low)], o_other, o_low, o_rows),
         half_fetch(here, send, [(output_ref, o_high, o_high)], o_other, o_high, o_rows),
-        block_gather(here, send, grad_ref, local_sem.at[6], g_blocks),
+        block_gather(here, send, grad_ref, local_sem.at[6], g_blocks)[0],
     ]
     run_rounds(
         work, {0: start, 2: own_part, 4: keys_part, 5: keys_forward, 6: queries_rest}
@@ -451,7 +433,7 @@
             jax.ShapeDtypeStruct((half, 2 * narrow), bf16),
             jax.ShapeDtypeStruct((half, wide), bf16),
             jax.ShapeDtypeStruct(output_weight.shape, bf16),
-            jax.ShapeDtypeStruct((spread, rows, width), bf16),
+            jax.ShapeDtypeStruct((spread * rows, width), bf16),
             jax.ShapeDtypeStruct((rows, width), bf16),
             jax.ShapeDtypeStruct((rows, wide), f32),
             jax.ShapeDtypeStruct((rows, 2 * narrow), f32),
@@ -478,28 +460,448 @@
     )
 
 
-def gather_kernel(mine_ref, blocks, send_sem, recv_sem, local_sem):
+def chip_rows(x, y, rows):
+    first = plane_slot(x, 0, y) * rows
+    return pl.ds(pl.multiple_of(first, rows), 2 * rows)
+
+
+def expert_kernel(
+    ffn_ref,
+    routes_ref,
+    router_ref,
+    g_hbm,
+    gate_up_hbm,
+    down_hbm,
+    rows_out,
+    hidden_out,
+    grad_out,
+    gate_grad_ref,
+    rows_v,
+    g_v,
+    gate_up_v,
+    down_v,
+    hidden_v,
+    grad_v,
+    total_v,
+    send_sem,
+    recv_sem,
+    local_sem,
+):
     here = Places()
     greet([here.to_y, here.to_c, here.to_x])
     send = Sender(send_sem, recv_sem)
-    run_rounds([block_gather(here, send, mine_ref, local_sem.at[0], blocks)], {})
+    count = ffn_ref.shape[0]
+    experts = router_ref.shape[1]
+    local_experts, ff, _ = down_hbm.shape
+    tile = 256
+    stages, got = block_gather(here, send, ffn_ref, local_sem.at[0], rows_v)
+    stages[0]()
+    loads = [
+        pltpu.make_async_copy(gate_up_hbm, gate_up_v, local_sem.at[1]),
+        pltpu.make_async_copy(down_hbm, down_v, local_sem.at[2]),
+        pltpu.make_async_copy(g_hbm, g_v, local_sem.at[3]),
+    ]
+    for load in loads:
+        load.start()
+    first_expert = plane_index(here) * local_experts
+    stores = []
+
+    def chunk(x, y):
+        some = chip_rows(x, y, count)
+        logits = dot(rows_v[some, :], router_ref[...])
+        ids = lax.broadcasted_iota(jnp.int32, logits.shape, 1)
+        routes = routes_ref[some, :]
+        chosen = ids < 0
+        for k in range(routes.shape[1]):
+            chosen = chosen | (routes[:, k : k + 1] == ids)
+        logits = jnp.where(chosen, logits, masked)
+        raised = jnp.exp(logits - jnp.max(logits, axis=-1, keepdims=True))
+        raised = jnp.where(chosen, raised, 0.0)
+        gates = raised / jnp.sum(raised, axis=-1, keepdims=True)
+        lane = lax.broadcasted_iota(jnp.int32, total_v.shape, 1)
+        total_v[...] = jnp.zeros(total_v.shape, f32)
+        for e in range(local_experts):
+            gate = jnp.sum(
+                jnp.where(ids == first_expert + e, gates, 0.0), axis=-1, keepdims=True
+            )
+            here_lane = (lane == first_expert + e) | (lane == first_expert + e + experts)
+
+            @pl.loop(0, ff // tile)
+            def _(f, e=e, gate=gate, here_lane=here_lane):
+                at = pl.multiple_of(f * tile, tile)
+                a = dot(rows_v[some, :], gate_up_v[e, :, pl.ds(at, tile)])
+                b = dot(rows_v[some, :], gate_up_v[e, :, pl.ds(ff + at, tile)])
+                q = lax.dot_general(
+                    g_v[some, :],
+                    down_v[e, pl.ds(at, tile), :],
+                    (((1,), (1,)), ((), ())),
+                    preferred_element_type=f32,
+                )
+                s = 1.0 / (1.0 + jnp.exp(-a))
+                raised_a = a * s
+                hidden = raised_a * b
+                total_v[...] = total_v[...] + jnp.where(
+                    here_lane, jnp.sum(hidden * q, axis=-1, keepdims=True), 0.0
+                )
+                back = gate * q
+                hidden_v[some, pl.ds(e * ff + at, tile)] = (gate * hidden).astype(bf16)
+                grad_v[some, pl.ds(2 * e * ff + at, tile)] = (
+                    back * b * s * (1.0 + a * (1.0 - s))
+                ).astype(bf16)
+                grad_v[some, pl.ds((2 * e + 1) * ff + at, tile)] = (back * raised_a).astype(bf16)
+
+        total = total_v[...]
+        high = total.astype(bf16).astype(f32)
+        gate_grad_ref[some, :] = jnp.where(lane < experts, high, total - high).astype(bf16)
+        for source, target in ((hidden_v, hidden_out), (grad_v, grad_out), (rows_v, rows_out)):
+            store = pltpu.make_async_copy(
+                source.at[some, :], target.at[some, :], local_sem.at[4 + len(stores)]
+            )
+            store.start()
+            stores.append(store)
+
+    x, y = here.x, here.y
+    for name in ("c", "own"):
+        arrive(got, name)
+    for load in loads:
+        load.wait()
+    chunk(x, y)
+    stages[1]()
+    arrive(got, "yc")
+    chunk(x, 1 - y)
+    stages[2]()
+    arrive(got, "xc")
+    chunk(1 - x, y)
+    arrive(got, "topc")
+    arrive(got, "lowc")
+    chunk(1 - x, 1 - y)
+    for store in stores:
+        store.wait()
     send.finish()
 
 
-def gather_blocks(v, collective_id):
+def arrive(got, name):
+    copy = got[name]
+    copy.wait() if name == "own" else copy.wait_recv()
+
+
+def plane_index(here):
+    return here.ctx * 2 + here.y
+
+
+def experts_of_plane(ffn_in, route_rows, router_weight, g_rows, gate_up, down_proj):
+    local_experts, ff, width = down_proj.shape
+    total = route_rows.shape[0]
+    vmem = pl.BlockSpec(memory_space=pltpu.VMEM)
     anywhere = pl.BlockSpec(memory_space=pl.ANY)
     return pl.pallas_call(
-        gather_kernel,
-        out_shape=jax.ShapeDtypeStruct((lax.axis_size(plane),) + v.shape, v.dtype),
-        in_specs=[anywhere],
-        out_specs=anywhere,
+        expert_kernel,
+        out_shape=[
+            jax.ShapeDtypeStruct((total, width), bf16),
+            jax.ShapeDtypeStruct((total, local_experts * ff), bf16),
+            jax.ShapeDtypeStruct((total, 2 * local_experts * ff), bf16),
+            jax.ShapeDtypeStruct((total, 128), bf16),
+        ],
+        in_specs=[vmem] * 3 + [anywhere] * 3,
+        out_specs=[anywhere] * 3 + [vmem],
         scratch_shapes=[
+            pltpu.VMEM((total, width), bf16),
+            pltpu.VMEM((total, width), bf16),
+            pltpu.VMEM(gate_up.shape, bf16),
+            pltpu.VMEM(down_proj.shape, bf16),
+            pltpu.VMEM((total, local_experts * ff), bf16),
+            pltpu.VMEM((total, 2 * local_experts * ff), bf16),
+            pltpu.VMEM((2 * ffn_in.shape[0], 128), f32),
             pltpu.SemaphoreType.DMA((9,)),
             pltpu.SemaphoreType.DMA((9,)),
-            pltpu.SemaphoreType.DMA((1,)),
+            pltpu.SemaphoreType.DMA((16,)),
         ],
-        compiler_params=pltpu.CompilerParams(collective_id=collective_id, has_side_effects=True),
-    )(v)
+        compiler_params=pltpu.CompilerParams(
+            collective_id=2, has_side_effects=True, vmem_limit_bytes=60 * 2**20
+        ),
+        cost_estimate=pl.CostEstimate(
+            flops=2 * total * width * 3 * local_experts * ff,
+            bytes_accessed=60 * 2**20,
+            transcendentals=0,
+        ),
+    )(ffn_in, route_rows, router_weight, g_rows, gate_up, down_proj)
+
+
+def plane_sum_kernel(across, *refs):
+    if across:
+        left_hbm, weight_hbm, extra_ref = refs[:3]
+        refs = refs[3:]
+    else:
+        left_hbm, weight_hbm = refs[:2]
+        extra_ref = None
+        refs = refs[2:]
+    (
+        out_ref, left_v, weight_v, part_v, core_v, edge_v, last_v, send_sem, recv_sem, local_sem,
+    ) = refs
+    here = Places()
+    greet([here.to_y, here.to_c, here.to_x])
+    send = Sender(send_sem, recv_sem)
+    count = out_ref.shape[0]
+    half = count // 2
+    experts = weight_hbm.shape[0]
+    depth = left_hbm.shape[1] // experts
+    width = weight_hbm.shape[1] if across else weight_hbm.shape[2]
+    tile = 256
+    x, y, c = here.x, here.y, here.c
+    chips = [(1 - x, 1 - y), (1 - x, y), (x, 1 - y), (x, y)]
+    weight_load = pltpu.make_async_copy(weight_hbm, weight_v, local_sem.at[0])
+    weight_load.start()
+    loads = []
+    for k, (cx, cy) in enumerate(chips):
+        load = pltpu.make_async_copy(
+            left_hbm.at[chip_rows(cx, cy, count), :], left_v.at[k], local_sem.at[1 + k]
+        )
+        load.start()
+        loads.append(load)
+    weight_load.wait()
+    to_core = []
+
+    def compute(k):
+        loads[k].wait()
+
+        @pl.loop(0, width // tile)
+        def _(n):
+            cols = pl.ds(pl.multiple_of(n * tile, tile), tile)
+            total = None
+            for e in range(experts):
+                left = left_v[k, :, e * depth : (e + 1) * depth]
+                if across:
+                    part = lax.dot_general(
+                        left,
+                        weight_v[e, cols, :],
+                        (((1,), (1,)), ((), ())),
+                        preferred_element_type=f32,
+                    )
+                else:
+                    part = dot(left, weight_v[e, :, cols])
+                total = part if total is None else total + part
+            part_v[k, :, cols] = total.astype(bf16)
+
+        if extra_ref is not None:
+            part_v[k, :, width:] = extra_ref[chip_rows(*chips[k], count), :]
+        to_core.append(
+            send(
+                part_v.at[k, pl.ds(pl.multiple_of((1 - c) * count, count), count)],
+                core_v.at[k],
+                here.to_c,
+            )
+        )
+
+    mine = pl.ds(pl.multiple_of(c * count, count), count)
+
+    def chip_sum(k):
+        to_core[k].wait_recv()
+        return part_v[k, mine, :].astype(f32) + core_v[k].astype(f32)
+
+    compute(0)
+    compute(1)
+    core_v[0] = chip_sum(0).astype(bf16)
+    from_x = send(core_v.at[0, pl.ds(0, half)], edge_v.at[0], here.to_x)
+    from_y = send(core_v.at[0, pl.ds(half, half)], edge_v.at[1], here.to_y)
+    compute(2)
+    over_x_sum = chip_sum(1)
+    core_v[1, :half] = over_x_sum[:half].astype(bf16)
+    from_y.wait_recv()
+    core_v[1, half:] = (over_x_sum[half:] + edge_v[1].astype(f32)).astype(bf16)
+    last_x = send(core_v.at[1], last_v.at[0], here.to_x)
+    over_y_sum = chip_sum(2)
+    core_v[2, half:] = over_y_sum[half:].astype(bf16)
+    from_x.wait_recv()
+    core_v[2, :half] = (over_y_sum[:half] + edge_v[0].astype(f32)).astype(bf16)
+    last_y = send(core_v.at[2], last_v.at[1], here.to_y)
+    compute(3)
+    out_ref[...] = chip_sum(3)
+    last_x.wait_recv()
+    last_y.wait_recv()
+    out_ref[...] = out_ref[...] + last_v[0].astype(f32) + last_v[1].astype(f32)
+    send.finish()
+
+
+def plane_sum(left, weight, extra, collective_id):
+    across = extra is not None
+    count = left.shape[0] // lax.axis_size(plane)
+    width = weight.shape[1] if across else weight.shape[2]
+    wide = width + (extra.shape[1] if across else 0)
+    vmem = pl.BlockSpec(memory_space=pltpu.VMEM)
+    anywhere = pl.BlockSpec(memory_space=pl.ANY)
+
+    def kernel(*refs):
+        plane_sum_kernel(across, *refs)
+
+    return pl.pallas_call(
+        kernel,
+        out_shape=jax.ShapeDtypeStruct((count, wide), f32),
+        in_specs=[anywhere] * 2 + [vmem] * across,
+        out_specs=vmem,
+        scratch_shapes=[
+            pltpu.VMEM((4, 2 * count, left.shape[1]), bf16),
+            pltpu.VMEM(weight.shape, bf16),
+            pltpu.VMEM((4, 2 * count, wide), bf16),
+            pltpu.VMEM((4, count, wide), bf16),
+            pltpu.VMEM((2, count // 2, wide), bf16),
+            pltpu.VMEM((2, count, wide), bf16),
+            pltpu.SemaphoreType.DMA((8,)),
+            pltpu.SemaphoreType.DMA((8,)),
+            pltpu.SemaphoreType.DMA((5,)),
+        ],
+        compiler_params=pltpu.CompilerParams(
+            collective_id=collective_id, has_side_effects=True, vmem_limit_bytes=60 * 2**20
+        ),
+        cost_estimate=pl.CostEstimate(
+            flops=2 * left.shape[0] * left.shape[1] * width,
+            bytes_accessed=40 * 2**20,
+            transcendentals=0,
+        ),
+    )(*([left, weight] + ([extra] if across else [])))
+
+
+def head_softmax(queries, keys, visible):
+    scores = lax.dot_general(
+        queries, keys, (((1,), (1,)), ((), ())), preferred_element_type=f32
+    ) * (HEAD_SIZE ** (-0.5))
+    scores = jnp.where(visible, scores, masked)
+    raised = jnp.exp(scores - jnp.max(scores, axis=-1, keepdims=True))
+    return raised / jnp.sum(raised, axis=-1, keepdims=True)
+
+
+def visible_keys(rows, keys):
+    row = lax.broadcasted_iota(jnp.int32, (rows, keys), 0)
+    key = lax.broadcasted_iota(jnp.int32, (rows, keys), 1)
+    prompt_all = keys - (rows - PROMPT_DEV)
+    own = lax.axis_index("ctx") * PROMPT_DEV + row
+    position = jnp.where(row < PROMPT_DEV, own, prompt_all + row - PROMPT_DEV)
+    return key <= position
+
+
+def attention_kernel(
+    query_pre_ref, gain_ref, cosine_ref, sine_ref, keys_ref, values_ref, queries_ref, attended_ref
+):
+    rows = query_pre_ref.shape[0]
+    visible = visible_keys(rows, keys_ref.shape[0])
+    keys = keys_ref[...]
+    values = values_ref[...]
+    for h in range(query_pre_ref.shape[1] // HEAD_SIZE):
+        cols = slice(h * HEAD_SIZE, (h + 1) * HEAD_SIZE)
+        v = query_pre_ref[:, cols]
+        v = v * head_norm(v) * gain_ref[...]
+        queries = (v * cosine_ref[...] + turn_half(v) * sine_ref[...]).astype(bf16)
+        queries_ref[:, cols] = queries
+        probs = head_softmax(queries, keys, visible).astype(bf16)
+        attended_ref[:, cols] = dot(probs, values).astype(bf16)
+
+
+def attention(query_pre, gain, cosine, sine, kv_all):
+    rows, wide = query_pre.shape
+    keys = kv_all.shape[0]
+    group = wide // KEY_VALUE_HEADS
+    small = pl.BlockSpec((rows, HEAD_SIZE), lambda i: (0, 0))
+    block = pl.BlockSpec((rows, group), lambda i: (0, i))
+    return pl.pallas_call(
+        attention_kernel,
+        grid=(KEY_VALUE_HEADS,),
+        out_shape=[jax.ShapeDtypeStruct((rows, wide), bf16)] * 2,
+        in_specs=[
+            block,
+            pl.BlockSpec((1, HEAD_SIZE), lambda i: (0, 0)),
+            small,
+            small,
+            pl.BlockSpec((keys, HEAD_SIZE), lambda i: (0, i)),
+            pl.BlockSpec((keys, HEAD_SIZE), lambda i: (0, KEY_VALUE_HEADS + i)),
+        ],
+        out_specs=[block, block],
+        compiler_params=pltpu.CompilerParams(vmem_limit_bytes=48 * 2**20),
+    )(query_pre, gain.reshape(1, HEAD_SIZE), cosine, sine, kv_all, kv_all)
+
+
+def transposed_dot(a, b):
+    return lax.dot_general(a, b, (((0,), (0,)), ((), ())), preferred_element_type=f32)
+
+
+def attention_back_kernel(
+    query_pre_ref,
+    gain_ref,
+    cosine_ref,
+    sine_ref,
+    keys_ref,
+    values_ref,
+    queries_ref,
+    grad_ref,
+    pre_grad_ref,
+    key_grad_ref,
+    value_grad_ref,
+    gain_grad_ref,
+):
+    rows = query_pre_ref.shape[0]
+    visible = visible_keys(rows, keys_ref.shape[0])
+    keys = keys_ref[...]
+    values = values_ref[...]
+    scale = HEAD_SIZE ** (-0.5)
+    gain_grad = jnp.zeros((rows, HEAD_SIZE), f32)
+    key_grad = jnp.zeros(keys_ref.shape, f32)
+    value_grad = jnp.zeros(keys_ref.shape, f32)
+    for h in range(query_pre_ref.shape[1] // HEAD_SIZE):
+        cols = slice(h * HEAD_SIZE, (h + 1) * HEAD_SIZE)
+        queries = queries_ref[:, cols]
+        grad = grad_ref[:, cols]
+        probs = head_softmax(queries, keys, visible)
+        prob_grad = lax.dot_general(
+            grad, values, (((1,), (1,)), ((), ())), preferred_element_type=f32
+        )
+        delta = jnp.sum(probs * prob_grad, axis=-1, keepdims=True)
+        score_grad = (probs * (prob_grad - delta)).astype(bf16)
+        key_grad = key_grad + transposed_dot(score_grad, queries)
+        value_grad = value_grad + transposed_dot(probs.astype(bf16), grad)
+        u = dot(score_grad, keys) * scale
+        u = u * cosine_ref[...] + turn_half(u * sine_ref[...])
+        v = query_pre_ref[:, cols]
+        inv = head_norm(v)
+        gain_grad = gain_grad + u * v * inv
+        pre_grad_ref[:, cols] = norm_back(v, inv, gain_ref[...], u).astype(bf16)
+    key_grad_ref[...] = (key_grad * scale).astype(key_grad_ref.dtype)
+    value_grad_ref[...] = value_grad.astype(value_grad_ref.dtype)
+    gain_grad_ref[0] = jnp.sum(gain_grad, axis=0, keepdims=True)
+
+
+def attention_back(query_pre, gain, cosine, sine, kv_all, queries, attended_grad):
+    rows, wide = query_pre.shape
+    keys, both = kv_all.shape
+    group = wide // KEY_VALUE_HEADS
+    small = pl.BlockSpec((rows, HEAD_SIZE), lambda i: (0, 0))
+    block = pl.BlockSpec((rows, group), lambda i: (0, i))
+    return pl.pallas_call(
+        attention_back_kernel,
+        grid=(KEY_VALUE_HEADS,),
+        out_shape=[
+            jax.ShapeDtypeStruct((rows, wide), bf16),
+            jax.ShapeDtypeStruct((keys, both // 2), f32),
+            jax.ShapeDtypeStruct((keys, both // 2), f32),
+            jax.ShapeDtypeStruct((KEY_VALUE_HEADS, 1, HEAD_SIZE), f32),
+        ],
+        in_specs=[
+            block,
+            pl.BlockSpec((1, HEAD_SIZE), lambda i: (0, 0)),
+            small,
+            small,
+            pl.BlockSpec((keys, HEAD_SIZE), lambda i: (0, i)),
+            pl.BlockSpec((keys, HEAD_SIZE), lambda i: (0, KEY_VALUE_HEADS + i)),
+            block,
+            block,
+        ],
+        out_specs=[
+            block,
+            pl.BlockSpec((keys, HEAD_SIZE), lambda i: (0, i)),
+            pl.BlockSpec((keys, HEAD_SIZE), lambda i: (0, i)),
+            pl.BlockSpec((1, 1, HEAD_SIZE), lambda i: (i, 0, 0)),
+        ],
+        compiler_params=pltpu.CompilerParams(vmem_limit_bytes=48 * 2**20),
+    )(
+        query_pre, gain.reshape(1, HEAD_SIZE), cosine, sine, kv_all, kv_all, queries, attended_grad
+    )
 
 
 def gather_small(v):
@@ -509,7 +911,9 @@
     v = jnp.concatenate([v, core(v)], axis=0)
     v = jnp.concatenate([v, over_x(v)], axis=0)
     blocks = v.reshape(lax.axis_size(plane), -1, v.shape[1])
-    blocks = jnp.take(blocks, jnp.arange(blocks.shape[0]) ^ lax.axis_index(plane), axis=0)
+    slot = jnp.arange(blocks.shape[0])
+    device = slot // 4 * 4 + slot % 2 * 2 + slot // 2 % 2
+    blocks = jnp.take(blocks, device ^ lax.axis_index(plane), axis=0)
     return blocks.reshape(v.shape)
 
 
@@ -569,8 +973,6 @@
     local_experts = gate_up.shape[0]
     count_of_rows = hidden_in.shape[0]
     prompt_all = PROMPT_DEV * ctx_count
-    heads_per_group = QUERY_HEADS // KEY_VALUE_HEADS
-    score_scale = HEAD_SIZE ** (-0.5)
     hidden_ff = gate_up.shape[2] // 2
     order = relative()
     member = lax.axis_index("ctx")
@@ -584,26 +986,25 @@
     route_rows = gather_small(routes)
     inputs = hidden_in.astype(f32)
     scale_in = rms_scale(inputs)
+    signed_sine = rope_sine * jnp.where(jnp.arange(HEAD_SIZE) < HEAD_SIZE // 2, -1.0, 1.0)
     if small_plane():
-        sign = jnp.where(jnp.arange(HEAD_SIZE) < HEAD_SIZE // 2, -1.0, 1.0)
         (
             kv_other,
             q_other,
             o_other,
-            g_blocks,
+            g_rows,
             normalized_input,
             query_pre,
             key_value_pre,
             kv_low,
             kv_blocks,
         ) = fetch_and_project(
-            hidden_in, attn_gain, key_gain, cosine, rope_sine * sign, key_matrix, value_matrix,
+            hidden_in, attn_gain, key_gain, cosine, signed_sine, key_matrix, value_matrix,
             query_weight, output_weight, out_grad,
         )
         kv_weights = [jnp.concatenate([key_matrix, value_matrix], axis=1), kv_other]
         q_weights = [query_weight, q_other]
         o_weights = [output_weight, o_other]
-        g_rows = g_blocks.reshape(spread_count * count_of_rows, MODEL_WIDTH)
         kv_blocks = kv_blocks.reshape(prompt_all, 2 * narrow)
     else:
         full = [
@@ -639,57 +1040,21 @@
         parts = [dot(v, w.T) for w in weights]
         return parts[0] if len(parts) == 1 else join_halves(*parts)
 
-    query_pre = query_pre.reshape(count_of_rows, QUERY_HEADS, HEAD_SIZE)
     key_before_norm = key_value_pre[:, :narrow].reshape(
         count_of_rows, KEY_VALUE_HEADS, HEAD_SIZE
     )
-    query_inv = rms_scale(query_pre)
     key_inv = rms_scale(key_before_norm)
-    cosine = cosine[:, None, :]
-    rope_sine = rope_sine[:, None, :]
-    query_reduced = rotate(query_pre * query_inv * query_gain, cosine, rope_sine).astype(bf16)
     kv_all = jnp.concatenate([kv_blocks, kv_low[PROMPT_DEV:]], axis=0)
-    keys_all, values_all = [
-        v.reshape(kv_all.shape[0], KEY_VALUE_HEADS, HEAD_SIZE)
-        for v in (kv_all[:, :narrow], kv_all[:, narrow:])
-    ]
-    key_position = jnp.arange(kv_all.shape[0], dtype=jnp.int32)
-    visible = key_position[None, :] <= position[:, None]
-    grouped_queries = query_reduced.reshape(
-        count_of_rows, KEY_VALUE_HEADS, heads_per_group, HEAD_SIZE
-    )
-
-    def scores_of():
-        raw_scores = (
-            jnp.einsum("rkgd,skd->kgrs", grouped_queries, keys_all, preferred_element_type=f32)
-            * score_scale
-        )
-        return jnp.where(visible, raw_scores, masked)
-
-    scores = scores_of()
-    row_max = jnp.max(scores, axis=-1, keepdims=True)
-    weights = jnp.exp(scores - row_max)
-    row_total = jnp.sum(weights, axis=-1, keepdims=True)
-    log_total = row_max + jnp.log(row_total)
-    attention = (weights / row_total).astype(bf16)
-    attended = (
-        jnp.einsum("kgrs,skd->rkgd", attention, values_all, preferred_element_type=f32)
-        .reshape(count_of_rows, QUERY_HEADS * HEAD_SIZE)
-        .astype(bf16)
-    )
+    queries, attended = attention(query_pre, query_gain, cosine, signed_sine, kv_all)
     residual = inputs + forward_dot(attended, o_weights)
     scale_ffn = rms_scale(residual)
     ffn_in = (residual * scale_ffn * ffn_gain).astype(bf16)
 
-    if small_plane():
-        rows = gather_blocks(ffn_in, 2).reshape(spread_count * count_of_rows, MODEL_WIDTH)
-    else:
-        rows = lax.all_gather(ffn_in, plane, axis=0, tiled=True)
     expert_count = local_experts * spread_count
     expert_ids = jnp.arange(expert_count, dtype=jnp.int32)
 
     def gates_of(some_rows, some_routes):
-        logits = jnp.dot(some_rows, router_weight, preferred_element_type=f32)
+        logits = dot(some_rows, router_weight)
         chosen = jnp.any(some_routes[:, :, None] == expert_ids[None, None, :], axis=1)
         logits = jnp.where(chosen, logits, masked)
         raised = jnp.where(
@@ -697,64 +1062,79 @@
         )
         return raised / jnp.sum(raised, axis=-1, keepdims=True)
 
-    gates_all = gates_of(rows, route_rows)
-    first_expert = lax.axis_index(plane) * local_experts
-    gates_mine = lax.dynamic_slice_in_dim(gates_all, first_expert, local_experts, axis=1)
-    moe_part = 0.0
-    row_part = 0.0
-    gate_grads = []
-    hiddens = []
-    projected_grads = []
-    for which in range(local_experts):
-        gate = gates_mine[:, which : which + 1]
-        projected = jnp.dot(rows, gate_up[which], preferred_element_type=f32)
-        back = jnp.dot(g_rows, down_proj[which].T, preferred_element_type=f32)
-        gate_part = projected[:, :hidden_ff]
-        up_part = projected[:, hidden_ff:]
-        sigmoid_gate = jax.nn.sigmoid(gate_part)
-        hidden = gate_part * sigmoid_gate * up_part
-        gate_grads.append(jnp.sum(hidden * back, axis=-1))
-        hidden_low = (gate * hidden).astype(bf16)
-        hidden_back = gate * back
-        gate_back = hidden_back * up_part * sigmoid_gate * (1.0 + gate_part * (1.0 - sigmoid_gate))
-        up_back = hidden_back * gate_part * sigmoid_gate
-        projected_grad = jnp.concatenate([gate_back, up_back], axis=-1).astype(bf16)
-        hiddens.append(hidden_low)
-        projected_grads.append(projected_grad)
-    gate_up_local = jnp.stack(
-        [jnp.dot(rows.T, v, preferred_element_type=f32).astype(bf16) for v in projected_grads]
-    )
-    down_local = jnp.stack(
-        [jnp.dot(v.T, g_rows, preferred_element_type=f32).astype(bf16) for v in hiddens]
-    )
-    gate_up_low = lax.psum_scatter(gate_up_local, "dp", scatter_dimension=1, tiled=True)
-    down_low = lax.psum_scatter(down_local, "dp", scatter_dimension=1, tiled=True)
-    gate_up_grad = gate_up_low.astype(f32)
+    gates = gates_of(ffn_in, routes)
+    if small_plane():
+        rows, hidden_low, projected_grad, gate_grads = experts_of_plane(
+            ffn_in, route_rows, router_weight, g_rows, gate_up, down_proj
+        )
+    else:
+        rows = lax.all_gather(ffn_in, plane, axis=0, tiled=True)
+        first_expert = lax.axis_index(plane) * local_experts
+        gates_mine = lax.dynamic_slice_in_dim(
+            gates_of(rows, route_rows), first_expert, local_experts, axis=1
+        )
+        gate_grads, hiddens, projected_grads = [], [], []
+        for which in range(local_experts):
+            gate = gates_mine[:, which : which + 1]
+            projected = dot(rows, gate_up[which])
+            back = dot(g_rows, down_proj[which].T)
+            gate_part = projected[:, :hidden_ff]
+            up_part = projected[:, hidden_ff:]
+            sigmoid_gate = jax.nn.sigmoid(gate_part)
+            hidden = gate_part * sigmoid_gate * up_part
+            gate_grads.append(jnp.sum(hidden * back, axis=-1))
+            hiddens.append((gate * hidden).astype(bf16))
+            back = gate * back
+            gate_back = back * up_part * sigmoid_gate * (1.0 + gate_part * (1.0 - sigmoid_gate))
+            up_back = back * gate_part * sigmoid_gate
+            projected_grads.append(jnp.concatenate([gate_back, up_back], axis=-1).astype(bf16))
+        hidden_low = jnp.concatenate(hiddens, axis=1)
+        projected_grad = jnp.concatenate(projected_grads, axis=1)
+    down_local = dot(hidden_low.T, g_rows).astype(bf16)
+    gate_up_local = dot(rows.T, projected_grad).astype(bf16)
+    down_low = lax.psum_scatter(
+        down_local.reshape(down_proj.shape), "dp", scatter_dimension=1, tiled=True
+    )
+    gate_up_low = lax.psum_scatter(gate_up_local, "dp", scatter_dimension=0, tiled=True)
     down_grad = down_low.astype(f32)
-    projected_grads, hiddens = lax.optimization_barrier(
-        ((projected_grads, hiddens), gate_up_local, down_local)
+    gate_up_grad = jnp.stack(
+        [
+            gate_up_low[:, i * 2 * hidden_ff : (i + 1) * 2 * hidden_ff].astype(f32)
+            for i in range(local_experts)
+        ]
+    )
+    projected_grad, hidden_low = lax.optimization_barrier(
+        ((projected_grad, hidden_low), gate_up_local, down_local)
     )[0]
-    for which in range(local_experts):
-        row_part = row_part + jnp.dot(
-            projected_grads[which], gate_up[which].T, preferred_element_type=f32
+    if small_plane():
+        back = plane_sum(projected_grad, gate_up, gate_grads, 3)
+        back_sum = back[:, :MODEL_WIDTH]
+        gate_grad = (
+            back[:, MODEL_WIDTH : MODEL_WIDTH + expert_count]
+            + back[:, MODEL_WIDTH + expert_count : MODEL_WIDTH + 2 * expert_count]
         )
-        moe_part = moe_part + jnp.dot(hiddens[which], down_proj[which], preferred_element_type=f32)
-
-    def blocks_of(v):
-        return [
-            lax.dynamic_slice_in_dim(v, i * count_of_rows, count_of_rows, axis=0) for i in order
+        moe_sum = plane_sum(after(hidden_low, back), down_proj, None, 4)
+    else:
+        moe_part = 0.0
+        row_part = 0.0
+        for which in range(local_experts):
+            grads = projected_grad[:, which * 2 * hidden_ff : (which + 1) * 2 * hidden_ff]
+            hidden = hidden_low[:, which * hidden_ff : (which + 1) * hidden_ff]
+            row_part = row_part + dot(grads, gate_up[which].T)
+            moe_part = moe_part + dot(hidden, down_proj[which])
+        moe_sum, back_sum = [
+            lax.psum_scatter(v.astype(bf16), plane, scatter_dimension=0, tiled=True).astype(f32)
+            for v in (moe_part, row_part)
         ]
-
-    moe_sum = scatter_plane(blocks_of(moe_part.astype(bf16)))
+        gate_grad = lax.all_to_all(
+            jnp.stack(gate_grads, axis=1).reshape(spread_count, count_of_rows, local_experts),
+            plane,
+            split_axis=0,
+            concat_axis=0,
+            tiled=True,
+        )
+        gate_grad = gate_grad.transpose(1, 0, 2).reshape(count_of_rows, expert_count)
     block_out = (residual + moe_sum).astype(bf16)
-    back_sum = scatter_plane(blocks_of(row_part.astype(bf16)))
-    gate_grad_blocks = exchange_plane(blocks_of(jnp.stack(gate_grads, axis=1)))
-    gate_grad = jnp.zeros((count_of_rows, expert_count), f32)
-    for r in range(spread_count):
-        gate_grad = lax.dynamic_update_slice_in_dim(
-            gate_grad, gate_grad_blocks[r], order[r] * local_experts, axis=1
-        )
-    gates = gates_of(ffn_in, routes)
     logit_grad = gates * (gate_grad - jnp.sum(gates * gate_grad, axis=-1, keepdims=True))
 
     grad_out = out_grad.astype(f32)
@@ -766,53 +1146,25 @@
     ffn_gain_local = jnp.sum(ffn_in_grad * residual * scale_ffn, axis=0)
     branch_low = residual_grad.astype(bf16)
     branch_rows = jnp.concatenate(gather_plane(branch_low), axis=0)
-    attended_grad = (
-        backward_dot(branch_low, o_weights)
-        .astype(bf16)
-        .reshape(count_of_rows, KEY_VALUE_HEADS, heads_per_group, HEAD_SIZE)
-    )
-    attention_again = jnp.exp(scores_of() - log_total)
-    prob_grad = jnp.einsum(
-        "rkgd,skd->kgrs", attended_grad, values_all, preferred_element_type=f32
-    )
-    row_delta = jnp.sum(attention_again * prob_grad, axis=-1, keepdims=True)
-    score_grad = (attention_again * (prob_grad - row_delta)).astype(bf16)
-    query_grad = (
-        jnp.einsum("kgrs,skd->rkgd", score_grad, keys_all, preferred_element_type=f32)
-        * score_scale
-    ).reshape(count_of_rows, QUERY_HEADS, HEAD_SIZE)
-    key_grad_all = (
-        jnp.einsum("kgrs,rkgd->skd", score_grad, grouped_queries, preferred_element_type=f32)
-        * score_scale
-    )
-    value_grad_all = jnp.einsum(
-        "kgrs,rkgd->skd",
-        attention_again.astype(bf16),
-        attended_grad,
-        preferred_element_type=f32,
-    )
+    attended_grad = backward_dot(branch_low, o_weights).astype(bf16)
+    query_pre_grad, key_grad_all, value_grad_all, query_gain_parts = attention_back(
+        query_pre, query_gain, cosine, signed_sine, kv_all, queries, attended_grad
+    )
+    query_gain_local = jnp.sum(query_gain_parts, axis=(0, 1))
     pair_grads = jnp.stack([key_grad_all[:prompt_all], value_grad_all[:prompt_all]]).astype(bf16)
     prompt_grads = ctx_sum(pair_grads)
-    key_grad = jnp.concatenate([prompt_grads[0], key_grad_all[prompt_all:]], axis=0)
+    key_grad = jnp.concatenate([prompt_grads[0], key_grad_all[prompt_all:]], axis=0).reshape(
+        count_of_rows, KEY_VALUE_HEADS, HEAD_SIZE
+    )
     value_gradient = jnp.concatenate([prompt_grads[1], value_grad_all[prompt_all:]], axis=0)
-    query_rot_grad = rotate_back(query_grad, cosine, rope_sine)
-    key_rot_grad = rotate_back(key_grad, cosine, rope_sine)
-    query_gain_local = jnp.sum(query_rot_grad * query_pre * query_inv, axis=(0, 1))
+    key_rot_grad = rotate_back(key_grad, cosine[:, None, :], rope_sine[:, None, :])
     key_gain_local = jnp.sum(key_rot_grad * key_before_norm * key_inv, axis=(0, 1))
-    query_pre_grad = (
-        norm_back(query_pre, query_inv, query_gain, query_rot_grad)
-        .astype(bf16)
-        .reshape(count_of_rows, QUERY_HEADS * HEAD_SIZE)
-    )
     key_pre_grad = (
         norm_back(key_before_norm, key_inv, key_gain, key_rot_grad)
         .astype(bf16)
         .reshape(count_of_rows, KEY_VALUE_HEADS * HEAD_SIZE)
     )
-    value_before_norm_gradient = value_gradient.astype(bf16).reshape(
-        count_of_rows, KEY_VALUE_HEADS * HEAD_SIZE
-    )
-    key_value_grad = jnp.concatenate([key_pre_grad, value_before_norm_gradient], axis=1)
+    key_value_grad = jnp.concatenate([key_pre_grad, value_gradient.astype(bf16)], axis=1)
     normed_grad = backward_dot(query_pre_grad, q_weights) + backward_dot(
         key_value_grad, kv_weights
     )

time: 904 us -> 773 us (0.86)
  Pallas kernels: 157 us -> 336 us
  matrix products: 237 us -> 104 us
  other arithmetic: 93.9 us -> 32.2 us
  local copies, waits for them, and re-layouts: 156 us -> 97.4 us
  waiting for transfers between devices: 182 us -> 144 us
  starting transfers between devices: 50.2 us -> 33.7 us
    dot_general x20 -> x0, matrix products: 178 us -> none  [the longest x2 31.4 us: body(): jnp.dot(projected_grads[which], gate_up[which].T, preferred_element_type=...]
    pallas_call x1 -> x5, Pallas kernels: 32.3 us -> 210 us  [the longest x2 94.9 us: plane_sum(): pl.pallas_call(kernel, out_shape=jax.ShapeDtypeStruct((count, wide), f32)...]
    dot_general x8 -> x11, matrix products: 36.5 us -> 79.1 us  [dot(): return jnp.dot(a, b, preferred_element_type=f32)]
    mul x7 -> x0, local copies, waits for them, and re-layouts: 23.1 us -> none  [the longest x3 8.19 us: body(): query_pre * query_inv * query_gain]
    ppermute x40 -> x24, waiting for transfers between devices: 87.4 us -> 66 us  [swap(): lax.ppermute(v, axis, [(i, i ^ bit) for i in range(lax.axis_size(axis))])]
    convert_element_type x9 -> x1, other arithmetic: 21.3 us -> 0.01 us  [angles(): rope_angle = position.astype(f32)[:, None] * inverse[None, :]]
    reduce_sum x4 -> x1, other arithmetic: 18.2 us -> 0.02 us  [body(): query_gain_local = jnp.sum(query_gain_parts, axis=(0, 1))]
    ppermute x21 -> x14, waiting for transfers between devices: 37.7 us -> 22.2 us  [exchange_plane(): out.append(lax.ppermute(blocks[r], plane, pairs))]
  transfers between devices with their start and end apart: 66 -> 43, of which waited for: 21 -> 16; matrix products, arithmetic and copies ran while one was open for 52% -> 26% of each run, Pallas kernels for 18% -> 35%
where the time goes in v3:
time: 773 us; the launch traced here: 763 us
  Pallas kernels  336 us (43%)
  waiting for transfers between devices  144 us (19%)
  matrix products  104 us (13%)
  local copies, waits for them, and re-layouts  97.4 us (13%)
  starting transfers between devices  33.7 us (4%)
  other arithmetic  32.2 us (4%)
  between operations  15.2 us (2%)
    pallas_call x1, Pallas kernels, fetch_and_project(): pl.pallas_call(fetch_kernel, out_shape=[jax.ShapeDtypeStruct((half, 2 * n...  125 us
    pallas_call x2, Pallas kernels, plane_sum(): pl.pallas_call(kernel, out_shape=jax.ShapeDtypeStruct((count, wide), f32)...  94.9 us
    dot_general x11, matrix products, dot(): return jnp.dot(a, b, preferred_element_type=f32)  79.1 us
    pallas_call x1, Pallas kernels, experts_of_plane(): pl.pallas_call(expert_kernel, out_shape=[jax.ShapeDtypeStruct((total, wid...  67.1 us
    ppermute x24, waiting for transfers between devices, swap(): lax.ppermute(v, axis, [(i, i ^ bit) for i in range(lax.axis_size(axis))])  66 us
    unnamed x150, local copies, waits for them, and re-layouts  52.4 us
    reduce_scatter x1, waiting for transfers between devices, body(): lax.psum_scatter(pre_local, 'dp', scatter_dimension=0, tiled=True)  47.4 us
    pallas_call x1, Pallas kernels, attention_back(): pl.pallas_call(attention_back_kernel, grid=(KEY_VALUE_HEADS,), out_shape=...  29.6 us
  transfers between devices with their start and end apart: 43, of which 16 were waited for; matrix products, arithmetic and copies ran while one was open for 26% of the time, Pallas kernels for 35%

profile of v3, /device:TPU:0, one launch (start us, length us, event | category | flops | bytes accessed | tf_op | source)
XLA Modules:
  0.0 762.7 jit_solution(15042226066988092231)
XLA Ops:
  7.2 3.0 collective-permute-start
  16.3 125.1 %shard_map.237 = (bf16[1024,1024]{1,0:T(8,128)(2,1)}, bf16[1024,4096]{1,0:T(8,128)(2,1)}, bf16[2048,2048]{1,0:T(8,128)(2,1)}, bf16[1536,2048]{1,0:T(8,128)(2,1)}...) custom-call(bf16[192,2048]{1,0:T(8,128)(2,1)S(1)} %copy-done, ...), custom_call_target="tpu_custom_call" | custom-call | tf_op jit(solution)/shard_map/pallas_call | solution.py:430
  143.9 18.7 %shard_map.238 = (bf16[192,4096]{1,0:T(8,128)(2,1)S(1)}, bf16[192,4096]{1,0:T(8,128)(2,1)S(1)}) custom-call(f32[192,4096]{1,0:T(8,128)} %get-tuple-element.39.query_pre_ref, f32[1,128]{1,0:T(1,128)S(1)} %bitcast.134, f32[192,128]{1,0:T(8,128)S(1)} %get-tuple-element.192.cosine_ref, f32[192,128]{1,0:T(8,128)S(1)} %get-tuple-element.191.sine_ref, ...), custom_call_target="tpu_custom_call" | custom-call | tf_op jit(solution)/shard_map/pallas_call | solution.py:804
  162.7 5.8 fusion.13
  168.5 2.0 multiply_reduce_fusion.2
  175.5 2.6 collective-permute-done.2
  180.0 2.3 bitcast_select_fusion.routes_ref
  182.3 67.1 %shard_map.239 = (bf16[1536,2048]{1,0:T(8,128)(2,1)}, bf16[1536,1536]{1,0:T(8,128)(2,1)}, bf16[1536,3072]{1,0:T(8,128)(2,1)}, bf16[1536,128]{1,0:T(8,128)(2,1)}) custom-call(bf16[192,2048]{1,0:T(8,128)(2,1)} %multiply_convert_fusion.ffn_ref, s32[1536,8]{1,0:T(8,128)} %bitcast_select_fusion.routes_ref, bf16[2048,16]{1,0:T(8,128)(2,1)} %copy.119.router_ref, ...), custom_call_target="tpu_custom_call" | custom-call | flops 28991029248 | bytes 62914560 | tf_op jit(solution)/shard_map/pallas_call | solution.py:597
  249.4 15.2 %convolution_convert_fusion.1 = bf16[1536,2048]{1,0:T(8,128)(2,1)} fusion(bf16[1536,1536]{1,0:T(8,128)(2,1)} %get-tuple-element.51.refs_0_, bf16[1536,2048]{1,0:T(8,128)(2,1)} %get-tuple-element.44.g_hbm), kind=kOutput, calls=%fused_computation.2 | convolution fusion | flops 9666822144 | bytes 17301504 | tf_op jit(solution)/shard_map/dot_general | solution.py:937
  264.7 26.3 %convolution_convert_fusion = bf16[2048,3072]{1,0:T(8,128)(2,1)} fusion(bf16[1536,2048]{1,0:T(8,128)(2,1)} %get-tuple-element.47, bf16[1536,3072]{1,0:T(8,128)(2,1)} %get-tuple-element.49.refs_0_), kind=kOutput, calls=%fused_computation.1 | convolution fusion | flops 19333644288 | bytes 28311552 | tf_op jit(solution)/shard_map/dot_general | solution.py:937
  293.2 1.6 fusion.52
  296.0 11.0 %dynamic-slice_reduce_fusion = (bf16[192,4,128]{2,1,0:T(4,128)(2,1)}, bf16[192,4,128]{2,1,0:T(4,128)(2,1)}, bf16[192,4,128]{2,1,0:T(4,128)(2,1)}, bf16[192,4,128...) fusion(bf16[192,4,8,128]{3,2,1,0:T(8,128)(2,1)S(1)} %bitcast.13, ...), kind=kLoop, calls=%fused_computation.69 | loop fusion | bytes 3145760 | tf_op jit(solution)/shard_map/jit(dynamic_index_in_dim)/dynamic_slice | solution.py:1185
  309.5 2.3 constant_dynamic-slice_fusion
  313.0 1.4 collective-permute-start.12
  316.5 52.0 %shard_map.240 = f32[192,2176]{1,0:T(8,128)} custom-call(bf16[1536,3072]{1,0:T(8,128)(2,1)} %get-tuple-element.49.refs_0_, bf16[2,2048,1536]{2,1,0:T(8,128)(2,1)} %refs_1_.2, bf16[1536,128]{1,0:T(8,128)(2,1)} %get-tuple-element.50.refs_2_), custom_call_target="tpu_custom_call" | custom-call | flops 19327352832 | bytes 41943040 | tf_op jit(solution)/shard_map/pallas_call | solution.py:736
  369.7 43.0 %shard_map.241 = f32[192,2048]{1,0:T(8,128)} custom-call(bf16[1536,1536]{1,0:T(8,128)(2,1)} %get-tuple-element.51.refs_0_, bf16[2,768,2048]{2,1,0:T(8,128)(2,1)} %refs_1_.3), custom_call_target="tpu_custom_call" | custom-call | flops 9663676416 | bytes 41943040 | tf_op jit(solution)/shard_map/pallas_call | solution.py:736
  412.7 4.3 multiply_reduce_fusion
  417.0 2.2 constant_dynamic-update-slice_fusion.28
  419.2 6.7 fusion.54
  426.0 4.0 select_convert_fusion.1
  431.3 29.6 %shard_map.242 = (bf16[192,4096]{1,0:T(8,128)(2,1)S(1)}, f32[576,512]{1,0:T(8,128)S(1)}, f32[576,512]{1,0:T(8,128)S(1)}, f32[4,1,128]{2,1,0:T(1,128)S(1)}) custom-call(f32[192,4096]{1,0:T(8,128)} %get-tuple-element.39.query_pre_ref, f32[1,128]{1,0:T(1,128)S(1)} %bitcast.135, f32[192,128]{1,0:T(8,128)S(1)} %get-tuple-element.192.cosine_ref, ...), custom_call_target="tpu_custom_call" | custom-call | tf_op jit(solution)/shard_map/pallas_call | solution.py:876
  468.2 2.5 collective-permute-start.8
  472.0 2.8 collective-permute-done.8
  474.8 1.3 collective-permute-start.32
  477.8 1.7 collective-permute-start.25
  479.5 2.4 concatenate.102
  482.0 1.5 collective-permute-start.26
  483.5 1.6 constant_dynamic-update-slice_fusion.18
  485.1 1.6 constant_dynamic-update-slice_fusion.17
  487.2 1.6 constant_dynamic-update-slice_fusion.16
  488.8 10.9 %collective-permute-done.25 = bf16[192,512]{1,0:T(8,128)(2,1)} collective-permute-done((bf16[192,512]{1,0:T(8,128)(2,1)}, bf16[192,512]{1,0:T(8,128)(2,1)}, u32[]{:S(2)}, u32[]{:S(2)}) %collective-permute-start.25) | collective-permute-done | bytes 196640 | tf_op jit(solution)/shard_map/ppermute | solution.py:109
  500.7 1.6 constant_dynamic-update-slice_fusion.15
  503.0 1.4 collective-permute-done.26
  506.0 1.8 collective-permute-done.27
  509.0 4.4 collective-permute-done.28
  514.2 3.6 collective-permute-done.5
  521.8 2.8 multiply_reduce_fusion.4
  532.7 2.4 fusion.4
  537.7 2.1 constant_dynamic-update-slice_fusion.27
  542.0 2.1 constant_dynamic-update-slice_fusion.26
  545.9 5.5 collective-permute-done.33
  553.3 35.8 %collective-permute-done.34 = bf16[96,2048]{1,0:T(8,128)(2,1)S(1)} collective-permute-done((bf16[96,2048]{1,0:T(8,128)(2,1)S(1)}, bf16[96,2048]{1,0:T(8,128)(2,1)S(1)}, u32[]{:S(2)}, u32[]{:S(2)}) %collective-permute-start.34) | collective-permute-done | bytes 393248 | tf_op jit(solution)/shard_map/ppermute | solution.py:66
  592.9 7.5 convolution_convert_fusion.3
  605.2 3.0 constant_dynamic-update-slice_fusion.10
  608.1 3.0 constant_dynamic-update-slice_fusion.9
  611.1 14.7 %collective-permute-done.17 = bf16[96,5120]{1,0:T(8,128)(2,1)S(1)} collective-permute-done((bf16[96,5120]{1,0:T(8,128)(2,1)S(1)}, bf16[96,5120]{1,0:T(8,128)(2,1)S(1)}, u32[]{:S(2)}, u32[]{:S(2)}) %collective-permute-start.17) | collective-permute-done | bytes 983072 | tf_op jit(solution)/shard_map/ppermute | solution.py:66
  625.9 2.1 collective-permute-done.18
  628.0 3.0 constant_dynamic-update-slice_fusion.8
  631.0 3.0 constant_dynamic-update-slice_fusion.7
  636.1 1.4 constant_dynamic-update-slice_fusion.4
  639.6 11.6 %convolution_convert_fusion.2 = bf16[256,5120]{1,0:T(8,128)(2,1)} fusion(bf16[1536,256]{0,1:T(8,128)(2,1)S(1)} %copy-done.34, bf16[1536,5120]{1,0:T(8,128)(2,1)} %constant_dynamic-update-slice_fusion.2), kind=kOutput, calls=%fused_computation.3 | convolution fusion | flops 4027842560 | bytes 19136512 | tf_op jit(solution)/shard_map/dot_general | solution.py:1194
  653.1 1.8 fusion.53
  656.4 6.7 fusion.55
  663.1 7.3 broadcast_select_fusion.3
  670.5 2.6 fusion.23
  676.4 5.0 all-to-all-start
  681.4 3.5 fusion.8
  685.0 8.5 %all-to-all-done = f32[32,1,1160]{2,1,0:T(1,128)S(1)} async-done(((f32[32,1,1160]{2,1,0:T(1,128)}), f32[32,1,1160]{2,1,0:T(1,128)S(1)}, u32[]{:S(2)}, u32[]{:S(2)}) %all-to-all-start) | async-done | bytes 148512 | tf_op jit(solution)/shard_map/all_to_all | solution.py:1215
  695.6 3.6 convert_element_type.90
  699.4 3.1 maximum_convert_fusion
  702.5 2.1 convert_element_type.89
  704.6 47.4 %reduce-scatter.9.cloned.1.call-done = bf16[64,5120]{1,0:T(8,128)(2,1)} async-done(((bf16[256,5120]{1,0:T(8,128)(2,1)}), bf16[64,5120]{1,0:T(8,128)(2,1)}) %reduce-scatter.9.cloned.1.call-update) | async-done | bytes 655376 | tf_op jit(solution)/shard_map/reduce_scatter | solution.py:1200
  752.1 1.6 fusion.48
  753.7 2.1 slice.126
  (293 shorter events, 85.0 us)
Async XLA Ops:
  7.2 644.0 %reduce-scatter.7.cloned.1.call-start = ((), (), s32[]{:S(2)}) async-start(), calls=%async_computation.6 | async-start | bytes 7864320 | tf_op jit(solution)/shard_map/reduce_scatter | solution.py:1095
  7.2 165.5 %collective-permute-start = (s32[192,8]{0,1:T(8,128)}, s32[192,8]{0,1:T(8,128)S(1)}, u32[]{:S(2)}, u32[]{:S(2)}) collective-permute-start(s32[192,8]{0,1:T(8,128)} %param.26), channel_id=1, source_target_pairs={{0,1},{1,0},{2,3},{3,2},{4,5},{5,4},{6,7},{7,6},{8,9},{9,8},{10,11... | collective-permute-start | bytes 18440 | tf_op jit(solution)/shard_map/ppermute | solution.py:66
  143.9 24.6 %slice-start.2 = ((s8[8388608]{0:T(1024)(128)(4,1)}), s8[4194304]{0:T(1024)(128)(4,1)S(1)}, s32[]{:S(2)}) async-start(s8[8388608]{0:T(1024)(128)(4,1)} %bitcast.164), calls=%async_computation.11 | async-start | bytes 8388608
  162.6 5.8 copy-start.5
  162.6 5.8 copy-start.1
  162.7 5.8 slice-start.3
  172.9 1.3 collective-permute-start.1
  174.3 3.8 collective-permute-start.2
  264.7 386.5 %reduce-scatter.5.cloned.1.call-start = ((), (), s32[]{:S(2)}) async-start(), calls=%async_computation.5 | async-start | bytes 15728640 | tf_op jit(solution)/shard_map/reduce_scatter | solution.py:1098
  291.1 411.4 %reduce-scatter.11.cloned.1.call-start = ((), (), s32[]{:S(2)}) async-start(), calls=%async_computation.8 | async-start | bytes 2621440 | tf_op jit(solution)/shard_map/reduce_scatter | solution.py:1199
  294.8 117.9 %copy-start.25 = (f32[192,16]{1,0:T(8,128)}, f32[192,16]{1,0:T(8,128)S(1)}, u32[]{:S(2)}) copy-start(f32[192,16]{1,0:T(8,128)S(1)} %get-tuple-element.206) | copy-start | bytes 36868
  295.9 12.3 %copy-start.9 = (bf16[192,2048]{1,0:T(8,128)(2,1)S(1)}, bf16[192,2048]{1,0:T(8,128)(2,1)}, u32[]{:S(2)}) copy-start(bf16[192,2048]{1,0:T(8,128)(2,1)} %copy-done.8) | copy-start | bytes 2359300
  307.6 174.4 %collective-permute-start.22 = (bf16[192,512]{1,0:T(8,128)(2,1)}, bf16[192,512]{1,0:T(8,128)(2,1)}, u32[]{:S(2)}, u32[]{:S(2)}) collective-permute-start(bf16[192,512]{1,0:T(8,128)(2,1)} %bitcast.129), channel_id=1, source_target_pairs={{0,1},{1,0},{2,3},{3,2},{4,5},{5,4},{6,7},{7,6},{8,9},{9,8},{10,11... | collective-permute-start | bytes 589832 | tf_op jit(solution)/shard_map/ppermute | solution.py:109
  311.8 156.3 %collective-permute-start.11 = (bf16[192,256]{0,1:T(8,128)(2,1)}, bf16[192,256]{0,1:T(8,128)(2,1)}, u32[]{:S(2)}, u32[]{:S(2)}) collective-permute-start(bf16[192,256]{0,1:T(8,128)(2,1)} %bitcast.20), channel_id=1, source_target_pairs={{0,6},{1,7},{2,4},{3,5},{4,2},{5,3},{6,0},{7,1},{8,14},{9,15},{10,... | collective-permute-start | bytes 294920 | tf_op jit(solution)/shard_map/ppermute | solution.py:109
  313.0 155.2 %collective-permute-start.12 = (bf16[192,256]{0,1:T(8,128)(2,1)}, bf16[192,256]{0,1:T(8,128)(2,1)}, u32[]{:S(2)}, u32[]{:S(2)}) collective-permute-start(bf16[192,256]{0,1:T(8,128)(2,1)} %bitcast.21), channel_id=1, source_target_pairs={{0,7},{1,6},{2,5},{3,4},{4,3},{5,2},{6,1},{7,0},{8,15},{9,14},{10,... | collective-permute-start | bytes 294920 | tf_op jit(solution)/shard_map/ppermute | solution.py:109
  314.4 156.2 %collective-permute-start.10 = (bf16[192,256]{0,1:T(8,128)(2,1)}, bf16[192,256]{0,1:T(8,128)(2,1)}, u32[]{:S(2)}, u32[]{:S(2)}) collective-permute-start(bf16[192,256]{0,1:T(8,128)(2,1)} %bitcast.19), channel_id=1, source_target_pairs={{0,5},{1,4},{2,7},{3,6},{4,1},{5,0},{6,3},{7,2},{8,13},{9,12},{10,... | collective-permute-start | bytes 294920 | tf_op jit(solution)/shard_map/ppermute | solution.py:109
  315.6 155.1 %collective-permute-start.9 = (bf16[192,256]{0,1:T(8,128)(2,1)}, bf16[192,256]{0,1:T(8,128)(2,1)}, u32[]{:S(2)}, u32[]{:S(2)}) collective-permute-start(bf16[192,256]{0,1:T(8,128)(2,1)} %bitcast.18), channel_id=1, source_target_pairs={{0,4},{1,5},{2,6},{3,7},{4,0},{5,1},{6,2},{7,3},{8,12},{9,13},{10,... | collective-permute-start | bytes 294920 | tf_op jit(solution)/shard_map/ppermute | solution.py:109
  369.7 43.0 %copy-start.50 = (f32[192]{0:T(256)}, f32[192]{0:T(256)S(1)}, u32[]{:S(2)}) copy-start(f32[192]{0:T(256)S(1)} %multiply_reduce_fusion.5) | copy-start | bytes 2308
  369.7 43.0 %copy-start.18 = (f32[192,2048]{1,0:T(8,128)S(1)}, f32[192,2048]{1,0:T(8,128)}, u32[]{:S(2)}) copy-start(f32[192,2048]{1,0:T(8,128)} %copy-done.17) | copy-start | bytes 4718596
  369.7 43.0 %copy-start.44 = (bf16[2048,16]{0,1:T(8,128)(2,1)S(1)}, bf16[2048,16]{0,1:T(8,128)(2,1)}, u32[]{:S(2)}) copy-start(bf16[2048,16]{0,1:T(8,128)(2,1)} %param.23) | copy-start | bytes 196612
  417.0 8.9 %slice-start = ((s8[8388608]{0:T(1024)(128)(4,1)}), s8[4194304]{0:T(1024)(128)(4,1)S(1)}, s32[]{:S(2)}) async-start(s8[8388608]{0:T(1024)(128)(4,1)} %bitcast.137), calls=%async_computation.9 | async-start | bytes 8388608
  419.2 6.8 slice-start.1
  463.2 8.8 %copy-start.28 = (f32[64,512]{1,0:T(8,128)}, f32[64,512]{1,0:T(8,128)S(1)}, u32[]{:S(2)}) copy-start(f32[64,512]{1,0:T(8,128)S(1)} %slice.93) | copy-start | bytes 393220
  468.2 17.0 %collective-permute-start.23 = (bf16[192,512]{1,0:T(8,128)(2,1)}, bf16[192,512]{1,0:T(8,128)(2,1)}, u32[]{:S(2)}, u32[]{:S(2)}) collective-permute-start(bf16[192,512]{1,0:T(8,128)(2,1)} %bitcast.128), channel_id=1, source_target_pairs={{0,2},{1,3},{2,0},{3,1},{4,6},{5,7},{6,4},{7,5},{8,10},{9,11},{10,... | collective-permute-start | bytes 589832 | tf_op jit(solution)/shard_map/ppermute | solution.py:109
  468.2 6.6 collective-permute-start.8
  470.7 5.5 collective-permute-start.7
  470.7 7.1 collective-permute-start.6
  474.8 61.9 %collective-permute-start.32 = (bf16[192,2048]{1,0:T(8,128)(2,1)}, bf16[192,2048]{1,0:T(8,128)(2,1)S(1)}, u32[]{:S(2)}, u32[]{:S(2)}) collective-permute-start(bf16[192,2048]{1,0:T(8,128)(2,1)} %get-tuple-element.158), channel_id=1, source_target_pairs={{0,4},{2,6},{4,0},{6,2},{1,5},{3,7},{5,1},{7,3},{8,12},{10,14},{12... | collective-permute-start | bytes 2359304 | tf_op jit(solution)/shard_map/ppermute | solution.py:66
  476.1 10.6 %collective-permute-start.24 = (bf16[192,512]{1,0:T(8,128)(2,1)}, bf16[192,512]{1,0:T(8,128)(2,1)}, u32[]{:S(2)}, u32[]{:S(2)}) collective-permute-start(bf16[192,512]{1,0:T(8,128)(2,1)} %bitcast.160), channel_id=1, source_target_pairs={{0,3},{1,2},{2,1},{3,0},{4,7},{5,6},{6,5},{7,4},{8,11},{9,10},{10,... | collective-permute-start | bytes 589832 | tf_op jit(solution)/shard_map/ppermute | solution.py:109
  477.8 21.9 %collective-permute-start.25 = (bf16[192,512]{1,0:T(8,128)(2,1)}, bf16[192,512]{1,0:T(8,128)(2,1)}, u32[]{:S(2)}, u32[]{:S(2)}) collective-permute-start(bf16[192,512]{1,0:T(8,128)(2,1)} %bitcast.159), channel_id=1, source_target_pairs={{0,4},{1,5},{2,6},{3,7},{4,0},{5,1},{6,2},{7,3},{8,12},{9,13},{10,... | collective-permute-start | bytes 589832 | tf_op jit(solution)/shard_map/ppermute | solution.py:109
  482.0 22.4 %collective-permute-start.26 = (bf16[192,512]{1,0:T(8,128)(2,1)}, bf16[192,512]{1,0:T(8,128)(2,1)S(1)}, u32[]{:S(2)}, u32[]{:S(2)}) collective-permute-start(bf16[192,512]{1,0:T(8,128)(2,1)} %bitcast.158), channel_id=1, source_target_pairs={{0,5},{1,4},{2,7},{3,6},{4,1},{5,0},{6,3},{7,2},{8,13},{9,12},{10,... | collective-permute-start | bytes 589832 | tf_op jit(solution)/shard_map/ppermute | solution.py:109
  485.1 17.2 %collective-permute-start.4 = (bf16[2,128,512]{2,1,0:T(8,128)(2,1)}, bf16[2,128,512]{2,1,0:T(8,128)(2,1)S(1)}, u32[]{:S(2)}, u32[]{:S(2)}) collective-permute-start(bf16[2,128,512]{2,1,0:T(8,128)(2,1)} %get-tuple-element.183), channel_id=1, source_target_pairs={{0,2},{2,0},{4,6},{6,4},{1,3},{3,1},{5,7},{7,5},{8,10},{10,8},{12,... | collective-permute-start | bytes 786440 | tf_op jit(solution)/shard_map/ppermute | solution.py:66
  486.7 21.1 %collective-permute-start.27 = (bf16[192,512]{1,0:T(8,128)(2,1)}, bf16[192,512]{1,0:T(8,128)(2,1)S(1)}, u32[]{:S(2)}, u32[]{:S(2)}) collective-permute-start(bf16[192,512]{1,0:T(8,128)(2,1)} %bitcast.157), channel_id=1, source_target_pairs={{0,6},{1,7},{2,4},{3,5},{4,2},{5,3},{6,0},{7,1},{8,14},{9,15},{10,... | collective-permute-start | bytes 589832 | tf_op jit(solution)/shard_map/ppermute | solution.py:109
  499.7 13.6 %collective-permute-start.28 = (bf16[192,512]{1,0:T(8,128)(2,1)}, bf16[192,512]{1,0:T(8,128)(2,1)S(1)}, u32[]{:S(2)}, u32[]{:S(2)}) collective-permute-start(bf16[192,512]{1,0:T(8,128)(2,1)} %bitcast.156), channel_id=1, source_target_pairs={{0,7},{1,6},{2,5},{3,4},{4,3},{5,2},{6,1},{7,0},{8,15},{9,14},{10,... | collective-permute-start | bytes 589832 | tf_op jit(solution)/shard_map/ppermute | solution.py:109
  502.3 11.9 %collective-permute-start.3 = (bf16[2,128,512]{2,1,0:T(8,128)(2,1)}, bf16[2,128,512]{2,1,0:T(8,128)(2,1)S(1)}, u32[]{:S(2)}, u32[]{:S(2)}) collective-permute-start(bf16[2,128,512]{2,1,0:T(8,128)(2,1)} %get-tuple-element.182), channel_id=1, source_target_pairs={{0,2},{2,0},{4,6},{6,4},{1,3},{3,1},{5,7},{7,5},{8,10},{10,8},{12,... | collective-permute-start | bytes 786440 | tf_op jit(solution)/shard_map/ppermute | solution.py:66
  504.4 13.4 %collective-permute-start.5 = (bf16[2,128,512]{2,1,0:T(8,128)(2,1)S(1)}, bf16[2,128,512]{2,1,0:T(8,128)(2,1)S(1)}, u32[]{:S(2)}, u32[]{:S(2)}) collective-permute-start(bf16[2,128,512]{2,1,0:T(8,128)(2,1)S(1)} %add_convert_fusion.1), channel_id=1, source_target_pairs={{0,4},{2,6},{4,0},{6,2},{1,5},{3,7},{5,1},{7,3},{8,12},{10,14},{12... | collective-permute-start | bytes 786440 | tf_op jit(solution)/shard_map/ppermute | solution.py:66
  507.8 33.1 %collective-permute-start.30 = (bf16[192,2048]{1,0:T(8,128)(2,1)}, bf16[192,2048]{1,0:T(8,128)(2,1)}, u32[]{:S(2)}, u32[]{:S(2)}) collective-permute-start(bf16[192,2048]{1,0:T(8,128)(2,1)} %get-tuple-element.158), channel_id=1, source_target_pairs={{0,2},{2,0},{4,6},{6,4},{1,3},{3,1},{5,7},{7,5},{8,10},{10,8},{12,... | collective-permute-start | bytes 2359304 | tf_op jit(solution)/shard_map/ppermute | solution.py:66
  513.3 19.3 %collective-permute-start.29 = (bf16[192,2048]{1,0:T(8,128)(2,1)}, bf16[192,2048]{1,0:T(8,128)(2,1)}, u32[]{:S(2)}, u32[]{:S(2)}) collective-permute-start(bf16[192,2048]{1,0:T(8,128)(2,1)} %get-tuple-element.158), channel_id=1, source_target_pairs={{0,1},{1,0},{2,3},{3,2},{4,5},{5,4},{6,7},{7,6},{8,9},{9,8},{10,11... | collective-permute-start | bytes 2359304 | tf_op jit(solution)/shard_map/ppermute | solution.py:66
  521.8 8.0 %copy-start.11 = (f32[192,1024]{1,0:T(8,128)S(1)}, f32[192,1024]{1,0:T(8,128)}, u32[]{:S(2)}) copy-start(f32[192,1024]{1,0:T(8,128)} %copy-done.10) | copy-start | bytes 2359300
  521.8 8.0 %copy-start.29 = (f32[64,512]{1,0:T(8,128)S(1)}, f32[64,512]{1,0:T(8,128)}, u32[]{:S(2)}) copy-start(f32[64,512]{1,0:T(8,128)} %copy-done.28) | copy-start | bytes 393220
  521.8 8.0 %copy-start.51 = (f32[512]{0:T(512)S(1)}, f32[512]{0:T(512)}, u32[]{:S(2)}) copy-start(f32[512]{0:T(512)} %broadcast_bitcast_fusion) | copy-start | bytes 6148
  532.7 11.4 %collective-permute-start.31 = (bf16[192,2048]{1,0:T(8,128)(2,1)}, bf16[192,2048]{1,0:T(8,128)(2,1)S(1)}, u32[]{:S(2)}, u32[]{:S(2)}) collective-permute-start(bf16[192,2048]{1,0:T(8,128)(2,1)} %collective-permute-done.29), channel_id=1, source_target_pairs={{0,2},{2,0},{4,6},{6,4},{1,3},{3,1},{5,7},{7,5},{8,10},{10,8},{12,... | collective-permute-start | bytes 2359304 | tf_op jit(solution)/shard_map/ppermute | solution.py:66
  535.1 73.0 %collective-permute-start.14 = (bf16[192,5120]{1,0:T(8,128)(2,1)}, bf16[192,5120]{1,0:T(8,128)(2,1)}, u32[]{:S(2)}, u32[]{:S(2)}) collective-permute-start(bf16[192,5120]{1,0:T(8,128)(2,1)} %get-tuple-element.165), channel_id=1, source_target_pairs={{0,2},{2,0},{4,6},{6,4},{1,3},{3,1},{5,7},{7,5},{8,10},{10,8},{12,... | collective-permute-start | bytes 5898248 | tf_op jit(solution)/shard_map/ppermute | solution.py:66
  535.6 57.2 %collective-permute-start.13 = (bf16[192,5120]{1,0:T(8,128)(2,1)}, bf16[192,5120]{1,0:T(8,128)(2,1)}, u32[]{:S(2)}, u32[]{:S(2)}) collective-permute-start(bf16[192,5120]{1,0:T(8,128)(2,1)} %get-tuple-element.165), channel_id=1, source_target_pairs={{0,1},{1,0},{2,3},{3,2},{4,5},{5,4},{6,7},{7,6},{8,9},{9,8},{10,11... | collective-permute-start | bytes 5898248 | tf_op jit(solution)/shard_map/ppermute | solution.py:66
  536.7 52.4 %collective-permute-start.34 = (bf16[96,2048]{1,0:T(8,128)(2,1)S(1)}, bf16[96,2048]{1,0:T(8,128)(2,1)S(1)}, u32[]{:S(2)}, u32[]{:S(2)}) collective-permute-start(bf16[96,2048]{1,0:T(8,128)(2,1)S(1)} %slice.125), channel_id=1, source_target_pairs={{0,1},{1,0},{2,3},{3,2},{4,5},{5,4},{6,7},{7,6},{8,9},{9,8},{10,11... | collective-permute-start | bytes 1179656 | tf_op jit(solution)/shard_map/ppermute | solution.py:66
  540.9 10.6 %collective-permute-start.33 = (bf16[96,2048]{1,0:T(8,128)(2,1)S(1)}, bf16[96,2048]{1,0:T(8,128)(2,1)S(1)}, u32[]{:S(2)}, u32[]{:S(2)}) collective-permute-start(bf16[96,2048]{1,0:T(8,128)(2,1)S(1)} %slice.124), channel_id=1, source_target_pairs={{0,4},{2,6},{4,0},{6,2},{1,5},{3,7},{5,1},{7,3},{8,12},{10,14},{12... | collective-permute-start | bytes 1179656 | tf_op jit(solution)/shard_map/ppermute | solution.py:66
  544.1 45.8 %collective-permute-start.35 = (bf16[192,2048]{1,0:T(8,128)(2,1)S(1)}, bf16[192,2048]{1,0:T(8,128)(2,1)S(1)}, u32[]{:S(2)}, u32[]{:S(2)}) collective-permute-start(bf16[192,2048]{1,0:T(8,128)(2,1)S(1)} %collective-permute-done.32), channel_id=1, source_target_pairs={{0,2},{2,0},{4,6},{6,4},{1,3},{3,1},{5,7},{7,5},{8,10},{10,8},{12,... | collective-permute-start | bytes 2359304 | tf_op jit(solution)/shard_map/ppermute | solution.py:66
  551.5 51.3 %collective-permute-start.16 = (bf16[192,5120]{1,0:T(8,128)(2,1)}, bf16[192,5120]{1,0:T(8,128)(2,1)}, u32[]{:S(2)}, u32[]{:S(2)}) collective-permute-start(bf16[192,5120]{1,0:T(8,128)(2,1)} %get-tuple-element.165), channel_id=1, source_target_pairs={{0,4},{2,6},{4,0},{6,2},{1,5},{3,7},{5,1},{7,3},{8,12},{10,14},{12... | collective-permute-start | bytes 5898248 | tf_op jit(solution)/shard_map/ppermute | solution.py:66
  553.3 39.6 %copy-start.49 = (bf16[1536,512]{1,0:T(8,128)(2,1)S(1)}, bf16[1536,512]{1,0:T(8,128)(2,1)}, u32[]{:S(2)}) copy-start(bf16[1536,512]{1,0:T(8,128)(2,1)} %constant_dynamic-update-slice_fusion.12) | copy-start | bytes 4718596
  589.0 2.2 collective-permute-start.36
  589.8 2.2 collective-permute-start.37
  592.9 35.1 %collective-permute-start.15 = (bf16[192,5120]{1,0:T(8,128)(2,1)}, bf16[192,5120]{1,0:T(8,128)(2,1)}, u32[]{:S(2)}, u32[]{:S(2)}) collective-permute-start(bf16[192,5120]{1,0:T(8,128)(2,1)} %collective-permute-done.13), channel_id=1, source_target_pairs={{0,2},{2,0},{4,6},{6,4},{1,3},{3,1},{5,7},{7,5},{8,10},{10,8},{12,... | collective-permute-start | bytes 5898248 | tf_op jit(solution)/shard_map/ppermute | solution.py:66
  601.6 24.2 %collective-permute-start.17 = (bf16[96,5120]{1,0:T(8,128)(2,1)S(1)}, bf16[96,5120]{1,0:T(8,128)(2,1)S(1)}, u32[]{:S(2)}, u32[]{:S(2)}) collective-permute-start(bf16[96,5120]{1,0:T(8,128)(2,1)S(1)} %slice.122), channel_id=1, source_target_pairs={{0,4},{2,6},{4,0},{6,2},{1,5},{3,7},{5,1},{7,3},{8,12},{10,14},{12... | collective-permute-start | bytes 2949128 | tf_op jit(solution)/shard_map/ppermute | solution.py:66
  604.0 23.9 %collective-permute-start.18 = (bf16[96,5120]{1,0:T(8,128)(2,1)S(1)}, bf16[96,5120]{1,0:T(8,128)(2,1)S(1)}, u32[]{:S(2)}, u32[]{:S(2)}) collective-permute-start(bf16[96,5120]{1,0:T(8,128)(2,1)S(1)} %slice.123), channel_id=1, source_target_pairs={{0,1},{1,0},{2,3},{3,2},{4,5},{5,4},{6,7},{7,6},{8,9},{9,8},{10,11... | collective-permute-start | bytes 2949128 | tf_op jit(solution)/shard_map/ppermute | solution.py:66
  605.2 30.9 %collective-permute-start.19 = (bf16[192,5120]{1,0:T(8,128)(2,1)}, bf16[192,5120]{1,0:T(8,128)(2,1)S(1)}, u32[]{:S(2)}, u32[]{:S(2)}) collective-permute-start(bf16[192,5120]{1,0:T(8,128)(2,1)} %collective-permute-done.16), channel_id=1, source_target_pairs={{0,2},{2,0},{4,6},{6,4},{1,3},{3,1},{5,7},{7,5},{8,10},{10,8},{12,... | collective-permute-start | bytes 5898248 | tf_op jit(solution)/shard_map/ppermute | solution.py:66
  625.8 11.7 %collective-permute-start.20 = (bf16[96,5120]{1,0:T(8,128)(2,1)S(1)}, bf16[96,5120]{1,0:T(8,128)(2,1)S(1)}, u32[]{:S(2)}, u32[]{:S(2)}) collective-permute-start(bf16[96,5120]{1,0:T(8,128)(2,1)S(1)} %collective-permute-done.17), channel_id=1, source_target_pairs={{0,2},{2,0},{4,6},{6,4},{1,3},{3,1},{5,7},{7,5},{8,10},{10,8},{12,... | collective-permute-start | bytes 2949128 | tf_op jit(solution)/shard_map/ppermute | solution.py:66
  628.0 10.6 %collective-permute-start.21 = (bf16[96,5120]{1,0:T(8,128)(2,1)S(1)}, bf16[96,5120]{1,0:T(8,128)(2,1)S(1)}, u32[]{:S(2)}, u32[]{:S(2)}) collective-permute-start(bf16[96,5120]{1,0:T(8,128)(2,1)S(1)} %collective-permute-done.18), channel_id=1, source_target_pairs={{0,2},{2,0},{4,6},{6,4},{1,3},{3,1},{5,7},{7,5},{8,10},{10,8},{12,... | collective-permute-start | bytes 2949128 | tf_op jit(solution)/shard_map/ppermute | solution.py:66
  651.2 100.9 %reduce-scatter.9.cloned.1.call-start = ((), (), s32[]{:S(2)}) async-start(), calls=%async_computation.7 | async-start | bytes 3276800 | tf_op jit(solution)/shard_map/reduce_scatter | solution.py:1200
  663.1 7.3 copy-start.52
  663.1 7.4 copy-start.33
  663.1 7.4 copy-start.46
  674.3 7.1 copy-start.20
  674.3 7.1 copy-start.53
  676.4 17.1 %all-to-all-start = ((f32[32,1,1160]{2,1,0:T(1,128)}), f32[32,1,1160]{2,1,0:T(1,128)S(1)}, u32[]{:S(2)}, u32[]{:S(2)}) async-start(f32[32,1,1160]{2,1,0:T(1,128)} %copy.129), calls=%async_computation | async-start | bytes 327680 | tf_op jit(solution)/shard_map/all_to_all | solution.py:1215
  (37 other events, 80.1 us)
Sparse Core Ops, SparseCore 0:
  264.8 111.6 reduce-scatter.6
  378.9 212.3 reduce-scatter.4
  651.3 46.9 reduce-scatter.10
  700.6 51.4 reduce-scatter.8

commit v4 on v3

--- a/solution.py
+++ b/solution.py
@@ -59,7 +59,7 @@
 
 
 def small_plane():
-    return lax.axis_size("ctx") == 4 and lax.axis_size("expert") == 2
+    return [lax.axis_size(a) for a in every] == [4, 4, 2]
 
 
 def swap(v, axis, bit):
@@ -76,38 +76,6 @@
 
 def over_y(v):
     return swap(v, "expert", 1)
-
-
-def relative():
-    count = lax.axis_size(plane)
-    me = lax.axis_index(plane)
-    if small_plane():
-        return [me ^ r for r in range(count)]
-    return list(range(count))
-
-
-def gather_plane(v):
-    if not small_plane():
-        out = lax.all_gather(v, plane, axis=0, tiled=False)
-        return [out[i] for i in range(out.shape[0])]
-    half = v.shape[0] // 2
-    vy, vx, vc = over_y(v), over_x(v), core(v)
-    top, low = over_x(vy[:half]), over_y(vx[half:])
-    vyc, vxc = core(vy), core(vx)
-    vxy = jnp.concatenate([top, low], axis=0)
-    vxyc = jnp.concatenate([core(top), core(low)], axis=0)
-    return [v, vy, vc, vyc, vx, vxy, vxc, vxyc]
-
-
-def exchange_plane(blocks):
-    if not small_plane():
-        out = lax.all_to_all(jnp.stack(blocks), plane, split_axis=0, concat_axis=0, tiled=True)
-        return [out[i] for i in range(out.shape[0])]
-    out = [blocks[0]]
-    for r in range(1, 8):
-        pairs = [(i, i ^ r) for i in range(8)]
-        out.append(lax.ppermute(blocks[r], plane, pairs))
-    return out
 
 
 def over_z(v):
@@ -169,23 +137,14 @@
             copy.wait_send()
 
 
-def run_rounds(work, between):
-    turns = max(i + len(todo) for i, todo in enumerate(work))
-    for turn in range(turns):
-        for i, todo in enumerate(work):
-            if 0 <= turn - i < len(todo):
-                todo[turn - i]()
-        if turn in between:
-            between[turn]()
-
-
-def half_fetch(here, send, sources, other, columns, rows):
+def half_fetch(here, send, sources, other, columns, rows, upper):
     def at(piece, part=None):
         first, size = piece * rows, rows
-        if part is not None:
-            size = rows // 2
-            first = first + part * size
-        return other.at[pl.ds(pl.multiple_of(first, size), size), columns]
+        if part == 0:
+            size = upper
+        elif part == 1:
+            first, size = first + upper, rows - upper
+        return other.at[pl.ds(pl.multiple_of(first, 16), size), columns]
 
     def piece(z, x, c):
         return z * 4 + x * 2 + c
@@ -236,7 +195,7 @@
     return [first, second, third, fourth, fifth]
 
 
-def block_gather(here, send, mine, local_sem, blocks):
+def block_gather(here, send, mine, local_sem, blocks, far_over_y=False, columns=None):
     rows = blocks.shape[0] // lax.axis_size(plane)
     half = rows // 2
     x, c, y = here.x, here.c, here.y
@@ -246,7 +205,8 @@
         first, size = slot * rows, rows
         if part is not None:
             first, size = first + part * half, half
-        return blocks.at[pl.ds(pl.multiple_of(first, size), size)]
+        rows_of = pl.ds(pl.multiple_of(first, size), size)
+        return blocks.at[rows_of] if columns is None else blocks.at[rows_of, columns]
 
     def first():
         slot = plane_slot(x, c, y)
@@ -259,12 +219,15 @@
     def second():
         got["y"].wait_recv()
         from_y = plane_slot(x, c, 1 - y)
-        got["top"] = send(at(from_y, 0), at(from_y, 0), here.to_x)
         got["yc"] = send(at(from_y), at(from_y), here.to_c)
+        if not far_over_y:
+            got["top"] = send(at(from_y, 0), at(from_y, 0), here.to_x)
         got["x"].wait_recv()
         from_x = plane_slot(1 - x, c, y)
+        got["xc"] = send(at(from_x), at(from_x), here.to_c)
+        if far_over_y:
+            got["top"] = send(at(from_x, 0), at(from_x, 0), here.to_y)
         got["low"] = send(at(from_x, 1), at(from_x, 1), here.to_y)
-        got["xc"] = send(at(from_x), at(from_x), here.to_c)
 
     def third():
         far = plane_slot(1 - x, c, 1 - y)
@@ -292,7 +255,9 @@
 def fetch_kernel(
     hidden_ref,
     attn_gain_ref,
+    query_gain_ref,
     key_gain_ref,
+    ffn_gain_ref,
     cosine_ref,
     sine_ref,
     key_ref,
@@ -300,19 +265,31 @@
     query_ref,
     output_ref,
     grad_ref,
+    routes_ref,
     kv_out,
     q_out,
-    o_other,
+    o_out,
     g_blocks,
+    route_blocks,
+    kv_all_out,
+    normed_owned,
+    attended_owned,
+    query_pre_ref,
+    key_pre_ref,
+    queries_ref,
+    residual_ref,
+    ffn_ref,
     normed_ref,
-    query_pre_ref,
-    kv_pre_ref,
-    kv_low_ref,
-    kv_blocks,
+    attended_ref,
     kv_own,
     kv_other,
     q_own,
     q_other,
+    o_own,
+    o_other,
+    kv_pre,
+    kv_low,
+    kv_all,
     send_sem,
     recv_sem,
     local_sem,
@@ -320,28 +297,37 @@
     here = Places()
     greet([here.to_y, here.to_z, here.to_c, here.to_x])
     send = Sender(send_sem, recv_sem)
-    width = hidden_ref.shape[1]
+    count, width = hidden_ref.shape
     half = width // 2
     narrow = key_ref.shape[1]
     wide = query_ref.shape[1]
+    prompt_all = kv_all.shape[0] - (count - PROMPT_DEV)
+    spread, groups = lax.axis_size(plane), lax.axis_size("dp")
     tile = 512
     loads = [
         pltpu.make_async_copy(key_ref, kv_own.at[:, pl.ds(0, narrow)], local_sem.at[0]),
         pltpu.make_async_copy(value_ref, kv_own.at[:, pl.ds(narrow, narrow)], local_sem.at[1]),
         pltpu.make_async_copy(query_ref, q_own, local_sem.at[2]),
+        pltpu.make_async_copy(output_ref, o_own, local_sem.at[3]),
     ]
     stores = [
-        pltpu.make_async_copy(kv_other, kv_out, local_sem.at[3]),
-        pltpu.make_async_copy(q_other, q_out, local_sem.at[4]),
+        pltpu.make_async_copy(kv_other, kv_out, local_sem.at[4]),
+        pltpu.make_async_copy(q_other, q_out, local_sem.at[5]),
+        pltpu.make_async_copy(o_other, o_out, local_sem.at[6]),
+        pltpu.make_async_copy(kv_all, kv_all_out, local_sem.at[7]),
     ]
-    mine = pl.ds(pl.multiple_of(here.y * half, half), half)
-    others = pl.ds(pl.multiple_of(half - here.y * half, half), half)
-
-    def project(weight, out, rows, first, count, add):
-        @pl.loop(first, first + count)
+
+    def part_of(size, which):
+        first = here.y * size if which == 0 else size - here.y * size
+        return pl.ds(pl.multiple_of(first, size), size)
+
+    def project(source, weight, out, which, first, count_of_tiles, add):
+        rows = part_of(weight.shape[0], which)
+
+        @pl.loop(first, first + count_of_tiles)
         def _(i):
             cols = pl.ds(pl.multiple_of(i * tile, tile), tile)
-            part = jnp.dot(normed_ref[:, rows], weight[:, cols], preferred_element_type=f32)
+            part = dot(source[:, rows], weight[:, cols])
             out[:, cols] = out[:, cols] + part if add else part
 
     def start():
@@ -351,43 +337,99 @@
         normed_ref[...] = (inputs * head_norm(inputs) * attn_gain_ref[...]).astype(bf16)
 
     def own_part():
-        for load in loads:
+        share = width // (spread * groups)
+        for s in range(spread):
+            normed_owned[s] = jnp.concatenate(
+                [
+                    normed_ref[:, (d * spread + s) * share : (d * spread + s + 1) * share]
+                    for d in range(groups)
+                ],
+                axis=1,
+            )
+        for load in loads[:3]:
             load.wait()
-        project(kv_own, kv_pre_ref, mine, 0, 2 * narrow // tile, False)
-        project(q_own, query_pre_ref, mine, 0, wide // tile, False)
+        project(normed_ref, kv_own, kv_pre, 0, 0, 2 * narrow // tile, False)
+        project(normed_ref, q_own, query_pre_ref, 0, 0, wide // tile, False)
 
     exchange = {}
 
     def keys_part():
-        project(kv_other, kv_pre_ref, others, 0, 2 * narrow // tile, True)
+        project(normed_ref, kv_other, kv_pre, 1, 0, 2 * narrow // tile, True)
         stores[0].start()
+        key_pre_ref[...] = kv_pre[:, :narrow]
         for h in range(narrow // HEAD_SIZE):
             cols = slice(h * HEAD_SIZE, (h + 1) * HEAD_SIZE)
-            v = kv_pre_ref[:, cols]
+            v = kv_pre[:, cols]
             v = v * head_norm(v) * key_gain_ref[...]
-            kv_low_ref[:, cols] = (v * cosine_ref[...] + turn_half(v) * sine_ref[...]).astype(bf16)
-        kv_low_ref[:, narrow:] = kv_pre_ref[:, narrow:].astype(bf16)
-        source = kv_low_ref.at[pl.ds(0, PROMPT_DEV)]
-        slot = kv_blocks.at[here.ctx]
-        exchange["own"] = pltpu.make_async_copy(source, slot, local_sem.at[5])
+            kv_low[:, cols] = (v * cosine_ref[...] + turn_half(v) * sine_ref[...]).astype(bf16)
+        kv_low[:, narrow:] = kv_pre[:, narrow:].astype(bf16)
+        kv_all[prompt_all:, :] = kv_low[PROMPT_DEV:, :]
+        source = kv_low.at[pl.ds(0, PROMPT_DEV)]
+        slot = kv_all.at[pl.ds(pl.multiple_of(here.ctx * PROMPT_DEV, PROMPT_DEV), PROMPT_DEV)]
+        exchange["own"] = pltpu.make_async_copy(source, slot, local_sem.at[8])
         exchange["own"].start()
         exchange["c"] = send(source, slot, here.to_c)
         exchange["x"] = send(source, slot, here.to_x)
 
     def keys_forward():
         exchange["x"].wait_recv()
-        slot = kv_blocks.at[(1 - here.x) * 2 + here.c]
+        first = ((1 - here.x) * 2 + here.c) * PROMPT_DEV
+        slot = kv_all.at[pl.ds(pl.multiple_of(first, PROMPT_DEV), PROMPT_DEV)]
         exchange["xc"] = send(slot, slot, here.to_c)
-        project(q_other, query_pre_ref, others, 0, wide // tile // 2, True)
+
+    def queries_first():
+        project(normed_ref, q_other, query_pre_ref, 1, 0, wide // tile // 2, True)
 
     def queries_rest():
         stores[1].start()
-        project(q_other, query_pre_ref, others, wide // tile // 2, wide // tile // 2, True)
+        project(
+            normed_ref, q_other, query_pre_ref, 1, wide // tile // 2, wide // tile // 2, True
+        )
+        for name in ("c", "xc"):
+            exchange[name].wait_recv()
+        exchange["own"].wait()
+        stores[3].start()
+
+    group = 4
+    pieces = 4
+
+    def attend(part):
+        visible = visible_keys(count, kv_all.shape[0])
+        blocks = wide // HEAD_SIZE // group // pieces
+
+        @pl.loop(part * blocks, (part + 1) * blocks)
+        def _(i):
+            first = lax.div(i * group, wide // narrow) * HEAD_SIZE
+            keys = kv_all[:, pl.ds(pl.multiple_of(first, HEAD_SIZE), HEAD_SIZE)]
+            values = kv_all[:, pl.ds(pl.multiple_of(narrow + first, HEAD_SIZE), HEAD_SIZE)]
+            for h in range(group):
+                cols = pl.ds(pl.multiple_of((i * group + h) * HEAD_SIZE, HEAD_SIZE), HEAD_SIZE)
+                v = query_pre_ref[:, cols]
+                v = v * head_norm(v) * query_gain_ref[...]
+                queries = (v * cosine_ref[...] + turn_half(v) * sine_ref[...]).astype(bf16)
+                queries_ref[:, cols] = queries
+                probs = head_softmax(queries, keys, visible).astype(bf16)
+                attended = dot(probs, values).astype(bf16)
+                attended_ref[:, cols] = attended
+                head = i * group + h
+                at = pl.multiple_of(lax.div(head, spread) * HEAD_SIZE, HEAD_SIZE)
+                attended_owned[lax.rem(head, spread), :, pl.ds(at, HEAD_SIZE)] = attended
+
+    def output_own():
+        loads[3].wait()
+        project(attended_ref, o_own, residual_ref, 0, 0, width // tile, False)
+
+    def finish_rows():
+        stores[2].start()
+        project(attended_ref, o_other, residual_ref, 1, 0, width // tile, True)
+        residual = residual_ref[...] + hidden_ref[...].astype(f32)
+        residual_ref[...] = residual
+        ffn_ref[...] = (residual * head_norm(residual) * ffn_gain_ref[...]).astype(bf16)
 
     low, high = pl.ds(0, wide // 2), pl.ds(wide // 2, wide // 2)
     o_low, o_high = pl.ds(0, width // 2), pl.ds(width // 2, width // 2)
     rows, o_rows = half // 8, output_ref.shape[0] // 8
-    work = [
+    kv, qa, qb, oa, ob, g, r = [
         half_fetch(
             here,
             send,
@@ -398,35 +440,44 @@
             kv_other,
             pl.ds(0, 2 * narrow),
             rows,
+            rows // 2,
         ),
-        half_fetch(here, send, [(query_ref, low, low)], q_other, low, rows),
-        half_fetch(here, send, [(query_ref, high, high)], q_other, high, rows),
-        half_fetch(here, send, [(output_ref, o_low, o_low)], o_other, o_low, o_rows),
-        half_fetch(here, send, [(output_ref, o_high, o_high)], o_other, o_high, o_rows),
-        block_gather(here, send, grad_ref, local_sem.at[6], g_blocks)[0],
+        half_fetch(here, send, [(query_ref, low, low)], q_other, low, rows, rows // 2),
+        half_fetch(here, send, [(query_ref, high, high)], q_other, high, rows, rows // 2),
+        half_fetch(here, send, [(output_ref, o_low, o_low)], o_other, o_low, o_rows, o_rows // 4),
+        half_fetch(
+            here, send, [(output_ref, o_high, o_high)], o_other, o_high, o_rows, o_rows // 4
+        ),
+        block_gather(here, send, grad_ref, local_sem.at[9], g_blocks, True)[0],
+        block_gather(here, send, routes_ref, local_sem.at[10], route_blocks)[0],
     ]
-    run_rounds(
-        work, {0: start, 2: own_part, 4: keys_part, 5: keys_forward, 6: queries_rest}
-    )
-    for name in ("c", "xc"):
-        exchange[name].wait_recv()
-    exchange["own"].wait()
+    steps = [
+        kv[0], start, kv[1], qa[0], kv[2], own_part, qa[1], qb[0],
+        kv[3], qa[2], qb[1], oa[0], kv[4], keys_part, qa[3], qb[2], oa[1], ob[0],
+        keys_forward, qa[4], queries_first, qb[3], ob[1], qb[4], queries_rest,
+        oa[2], g[0], r[0], lambda: attend(0), lambda: attend(1),
+        oa[3], ob[2], g[1], r[1], lambda: attend(2), lambda: attend(3), oa[4], output_own,
+        ob[3], g[2], r[2], ob[4], finish_rows, g[3], r[3],
+    ]
+    for step in steps:
+        step()
     for store in stores:
         store.wait()
     send.finish()
 
 
-def fetch_and_project(
-    hidden_in, attn_gain, key_gain, cosine, sine, key_matrix, value_matrix, query_weight,
-    output_weight, out_grad,
+def fetch_and_attend(
+    hidden_in, attn_gain, query_gain, key_gain, ffn_gain, cosine, sine, key_matrix, value_matrix,
+    query_weight, output_weight, out_grad, routes,
 ):
     rows, width = hidden_in.shape
     half, wide = query_weight.shape
     narrow = key_matrix.shape[1]
     spread = lax.axis_size(plane)
+    keys = lax.axis_size("ctx") * PROMPT_DEV + rows - PROMPT_DEV
     vmem = pl.BlockSpec(memory_space=pltpu.VMEM)
     anywhere = pl.BlockSpec(memory_space=pl.ANY)
-    copies = 5 * 10 + 1 + 9 + 3
+    copies = 5 * 10 + 1 + 2 * 9 + 3
     return pl.pallas_call(
         fetch_kernel,
         out_shape=[
@@ -434,29 +485,46 @@
             jax.ShapeDtypeStruct((half, wide), bf16),
             jax.ShapeDtypeStruct(output_weight.shape, bf16),
             jax.ShapeDtypeStruct((spread * rows, width), bf16),
+            jax.ShapeDtypeStruct((spread * rows, routes.shape[1]), jnp.int32),
+            jax.ShapeDtypeStruct((keys, 2 * narrow), bf16),
+            jax.ShapeDtypeStruct((spread, rows, width // spread), bf16),
+            jax.ShapeDtypeStruct((spread, rows, wide // spread), bf16),
+            jax.ShapeDtypeStruct((rows, wide), f32),
+            jax.ShapeDtypeStruct((rows, narrow), f32),
+            jax.ShapeDtypeStruct((rows, wide), bf16),
+            jax.ShapeDtypeStruct((rows, width), f32),
             jax.ShapeDtypeStruct((rows, width), bf16),
-            jax.ShapeDtypeStruct((rows, wide), f32),
-            jax.ShapeDtypeStruct((rows, 2 * narrow), f32),
-            jax.ShapeDtypeStruct((rows, 2 * narrow), bf16),
-            jax.ShapeDtypeStruct((lax.axis_size("ctx"), PROMPT_DEV, 2 * narrow), bf16),
         ],
-        in_specs=[vmem] * 5 + [anywhere] * 5,
-        out_specs=[anywhere] * 4 + [vmem] * 4 + [anywhere],
+        in_specs=[vmem] * 7 + [anywhere] * 6,
+        out_specs=[anywhere] * 6 + [vmem] * 7,
         scratch_shapes=[
+            pltpu.VMEM((rows, width), bf16),
+            pltpu.VMEM((rows, wide), bf16),
             pltpu.VMEM((half, 2 * narrow), bf16),
             pltpu.VMEM((half, 2 * narrow), bf16),
             pltpu.VMEM((half, wide), bf16),
             pltpu.VMEM((half, wide), bf16),
+            pltpu.VMEM(output_weight.shape, bf16),
+            pltpu.VMEM(output_weight.shape, bf16),
+            pltpu.VMEM((rows, 2 * narrow), f32),
+            pltpu.VMEM((rows, 2 * narrow), bf16),
+            pltpu.VMEM((keys, 2 * narrow), bf16),
             pltpu.SemaphoreType.DMA((copies,)),
             pltpu.SemaphoreType.DMA((copies,)),
-            pltpu.SemaphoreType.DMA((7,)),
+            pltpu.SemaphoreType.DMA((11,)),
         ],
         compiler_params=pltpu.CompilerParams(
-            collective_id=1, has_side_effects=True, vmem_limit_bytes=48 * 2**20
+            collective_id=1, has_side_effects=True, vmem_limit_bytes=60 * 2**20
+        ),
+        cost_estimate=pl.CostEstimate(
+            flops=2 * rows * width * (2 * wide + 2 * narrow) * 2,
+            bytes_accessed=60 * 2**20,
+            transcendentals=0,
         ),
     )(
-        hidden_in, attn_gain.reshape(1, width), key_gain.reshape(1, HEAD_SIZE), cosine, sine,
-        key_matrix, value_matrix, query_weight, output_weight, out_grad,
+        hidden_in, attn_gain.reshape(1, width), query_gain.reshape(1, HEAD_SIZE),
+        key_gain.reshape(1, HEAD_SIZE), ffn_gain.reshape(1, width), cosine, sine,
+        key_matrix, value_matrix, query_weight, output_weight, out_grad, routes,
     )
 
 
@@ -465,7 +533,34 @@
     return pl.ds(pl.multiple_of(first, rows), 2 * rows)
 
 
-def expert_kernel(
+def expert_chunk(some, first, rows_v, g_v, gate_up_v, down_v, hidden_v, grad_v, total_v, gate, mark):
+    ff = down_v.shape[0]
+    tile = 256
+
+    @pl.loop(0, ff // tile, unroll=True)
+    def _(f):
+        at = pl.multiple_of(f * tile, tile)
+        a = dot(rows_v[some, :], gate_up_v[:, pl.ds(at, tile)])
+        b = dot(rows_v[some, :], gate_up_v[:, pl.ds(ff + at, tile)])
+        q = lax.dot_general(
+            g_v[some, :],
+            down_v[pl.ds(at, tile), :],
+            (((1,), (1,)), ((), ())),
+            preferred_element_type=f32,
+        )
+        s = 1.0 / (1.0 + jnp.exp(-a))
+        raised_a = a * s
+        hidden = raised_a * b
+        total_v[...] = total_v[...] + jnp.where(
+            mark, jnp.sum(hidden * q, axis=-1, keepdims=True), 0.0
+        )
+        back = gate * q
+        hidden_v[some, pl.ds(at, tile)] = (gate * hidden).astype(bf16)
+        grad_v[some, pl.ds(at, tile)] = (back * b * s * (1.0 + a * (1.0 - s))).astype(bf16)
+        grad_v[some, pl.ds(ff + at, tile)] = (back * raised_a).astype(bf16)
+
+
+def first_expert_kernel(
     ffn_ref,
     routes_ref,
     router_ref,
@@ -475,6 +570,7 @@
     rows_out,
     hidden_out,
     grad_out,
+    gates_ref,
     gate_grad_ref,
     rows_v,
     g_v,
@@ -492,13 +588,12 @@
     send = Sender(send_sem, recv_sem)
     count = ffn_ref.shape[0]
     experts = router_ref.shape[1]
-    local_experts, ff, _ = down_hbm.shape
-    tile = 256
+    local_experts = down_hbm.shape[0]
     stages, got = block_gather(here, send, ffn_ref, local_sem.at[0], rows_v)
     stages[0]()
     loads = [
-        pltpu.make_async_copy(gate_up_hbm, gate_up_v, local_sem.at[1]),
-        pltpu.make_async_copy(down_hbm, down_v, local_sem.at[2]),
+        pltpu.make_async_copy(gate_up_hbm.at[0], gate_up_v, local_sem.at[1]),
+        pltpu.make_async_copy(down_hbm.at[0], down_v, local_sem.at[2]),
         pltpu.make_async_copy(g_hbm, g_v, local_sem.at[3]),
     ]
     for load in loads:
@@ -520,39 +615,19 @@
         gates = raised / jnp.sum(raised, axis=-1, keepdims=True)
         lane = lax.broadcasted_iota(jnp.int32, total_v.shape, 1)
         total_v[...] = jnp.zeros(total_v.shape, f32)
+        columns = [
+            jnp.sum(jnp.where(ids == first_expert + e, gates, 0.0), axis=-1, keepdims=True)
+            for e in range(local_experts)
+        ]
+        spread = jnp.zeros(total_v.shape, f32)
         for e in range(local_experts):
-            gate = jnp.sum(
-                jnp.where(ids == first_expert + e, gates, 0.0), axis=-1, keepdims=True
-            )
-            here_lane = (lane == first_expert + e) | (lane == first_expert + e + experts)
-
-            @pl.loop(0, ff // tile)
-            def _(f, e=e, gate=gate, here_lane=here_lane):
-                at = pl.multiple_of(f * tile, tile)
-                a = dot(rows_v[some, :], gate_up_v[e, :, pl.ds(at, tile)])
-                b = dot(rows_v[some, :], gate_up_v[e, :, pl.ds(ff + at, tile)])
-                q = lax.dot_general(
-                    g_v[some, :],
-                    down_v[e, pl.ds(at, tile), :],
-                    (((1,), (1,)), ((), ())),
-                    preferred_element_type=f32,
-                )
-                s = 1.0 / (1.0 + jnp.exp(-a))
-                raised_a = a * s
-                hidden = raised_a * b
-                total_v[...] = total_v[...] + jnp.where(
-                    here_lane, jnp.sum(hidden * q, axis=-1, keepdims=True), 0.0
-                )
-                back = gate * q
-                hidden_v[some, pl.ds(e * ff + at, tile)] = (gate * hidden).astype(bf16)
-                grad_v[some, pl.ds(2 * e * ff + at, tile)] = (
-                    back * b * s * (1.0 + a * (1.0 - s))
-                ).astype(bf16)
-                grad_v[some, pl.ds((2 * e + 1) * ff + at, tile)] = (back * raised_a).astype(bf16)
-
-        total = total_v[...]
-        high = total.astype(bf16).astype(f32)
-        gate_grad_ref[some, :] = jnp.where(lane < experts, high, total - high).astype(bf16)
+            spread = jnp.where(lane == e, columns[e], spread)
+        gates_ref[some, :] = spread
+        mark = (lane == first_expert) | (lane == first_expert + experts)
+        expert_chunk(
+            some, 0, rows_v, g_v, gate_up_v, down_v, hidden_v, grad_v, total_v, columns[0], mark
+        )
+        gate_grad_ref[some, :] = total_v[...]
         for source, target in ((hidden_v, hidden_out), (grad_v, grad_out), (rows_v, rows_out)):
             store = pltpu.make_async_copy(
                 source.at[some, :], target.at[some, :], local_sem.at[4 + len(stores)]
@@ -580,61 +655,200 @@
     send.finish()
 
 
-def arrive(got, name):
-    copy = got[name]
-    copy.wait() if name == "own" else copy.wait_recv()
-
-
-def plane_index(here):
-    return here.ctx * 2 + here.y
-
-
-def experts_of_plane(ffn_in, route_rows, router_weight, g_rows, gate_up, down_proj):
-    local_experts, ff, width = down_proj.shape
+def gather_first_expert(ffn_in, route_rows, router_weight, g_rows, gate_up, down_proj):
+    ff, width = down_proj.shape[1:]
     total = route_rows.shape[0]
     vmem = pl.BlockSpec(memory_space=pltpu.VMEM)
     anywhere = pl.BlockSpec(memory_space=pl.ANY)
     return pl.pallas_call(
-        expert_kernel,
+        first_expert_kernel,
         out_shape=[
             jax.ShapeDtypeStruct((total, width), bf16),
-            jax.ShapeDtypeStruct((total, local_experts * ff), bf16),
-            jax.ShapeDtypeStruct((total, 2 * local_experts * ff), bf16),
-            jax.ShapeDtypeStruct((total, 128), bf16),
+            jax.ShapeDtypeStruct((total, ff), bf16),
+            jax.ShapeDtypeStruct((total, 2 * ff), bf16),
+            jax.ShapeDtypeStruct((total, 128), f32),
+            jax.ShapeDtypeStruct((total, 128), f32),
         ],
         in_specs=[vmem] * 3 + [anywhere] * 3,
-        out_specs=[anywhere] * 3 + [vmem],
+        out_specs=[anywhere] * 3 + [vmem] * 2,
         scratch_shapes=[
             pltpu.VMEM((total, width), bf16),
             pltpu.VMEM((total, width), bf16),
-            pltpu.VMEM(gate_up.shape, bf16),
-            pltpu.VMEM(down_proj.shape, bf16),
-            pltpu.VMEM((total, local_experts * ff), bf16),
-            pltpu.VMEM((total, 2 * local_experts * ff), bf16),
+            pltpu.VMEM(gate_up.shape[1:], bf16),
+            pltpu.VMEM(down_proj.shape[1:], bf16),
+            pltpu.VMEM((total, ff), bf16),
+            pltpu.VMEM((total, 2 * ff), bf16),
             pltpu.VMEM((2 * ffn_in.shape[0], 128), f32),
             pltpu.SemaphoreType.DMA((9,)),
             pltpu.SemaphoreType.DMA((9,)),
             pltpu.SemaphoreType.DMA((16,)),
         ],
         compiler_params=pltpu.CompilerParams(
-            collective_id=2, has_side_effects=True, vmem_limit_bytes=60 * 2**20
+            collective_id=2, has_side_effects=True, vmem_limit_bytes=56 * 2**20
         ),
         cost_estimate=pl.CostEstimate(
-            flops=2 * total * width * 3 * local_experts * ff,
-            bytes_accessed=60 * 2**20,
+            flops=2 * total * width * 3 * ff,
+            bytes_accessed=40 * 2**20,
             transcendentals=0,
         ),
     )(ffn_in, route_rows, router_weight, g_rows, gate_up, down_proj)
 
 
-def plane_sum_kernel(across, *refs):
-    if across:
-        left_hbm, weight_hbm, extra_ref = refs[:3]
-        refs = refs[3:]
-    else:
-        left_hbm, weight_hbm = refs[:2]
-        extra_ref = None
-        refs = refs[2:]
+def next_expert_kernel(
+    which, experts, rows_v, g_v, gates_ref, totals_ref, gate_up_v, down_v, hidden_v, grad_v,
+    gate_grad_ref, total_v,
+):
+    lane = lax.broadcasted_iota(jnp.int32, total_v.shape, 1)
+    expert = lax.axis_index(plane) * lax.div(experts, lax.axis_size(plane)) + which
+    mark = (lane == expert) | (lane == expert + experts)
+    total_v[...] = totals_ref[...]
+    gate = jnp.sum(jnp.where(lane == which, gates_ref[...], 0.0), axis=-1, keepdims=True)
+    some = pl.ds(0, rows_v.shape[0])
+    expert_chunk(
+        some, 0, rows_v, g_v, gate_up_v.at[0], down_v.at[0], hidden_v, grad_v, total_v, gate, mark
+    )
+    total = total_v[...]
+    high = total.astype(bf16).astype(f32)
+    gate_grad_ref[...] = jnp.where(lane < experts, high, total - high).astype(bf16)
+
+
+def last_expert(which, experts, rows, g_rows, gates, totals, gate_up, down_proj):
+    ff, width = down_proj.shape[1:]
+    total = rows.shape[0]
+    step = total // 4
+
+    def block(columns):
+        return pl.BlockSpec((step, columns), lambda i: (i, 0))
+
+    def whole(shape):
+        return pl.BlockSpec((1,) + shape[1:], lambda i: (which, 0, 0))
+
+    def kernel(*refs):
+        next_expert_kernel(which, experts, *refs)
+
+    return pl.pallas_call(
+        kernel,
+        grid=(4,),
+        out_shape=[
+            jax.ShapeDtypeStruct((total, ff), bf16),
+            jax.ShapeDtypeStruct((total, 2 * ff), bf16),
+            jax.ShapeDtypeStruct((total, 128), bf16),
+        ],
+        in_specs=[
+            block(width), block(width), block(128), block(128),
+            whole(gate_up.shape), whole(down_proj.shape),
+        ],
+        out_specs=[block(ff), block(2 * ff), block(128)],
+        scratch_shapes=[pltpu.VMEM((step, 128), f32)],
+        compiler_params=pltpu.CompilerParams(vmem_limit_bytes=56 * 2**20),
+        cost_estimate=pl.CostEstimate(flops=10**6, bytes_accessed=10**6, transcendentals=0),
+    )(rows, g_rows, gates, totals, gate_up, down_proj)
+
+
+def weight_grad_kernel(
+    query_grad, kv_grad, branch, attended_owned, normed_owned, out_local, pre_local,
+    pre_v, branch_v, attended_v, normed_v, send_sem, recv_sem, local_sem,
+):
+    here = Places()
+    greet([here.to_y, here.to_c, here.to_x])
+    send = Sender(send_sem, recv_sem)
+    count, wide = query_grad.shape
+    narrow = kv_grad.shape[1]
+    spread = lax.axis_size(plane)
+    tile = 1024
+    half = wide // 2
+    low, high, last = pl.ds(0, half), pl.ds(half, half), pl.ds(wide, narrow)
+    b, _ = block_gather(here, send, branch, local_sem.at[0], branch_v)
+    qa, _ = block_gather(
+        here, send, query_grad.at[:, low], local_sem.at[1], pre_v, False, low
+    )
+    qb, _ = block_gather(
+        here, send, query_grad.at[:, high], local_sem.at[2], pre_v, False, high
+    )
+    kv, _ = block_gather(here, send, kv_grad, local_sem.at[3], pre_v, False, last)
+    loads = []
+    for device in range(spread):
+        slot = plane_slot(device // 4, device // 2 % 2, device % 2)
+        rows = pl.ds(slot * count, count)
+        for source, target in ((attended_owned, attended_v), (normed_owned, normed_v)):
+            loads.append(
+                pltpu.make_async_copy(
+                    source.at[device], target.at[rows], local_sem.at[4 + len(loads)]
+                )
+            )
+
+    def start():
+        for load in loads:
+            load.start()
+
+    def product(left, right, out, first, tiles):
+        @pl.loop(first, first + tiles)
+        def _(i):
+            cols = pl.ds(pl.multiple_of(i * tile, tile), tile)
+            out[:, cols] = transposed_dot(left[...], right[:, cols]).astype(bf16)
+
+    def output_product():
+        for load in loads:
+            load.wait()
+        product(attended_v, branch_v, out_local, 0, branch.shape[1] // tile)
+
+    steps = [
+        b[0], start, b[1], qa[0], b[2], qa[1], qb[0], b[3], output_product,
+        qa[2], qb[1], kv[0], qa[3],
+        lambda: product(normed_v, pre_v, pre_local, 0, half // tile),
+        qb[2], kv[1], qb[3],
+        lambda: product(normed_v, pre_v, pre_local, half // tile, half // tile),
+        kv[2], kv[3],
+        lambda: product(normed_v, pre_v, pre_local, wide // tile, narrow // tile),
+    ]
+    for step in steps:
+        step()
+    send.finish()
+
+
+def weight_grads(query_grad, kv_grad, branch, attended_owned, normed_owned):
+    count, wide = query_grad.shape
+    narrow, width = kv_grad.shape[1], branch.shape[1]
+    spread = lax.axis_size(plane)
+    vmem = pl.BlockSpec(memory_space=pltpu.VMEM)
+    anywhere = pl.BlockSpec(memory_space=pl.ANY)
+    return pl.pallas_call(
+        weight_grad_kernel,
+        out_shape=[
+            jax.ShapeDtypeStruct((attended_owned.shape[2], width), bf16),
+            jax.ShapeDtypeStruct((normed_owned.shape[2], wide + narrow), bf16),
+        ],
+        in_specs=[anywhere] * 5,
+        out_specs=[vmem] * 2,
+        scratch_shapes=[
+            pltpu.VMEM((spread * count, wide + narrow), bf16),
+            pltpu.VMEM((spread * count, width), bf16),
+            pltpu.VMEM((spread * count, attended_owned.shape[2]), bf16),
+            pltpu.VMEM((spread * count, normed_owned.shape[2]), bf16),
+            pltpu.SemaphoreType.DMA((36,)),
+            pltpu.SemaphoreType.DMA((36,)),
+            pltpu.SemaphoreType.DMA((4 + 2 * spread,)),
+        ],
+        compiler_params=pltpu.CompilerParams(
+            collective_id=5, has_side_effects=True, vmem_limit_bytes=56 * 2**20
+        ),
+        cost_estimate=pl.CostEstimate(flops=10**6, bytes_accessed=10**6, transcendentals=0),
+    )(query_grad, kv_grad, branch, attended_owned, normed_owned)
+
+
+def arrive(got, name):
+    copy = got[name]
+    copy.wait() if name == "own" else copy.wait_recv()
+
+
+def plane_index(here):
+    return here.ctx * 2 + here.y
+
+
+def plane_sum_kernel(across, experts, *refs):
+    lefts, weight_hbm = refs[:experts], refs[experts]
+    extra_ref = refs[experts + 1] if across else None
+    refs = refs[experts + 1 + across :]
     (
         out_ref, left_v, weight_v, part_v, core_v, edge_v, last_v, send_sem, recv_sem, local_sem,
     ) = refs
@@ -643,8 +857,7 @@
     send = Sender(send_sem, recv_sem)
     count = out_ref.shape[0]
     half = count // 2
-    experts = weight_hbm.shape[0]
-    depth = left_hbm.shape[1] // experts
+    depth = lefts[0].shape[1]
     width = weight_hbm.shape[1] if across else weight_hbm.shape[2]
     tile = 256
     x, y, c = here.x, here.y, here.c
@@ -653,16 +866,25 @@
     weight_load.start()
     loads = []
     for k, (cx, cy) in enumerate(chips):
-        load = pltpu.make_async_copy(
-            left_hbm.at[chip_rows(cx, cy, count), :], left_v.at[k], local_sem.at[1 + k]
-        )
-        load.start()
-        loads.append(load)
+        some = chip_rows(cx, cy, count)
+        loads.append(
+            [
+                pltpu.make_async_copy(
+                    left.at[some, :],
+                    left_v.at[k, :, pl.ds(e * depth, depth)],
+                    local_sem.at[1 + experts * k + e],
+                )
+                for e, left in enumerate(lefts)
+            ]
+        )
+        for load in loads[-1]:
+            load.start()
     weight_load.wait()
     to_core = []
 
     def compute(k):
-        loads[k].wait()
+        for load in loads[k]:
+            load.wait()
 
         @pl.loop(0, width // tile)
         def _(n):
@@ -722,24 +944,25 @@
     send.finish()
 
 
-def plane_sum(left, weight, extra, collective_id):
+def plane_sum(lefts, weight, extra, collective_id):
     across = extra is not None
-    count = left.shape[0] // lax.axis_size(plane)
+    count = lefts[0].shape[0] // lax.axis_size(plane)
     width = weight.shape[1] if across else weight.shape[2]
     wide = width + (extra.shape[1] if across else 0)
+    experts, depth = len(lefts), lefts[0].shape[1]
     vmem = pl.BlockSpec(memory_space=pltpu.VMEM)
     anywhere = pl.BlockSpec(memory_space=pl.ANY)
 
     def kernel(*refs):
-        plane_sum_kernel(across, *refs)
+        plane_sum_kernel(across, experts, *refs)
 
     return pl.pallas_call(
         kernel,
         out_shape=jax.ShapeDtypeStruct((count, wide), f32),
-        in_specs=[anywhere] * 2 + [vmem] * across,
+        in_specs=[anywhere] * (experts + 1) + [vmem] * across,
         out_specs=vmem,
         scratch_shapes=[
-            pltpu.VMEM((4, 2 * count, left.shape[1]), bf16),
+            pltpu.VMEM((4, 2 * count, experts * depth), bf16),
             pltpu.VMEM(weight.shape, bf16),
             pltpu.VMEM((4, 2 * count, wide), bf16),
             pltpu.VMEM((4, count, wide), bf16),
@@ -747,17 +970,13 @@
             pltpu.VMEM((2, count, wide), bf16),
             pltpu.SemaphoreType.DMA((8,)),
             pltpu.SemaphoreType.DMA((8,)),
-            pltpu.SemaphoreType.DMA((5,)),
+            pltpu.SemaphoreType.DMA((1 + 4 * experts,)),
         ],
         compiler_params=pltpu.CompilerParams(
             collective_id=collective_id, has_side_effects=True, vmem_limit_bytes=60 * 2**20
         ),
-        cost_estimate=pl.CostEstimate(
-            flops=2 * left.shape[0] * left.shape[1] * width,
-            bytes_accessed=40 * 2**20,
-            transcendentals=0,
-        ),
-    )(*([left, weight] + ([extra] if across else [])))
+        cost_estimate=pl.CostEstimate(flops=10**6, bytes_accessed=10**6, transcendentals=0),
+    )(*lefts, weight, *([extra] if across else []))
 
 
 def head_softmax(queries, keys, visible):
@@ -898,31 +1117,10 @@
             pl.BlockSpec((keys, HEAD_SIZE), lambda i: (0, i)),
             pl.BlockSpec((1, 1, HEAD_SIZE), lambda i: (i, 0, 0)),
         ],
+        cost_estimate=pl.CostEstimate(flops=10**6, bytes_accessed=10**6, transcendentals=0),
         compiler_params=pltpu.CompilerParams(vmem_limit_bytes=48 * 2**20),
     )(
         query_pre, gain.reshape(1, HEAD_SIZE), cosine, sine, kv_all, kv_all, queries, attended_grad
-    )
-
-
-def gather_small(v):
-    if not small_plane():
-        return lax.all_gather(v, plane, axis=0, tiled=True)
-    v = jnp.concatenate([v, over_y(v)], axis=0)
-    v = jnp.concatenate([v, core(v)], axis=0)
-    v = jnp.concatenate([v, over_x(v)], axis=0)
-    blocks = v.reshape(lax.axis_size(plane), -1, v.shape[1])
-    slot = jnp.arange(blocks.shape[0])
-    device = slot // 4 * 4 + slot % 2 * 2 + slot // 2 % 2
-    blocks = jnp.take(blocks, device ^ lax.axis_index(plane), axis=0)
-    return blocks.reshape(v.shape)
-
-
-def halves(v):
-    half = v.shape[1] // 2
-    mine = lax.axis_index("expert") * half
-    return (
-        lax.dynamic_slice_in_dim(v, mine, half, axis=1),
-        lax.dynamic_slice_in_dim(v, half - mine, half, axis=1),
     )
 
 
@@ -974,7 +1172,6 @@
     count_of_rows = hidden_in.shape[0]
     prompt_all = PROMPT_DEV * ctx_count
     hidden_ff = gate_up.shape[2] // 2
-    order = relative()
     member = lax.axis_index("ctx")
     offsets = jnp.arange(count_of_rows, dtype=jnp.int32)
     position = jnp.where(
@@ -983,9 +1180,13 @@
     cosine, rope_sine = angles(position, HEAD_SIZE)
     narrow = KEY_VALUE_HEADS * HEAD_SIZE
     wide = QUERY_HEADS * HEAD_SIZE
-    route_rows = gather_small(routes)
     inputs = hidden_in.astype(f32)
     scale_in = rms_scale(inputs)
+
+    def by_owner(v):
+        v = v.reshape(count_of_rows, dp_count, spread_count, -1)
+        return v.transpose(2, 0, 1, 3).reshape(spread_count, count_of_rows, -1)
+
     signed_sine = rope_sine * jnp.where(jnp.arange(HEAD_SIZE) < HEAD_SIZE // 2, -1.0, 1.0)
     if small_plane():
         (
@@ -993,19 +1194,22 @@
             q_other,
             o_other,
             g_rows,
-            normalized_input,
+            route_rows,
+            kv_all,
+            normed_owned,
+            attended_owned,
             query_pre,
-            key_value_pre,
-            kv_low,
-            kv_blocks,
-        ) = fetch_and_project(
-            hidden_in, attn_gain, key_gain, cosine, signed_sine, key_matrix, value_matrix,
-            query_weight, output_weight, out_grad,
+            key_pre,
+            queries,
+            residual,
+            ffn_in,
+        ) = fetch_and_attend(
+            hidden_in, attn_gain, query_gain, key_gain, ffn_gain, cosine, signed_sine,
+            key_matrix, value_matrix, query_weight, output_weight, out_grad, routes,
         )
         kv_weights = [jnp.concatenate([key_matrix, value_matrix], axis=1), kv_other]
         q_weights = [query_weight, q_other]
         o_weights = [output_weight, o_other]
-        kv_blocks = kv_blocks.reshape(prompt_all, 2 * narrow)
     else:
         full = [
             lax.all_gather(w, "expert", axis=0, tiled=True)
@@ -1017,38 +1221,37 @@
         ]
         kv_weights, q_weights, o_weights = [[w] for w in full]
         g_rows = lax.all_gather(out_grad, plane, axis=0, tiled=True)
+        route_rows = lax.all_gather(routes, plane, axis=0, tiled=True)
         normalized_input = (inputs * scale_in * attn_gain).astype(bf16)
         query_pre = dot(normalized_input, q_weights[0])
         key_value_pre = dot(normalized_input, kv_weights[0])
-        key_pre = key_value_pre[:, :narrow].reshape(count_of_rows, KEY_VALUE_HEADS, HEAD_SIZE)
+        key_pre = key_value_pre[:, :narrow]
+        key_heads = key_pre.reshape(count_of_rows, KEY_VALUE_HEADS, HEAD_SIZE)
         key_low = rotate(
-            key_pre * rms_scale(key_pre) * key_gain, cosine[:, None, :], rope_sine[:, None, :]
+            key_heads * rms_scale(key_heads) * key_gain, cosine[:, None, :], rope_sine[:, None, :]
         ).astype(bf16)
         kv_low = jnp.concatenate(
             [key_low.reshape(count_of_rows, narrow), key_value_pre[:, narrow:].astype(bf16)],
             axis=1,
         )
         kv_blocks = lax.all_gather(kv_low[:PROMPT_DEV], "ctx", axis=0, tiled=True)
-
-    def forward_dot(v, weights):
-        if len(weights) == 1:
-            return dot(v, weights[0])
-        mine, other = halves(v)
-        return dot(mine, weights[0]) + dot(other, weights[1])
+        kv_all = jnp.concatenate([kv_blocks, kv_low[PROMPT_DEV:]], axis=0)
+        queries, attended = attention(query_pre, query_gain, cosine, signed_sine, kv_all)
+        residual = inputs + dot(attended, o_weights[0])
+        ffn_in = (residual * rms_scale(residual) * ffn_gain).astype(bf16)
+        normed_owned = by_owner(normalized_input)
+        attended_owned = by_owner(attended)
+
+    def owned(v):
+        return lax.all_to_all(v, plane, split_axis=0, concat_axis=0, tiled=True)
 
     def backward_dot(v, weights):
         parts = [dot(v, w.T) for w in weights]
         return parts[0] if len(parts) == 1 else join_halves(*parts)
 
-    key_before_norm = key_value_pre[:, :narrow].reshape(
-        count_of_rows, KEY_VALUE_HEADS, HEAD_SIZE
-    )
+    key_before_norm = key_pre.reshape(count_of_rows, KEY_VALUE_HEADS, HEAD_SIZE)
     key_inv = rms_scale(key_before_norm)
-    kv_all = jnp.concatenate([kv_blocks, kv_low[PROMPT_DEV:]], axis=0)
-    queries, attended = attention(query_pre, query_gain, cosine, signed_sine, kv_all)
-    residual = inputs + forward_dot(attended, o_weights)
     scale_ffn = rms_scale(residual)
-    ffn_in = (residual * scale_ffn * ffn_gain).astype(bf16)
 
     expert_count = local_experts * spread_count
     expert_ids = jnp.arange(expert_count, dtype=jnp.int32)
@@ -1062,11 +1265,34 @@
         )
         return raised / jnp.sum(raised, axis=-1, keepdims=True)
 
+    def reduce_expert(which, rows, hidden, grads, g_rows):
+        down_part = dot(hidden.T, g_rows).astype(bf16)
+        gate_up_part = dot(rows.T, grads).astype(bf16)
+        return (
+            lax.psum_scatter(down_part, "dp", scatter_dimension=0, tiled=True),
+            lax.psum_scatter(gate_up_part, "dp", scatter_dimension=0, tiled=True),
+            down_part,
+            gate_up_part,
+        )
+
     gates = gates_of(ffn_in, routes)
     if small_plane():
-        rows, hidden_low, projected_grad, gate_grads = experts_of_plane(
+        rows, hidden, grads, gates_mine, totals = gather_first_expert(
             ffn_in, route_rows, router_weight, g_rows, gate_up, down_proj
         )
+        hiddens, projected_grads = [hidden], [grads]
+        sums = [reduce_expert(0, rows, hidden, grads, g_rows)]
+        rows = after(rows, *sums[0][2:])
+        attended_owned, normed_owned = [
+            owned(after(v, *sums[0][2:])) for v in (attended_owned, normed_owned)
+        ]
+        for which in range(1, local_experts):
+            hidden, grads, gate_grads = last_expert(
+                which, expert_count, rows, g_rows, gates_mine, totals, gate_up, down_proj
+            )
+            hiddens.append(hidden)
+            projected_grads.append(grads)
+            sums.append(reduce_expert(which, rows, hidden, grads, g_rows))
     else:
         rows = lax.all_gather(ffn_in, plane, axis=0, tiled=True)
         first_expert = lax.axis_index(plane) * local_experts
@@ -1088,40 +1314,32 @@
             gate_back = back * up_part * sigmoid_gate * (1.0 + gate_part * (1.0 - sigmoid_gate))
             up_back = back * gate_part * sigmoid_gate
             projected_grads.append(jnp.concatenate([gate_back, up_back], axis=-1).astype(bf16))
-        hidden_low = jnp.concatenate(hiddens, axis=1)
-        projected_grad = jnp.concatenate(projected_grads, axis=1)
-    down_local = dot(hidden_low.T, g_rows).astype(bf16)
-    gate_up_local = dot(rows.T, projected_grad).astype(bf16)
-    down_low = lax.psum_scatter(
-        down_local.reshape(down_proj.shape), "dp", scatter_dimension=1, tiled=True
-    )
-    gate_up_low = lax.psum_scatter(gate_up_local, "dp", scatter_dimension=0, tiled=True)
-    down_grad = down_low.astype(f32)
-    gate_up_grad = jnp.stack(
-        [
-            gate_up_low[:, i * 2 * hidden_ff : (i + 1) * 2 * hidden_ff].astype(f32)
-            for i in range(local_experts)
+        attended_owned, normed_owned = owned(attended_owned), owned(normed_owned)
+        sums = [
+            reduce_expert(i, rows, hidden, grads, g_rows)
+            for i, (hidden, grads) in enumerate(zip(hiddens, projected_grads))
         ]
-    )
-    projected_grad, hidden_low = lax.optimization_barrier(
-        ((projected_grad, hidden_low), gate_up_local, down_local)
+    down_low = [v[0] for v in sums]
+    gate_up_low = [v[1] for v in sums]
+    down_grad = jnp.stack([v.astype(f32) for v in down_low])
+    gate_up_grad = jnp.stack([v.astype(f32) for v in gate_up_low])
+    projected_grads, hiddens = lax.optimization_barrier(
+        ((projected_grads, hiddens), [v[2:] for v in sums], attended_owned, normed_owned)
     )[0]
     if small_plane():
-        back = plane_sum(projected_grad, gate_up, gate_grads, 3)
+        back = plane_sum(projected_grads, gate_up, gate_grads, 3)
         back_sum = back[:, :MODEL_WIDTH]
         gate_grad = (
             back[:, MODEL_WIDTH : MODEL_WIDTH + expert_count]
             + back[:, MODEL_WIDTH + expert_count : MODEL_WIDTH + 2 * expert_count]
         )
-        moe_sum = plane_sum(after(hidden_low, back), down_proj, None, 4)
+        moe_sum = None
     else:
         moe_part = 0.0
         row_part = 0.0
         for which in range(local_experts):
-            grads = projected_grad[:, which * 2 * hidden_ff : (which + 1) * 2 * hidden_ff]
-            hidden = hidden_low[:, which * hidden_ff : (which + 1) * hidden_ff]
-            row_part = row_part + dot(grads, gate_up[which].T)
-            moe_part = moe_part + dot(hidden, down_proj[which])
+            row_part = row_part + dot(projected_grads[which], gate_up[which].T)
+            moe_part = moe_part + dot(hiddens[which], down_proj[which])
         moe_sum, back_sum = [
             lax.psum_scatter(v.astype(bf16), plane, scatter_dimension=0, tiled=True).astype(f32)
             for v in (moe_part, row_part)
@@ -1134,7 +1352,6 @@
             tiled=True,
         )
         gate_grad = gate_grad.transpose(1, 0, 2).reshape(count_of_rows, expert_count)
-    block_out = (residual + moe_sum).astype(bf16)
     logit_grad = gates * (gate_grad - jnp.sum(gates * gate_grad, axis=-1, keepdims=True))
 
     grad_out = out_grad.astype(f32)
@@ -1145,7 +1362,6 @@
     residual_grad = grad_out + norm_back(residual, scale_ffn, ffn_gain, ffn_in_grad)
     ffn_gain_local = jnp.sum(ffn_in_grad * residual * scale_ffn, axis=0)
     branch_low = residual_grad.astype(bf16)
-    branch_rows = jnp.concatenate(gather_plane(branch_low), axis=0)
     attended_grad = backward_dot(branch_low, o_weights).astype(bf16)
     query_pre_grad, key_grad_all, value_grad_all, query_gain_parts = attention_back(
         query_pre, query_gain, cosine, signed_sine, kv_all, queries, attended_grad
@@ -1165,39 +1381,38 @@
         .reshape(count_of_rows, KEY_VALUE_HEADS * HEAD_SIZE)
     )
     key_value_grad = jnp.concatenate([key_pre_grad, value_gradient.astype(bf16)], axis=1)
+    if small_plane():
+        output_local, pre_local = weight_grads(
+            query_pre_grad, key_value_grad, branch_low, attended_owned, normed_owned
+        )
+    else:
+        branch_rows = lax.all_gather(branch_low, plane, axis=0, tiled=True)
+        pre_rows = lax.all_gather(
+            jnp.concatenate([query_pre_grad, key_value_grad], axis=1), plane, axis=0, tiled=True
+        )
+        attended_owned, normed_owned = [
+            v.reshape(spread_count * count_of_rows, -1) for v in (attended_owned, normed_owned)
+        ]
+        output_local = dot(attended_owned.T, branch_rows).astype(bf16)
+        pre_local = dot(normed_owned.T, pre_rows).astype(bf16)
+    query_pre_grad, key_value_grad = lax.optimization_barrier(
+        ((query_pre_grad, key_value_grad), pre_local)
+    )[0]
     normed_grad = backward_dot(query_pre_grad, q_weights) + backward_dot(
         key_value_grad, kv_weights
     )
     attn_gain_local = jnp.sum(normed_grad * inputs * scale_in, axis=0)
     hidden_grad = residual_grad + norm_back(inputs, scale_in, attn_gain, normed_grad)
-
-    pre_rows = jnp.concatenate(
-        gather_plane(
-            jnp.concatenate([query_pre_grad, key_value_grad], axis=1)
-        ),
-        axis=0,
-    )
-
-    def owned(v):
-        width = v.shape[1] // device_count
-        split = v.reshape(count_of_rows, dp_count, spread_count, width)
-        parts = [
-            lax.dynamic_index_in_dim(split, o, axis=2, keepdims=False).reshape(
-                count_of_rows, dp_count * width
-            )
-            for o in order
-        ]
-        return jnp.concatenate(exchange_plane(parts), axis=0)
-
-    normed_owned = owned(after(normalized_input, rows))
-    attended_owned = owned(after(attended, rows))
-    pre_local = jnp.dot(normed_owned.T, pre_rows, preferred_element_type=f32)
-    output_local = jnp.dot(attended_owned.T, branch_rows, preferred_element_type=f32)
-    pre_local, output_local = lax.optimization_barrier(
-        ((pre_local.astype(bf16), output_local.astype(bf16)), gate_up_low, down_low)
+    if small_plane():
+        moe_sum = plane_sum(after(hiddens, pre_local), down_proj, None, 4)
+    block_out = (residual + moe_sum).astype(bf16)
+    output_local, pre_local = lax.optimization_barrier(
+        ((output_local, pre_local), gate_up_low, down_low)
     )[0]
-    output_sum = lax.psum_scatter(output_local, "dp", scatter_dimension=0, tiled=True).astype(f32)
-    pre_sum = lax.psum_scatter(pre_local, "dp", scatter_dimension=0, tiled=True).astype(f32)
+    output_sum, pre_sum = [
+        lax.psum_scatter(v, "dp", scatter_dimension=0, tiled=True).astype(f32)
+        for v in (output_local, pre_local)
+    ]
 
     small = jnp.concatenate(
         [

time: 773 us -> 683 us (0.88)
  Pallas kernels: 336 us -> 437 us
  local copies, waits for them, and re-layouts: 97.4 us -> 24.9 us
  waiting for transfers between devices: 144 us -> 79.1 us
  matrix products: 104 us -> 77.4 us
  starting transfers between devices: 33.7 us -> 13.8 us
    pallas_call x3 -> x4, Pallas kernels: 211 us -> 310 us  [the longest x1 132 us: fetch_and_attend(): pl.pallas_call(fetch_kernel, out_shape=[jax.ShapeDtypeStruct((half, 2 * n...]
    ppermute x24 -> x3, waiting for transfers between devices: 66 us -> 7.46 us  [swap(): lax.ppermute(v, axis, [(i, i ^ bit) for i in range(lax.axis_size(axis))])]
    unnamed x150 -> x98, local copies, waits for them, and re-layouts: 52.4 us -> 10 us
    all_to_all x0 -> x2, waiting for transfers between devices: none -> 29.5 us  [owned(): return lax.all_to_all(v, plane, split_axis=0, concat_axis=0, tiled=True)]
    ppermute x14 -> x0, waiting for transfers between devices: 22.2 us -> none  [exchange_plane(): out.append(lax.ppermute(blocks[r], plane, pairs))]
    dot_general x2 -> x0, matrix products: 19.1 us -> none  [the longest x1 11.6 us: body(): pre_local = jnp.dot(normed_owned.T, pre_rows, preferred_element_type=f32)]
    ppermute x14 -> x0, starting transfers between devices: 13.7 us -> none  [exchange_plane(): out.append(lax.ppermute(blocks[r], plane, pairs))]
    ppermute x24 -> x3, starting transfers between devices: 14.5 us -> 1.11 us  [swap(): lax.ppermute(v, axis, [(i, i ^ bit) for i in range(lax.axis_size(axis))])]
  transfers between devices with their start and end apart: 43 -> 12, of which waited for: 16 -> 6; matrix products, arithmetic and copies ran while one was open for 26% -> 16% of each run, Pallas kernels for 35% -> 37%
where the time goes in v4:
time: 683 us; the launch traced here: 674 us
  Pallas kernels  437 us (64%)
  waiting for transfers between devices  79.1 us (12%)
  matrix products  77.4 us (11%)
  other arithmetic  26.7 us (4%)
  local copies, waits for them, and re-layouts  24.9 us (4%)
  between operations  15.5 us (2%)
  starting transfers between devices  13.8 us (2%)
    pallas_call x1, Pallas kernels, fetch_and_attend(): pl.pallas_call(fetch_kernel, out_shape=[jax.ShapeDtypeStruct((half, 2 * n...  132 us
    pallas_call x1, Pallas kernels, weight_grads(): pl.pallas_call(weight_grad_kernel, out_shape=[jax.ShapeDtypeStruct((atten...  99.1 us
    pallas_call x2, Pallas kernels, plane_sum(): pl.pallas_call(kernel, out_shape=jax.ShapeDtypeStruct((count, wide), f32)...  96.6 us
    dot_general x11, matrix products, dot(): return jnp.dot(a, b, preferred_element_type=f32)  72.7 us
    pallas_call x1, Pallas kernels, gather_first_expert(): pl.pallas_call(first_expert_kernel, out_shape=[jax.ShapeDtypeStruct((tota...  55.4 us
    pallas_call x1, Pallas kernels, attention_back(): pl.pallas_call(attention_back_kernel, grid=(KEY_VALUE_HEADS,), out_shape=...  29.8 us
    all_to_all x2, waiting for transfers between devices, owned(): return lax.all_to_all(v, plane, split_axis=0, concat_axis=0, tiled=True)  29.5 us
    reduce_scatter x2, waiting for transfers between devices, reduce_expert(): lax.psum_scatter(gate_up_part, 'dp', scatter_dimension=0, tiled=True)  23.8 us
  transfers between devices with their start and end apart: 12, of which 6 were waited for; matrix products, arithmetic and copies ran while one was open for 16% of the time, Pallas kernels for 37%

profile of v4, /device:TPU:0, one launch (start us, length us, event | category | flops | bytes accessed | tf_op | source)
XLA Modules:
  0.0 674.0 jit_solution(10925345667441415082)
XLA Ops:
  7.3 1.5 copy.63.routes_ref
  8.7 1.8 copy.64.router_ref
  10.7 1.1 fusion.21
  11.8 132.2 %shard_map.237 = (bf16[1024,1024]{1,0:T(8,128)(2,1)}, bf16[1024,4096]{1,0:T(8,128)(2,1)}, bf16[2048,2048]{1,0:T(8,128)(2,1)}, bf16[1536,2048]{1,0:T(8,128)(2,1)}...) custom-call(bf16[192,2048]{1,0:T(8,128)(2,1)} %hidden_ref.1, ...), custom_call_target="tpu_custom_call" | custom-call | flops 14495514624 | bytes 62914560 | tf_op jit(solution)/shard_map/pallas_call | solution.py:481
  144.0 55.4 %shard_map.238 = (bf16[1536,2048]{1,0:T(8,128)(2,1)}, bf16[1536,768]{1,0:T(8,128)(2,1)}, bf16[1536,1536]{1,0:T(8,128)(2,1)}, f32[1536,128]{1,0:T(8,128)}, f32[1536,128]{1,0:T(8,128)}) custom-call(bf16[192,2048]{1,0:T(8,128)(2,1)} %get-tuple-element.54.ffn_ref, s32[1536,8]{1,0:T(8,128)} %get-tuple-element.55.routes_ref, bf16[2048,16]{1,0:T(8,128)(2,1)} %copy.64.router_ref, ...), custom_call_target="tpu_custom_call" | custom-call | flops 14495514624 | bytes 41943040 | tf_op jit(solution)/shard_map/pallas_call | solution.py:663
  199.5 8.2 %convolution_convert_fusion.3 = bf16[768,2048]{1,0:T(8,128)(2,1)} fusion(bf16[1536,768]{1,0:T(8,128)(2,1)} %get-tuple-element.83.refs_0_, bf16[1536,2048]{1,0:T(8,128)(2,1)S(1)} %copy-done.12), kind=kOutput, calls=%fused_computation.3 | convolution fusion | flops 4833411072 | bytes 11796480 | tf_op jit(solution)/shard_map/dot_general | solution.py:1135
  207.7 15.3 %convolution_convert_fusion.1 = bf16[2048,1536]{1,0:T(8,128)(2,1)} fusion(bf16[1536,2048]{1,0:T(8,128)(2,1)} %get-tuple-element.60.refs_0_, bf16[1536,1536]{1,0:T(8,128)(2,1)} %get-tuple-element.74.refs_0_), kind=kOutput, calls=%fused_computation.1 | convolution fusion | flops 9666822144 | bytes 17301504 | tf_op jit(solution)/shard_map/dot_general | solution.py:1135
  223.0 23.3 %shard_map.239 = (bf16[1536,768]{1,0:T(8,128)(2,1)}, bf16[1536,1536]{1,0:T(8,128)(2,1)}, bf16[1536,128]{1,0:T(8,128)(2,1)}) custom-call(bf16[1536,2048]{1,0:T(8,128)(2,1)} %get-tuple-element.60.refs_0_, bf16[1536,2048]{1,0:T(8,128)(2,1)} %get-tuple-element.56.g_hbm.refs_1_, f32[1536,128]{1,0:T(8,128)} %get-tuple-element.61.refs_2_, ...), custom_call_target="tpu_custom_call" | custom-call | flops 1000000 | bytes 1000000 | tf_op jit(solution)/shard_map/pallas_call | solution.py:729
  246.3 9.1 %convolution_convert_fusion.2 = bf16[768,2048]{1,0:T(8,128)(2,1)} fusion(bf16[1536,768]{1,0:T(8,128)(2,1)} %get-tuple-element.84.refs_1_, bf16[1536,2048]{1,0:T(8,128)(2,1)} %get-tuple-element.56.g_hbm.refs_1_), kind=kOutput, calls=%fused_computation.2 | convolution fusion | flops 4833411072 | bytes 11796480 | tf_op jit(solution)/shard_map/dot_general | solution.py:1135
  255.5 0.7 reduce-scatter.7.cloned.1.call-update
  256.2 15.5 %convolution_convert_fusion = bf16[2048,1536]{1,0:T(8,128)(2,1)} fusion(bf16[1536,2048]{1,0:T(8,128)(2,1)} %get-tuple-element.60.refs_0_, bf16[1536,1536]{1,0:T(8,128)(2,1)} %get-tuple-element.75.refs_1_), kind=kOutput, calls=%fused_computation | convolution fusion | flops 9666822144 | bytes 17301504 | tf_op jit(solution)/shard_map/dot_general | solution.py:1135
  271.7 3.6 all-to-all-start.1
  275.3 11.6 %all-to-all-done.1.normed_owned = bf16[8,192,256]{2,1,0:T(8,128)(2,1)S(1)} async-done(((bf16[8,192,256]{2,1,0:T(8,128)(2,1)}), bf16[8,192,256]{2,1,0:T(8,128)(2,1)S(1)}, u32[]{:S(2)}, u32[]{:S(2)}) %all-to-all-start.1) | async-done | bytes 786464 | tf_op jit(solution)/shard_map/all_to_all | solution.py:1246
  286.9 0.9 copy-done.17
  287.8 3.6 all-to-all-start
  291.6 1.6 fusion.32
  293.6 17.9 %all-to-all-done.attended_owned = bf16[8,192,512]{2,1,0:T(8,128)(2,1)S(1)} async-done(((bf16[8,192,512]{2,1,0:T(8,128)(2,1)}), bf16[8,192,512]{2,1,0:T(8,128)(2,1)S(1)}, u32[]{:S(2)}, u32[]{:S(2)}) %all-to-all-start) | async-done | bytes 1572896 | tf_op jit(solution)/shard_map/all_to_all | solution.py:1246
  311.5 53.3 %shard_map.240 = f32[192,2176]{1,0:T(8,128)} custom-call(bf16[1536,1536]{1,0:T(8,128)(2,1)} %get-tuple-element.74.refs_0_, bf16[1536,1536]{1,0:T(8,128)(2,1)} %get-tuple-element.75.refs_1_, bf16[2,2048,1536]{2,1,0:T(8,128)(2,1)} %refs_2_.2, bf16[1536,128]{1,0:T(8,128)(2,1)} %get-tuple-element.76.refs_3_), custom_call_target="tpu_custom_call" | custom-call | flops 1000000 | bytes 1000000 | tf_op jit(solution)/shard_map/pallas_call | solution.py:959
  364.9 1.2 multiply_reduce_fusion.5
  366.1 2.9 multiply_reduce_fusion
  369.0 1.7 fusion.27
  370.7 6.7 fusion.34
  377.5 2.9 select_convert_fusion.1
  380.4 1.3 pad_maximum_fusion.grad_ref
  382.2 29.8 %shard_map.241 = (bf16[192,4096]{1,0:T(8,128)(2,1)S(1)}, f32[576,512]{1,0:T(8,128)S(1)}, f32[576,512]{1,0:T(8,128)S(1)}, f32[4,1,128]{2,1,0:T(1,128)S(1)}) custom-call(f32[192,4096]{1,0:T(8,128)} %get-tuple-element.71.query_pre_ref, f32[1,128]{1,0:T(1,128)S(1)} %bitcast.81, f32[192,128]{1,0:T(8,128)S(1)} %copy-done.3, f32[192,128]{1,0:T(8,128)S(1)} %copy-done.4, ...), custom_call_target="tpu_custom_call" | custom-call | flops 1000000 | bytes 1000000 | tf_op jit(solution)/shard_map/pallas_call | solution.py:1095
  412.2 1.0 copy-done
  413.2 0.8 copy-done.7
  414.0 0.8 fusion.17
  415.4 1.4 collective-permute-done.1
  416.8 1.7 add_convert_fusion.1
  419.1 1.9 reshape.220
  421.1 6.1 collective-permute-done.2
  427.2 1.2 convert_add_fusion
  428.6 0.7 copy-done.28
  429.7 1.2 multiply_reduce_fusion.4
  430.9 1.0 copy.68
  431.9 0.8 copy.69
  432.7 0.8 copy.70
  433.5 1.2 mul.262
  435.3 0.9 fusion.14
  436.2 0.8 maximum_maximum_fusion.kv_grad
  437.0 99.1 %shard_map.242 = (bf16[512,2048]{1,0:T(8,128)(2,1)}, bf16[256,5120]{1,0:T(8,128)(2,1)}) custom-call(bf16[192,4096]{1,0:T(8,128)(2,1)} %copy-done, bf16[192,1024]{1,0:T(8,128)(2,1)} %maximum_maximum_fusion.kv_grad, bf16[192,2048]{1,0:T(8,128)(2,1)} %copy-done.14, bf16[8,192,512]{2,1,0:T(8,128)(2,1)} %copy-done.11, bf16[8,192,256]{2,1,0:T(8,128)(2,1)} %copy-done.17), custom_call_target="tpu_custom_call" | custom-call | flops 1000000 | bytes 1000000 | tf_op jit(solution)/shard_map/pallas_call | solution.py:815
  536.3 23.8 %reduce-scatter.9.cloned.1.call-done = bf16[512,1536]{1,0:T(8,128)(2,1)} async-done(((bf16[2048,1536]{1,0:T(8,128)(2,1)}), bf16[512,1536]{1,0:T(8,128)(2,1)}) %reduce-scatter.9.cloned.1.call-update) | async-done | bytes 1572880 | tf_op jit(solution)/shard_map/reduce_scatter | solution.py:1273
  561.3 0.7 reshape.222
  562.0 0.7 reshape.223
  562.7 1.8 fusion.33
  565.1 2.7 fusion.36
  567.9 0.8 broadcast_select_fusion.1
  568.7 0.8 copy-done.1
  569.6 7.1 %fusion.35 = f32[192,1024]{1,0:T(8,128)S(1)} fusion(bf16[192,4096]{1,0:T(8,128)(2,1)S(1)} %copy-done.1, bf16[1024,4096]{1,0:T(8,128)(2,1)} %get-tuple-element.86), kind=kOutput, calls=%fused_computation.110 | convolution fusion | flops 1610612736 | bytes 10747904 | tf_op jit(solution)/shard_map/dot_general | solution.py:1135
  576.7 2.9 broadcast_select_fusion.3
  580.8 0.8 copy.74
  581.6 5.3 all-to-all-start.2
  587.0 43.3 %shard_map.243 = f32[192,2048]{1,0:T(8,128)} custom-call(bf16[1536,768]{1,0:T(8,128)(2,1)} %get-tuple-element.83.refs_0_, bf16[1536,768]{1,0:T(8,128)(2,1)} %get-tuple-element.84.refs_1_, bf16[2,768,2048]{2,1,0:T(8,128)(2,1)} %refs_2_.3), custom_call_target="tpu_custom_call" | custom-call | flops 1000000 | bytes 1000000 | tf_op jit(solution)/shard_map/pallas_call | solution.py:959
  630.3 3.9 fusion.7
  634.3 1.1 add_convert_fusion
  635.6 0.7 copy.75
  637.5 1.9 maximum_convert_fusion.1
  639.5 1.0 copy-done.20
  640.5 3.1 maximum_convert_fusion
  643.6 2.1 convert_element_type.84
  645.7 17.3 %reduce-scatter.15.cloned.1.call-done = bf16[64,5120]{1,0:T(8,128)(2,1)} async-done(((bf16[256,5120]{1,0:T(8,128)(2,1)}), bf16[64,5120]{1,0:T(8,128)(2,1)}) %reduce-scatter.15.cloned.1.call-update) | async-done | bytes 655376 | tf_op jit(solution)/shard_map/reduce_scatter | solution.py:1413
  663.0 2.1 slice.88
  665.1 1.6 fusion.28
  (154 shorter events, 8.6 us)
Async XLA Ops:
  7.2 529.0 %reduce-scatter.11.cloned.1.call-start = ((), (), s32[]{:S(2)}) async-start(), calls=%async_computation.11 | async-start | bytes 3932160 | tf_op jit(solution)/shard_map/reduce_scatter | solution.py:1272
  144.0 55.4 %copy-start.12 = (bf16[1536,2048]{1,0:T(8,128)(2,1)S(1)}, bf16[1536,2048]{1,0:T(8,128)(2,1)}, u32[]{:S(2)}) copy-start(bf16[1536,2048]{1,0:T(8,128)(2,1)} %get-tuple-element.56.g_hbm.refs_1_) | copy-start | bytes 18874372
  207.7 328.5 %reduce-scatter.13.cloned.1.call-start = ((), (), s32[]{:S(2)}) async-start(), calls=%async_computation.12 | async-start | bytes 3932160 | tf_op jit(solution)/shard_map/reduce_scatter | solution.py:1272
  255.4 280.9 %reduce-scatter.7.cloned.1.call-start = ((), (), s32[]{:S(2)}) async-start(), calls=%async_computation.9 | async-start | bytes 7864320 | tf_op jit(solution)/shard_map/reduce_scatter | solution.py:1273
  256.1 303.9 %reduce-scatter.9.cloned.1.call-start = ((), (), s32[]{:S(2)}) async-start(), calls=%async_computation.10 | async-start | bytes 7864320 | tf_op jit(solution)/shard_map/reduce_scatter | solution.py:1273
  271.7 15.2 %all-to-all-start.1 = ((bf16[8,192,256]{2,1,0:T(8,128)(2,1)}), bf16[8,192,256]{2,1,0:T(8,128)(2,1)S(1)}, u32[]{:S(2)}, u32[]{:S(2)}) async-start(bf16[8,192,256]{2,1,0:T(8,128)(2,1)} %get-tuple-element.68), calls=%async_computation.1 | async-start | bytes 1572864 | tf_op jit(solution)/shard_map/all_to_all | solution.py:1246
  275.3 16.2 %copy-start.34 = (s32[192,8]{0,1:T(8,128)S(1)}, s32[192,8]{0,1:T(8,128)}, u32[]{:S(2)}) copy-start(s32[192,8]{0,1:T(8,128)} %param.26) | copy-start | bytes 18436
  275.3 16.4 %copy-start.30 = (bf16[2048,16]{0,1:T(8,128)(2,1)S(1)}, bf16[2048,16]{0,1:T(8,128)(2,1)}, u32[]{:S(2)}) copy-start(bf16[2048,16]{0,1:T(8,128)(2,1)} %param.23) | copy-start | bytes 196612
  275.3 18.1 %copy-start.6 = (f32[192,2048]{1,0:T(8,128)S(1)}, f32[192,2048]{1,0:T(8,128)}, u32[]{:S(2)}) copy-start(f32[192,2048]{1,0:T(8,128)} %get-tuple-element.53) | copy-start | bytes 4718596
  286.9 0.9 copy-start.17
  287.8 23.7 %all-to-all-start = ((bf16[8,192,512]{2,1,0:T(8,128)(2,1)}), bf16[8,192,512]{2,1,0:T(8,128)(2,1)S(1)}, u32[]{:S(2)}, u32[]{:S(2)}) async-start(bf16[8,192,512]{2,1,0:T(8,128)(2,1)} %get-tuple-element.66), calls=%async_computation | async-start | bytes 3145728 | tf_op jit(solution)/shard_map/all_to_all | solution.py:1246
  291.4 352.2 %reduce-scatter.17.cloned.1.call-start = ((), (), s32[]{:S(2)}) async-start(), calls=%async_computation.14 | async-start | bytes 2621440 | tf_op jit(solution)/shard_map/reduce_scatter | solution.py:1413
  293.2 72.9 %copy-start.23 = (f32[192,16]{1,0:T(8,128)}, f32[192,16]{1,0:T(8,128)S(1)}, u32[]{:S(2)}) copy-start(f32[192,16]{1,0:T(8,128)S(1)} %get-tuple-element.197) | copy-start | bytes 36868
  311.5 53.4 %copy-start.11 = (bf16[8,192,512]{2,1,0:T(8,128)(2,1)}, bf16[8,192,512]{2,1,0:T(8,128)(2,1)S(1)}, u32[]{:S(2)}) copy-start(bf16[8,192,512]{2,1,0:T(8,128)(2,1)S(1)} %all-to-all-done.attended_owned) | copy-start | bytes 4718596
  311.5 54.6 %copy-start.35 = (f32[2048]{0:T(1024)S(1)}, f32[2048]{0:T(1024)}, u32[]{:S(2)}) copy-start(f32[2048]{0:T(1024)} %param.22) | copy-start | bytes 24580
  366.1 2.9 copy-start.37
  366.1 2.9 copy-start.25
  369.0 8.5 %slice-start.3 = ((s8[8388608]{0:T(1024)(128)(4,1)}), s8[4194304]{0:T(1024)(128)(4,1)S(1)}, s32[]{:S(2)}) async-start(s8[8388608]{0:T(1024)(128)(4,1)} %bitcast.97), calls=%async_computation.18 | async-start | bytes 8388608
  370.7 6.7 %copy-start.14 = (bf16[192,2048]{1,0:T(8,128)(2,1)}, bf16[192,2048]{1,0:T(8,128)(2,1)S(1)}, u32[]{:S(2)}) copy-start(bf16[192,2048]{1,0:T(8,128)(2,1)S(1)} %get-tuple-element.165.branch) | copy-start | bytes 2359300
  370.7 6.8 %slice-start.4 = ((s8[8388608]{0:T(1024)(128)(4,1)}), s8[4194304]{0:T(1024)(128)(4,1)S(1)}, s32[]{:S(2)}) async-start(s8[8388608]{0:T(1024)(128)(4,1)} %bitcast.97), calls=%async_computation.19 | async-start | bytes 8388608
  380.4 1.6 copy-start.2
  380.4 1.6 copy-start.3
  380.4 1.7 copy-start.4
  380.4 1.7 copy-start.5
  412.0 1.2 copy-start
  412.1 2.8 copy-start.18
  413.2 0.8 copy-start.7
  414.9 6.1 copy-start.39
  414.9 1.9 collective-permute-start.1
  414.9 6.2 collective-permute-start
  418.5 8.7 %collective-permute-start.2 = (bf16[2,128,512]{2,1,0:T(8,128)(2,1)}, bf16[2,128,512]{2,1,0:T(8,128)(2,1)}, u32[]{:S(2)}, u32[]{:S(2)}) collective-permute-start(bf16[2,128,512]{2,1,0:T(8,128)(2,1)} %add_convert_fusion.1), channel_id=1, source_target_pairs={{0,4},{2,6},{4,0},{6,2},{1,5},{3,7},{5,1},{7,3},{8,12},{10,14},{12... | collective-permute-start | bytes 786440 | tf_op jit(solution)/shard_map/ppermute | solution.py:66
  428.3 0.9 copy-start.28
  428.5 1.1 copy-start.21
  428.5 1.1 copy-start.40
  430.9 4.4 copy-start.22
  433.4 1.6 copy-start.29
  435.3 1.0 slice-start.2
  536.2 24.0 %copy-start.8 = (bf16[192,2048]{1,0:T(8,128)(2,1)S(1)}, bf16[192,2048]{1,0:T(8,128)(2,1)}, u32[]{:S(2)}) copy-start(bf16[192,2048]{1,0:T(8,128)(2,1)} %hidden_ref.1) | copy-start | bytes 2359300
  560.1 2.6 copy-start.24
  560.1 102.9 %reduce-scatter.15.cloned.1.call-start = ((), (), s32[]{:S(2)}) async-start(), calls=%async_computation.13 | async-start | bytes 3276800 | tf_op jit(solution)/shard_map/reduce_scatter | solution.py:1413
  565.1 2.7 copy-start.13
  565.1 2.7 copy-start.41
  565.1 2.7 copy-start.42
  567.8 1.7 copy-start.1
  567.9 8.8 %slice-start = ((s8[8388608]{0:T(1024)(128)(4,1)}), s8[4194304]{0:T(1024)(128)(4,1)S(1)}, s32[]{:S(2)}) async-start(s8[8388608]{0:T(1024)(128)(4,1)} %bitcast.82), calls=%async_computation.15 | async-start | bytes 8388608
  568.7 10.9 %copy-start.15 = (f32[192,1024]{1,0:T(8,128)}, f32[192,1024]{1,0:T(8,128)S(1)}, u32[]{:S(2)}) copy-start(f32[192,1024]{1,0:T(8,128)S(1)} %get-tuple-element.171) | copy-start | bytes 2359300
  568.7 10.9 %copy-start.16 = (f32[192,1024]{1,0:T(8,128)}, f32[192,1024]{1,0:T(8,128)S(1)}, u32[]{:S(2)}) copy-start(f32[192,1024]{1,0:T(8,128)S(1)} %get-tuple-element.172) | copy-start | bytes 2359300
  569.6 7.1 %slice-start.1 = ((s8[8388608]{0:T(1024)(128)(4,1)}), s8[4194304]{0:T(1024)(128)(4,1)S(1)}, s32[]{:S(2)}) async-start(s8[8388608]{0:T(1024)(128)(4,1)} %bitcast.82), calls=%async_computation.16 | async-start | bytes 8388608
  576.7 2.9 copy-start.33
  579.6 0.9 copy-start.9
  579.6 0.9 copy-start.36
  579.6 1.0 copy-start.31
  579.6 1.0 copy-start.32
  581.6 53.7 %all-to-all-start.2 = ((f32[32,1,1160]{2,1,0:T(1,128)}), f32[32,1,1160]{2,1,0:T(1,128)S(1)}, u32[]{:S(2)}, u32[]{:S(2)}) async-start(f32[32,1,1160]{2,1,0:T(1,128)} %copy.74), calls=%async_computation.2 | async-start | bytes 327680 | tf_op jit(solution)/shard_map/all_to_all | solution.py:1430
  587.0 43.3 %copy-start.38 = (f32[192]{0:T(256)S(1)}, f32[192]{0:T(256)}, u32[]{:S(2)}) copy-start(f32[192]{0:T(256)} %get-tuple-element.192) | copy-start | bytes 2308
  630.3 3.9 copy-start.10
  634.3 3.2 copy-start.26
  634.3 3.2 copy-start.27
  637.5 2.0 copy-start.19
  637.5 3.0 copy-start.20
Sparse Core Ops, SparseCore 0:
  207.8 61.8 reduce-scatter.10
  272.6 60.2 reduce-scatter.12
  335.2 110.7 reduce-scatter.6
  448.8 111.2 reduce-scatter.8
  562.2 47.0 reduce-scatter.16
  611.6 51.3 reduce-scatter.14

commit v5 on v4

--- a/solution.py
+++ b/solution.py
@@ -452,10 +452,10 @@
         block_gather(here, send, routes_ref, local_sem.at[10], route_blocks)[0],
     ]
     steps = [
-        kv[0], start, kv[1], qa[0], kv[2], own_part, qa[1], qb[0],
-        kv[3], qa[2], qb[1], oa[0], kv[4], keys_part, qa[3], qb[2], oa[1], ob[0],
+        kv[0], qa[0], qb[0], oa[0], ob[0], g[0], start, kv[1], kv[2], own_part, qa[1],
+        kv[3], qa[2], qb[1], kv[4], keys_part, qa[3], qb[2], oa[1],
         keys_forward, qa[4], queries_first, qb[3], ob[1], qb[4], queries_rest,
-        oa[2], g[0], r[0], lambda: attend(0), lambda: attend(1),
+        oa[2], r[0], lambda: attend(0), lambda: attend(1),
         oa[3], ob[2], g[1], r[1], lambda: attend(2), lambda: attend(3), oa[4], output_own,
         ob[3], g[2], r[2], ob[4], finish_rows, g[3], r[3],
     ]
@@ -629,8 +629,9 @@
         )
         gate_grad_ref[some, :] = total_v[...]
         for source, target in ((hidden_v, hidden_out), (grad_v, grad_out), (rows_v, rows_out)):
+            columns = pl.ds(0, source.shape[1])
             store = pltpu.make_async_copy(
-                source.at[some, :], target.at[some, :], local_sem.at[4 + len(stores)]
+                source.at[some, :], target.at[some, columns], local_sem.at[4 + len(stores)]
             )
             store.start()
             stores.append(store)
@@ -656,7 +657,7 @@
 
 
 def gather_first_expert(ffn_in, route_rows, router_weight, g_rows, gate_up, down_proj):
-    ff, width = down_proj.shape[1:]
+    experts, ff, width = down_proj.shape
     total = route_rows.shape[0]
     vmem = pl.BlockSpec(memory_space=pltpu.VMEM)
     anywhere = pl.BlockSpec(memory_space=pl.ANY)
@@ -665,7 +666,7 @@
         out_shape=[
             jax.ShapeDtypeStruct((total, width), bf16),
             jax.ShapeDtypeStruct((total, ff), bf16),
-            jax.ShapeDtypeStruct((total, 2 * ff), bf16),
+            jax.ShapeDtypeStruct((total, 2 * experts * ff), bf16),
             jax.ShapeDtypeStruct((total, 128), f32),
             jax.ShapeDtypeStruct((total, 128), f32),
         ],
@@ -695,7 +696,7 @@
 
 
 def next_expert_kernel(
-    which, experts, rows_v, g_v, gates_ref, totals_ref, gate_up_v, down_v, hidden_v, grad_v,
+    which, experts, rows_v, g_v, gates_ref, totals_ref, gate_up_v, down_v, _, hidden_v, grad_v,
     gate_grad_ref, total_v,
 ):
     lane = lax.broadcasted_iota(jnp.int32, total_v.shape, 1)
@@ -712,7 +713,7 @@
     gate_grad_ref[...] = jnp.where(lane < experts, high, total - high).astype(bf16)
 
 
-def last_expert(which, experts, rows, g_rows, gates, totals, gate_up, down_proj):
+def last_expert(which, experts, rows, g_rows, gates, totals, gate_up, down_proj, grads):
     ff, width = down_proj.shape[1:]
     total = rows.shape[0]
     step = total // 4
@@ -731,22 +732,25 @@
         grid=(4,),
         out_shape=[
             jax.ShapeDtypeStruct((total, ff), bf16),
-            jax.ShapeDtypeStruct((total, 2 * ff), bf16),
+            jax.ShapeDtypeStruct(grads.shape, bf16),
             jax.ShapeDtypeStruct((total, 128), bf16),
         ],
         in_specs=[
             block(width), block(width), block(128), block(128),
-            whole(gate_up.shape), whole(down_proj.shape),
+            whole(gate_up.shape), whole(down_proj.shape), pl.BlockSpec(memory_space=pl.ANY),
         ],
-        out_specs=[block(ff), block(2 * ff), block(128)],
+        out_specs=[
+            block(ff), pl.BlockSpec((step, 2 * ff), lambda i: (i, which)), block(128)
+        ],
+        input_output_aliases={6: 1},
         scratch_shapes=[pltpu.VMEM((step, 128), f32)],
         compiler_params=pltpu.CompilerParams(vmem_limit_bytes=56 * 2**20),
         cost_estimate=pl.CostEstimate(flops=10**6, bytes_accessed=10**6, transcendentals=0),
-    )(rows, g_rows, gates, totals, gate_up, down_proj)
+    )(rows, g_rows, gates, totals, gate_up, down_proj, grads)
 
 
 def weight_grad_kernel(
-    query_grad, kv_grad, branch, attended_owned, normed_owned, out_local, pre_local,
+    query_grad, kv_grad, branch, attended_owned, normed_owned, sums_ref,
     pre_v, branch_v, attended_v, normed_v, send_sem, recv_sem, local_sem,
 ):
     here = Places()
@@ -755,7 +759,8 @@
     count, wide = query_grad.shape
     narrow = kv_grad.shape[1]
     spread = lax.axis_size(plane)
-    tile = 1024
+    tile = sums_ref.shape[1]
+    groups = lax.axis_size("dp")
     half = wide // 2
     low, high, last = pl.ds(0, half), pl.ds(half, half), pl.ds(wide, narrow)
     b, _ = block_gather(here, send, branch, local_sem.at[0], branch_v)
@@ -781,25 +786,34 @@
         for load in loads:
             load.start()
 
-    def product(left, right, out, first, tiles):
+    def product(left, right, base, first, tiles):
+        rows = left.shape[1] // groups
+
         @pl.loop(first, first + tiles)
         def _(i):
             cols = pl.ds(pl.multiple_of(i * tile, tile), tile)
-            out[:, cols] = transposed_dot(left[...], right[:, cols]).astype(bf16)
+            part = transposed_dot(left[...], right[:, cols]).astype(bf16)
+            for d in range(groups):
+                at = d * (sums_ref.shape[0] // groups) + base + i * rows
+                sums_ref[pl.ds(pl.multiple_of(at, 64), rows), :] = part[
+                    d * rows : (d + 1) * rows
+                ]
+
+    output_rows = attended_v.shape[1] // groups * (branch.shape[1] // tile)
 
     def output_product():
         for load in loads:
             load.wait()
-        product(attended_v, branch_v, out_local, 0, branch.shape[1] // tile)
+        product(attended_v, branch_v, 0, 0, branch.shape[1] // tile)
 
     steps = [
         b[0], start, b[1], qa[0], b[2], qa[1], qb[0], b[3], output_product,
         qa[2], qb[1], kv[0], qa[3],
-        lambda: product(normed_v, pre_v, pre_local, 0, half // tile),
+        lambda: product(normed_v, pre_v, output_rows, 0, half // tile),
         qb[2], kv[1], qb[3],
-        lambda: product(normed_v, pre_v, pre_local, half // tile, half // tile),
+        lambda: product(normed_v, pre_v, output_rows, half // tile, half // tile),
         kv[2], kv[3],
-        lambda: product(normed_v, pre_v, pre_local, wide // tile, narrow // tile),
+        lambda: product(normed_v, pre_v, output_rows, wide // tile, narrow // tile),
     ]
     for step in steps:
         step()
@@ -810,16 +824,15 @@
     count, wide = query_grad.shape
     narrow, width = kv_grad.shape[1], branch.shape[1]
     spread = lax.axis_size(plane)
+    tile = narrow
+    elements = attended_owned.shape[2] * width + normed_owned.shape[2] * (wide + narrow)
     vmem = pl.BlockSpec(memory_space=pltpu.VMEM)
     anywhere = pl.BlockSpec(memory_space=pl.ANY)
     return pl.pallas_call(
         weight_grad_kernel,
-        out_shape=[
-            jax.ShapeDtypeStruct((attended_owned.shape[2], width), bf16),
-            jax.ShapeDtypeStruct((normed_owned.shape[2], wide + narrow), bf16),
-        ],
+        out_shape=jax.ShapeDtypeStruct((elements // tile, tile), bf16),
         in_specs=[anywhere] * 5,
-        out_specs=[vmem] * 2,
+        out_specs=vmem,
         scratch_shapes=[
             pltpu.VMEM((spread * count, wide + narrow), bf16),
             pltpu.VMEM((spread * count, width), bf16),
@@ -845,10 +858,10 @@
     return here.ctx * 2 + here.y
 
 
-def plane_sum_kernel(across, experts, *refs):
-    lefts, weight_hbm = refs[:experts], refs[experts]
-    extra_ref = refs[experts + 1] if across else None
-    refs = refs[experts + 1 + across :]
+def plane_sum_kernel(across, parts, *refs):
+    lefts, weight_hbm = refs[:parts], refs[parts]
+    extra_ref = refs[parts + 1] if across else None
+    refs = refs[parts + 1 + across :]
     (
         out_ref, left_v, weight_v, part_v, core_v, edge_v, last_v, send_sem, recv_sem, local_sem,
     ) = refs
@@ -857,7 +870,9 @@
     send = Sender(send_sem, recv_sem)
     count = out_ref.shape[0]
     half = count // 2
-    depth = lefts[0].shape[1]
+    experts = weight_hbm.shape[0]
+    part_depth = lefts[0].shape[1]
+    depth = part_depth * parts // experts
     width = weight_hbm.shape[1] if across else weight_hbm.shape[2]
     tile = 256
     x, y, c = here.x, here.y, here.c
@@ -871,8 +886,8 @@
             [
                 pltpu.make_async_copy(
                     left.at[some, :],
-                    left_v.at[k, :, pl.ds(e * depth, depth)],
-                    local_sem.at[1 + experts * k + e],
+                    left_v.at[k, :, pl.ds(e * part_depth, part_depth)],
+                    local_sem.at[1 + parts * k + e],
                 )
                 for e, left in enumerate(lefts)
             ]
@@ -949,20 +964,20 @@
     count = lefts[0].shape[0] // lax.axis_size(plane)
     width = weight.shape[1] if across else weight.shape[2]
     wide = width + (extra.shape[1] if across else 0)
-    experts, depth = len(lefts), lefts[0].shape[1]
+    parts, depth = len(lefts), lefts[0].shape[1]
     vmem = pl.BlockSpec(memory_space=pltpu.VMEM)
     anywhere = pl.BlockSpec(memory_space=pl.ANY)
 
     def kernel(*refs):
-        plane_sum_kernel(across, experts, *refs)
+        plane_sum_kernel(across, parts, *refs)
 
     return pl.pallas_call(
         kernel,
         out_shape=jax.ShapeDtypeStruct((count, wide), f32),
-        in_specs=[anywhere] * (experts + 1) + [vmem] * across,
+        in_specs=[anywhere] * (parts + 1) + [vmem] * across,
         out_specs=vmem,
         scratch_shapes=[
-            pltpu.VMEM((4, 2 * count, experts * depth), bf16),
+            pltpu.VMEM((4, 2 * count, parts * depth), bf16),
             pltpu.VMEM(weight.shape, bf16),
             pltpu.VMEM((4, 2 * count, wide), bf16),
             pltpu.VMEM((4, count, wide), bf16),
@@ -970,7 +985,7 @@
             pltpu.VMEM((2, count, wide), bf16),
             pltpu.SemaphoreType.DMA((8,)),
             pltpu.SemaphoreType.DMA((8,)),
-            pltpu.SemaphoreType.DMA((1 + 4 * experts,)),
+            pltpu.SemaphoreType.DMA((1 + 4 * parts,)),
         ],
         compiler_params=pltpu.CompilerParams(
             collective_id=collective_id, has_side_effects=True, vmem_limit_bytes=60 * 2**20
@@ -1265,34 +1280,24 @@
         )
         return raised / jnp.sum(raised, axis=-1, keepdims=True)
 
-    def reduce_expert(which, rows, hidden, grads, g_rows):
-        down_part = dot(hidden.T, g_rows).astype(bf16)
-        gate_up_part = dot(rows.T, grads).astype(bf16)
-        return (
-            lax.psum_scatter(down_part, "dp", scatter_dimension=0, tiled=True),
-            lax.psum_scatter(gate_up_part, "dp", scatter_dimension=0, tiled=True),
-            down_part,
-            gate_up_part,
-        )
-
     gates = gates_of(ffn_in, routes)
     if small_plane():
         rows, hidden, grads, gates_mine, totals = gather_first_expert(
             ffn_in, route_rows, router_weight, g_rows, gate_up, down_proj
         )
-        hiddens, projected_grads = [hidden], [grads]
-        sums = [reduce_expert(0, rows, hidden, grads, g_rows)]
-        rows = after(rows, *sums[0][2:])
-        attended_owned, normed_owned = [
-            owned(after(v, *sums[0][2:])) for v in (attended_owned, normed_owned)
-        ]
-        for which in range(1, local_experts):
-            hidden, grads, gate_grads = last_expert(
-                which, expert_count, rows, g_rows, gates_mine, totals, gate_up, down_proj
-            )
-            hiddens.append(hidden)
-            projected_grads.append(grads)
-            sums.append(reduce_expert(which, rows, hidden, grads, g_rows))
+        hiddens = [hidden]
+        down_parts = [dot(hidden.T, g_rows).astype(bf16)]
+        rows, grads, attended_owned, normed_owned = lax.optimization_barrier(
+            ((rows, grads, attended_owned, normed_owned), down_parts)
+        )[0]
+        attended_owned, normed_owned = owned(attended_owned), owned(normed_owned)
+        hidden, grads, gate_grads = last_expert(
+            1, expert_count, rows, g_rows, gates_mine, totals, gate_up, down_proj, grads
+        )
+        hiddens.append(hidden)
+        projected_grads = [grads]
+        down_parts.append(dot(hidden.T, g_rows).astype(bf16))
+        gate_up_parts = [dot(after(rows, down_parts).T, grads).astype(bf16)]
     else:
         rows = lax.all_gather(ffn_in, plane, axis=0, tiled=True)
         first_expert = lax.axis_index(plane) * local_experts
@@ -1315,16 +1320,22 @@
             up_back = back * gate_part * sigmoid_gate
             projected_grads.append(jnp.concatenate([gate_back, up_back], axis=-1).astype(bf16))
         attended_owned, normed_owned = owned(attended_owned), owned(normed_owned)
-        sums = [
-            reduce_expert(i, rows, hidden, grads, g_rows)
-            for i, (hidden, grads) in enumerate(zip(hiddens, projected_grads))
+        down_parts = [dot(v.T, g_rows).astype(bf16) for v in hiddens]
+        gate_up_parts = [dot(rows.T, v).astype(bf16) for v in projected_grads]
+    down_low, gate_up_low = [
+        [lax.psum_scatter(v, "dp", scatter_dimension=0, tiled=True) for v in parts]
+        for parts in (down_parts, gate_up_parts)
+    ]
+    down_grad = jnp.stack([v.astype(f32) for v in down_low])
+    gate_up_grad = jnp.stack(
+        [
+            part.astype(f32)
+            for v in gate_up_low
+            for part in jnp.split(v, v.shape[1] // (2 * hidden_ff), axis=1)
         ]
-    down_low = [v[0] for v in sums]
-    gate_up_low = [v[1] for v in sums]
-    down_grad = jnp.stack([v.astype(f32) for v in down_low])
-    gate_up_grad = jnp.stack([v.astype(f32) for v in gate_up_low])
+    )
     projected_grads, hiddens = lax.optimization_barrier(
-        ((projected_grads, hiddens), [v[2:] for v in sums], attended_owned, normed_owned)
+        ((projected_grads, hiddens), down_parts, gate_up_parts, attended_owned, normed_owned)
     )[0]
     if small_plane():
         back = plane_sum(projected_grads, gate_up, gate_grads, 3)
@@ -1382,9 +1393,9 @@
     )
     key_value_grad = jnp.concatenate([key_pre_grad, value_gradient.astype(bf16)], axis=1)
     if small_plane():
-        output_local, pre_local = weight_grads(
-            query_pre_grad, key_value_grad, branch_low, attended_owned, normed_owned
-        )
+        local = [
+            weight_grads(query_pre_grad, key_value_grad, branch_low, attended_owned, normed_owned)
+        ]
     else:
         branch_rows = lax.all_gather(branch_low, plane, axis=0, tiled=True)
         pre_rows = lax.all_gather(
@@ -1393,10 +1404,12 @@
         attended_owned, normed_owned = [
             v.reshape(spread_count * count_of_rows, -1) for v in (attended_owned, normed_owned)
         ]
-        output_local = dot(attended_owned.T, branch_rows).astype(bf16)
-        pre_local = dot(normed_owned.T, pre_rows).astype(bf16)
+        local = [
+            dot(attended_owned.T, branch_rows).astype(bf16),
+            dot(normed_owned.T, pre_rows).astype(bf16),
+        ]
     query_pre_grad, key_value_grad = lax.optimization_barrier(
-        ((query_pre_grad, key_value_grad), pre_local)
+        ((query_pre_grad, key_value_grad), local)
     )[0]
     normed_grad = backward_dot(query_pre_grad, q_weights) + backward_dot(
         key_value_grad, kv_weights
@@ -1404,15 +1417,26 @@
     attn_gain_local = jnp.sum(normed_grad * inputs * scale_in, axis=0)
     hidden_grad = residual_grad + norm_back(inputs, scale_in, attn_gain, normed_grad)
     if small_plane():
-        moe_sum = plane_sum(after(hiddens, pre_local), down_proj, None, 4)
+        moe_sum = plane_sum(after(hiddens, local), down_proj, None, 4)
     block_out = (residual + moe_sum).astype(bf16)
-    output_local, pre_local = lax.optimization_barrier(
-        ((output_local, pre_local), gate_up_low, down_low)
-    )[0]
-    output_sum, pre_sum = [
-        lax.psum_scatter(v, "dp", scatter_dimension=0, tiled=True).astype(f32)
-        for v in (output_local, pre_local)
+    local = lax.optimization_barrier((local, gate_up_low, down_low))[0]
+    summed = [
+        lax.psum_scatter(v, "dp", scatter_dimension=0, tiled=True).astype(f32) for v in local
     ]
+    share = MODEL_WIDTH // device_count
+    if small_plane():
+        tile = summed[0].shape[1]
+        cut = wide // device_count * (MODEL_WIDTH // tile)
+
+        def untile(v, rows):
+            return jnp.concatenate(
+                [v[i : i + rows] for i in range(0, v.shape[0], rows)], axis=1
+            )
+
+        output_sum = untile(summed[0][:cut], wide // device_count)
+        pre_sum = untile(summed[0][cut:], share)
+    else:
+        output_sum, pre_sum = summed
 
     small = jnp.concatenate(
         [
@@ -1429,7 +1453,6 @@
     )
     small = lax.all_to_all(small[:, None], every, split_axis=0, concat_axis=0, tiled=True)
     small = jnp.sum(small[:, 0], axis=0)
-    share = MODEL_WIDTH // device_count
     head_share = HEAD_SIZE // device_count
     cuts = [share, share, head_share, head_share, share * expert_count]
     ends = [sum(cuts[: i + 1]) for i in range(5)]

time: 683 us -> 640 us (0.937)
  waiting for transfers between devices: 79.1 us -> 47.3 us
  Pallas kernels: 437 us -> 419 us
  blocking collectives: 0 us -> 15.7 us
    all_to_all x0 -> x1, blocking collectives: none -> 15.7 us  [owned(): return lax.all_to_all(v, plane, split_axis=0, concat_axis=0, tiled=True)]
    pallas_call x1, Pallas kernels: 55.4 us -> 43.7 us  [gather_first_expert(): pl.pallas_call(first_expert_kernel, out_shape=[jax.ShapeDtypeStruct((tota...]
    all_to_all x2 -> x1, waiting for transfers between devices: 29.5 us -> 17.9 us  [owned(): return lax.all_to_all(v, plane, split_axis=0, concat_axis=0, tiled=True)]
    reduce_scatter x2 -> x1, waiting for transfers between devices: 17.3 us -> 6.6 us  [body(): lax.psum_scatter(v, 'dp', scatter_dimension=0, tiled=True).astype(f32)]
    reduce_scatter x4 -> x3, waiting for transfers between devices: 23.9 us -> 15.2 us  [body(): lax.psum_scatter(v, 'dp', scatter_dimension=0, tiled=True)]
    dot_general x11 -> x10, matrix products: 72.7 us -> 68.1 us  [dot(): return jnp.dot(a, b, preferred_element_type=f32)]
  transfers between devices with their start and end apart: 12 -> 9, of which waited for: 6 -> 5; matrix products, arithmetic and copies ran while one was open for 16% -> 16% of each run, Pallas kernels for 37% -> 40%
where the time goes in v5:
time: 640 us; the launch traced here: 631 us
  Pallas kernels  419 us (65%)
  matrix products  72.8 us (11%)
  waiting for transfers between devices  47.3 us (7%)
  other arithmetic  26.7 us (4%)
  local copies, waits for them, and re-layouts  23.9 us (4%)
  blocking collectives  15.7 us (2%)
  between operations  14.9 us (2%)
  starting transfers between devices  10.8 us (2%)
    pallas_call x1, Pallas kernels, fetch_and_attend(): pl.pallas_call(fetch_kernel, out_shape=[jax.ShapeDtypeStruct((half, 2 * n...  125 us
    pallas_call x1, Pallas kernels, weight_grads(): pl.pallas_call(weight_grad_kernel, out_shape=jax.ShapeDtypeStruct((elemen...  99.4 us
    pallas_call x2, Pallas kernels, plane_sum(): pl.pallas_call(kernel, out_shape=jax.ShapeDtypeStruct((count, wide), f32)...  96.8 us
    dot_general x10, matrix products, dot(): return jnp.dot(a, b, preferred_element_type=f32)  68.1 us
    pallas_call x1, Pallas kernels, gather_first_expert(): pl.pallas_call(first_expert_kernel, out_shape=[jax.ShapeDtypeStruct((tota...  43.7 us
    pallas_call x1, Pallas kernels, attention_back(): pl.pallas_call(attention_back_kernel, grid=(KEY_VALUE_HEADS,), out_shape=...  30.1 us
    pallas_call x1, Pallas kernels, last_expert(): pl.pallas_call(kernel, grid=(4,), out_shape=[jax.ShapeDtypeStruct((total,...  23.4 us
    all_to_all x1, waiting for transfers between devices, owned(): return lax.all_to_all(v, plane, split_axis=0, concat_axis=0, tiled=True)  17.9 us
  transfers between devices with their start and end apart: 9, of which 5 were waited for; matrix products, arithmetic and copies ran while one was open for 16% of the time, Pallas kernels for 40%

profile of v5, /device:TPU:0, one launch (start us, length us, event | category | flops | bytes accessed | tf_op | source)
XLA Modules:
  0.0 631.1 jit_solution(11463695500146194041)
XLA Ops:
  7.3 1.5 copy.64.routes_ref
  8.7 1.8 copy.65.router_ref
  10.7 1.1 fusion.21
  11.8 125.5 %shard_map.237 = (bf16[1024,1024]{1,0:T(8,128)(2,1)}, bf16[1024,4096]{1,0:T(8,128)(2,1)}, bf16[2048,2048]{1,0:T(8,128)(2,1)}, bf16[1536,2048]{1,0:T(8,128)(2,1)}...) custom-call(bf16[192,2048]{1,0:T(8,128)(2,1)} %hidden_ref.1, ...), custom_call_target="tpu_custom_call" | custom-call | flops 14495514624 | bytes 62914560 | tf_op jit(solution)/shard_map/pallas_call | solution.py:481
  137.3 43.7 %shard_map.238 = (bf16[1536,2048]{1,0:T(8,128)(2,1)}, bf16[1536,768]{1,0:T(8,128)(2,1)}, bf16[1536,3072]{1,0:T(8,128)(2,1)}, f32[1536,128]{1,0:T(8,128)}, f32[1536,128]{1,0:T(8,128)}) custom-call(bf16[192,2048]{1,0:T(8,128)(2,1)} %get-tuple-element.52.ffn_ref, s32[1536,8]{1,0:T(8,128)} %get-tuple-element.53.routes_ref, bf16[2048,16]{1,0:T(8,128)(2,1)} %copy.65.router_ref, ...), custom_call_target="tpu_custom_call" | custom-call | flops 14495514624 | bytes 41943040 | tf_op jit(solution)/shard_map/pallas_call | solution.py:664
  181.0 8.1 %convolution_convert_fusion.2 = bf16[768,2048]{1,0:T(8,128)(2,1)} fusion(bf16[1536,768]{1,0:T(8,128)(2,1)} %get-tuple-element.81.refs_0_, bf16[1536,2048]{1,0:T(8,128)(2,1)S(1)} %copy-done.12), kind=kOutput, calls=%fused_computation.2 | convolution fusion | flops 4833411072 | bytes 11796480 | tf_op jit(solution)/shard_map/dot_general | solution.py:1150
  189.3 23.4 %shard_map.239 = (bf16[1536,768]{1,0:T(8,128)(2,1)}, bf16[1536,3072]{1,0:T(8,128)(2,1)}, bf16[1536,128]{1,0:T(8,128)(2,1)}) custom-call(bf16[1536,2048]{1,0:T(8,128)(2,1)} %get-tuple-element.66.refs_0_, bf16[1536,2048]{1,0:T(8,128)(2,1)} %get-tuple-element.54.g_hbm.refs_1_, f32[1536,128]{1,0:T(8,128)} %get-tuple-element.61.refs_2_, ...), custom_call_target="tpu_custom_call", output_to_operand_aliasing={{1}: (6, {})} | custom-call | flops 1000000 | bytes 1000000 | tf_op jit(solution)/shard_map/pallas_call | solution.py:730
  212.7 8.2 %convolution_convert_fusion.1 = bf16[768,2048]{1,0:T(8,128)(2,1)} fusion(bf16[1536,768]{1,0:T(8,128)(2,1)} %get-tuple-element.82.refs_1_, bf16[1536,2048]{1,0:T(8,128)(2,1)S(1)} %bitcast.85), kind=kOutput, calls=%fused_computation.1 | convolution fusion | flops 4833411072 | bytes 11796480 | tf_op jit(solution)/shard_map/dot_general | solution.py:1150
  220.9 26.6 %convolution_convert_fusion = bf16[2048,3072]{1,0:T(8,128)(2,1)} fusion(bf16[1536,2048]{1,0:T(8,128)(2,1)} %get-tuple-element.66.refs_0_, bf16[1536,3072]{1,0:T(8,128)(2,1)} %get-tuple-element.74.refs_0_), kind=kOutput, calls=%fused_computation | convolution fusion | flops 19333644288 | bytes 28311552 | tf_op jit(solution)/shard_map/dot_general | solution.py:1150
  247.5 1.1 copy-done.27
  248.6 15.7 %all_to_all.15.normed_owned = bf16[8,192,256]{2,1,0:T(8,128)(2,1)} all-to-all(bf16[8,192,256]{2,1,0:T(8,128)(2,1)S(1)} %copy-done.27), channel_id=1, replica_groups=mesh['dp'=4,'ctx'=4,'expert'=2] {'ctx','expert'}, dimensions={0} | all-to-all | bytes 1572864 | tf_op jit(solution)/shard_map/all_to_all | solution.py:1261
  264.4 3.7 all-to-all-start
  268.3 1.6 fusion.34
  270.3 17.9 %all-to-all-done.attended_owned = bf16[8,192,512]{2,1,0:T(8,128)(2,1)S(1)} async-done(((bf16[8,192,512]{2,1,0:T(8,128)(2,1)}), bf16[8,192,512]{2,1,0:T(8,128)(2,1)S(1)}, u32[]{:S(2)}, u32[]{:S(2)}) %all-to-all-start) | async-done | bytes 1572896 | tf_op jit(solution)/shard_map/all_to_all | solution.py:1261
  288.2 53.3 %shard_map.240 = f32[192,2176]{1,0:T(8,128)} custom-call(bf16[1536,3072]{1,0:T(8,128)(2,1)} %get-tuple-element.74.refs_0_, bf16[2,2048,1536]{2,1,0:T(8,128)(2,1)} %refs_1_.1, bf16[1536,128]{1,0:T(8,128)(2,1)} %get-tuple-element.75.refs_2_), custom_call_target="tpu_custom_call" | custom-call | flops 1000000 | bytes 1000000 | tf_op jit(solution)/shard_map/pallas_call | solution.py:974
  341.5 1.2 multiply_reduce_fusion.5
  342.7 2.9 multiply_reduce_fusion
  345.7 1.7 fusion.27
  347.4 6.7 %fusion.36 = bf16[192,2048]{1,0:T(8,128)(2,1)S(1)} fusion(bf16[192,2048]{1,0:T(8,128)(2,1)S(1)} %get-tuple-element.161.branch, bf16[2048,2048]{1,0:T(8,128)(2,1)} %get-tuple-element.76), kind=kOutput, calls=%fused_computation.114 | convolution fusion | flops 1610612736 | bytes 9961472 | tf_op jit(solution)/shard_map/dot_general | solution.py:1150
  354.2 2.9 select_convert_fusion.1
  357.1 1.3 pad_maximum_fusion.grad_ref
  358.8 30.1 %shard_map.241 = (bf16[192,4096]{1,0:T(8,128)(2,1)S(1)}, f32[576,512]{1,0:T(8,128)S(1)}, f32[576,512]{1,0:T(8,128)S(1)}, f32[4,1,128]{2,1,0:T(1,128)S(1)}) custom-call(f32[192,4096]{1,0:T(8,128)} %get-tuple-element.71.query_pre_ref, f32[1,128]{1,0:T(1,128)S(1)} %bitcast.81, f32[192,128]{1,0:T(8,128)S(1)} %copy-done.3, f32[192,128]{1,0:T(8,128)S(1)} %copy-done.4, ...), custom_call_target="tpu_custom_call" | custom-call | flops 1000000 | bytes 1000000 | tf_op jit(solution)/shard_map/pallas_call | solution.py:1110
  389.1 0.9 copy-done
  390.0 0.8 copy-done.7
  390.8 0.8 fusion.17
  392.2 1.4 collective-permute-done.1
  393.6 1.7 add_convert_fusion.1
  395.8 1.9 reshape.220
  397.8 6.2 collective-permute-done.2
  404.0 1.2 convert_add_fusion
  405.4 0.6 copy-done.28
  406.4 1.2 multiply_reduce_fusion.4
  407.6 1.0 copy.69
  408.7 0.8 copy.70
  409.5 0.8 copy.71
  410.3 1.2 mul.262
  412.1 0.9 fusion.14
  413.1 0.8 maximum_maximum_fusion.kv_grad
  413.8 99.4 %shard_map.242 = bf16[2304,1024]{1,0:T(8,128)(2,1)} custom-call(bf16[192,4096]{1,0:T(8,128)(2,1)} %copy-done, bf16[192,1024]{1,0:T(8,128)(2,1)} %maximum_maximum_fusion.kv_grad, bf16[192,2048]{1,0:T(8,128)(2,1)} %copy-done.15, bf16[8,192,512]{2,1,0:T(8,128)(2,1)} %copy-done.10, bf16[8,192,256]{2,1,0:T(8,128)(2,1)} %all_to_all.15.normed_owned), custom_call_target="tpu_custom_call" | custom-call | flops 1000000 | bytes 1000000 | tf_op jit(solution)/shard_map/pallas_call | solution.py:831
  513.4 15.2 %reduce-scatter.5.cloned.1.call-done = bf16[512,3072]{1,0:T(8,128)(2,1)} async-done(((bf16[2048,3072]{1,0:T(8,128)(2,1)}), bf16[512,3072]{1,0:T(8,128)(2,1)}) %reduce-scatter.5.cloned.1.call-update) | async-done | bytes 3145744 | tf_op jit(solution)/shard_map/reduce_scatter | solution.py:1326
  529.4 0.7 reshape.222
  530.1 0.7 reshape.223
  530.8 1.8 fusion.35
  532.6 0.6 reshape.225
  533.3 2.7 fusion.38
  536.0 0.8 broadcast_select_fusion.1
  537.4 7.6 %fusion.37 = f32[192,1024]{1,0:T(8,128)S(1)} fusion(bf16[192,4096]{1,0:T(8,128)(2,1)S(1)} %copy-done.1, bf16[1024,4096]{1,0:T(8,128)(2,1)} %get-tuple-element.84), kind=kOutput, calls=%fused_computation.115 | convolution fusion | flops 1610612736 | bytes 10747904 | tf_op jit(solution)/shard_map/dot_general | solution.py:1150
  545.1 2.9 broadcast_select_fusion.3
  548.1 0.7 fusion.10
  549.2 0.8 copy.75
  550.1 5.9 all-to-all-start.2
  556.0 43.5 %shard_map.243 = f32[192,2048]{1,0:T(8,128)} custom-call(bf16[1536,768]{1,0:T(8,128)(2,1)} %get-tuple-element.81.refs_0_, bf16[1536,768]{1,0:T(8,128)(2,1)} %get-tuple-element.82.refs_1_, bf16[2,768,2048]{2,1,0:T(8,128)(2,1)} %refs_2_.1), custom_call_target="tpu_custom_call" | custom-call | flops 1000000 | bytes 1000000 | tf_op jit(solution)/shard_map/pallas_call | solution.py:974
  599.6 4.0 fusion.7
  603.6 1.1 add_convert_fusion
  604.9 0.7 copy.76
  606.7 1.9 maximum_convert_fusion.1
  608.6 1.2 copy-done.18
  610.0 3.1 maximum_convert_fusion
  613.1 6.6 %reduce-scatter.11.cloned.1.call-done = bf16[576,1024]{1,0:T(8,128)(2,1)} async-done(((bf16[2304,1024]{1,0:T(8,128)(2,1)}), bf16[576,1024]{1,0:T(8,128)(2,1)}) %reduce-scatter.11.cloned.1.call-update) | async-done | bytes 1179664 | tf_op jit(solution)/shard_map/reduce_scatter | solution.py:1424
  619.7 1.1 fusion.28
  620.9 1.0 pad_maximum_fusion.2
  621.9 0.6 copy-done.13
  622.6 1.0 pad_maximum_fusion.1
  623.7 0.7 fusion.29
  (154 shorter events, 7.6 us)
Async XLA Ops:
  7.2 506.2 %reduce-scatter.7.cloned.1.call-start = ((), (), s32[]{:S(2)}) async-start(), calls=%async_computation.8 | async-start | bytes 3932160 | tf_op jit(solution)/shard_map/reduce_scatter | solution.py:1326
  137.3 43.7 %copy-start.12 = (bf16[1536,2048]{1,0:T(8,128)(2,1)S(1)}, bf16[1536,2048]{1,0:T(8,128)(2,1)}, u32[]{:S(2)}) copy-start(bf16[1536,2048]{1,0:T(8,128)(2,1)} %get-tuple-element.54.g_hbm.refs_1_) | copy-start | bytes 18874372
  189.2 23.5 %slice-start.2 = ((s8[6291456]{0:T(1024)(128)(4,1)}), s8[2097152]{0:T(1024)(128)(4,1)S(1)}, s32[]{:S(2)}) async-start(s8[6291456]{0:T(1024)(128)(4,1)} %bitcast.84), calls=%async_computation.13 | async-start | bytes 4194304
  189.2 324.2 %reduce-scatter.9.cloned.1.call-start = ((), (), s32[]{:S(2)}) async-start(), calls=%async_computation.9 | async-start | bytes 3932160 | tf_op jit(solution)/shard_map/reduce_scatter | solution.py:1326
  189.2 23.4 %slice-start.3 = ((s8[6291456]{0:T(1024)(128)(4,1)}), s8[4194304]{0:T(1024)(128)(4,1)S(1)}, s32[]{:S(2)}) async-start(s8[6291456]{0:T(1024)(128)(4,1)} %bitcast.84), calls=%async_computation.14 | async-start | bytes 8388608
  220.9 307.7 %reduce-scatter.5.cloned.1.call-start = ((), (), s32[]{:S(2)}) async-start(), calls=%async_computation.7 | async-start | bytes 15728640 | tf_op jit(solution)/shard_map/reduce_scatter | solution.py:1326
  247.5 1.1 copy-start.27
  264.4 3.8 copy-start.34
  264.4 4.0 copy-start.30
  264.4 5.7 copy-start.6
  264.4 23.8 %all-to-all-start = ((bf16[8,192,512]{2,1,0:T(8,128)(2,1)}), bf16[8,192,512]{2,1,0:T(8,128)(2,1)S(1)}, u32[]{:S(2)}, u32[]{:S(2)}) async-start(bf16[8,192,512]{2,1,0:T(8,128)(2,1)} %get-tuple-element.67), calls=%async_computation | async-start | bytes 3145728 | tf_op jit(solution)/shard_map/all_to_all | solution.py:1261
  268.1 351.6 %reduce-scatter.11.cloned.1.call-start = ((), (), s32[]{:S(2)}) async-start(), calls=%async_computation.10 | async-start | bytes 5898240 | tf_op jit(solution)/shard_map/reduce_scatter | solution.py:1424
  269.9 72.8 %copy-start.22 = (f32[192,16]{1,0:T(8,128)}, f32[192,16]{1,0:T(8,128)S(1)}, u32[]{:S(2)}) copy-start(f32[192,16]{1,0:T(8,128)S(1)} %get-tuple-element.201) | copy-start | bytes 36868
  288.2 53.3 %copy-start.10 = (bf16[8,192,512]{2,1,0:T(8,128)(2,1)}, bf16[8,192,512]{2,1,0:T(8,128)(2,1)S(1)}, u32[]{:S(2)}) copy-start(bf16[8,192,512]{2,1,0:T(8,128)(2,1)S(1)} %all-to-all-done.attended_owned) | copy-start | bytes 4718596
  288.2 54.5 %copy-start.35 = (f32[2048]{0:T(1024)S(1)}, f32[2048]{0:T(1024)}, u32[]{:S(2)}) copy-start(f32[2048]{0:T(1024)} %param.22) | copy-start | bytes 24580
  342.7 3.0 copy-start.37
  342.7 3.0 copy-start.24
  345.7 8.4 %slice-start.5 = ((s8[8388608]{0:T(1024)(128)(4,1)}), s8[4194304]{0:T(1024)(128)(4,1)S(1)}, s32[]{:S(2)}) async-start(s8[8388608]{0:T(1024)(128)(4,1)} %bitcast.97), calls=%async_computation.16 | async-start | bytes 8388608
  347.4 6.7 %copy-start.15 = (bf16[192,2048]{1,0:T(8,128)(2,1)}, bf16[192,2048]{1,0:T(8,128)(2,1)S(1)}, u32[]{:S(2)}) copy-start(bf16[192,2048]{1,0:T(8,128)(2,1)S(1)} %get-tuple-element.161.branch) | copy-start | bytes 2359300
  347.4 6.7 %slice-start.6 = ((s8[8388608]{0:T(1024)(128)(4,1)}), s8[4194304]{0:T(1024)(128)(4,1)S(1)}, s32[]{:S(2)}) async-start(s8[8388608]{0:T(1024)(128)(4,1)} %bitcast.97), calls=%async_computation.17 | async-start | bytes 8388608
  357.1 1.6 copy-start.2
  357.1 1.6 copy-start.3
  357.1 1.7 copy-start.4
  357.1 1.7 copy-start.5
  388.9 1.1 copy-start
  389.0 2.7 copy-start.19
  390.0 0.8 copy-start.7
  391.7 6.0 copy-start.39
  391.7 1.9 collective-permute-start.1
  391.7 6.1 collective-permute-start
  395.3 8.7 %collective-permute-start.2 = (bf16[2,128,512]{2,1,0:T(8,128)(2,1)}, bf16[2,128,512]{2,1,0:T(8,128)(2,1)}, u32[]{:S(2)}, u32[]{:S(2)}) collective-permute-start(bf16[2,128,512]{2,1,0:T(8,128)(2,1)} %add_convert_fusion.1), channel_id=1, source_target_pairs={{0,4},{2,6},{4,0},{6,2},{1,5},{3,7},{5,1},{7,3},{8,12},{10,14},{12... | collective-permute-start | bytes 786440 | tf_op jit(solution)/shard_map/ppermute | solution.py:66
  405.1 0.9 copy-start.28
  405.3 1.1 copy-start.20
  405.3 1.1 copy-start.40
  407.6 4.5 copy-start.21
  410.2 1.6 copy-start.29
  412.1 1.0 slice-start.4
  513.3 15.3 %copy-start.8 = (bf16[192,2048]{1,0:T(8,128)(2,1)S(1)}, bf16[192,2048]{1,0:T(8,128)(2,1)}, u32[]{:S(2)}) copy-start(bf16[192,2048]{1,0:T(8,128)(2,1)} %hidden_ref.1) | copy-start | bytes 2359300
  513.3 17.5 %copy-start.23 = (f32[192,16]{1,0:T(8,128)S(1)}, f32[192,16]{1,0:T(8,128)}, u32[]{:S(2)}) copy-start(f32[192,16]{1,0:T(8,128)} %copy-done.22) | copy-start | bytes 36868
  533.2 2.7 copy-start.14
  533.2 2.7 copy-start.41
  533.3 2.7 copy-start.42
  536.0 1.4 copy-start.1
  536.0 9.0 %slice-start = ((s8[8388608]{0:T(1024)(128)(4,1)}), s8[4194304]{0:T(1024)(128)(4,1)S(1)}, s32[]{:S(2)}) async-start(s8[8388608]{0:T(1024)(128)(4,1)} %bitcast.82), calls=%async_computation.11 | async-start | bytes 8388608
  536.9 11.2 %copy-start.16 = (f32[192,1024]{1,0:T(8,128)}, f32[192,1024]{1,0:T(8,128)S(1)}, u32[]{:S(2)}) copy-start(f32[192,1024]{1,0:T(8,128)S(1)} %get-tuple-element.169) | copy-start | bytes 2359300
  536.9 11.1 %copy-start.17 = (f32[192,1024]{1,0:T(8,128)}, f32[192,1024]{1,0:T(8,128)S(1)}, u32[]{:S(2)}) copy-start(f32[192,1024]{1,0:T(8,128)S(1)} %get-tuple-element.170) | copy-start | bytes 2359300
  537.4 7.7 %slice-start.1 = ((s8[8388608]{0:T(1024)(128)(4,1)}), s8[4194304]{0:T(1024)(128)(4,1)S(1)}, s32[]{:S(2)}) async-start(s8[8388608]{0:T(1024)(128)(4,1)} %bitcast.82), calls=%async_computation.12 | async-start | bytes 8388608
  545.1 2.9 copy-start.33
  548.0 0.9 copy-start.9
  548.0 0.9 copy-start.36
  548.1 1.0 copy-start.31
  548.1 1.0 copy-start.32
  550.1 54.5 %all-to-all-start.2 = ((f32[32,1,1160]{2,1,0:T(1,128)}), f32[32,1,1160]{2,1,0:T(1,128)S(1)}, u32[]{:S(2)}, u32[]{:S(2)}) async-start(f32[32,1,1160]{2,1,0:T(1,128)} %copy.75), calls=%async_computation.2 | async-start | bytes 327680 | tf_op jit(solution)/shard_map/all_to_all | solution.py:1454
  556.0 43.6 %copy-start.38 = (f32[192]{0:T(256)S(1)}, f32[192]{0:T(256)}, u32[]{:S(2)}) copy-start(f32[192]{0:T(256)} %get-tuple-element.196) | copy-start | bytes 2308
  599.5 4.0 copy-start.11
  603.5 3.2 copy-start.25
  603.6 3.2 copy-start.26
  606.7 3.1 copy-start.18
  620.8 1.7 copy-start.13
Sparse Core Ops, SparseCore 0:
  189.3 61.7 reduce-scatter.6
  254.0 60.2 reduce-scatter.8
  316.7 211.8 reduce-scatter.4
  530.7 88.9 reduce-scatter.10

commit v6 on v5

--- a/solution.py
+++ b/solution.py
@@ -99,6 +99,15 @@
         self.to_c = {"ctx": self.x * 2 + 1 - self.c}
         self.to_y = {"expert": 1 - self.y}
         self.to_z = {"dp": self.dp + 1 - 2 * self.z}
+
+    def peers(self):
+        found = []
+        for r in range(1, 8):
+            x, c, y = [
+                1 - v if r & bit else v for v, bit in ((self.x, 4), (self.c, 2), (self.y, 1))
+            ]
+            found.append((x * 4 + c * 2 + y, {"ctx": x * 2 + c, "expert": y}))
+        return found
 
 
 def plane_slot(x, c, y):
@@ -572,6 +581,7 @@
     grad_out,
     gates_ref,
     gate_grad_ref,
+    down_grad_ref,
     rows_v,
     g_v,
     gate_up_v,
@@ -579,6 +589,7 @@
     hidden_v,
     grad_v,
     total_v,
+    down_total,
     send_sem,
     recv_sem,
     local_sem,
@@ -587,7 +598,7 @@
     greet([here.to_y, here.to_c, here.to_x])
     send = Sender(send_sem, recv_sem)
     count = ffn_ref.shape[0]
-    experts = router_ref.shape[1]
+    experts = router_ref.shape[0]
     local_experts = down_hbm.shape[0]
     stages, got = block_gather(here, send, ffn_ref, local_sem.at[0], rows_v)
     stages[0]()
@@ -603,7 +614,12 @@
 
     def chunk(x, y):
         some = chip_rows(x, y, count)
-        logits = dot(rows_v[some, :], router_ref[...])
+        logits = lax.dot_general(
+            rows_v[some, :],
+            router_ref[...],
+            (((1,), (1,)), ((), ())),
+            preferred_element_type=f32,
+        )
         ids = lax.broadcasted_iota(jnp.int32, logits.shape, 1)
         routes = routes_ref[some, :]
         chosen = ids < 0
@@ -635,6 +651,21 @@
             )
             store.start()
             stores.append(store)
+        add_down(some, len(stores) == 3, len(stores) == 12)
+
+    def add_down(some, is_first, is_last):
+        tile = 512
+
+        @pl.loop(0, down_total.shape[1] // tile)
+        def _(i):
+            cols = pl.ds(pl.multiple_of(i * tile, tile), tile)
+            part = transposed_dot(hidden_v[some, :], g_v[some, cols])
+            if not is_first:
+                part = part + down_total[:, cols]
+            if is_last:
+                down_grad_ref[:, cols] = part.astype(bf16)
+            else:
+                down_total[:, cols] = part
 
     x, y = here.x, here.y
     for name in ("c", "own"):
@@ -669,9 +700,10 @@
             jax.ShapeDtypeStruct((total, 2 * experts * ff), bf16),
             jax.ShapeDtypeStruct((total, 128), f32),
             jax.ShapeDtypeStruct((total, 128), f32),
+            jax.ShapeDtypeStruct((ff, width), bf16),
         ],
         in_specs=[vmem] * 3 + [anywhere] * 3,
-        out_specs=[anywhere] * 3 + [vmem] * 2,
+        out_specs=[anywhere] * 3 + [vmem] * 3,
         scratch_shapes=[
             pltpu.VMEM((total, width), bf16),
             pltpu.VMEM((total, width), bf16),
@@ -680,6 +712,7 @@
             pltpu.VMEM((total, ff), bf16),
             pltpu.VMEM((total, 2 * ff), bf16),
             pltpu.VMEM((2 * ffn_in.shape[0], 128), f32),
+            pltpu.VMEM((ff, width), f32),
             pltpu.SemaphoreType.DMA((9,)),
             pltpu.SemaphoreType.DMA((9,)),
             pltpu.SemaphoreType.DMA((16,)),
@@ -692,7 +725,7 @@
             bytes_accessed=40 * 2**20,
             transcendentals=0,
         ),
-    )(ffn_in, route_rows, router_weight, g_rows, gate_up, down_proj)
+    )(ffn_in, route_rows, router_weight.T, g_rows, gate_up, down_proj)
 
 
 def next_expert_kernel(
@@ -750,7 +783,7 @@
 
 
 def weight_grad_kernel(
-    query_grad, kv_grad, branch, attended_owned, normed_owned, sums_ref,
+    query_grad, kv_grad, branch, attended_owned, normed_owned, down_part, sums_ref,
     pre_v, branch_v, attended_v, normed_v, send_sem, recv_sem, local_sem,
 ):
     here = Places()
@@ -763,7 +796,6 @@
     groups = lax.axis_size("dp")
     half = wide // 2
     low, high, last = pl.ds(0, half), pl.ds(half, half), pl.ds(wide, narrow)
-    b, _ = block_gather(here, send, branch, local_sem.at[0], branch_v)
     qa, _ = block_gather(
         here, send, query_grad.at[:, low], local_sem.at[1], pre_v, False, low
     )
@@ -771,20 +803,38 @@
         here, send, query_grad.at[:, high], local_sem.at[2], pre_v, False, high
     )
     kv, _ = block_gather(here, send, kv_grad, local_sem.at[3], pre_v, False, last)
-    loads = []
+    loads = [pltpu.make_async_copy(branch, branch_v, local_sem.at[0])]
     for device in range(spread):
         slot = plane_slot(device // 4, device // 2 % 2, device % 2)
         rows = pl.ds(slot * count, count)
         for source, target in ((attended_owned, attended_v), (normed_owned, normed_v)):
             loads.append(
                 pltpu.make_async_copy(
-                    source.at[device], target.at[rows], local_sem.at[4 + len(loads)]
+                    source.at[device], target.at[rows], local_sem.at[3 + len(loads)]
                 )
             )
 
+    output_rows = attended_v.shape[1] // groups * (branch.shape[1] // tile)
+    pre_rows = normed_v.shape[1] // groups * ((wide + narrow) // tile)
+    down_rows = down_part.shape[0] // groups
+    kept = [
+        pltpu.make_async_copy(
+            down_part.at[pl.ds(d * down_rows, down_rows), pl.ds(i * tile, tile)],
+            sums_ref.at[
+                pl.ds(
+                    d * (sums_ref.shape[0] // groups) + output_rows + pre_rows + i * down_rows,
+                    down_rows,
+                )
+            ],
+            local_sem.at[4 + 2 * spread + d * (down_part.shape[1] // tile) + i],
+        )
+        for d in range(groups)
+        for i in range(down_part.shape[1] // tile)
+    ]
+
     def start():
-        for load in loads:
-            load.start()
+        for copy in loads + kept:
+            copy.start()
 
     def product(left, right, base, first, tiles):
         rows = left.shape[1] // groups
@@ -799,54 +849,55 @@
                     d * rows : (d + 1) * rows
                 ]
 
-    output_rows = attended_v.shape[1] // groups * (branch.shape[1] // tile)
-
     def output_product():
         for load in loads:
             load.wait()
         product(attended_v, branch_v, 0, 0, branch.shape[1] // tile)
 
     steps = [
-        b[0], start, b[1], qa[0], b[2], qa[1], qb[0], b[3], output_product,
-        qa[2], qb[1], kv[0], qa[3],
+        qa[0], qb[0], kv[0], start, output_product, qa[1], qb[1], qa[2], kv[1], qb[2], qa[3],
         lambda: product(normed_v, pre_v, output_rows, 0, half // tile),
-        qb[2], kv[1], qb[3],
+        kv[2], qb[3],
         lambda: product(normed_v, pre_v, output_rows, half // tile, half // tile),
-        kv[2], kv[3],
+        kv[3],
         lambda: product(normed_v, pre_v, output_rows, wide // tile, narrow // tile),
     ]
     for step in steps:
         step()
+    for copy in kept:
+        copy.wait()
     send.finish()
 
 
-def weight_grads(query_grad, kv_grad, branch, attended_owned, normed_owned):
+def weight_grads(query_grad, kv_grad, branch, attended_owned, normed_owned, down_part):
     count, wide = query_grad.shape
     narrow, width = kv_grad.shape[1], branch.shape[1]
     spread = lax.axis_size(plane)
     tile = narrow
     elements = attended_owned.shape[2] * width + normed_owned.shape[2] * (wide + narrow)
+    elements += math.prod(down_part.shape)
+    groups = lax.axis_size("dp")
     vmem = pl.BlockSpec(memory_space=pltpu.VMEM)
     anywhere = pl.BlockSpec(memory_space=pl.ANY)
     return pl.pallas_call(
         weight_grad_kernel,
         out_shape=jax.ShapeDtypeStruct((elements // tile, tile), bf16),
-        in_specs=[anywhere] * 5,
+        in_specs=[anywhere] * 6,
         out_specs=vmem,
         scratch_shapes=[
             pltpu.VMEM((spread * count, wide + narrow), bf16),
             pltpu.VMEM((spread * count, width), bf16),
             pltpu.VMEM((spread * count, attended_owned.shape[2]), bf16),
             pltpu.VMEM((spread * count, normed_owned.shape[2]), bf16),
-            pltpu.SemaphoreType.DMA((36,)),
-            pltpu.SemaphoreType.DMA((36,)),
-            pltpu.SemaphoreType.DMA((4 + 2 * spread,)),
+            pltpu.SemaphoreType.DMA((27,)),
+            pltpu.SemaphoreType.DMA((27,)),
+            pltpu.SemaphoreType.DMA((4 + 2 * spread + groups * (down_part.shape[1] // tile),)),
         ],
         compiler_params=pltpu.CompilerParams(
             collective_id=5, has_side_effects=True, vmem_limit_bytes=56 * 2**20
         ),
         cost_estimate=pl.CostEstimate(flops=10**6, bytes_accessed=10**6, transcendentals=0),
-    )(query_grad, kv_grad, branch, attended_owned, normed_owned)
+    )(query_grad, kv_grad, branch, attended_owned, normed_owned, down_part)
 
 
 def arrive(got, name):
@@ -860,13 +911,17 @@
 
 def plane_sum_kernel(across, parts, *refs):
     lefts, weight_hbm = refs[:parts], refs[parts]
-    extra_ref = refs[parts + 1] if across else None
-    refs = refs[parts + 1 + across :]
+    refs = refs[parts + 1 :]
+    extra_ref, sources, targets = None, [], []
+    if across:
+        extra_ref, sources, targets = refs[0], refs[1:3], refs[4:6]
+        refs = (refs[3],) + refs[6:]
     (
         out_ref, left_v, weight_v, part_v, core_v, edge_v, last_v, send_sem, recv_sem, local_sem,
     ) = refs
     here = Places()
-    greet([here.to_y, here.to_c, here.to_x])
+    peers = here.peers() if across else []
+    greet([device for _, device in peers] or [here.to_y, here.to_c, here.to_x])
     send = Sender(send_sem, recv_sem)
     count = out_ref.shape[0]
     half = count // 2
@@ -894,6 +949,20 @@
         )
         for load in loads[-1]:
             load.start()
+    owned = []
+    for index, device in peers:
+        for source, target in zip(sources, targets):
+            owned.append(send(source.at[index], target.at[plane_index(here)], device))
+    kept = [
+        pltpu.make_async_copy(
+            source.at[plane_index(here)],
+            target.at[plane_index(here)],
+            local_sem.at[1 + 4 * parts + i],
+        )
+        for i, (source, target) in enumerate(zip(sources, targets))
+    ]
+    for copy in kept:
+        copy.start()
     weight_load.wait()
     to_core = []
 
@@ -956,10 +1025,14 @@
     last_x.wait_recv()
     last_y.wait_recv()
     out_ref[...] = out_ref[...] + last_v[0].astype(f32) + last_v[1].astype(f32)
+    for copy in owned:
+        copy.wait_recv()
+    for copy in kept:
+        copy.wait()
     send.finish()
 
 
-def plane_sum(lefts, weight, extra, collective_id):
+def plane_sum(lefts, weight, extra, owned, collective_id):
     across = extra is not None
     count = lefts[0].shape[0] // lax.axis_size(plane)
     width = weight.shape[1] if across else weight.shape[2]
@@ -973,9 +1046,10 @@
 
     return pl.pallas_call(
         kernel,
-        out_shape=jax.ShapeDtypeStruct((count, wide), f32),
-        in_specs=[anywhere] * (parts + 1) + [vmem] * across,
-        out_specs=vmem,
+        out_shape=[jax.ShapeDtypeStruct((count, wide), f32)]
+        + [jax.ShapeDtypeStruct(v.shape, v.dtype) for v in owned],
+        in_specs=[anywhere] * (parts + 1) + [vmem] * across + [anywhere] * len(owned),
+        out_specs=[vmem] + [anywhere] * len(owned),
         scratch_shapes=[
             pltpu.VMEM((4, 2 * count, parts * depth), bf16),
             pltpu.VMEM(weight.shape, bf16),
@@ -983,15 +1057,15 @@
             pltpu.VMEM((4, count, wide), bf16),
             pltpu.VMEM((2, count // 2, wide), bf16),
             pltpu.VMEM((2, count, wide), bf16),
-            pltpu.SemaphoreType.DMA((8,)),
-            pltpu.SemaphoreType.DMA((8,)),
-            pltpu.SemaphoreType.DMA((1 + 4 * parts,)),
+            pltpu.SemaphoreType.DMA((8 + 7 * len(owned),)),
+            pltpu.SemaphoreType.DMA((8 + 7 * len(owned),)),
+            pltpu.SemaphoreType.DMA((1 + 4 * parts + len(owned),)),
         ],
         compiler_params=pltpu.CompilerParams(
             collective_id=collective_id, has_side_effects=True, vmem_limit_bytes=60 * 2**20
         ),
         cost_estimate=pl.CostEstimate(flops=10**6, bytes_accessed=10**6, transcendentals=0),
-    )(*lefts, weight, *([extra] if across else []))
+    )(*lefts, weight, *([extra] if across else []), *owned)
 
 
 def head_softmax(queries, keys, visible):
@@ -1056,7 +1130,11 @@
     return lax.dot_general(a, b, (((0,), (0,)), ((), ())), preferred_element_type=f32)
 
 
-def attention_back_kernel(
+def back_heads(
+    first,
+    key_at,
+    value_at,
+    out_at,
     query_pre_ref,
     gain_ref,
     cosine_ref,
@@ -1068,18 +1146,17 @@
     pre_grad_ref,
     key_grad_ref,
     value_grad_ref,
-    gain_grad_ref,
 ):
     rows = query_pre_ref.shape[0]
     visible = visible_keys(rows, keys_ref.shape[0])
-    keys = keys_ref[...]
-    values = values_ref[...]
+    keys = keys_ref[:, pl.ds(key_at, HEAD_SIZE)]
+    values = values_ref[:, pl.ds(value_at, HEAD_SIZE)]
     scale = HEAD_SIZE ** (-0.5)
     gain_grad = jnp.zeros((rows, HEAD_SIZE), f32)
-    key_grad = jnp.zeros(keys_ref.shape, f32)
-    value_grad = jnp.zeros(keys_ref.shape, f32)
-    for h in range(query_pre_ref.shape[1] // HEAD_SIZE):
-        cols = slice(h * HEAD_SIZE, (h + 1) * HEAD_SIZE)
+    key_grad = jnp.zeros(keys.shape, f32)
+    value_grad = jnp.zeros(keys.shape, f32)
+    for h in range(QUERY_HEADS // KEY_VALUE_HEADS):
+        cols = pl.ds(first + h * HEAD_SIZE, HEAD_SIZE)
         queries = queries_ref[:, cols]
         grad = grad_ref[:, cols]
         probs = head_softmax(queries, keys, visible)
@@ -1096,9 +1173,87 @@
         inv = head_norm(v)
         gain_grad = gain_grad + u * v * inv
         pre_grad_ref[:, cols] = norm_back(v, inv, gain_ref[...], u).astype(bf16)
-    key_grad_ref[...] = (key_grad * scale).astype(key_grad_ref.dtype)
-    value_grad_ref[...] = value_grad.astype(value_grad_ref.dtype)
-    gain_grad_ref[0] = jnp.sum(gain_grad, axis=0, keepdims=True)
+    out = pl.ds(out_at, HEAD_SIZE)
+    key_grad_ref[:, out] = (key_grad * scale).astype(key_grad_ref.dtype)
+    value_grad_ref[:, out] = value_grad.astype(value_grad_ref.dtype)
+    return jnp.sum(gain_grad, axis=0, keepdims=True)
+
+
+def attention_back_kernel(*refs):
+    refs[-1][0] = back_heads(0, 0, 0, 0, *refs[:-1])
+
+
+def attention_back_gather_kernel(
+    query_pre_ref, gain_ref, cosine_ref, sine_ref, kv_ref, queries_ref, grad_ref, branch,
+    pre_grad_ref, key_grad_ref, value_grad_ref, gain_grad_ref, branch_rows,
+    send_sem, recv_sem, local_sem,
+):
+    here = Places()
+    greet([here.to_y, here.to_c, here.to_x])
+    send = Sender(send_sem, recv_sem)
+    stages, _ = block_gather(here, send, branch, local_sem.at[0], branch_rows)
+    group = query_pre_ref.shape[1] // KEY_VALUE_HEADS
+    narrow = kv_ref.shape[1] // 2
+
+    def heads(first, count):
+        @pl.loop(first, first + count)
+        def _(i):
+            at = pl.multiple_of(i * HEAD_SIZE, HEAD_SIZE)
+            gain_grad_ref[i] = back_heads(
+                pl.multiple_of(i * group, group),
+                at,
+                pl.multiple_of(narrow + i * HEAD_SIZE, HEAD_SIZE),
+                at,
+                query_pre_ref,
+                gain_ref,
+                cosine_ref,
+                sine_ref,
+                kv_ref,
+                kv_ref,
+                queries_ref,
+                grad_ref,
+                pre_grad_ref,
+                key_grad_ref,
+                value_grad_ref,
+            )
+
+    stages[0]()
+    heads(0, KEY_VALUE_HEADS - 1)
+    stages[1]()
+    heads(KEY_VALUE_HEADS - 1, 1)
+    stages[2]()
+    stages[3]()
+    send.finish()
+
+
+def attention_back_gather(query_pre, gain, cosine, sine, kv_all, queries, attended_grad, branch):
+    rows, wide = query_pre.shape
+    keys, both = kv_all.shape
+    vmem = pl.BlockSpec(memory_space=pltpu.VMEM)
+    anywhere = pl.BlockSpec(memory_space=pl.ANY)
+    return pl.pallas_call(
+        attention_back_gather_kernel,
+        out_shape=[
+            jax.ShapeDtypeStruct((rows, wide), bf16),
+            jax.ShapeDtypeStruct((keys, both // 2), f32),
+            jax.ShapeDtypeStruct((keys, both // 2), f32),
+            jax.ShapeDtypeStruct((KEY_VALUE_HEADS, 1, HEAD_SIZE), f32),
+            jax.ShapeDtypeStruct((lax.axis_size(plane) * rows, branch.shape[1]), bf16),
+        ],
+        in_specs=[vmem] * 7 + [anywhere],
+        out_specs=[vmem] * 4 + [anywhere],
+        scratch_shapes=[
+            pltpu.SemaphoreType.DMA((9,)),
+            pltpu.SemaphoreType.DMA((9,)),
+            pltpu.SemaphoreType.DMA((1,)),
+        ],
+        compiler_params=pltpu.CompilerParams(
+            collective_id=6, has_side_effects=True, vmem_limit_bytes=48 * 2**20
+        ),
+        cost_estimate=pl.CostEstimate(flops=10**6, bytes_accessed=10**6, transcendentals=0),
+    )(
+        query_pre, gain.reshape(1, HEAD_SIZE), cosine, sine, kv_all, queries, attended_grad, branch
+    )
 
 
 def attention_back(query_pre, gain, cosine, sine, kv_all, queries, attended_grad):
@@ -1282,22 +1437,19 @@
 
     gates = gates_of(ffn_in, routes)
     if small_plane():
-        rows, hidden, grads, gates_mine, totals = gather_first_expert(
+        rows, hidden, grads, gates_mine, totals, down_part = gather_first_expert(
             ffn_in, route_rows, router_weight, g_rows, gate_up, down_proj
         )
         hiddens = [hidden]
-        down_parts = [dot(hidden.T, g_rows).astype(bf16)]
-        rows, grads, attended_owned, normed_owned = lax.optimization_barrier(
-            ((rows, grads, attended_owned, normed_owned), down_parts)
-        )[0]
-        attended_owned, normed_owned = owned(attended_owned), owned(normed_owned)
+        down_parts = [down_part]
+        rows, grads = after((rows, grads), down_parts)
         hidden, grads, gate_grads = last_expert(
             1, expert_count, rows, g_rows, gates_mine, totals, gate_up, down_proj, grads
         )
         hiddens.append(hidden)
         projected_grads = [grads]
-        down_parts.append(dot(hidden.T, g_rows).astype(bf16))
-        gate_up_parts = [dot(after(rows, down_parts).T, grads).astype(bf16)]
+        gate_up_parts = [dot(rows.T, grads).astype(bf16)]
+        down_late = dot(after(hidden, gate_up_parts).T, g_rows).astype(bf16)
     else:
         rows = lax.all_gather(ffn_in, plane, axis=0, tiled=True)
         first_expert = lax.axis_index(plane) * local_experts
@@ -1326,7 +1478,6 @@
         [lax.psum_scatter(v, "dp", scatter_dimension=0, tiled=True) for v in parts]
         for parts in (down_parts, gate_up_parts)
     ]
-    down_grad = jnp.stack([v.astype(f32) for v in down_low])
     gate_up_grad = jnp.stack(
         [
             part.astype(f32)
@@ -1335,10 +1486,12 @@
         ]
     )
     projected_grads, hiddens = lax.optimization_barrier(
-        ((projected_grads, hiddens), down_parts, gate_up_parts, attended_owned, normed_owned)
+        ((projected_grads, hiddens), down_parts, gate_up_parts)
     )[0]
     if small_plane():
-        back = plane_sum(projected_grads, gate_up, gate_grads, 3)
+        back, attended_owned, normed_owned = plane_sum(
+            projected_grads, gate_up, gate_grads, [attended_owned, normed_owned], 3
+        )
         back_sum = back[:, :MODEL_WIDTH]
         gate_grad = (
             back[:, MODEL_WIDTH : MODEL_WIDTH + expert_count]
@@ -1374,9 +1527,12 @@
     ffn_gain_local = jnp.sum(ffn_in_grad * residual * scale_ffn, axis=0)
     branch_low = residual_grad.astype(bf16)
     attended_grad = backward_dot(branch_low, o_weights).astype(bf16)
-    query_pre_grad, key_grad_all, value_grad_all, query_gain_parts = attention_back(
-        query_pre, query_gain, cosine, signed_sine, kv_all, queries, attended_grad
-    )
+    operands = (query_pre, query_gain, cosine, signed_sine, kv_all, queries, attended_grad)
+    if small_plane():
+        *attention_grads, branch_rows = attention_back_gather(*operands, branch_low)
+    else:
+        attention_grads = attention_back(*operands)
+    query_pre_grad, key_grad_all, value_grad_all, query_gain_parts = attention_grads
     query_gain_local = jnp.sum(query_gain_parts, axis=(0, 1))
     pair_grads = jnp.stack([key_grad_all[:prompt_all], value_grad_all[:prompt_all]]).astype(bf16)
     prompt_grads = ctx_sum(pair_grads)
@@ -1394,7 +1550,9 @@
     key_value_grad = jnp.concatenate([key_pre_grad, value_gradient.astype(bf16)], axis=1)
     if small_plane():
         local = [
-            weight_grads(query_pre_grad, key_value_grad, branch_low, attended_owned, normed_owned)
+            weight_grads(
+                query_pre_grad, key_value_grad, branch_rows, attended_owned, normed_owned, down_late
+            )
         ]
     else:
         branch_rows = lax.all_gather(branch_low, plane, axis=0, tiled=True)
@@ -1417,7 +1575,7 @@
     attn_gain_local = jnp.sum(normed_grad * inputs * scale_in, axis=0)
     hidden_grad = residual_grad + norm_back(inputs, scale_in, attn_gain, normed_grad)
     if small_plane():
-        moe_sum = plane_sum(after(hiddens, local), down_proj, None, 4)
+        moe_sum = plane_sum(after(hiddens, local), down_proj, None, [], 4)[0]
     block_out = (residual + moe_sum).astype(bf16)
     local = lax.optimization_barrier((local, gate_up_low, down_low))[0]
     summed = [
@@ -1433,10 +1591,13 @@
                 [v[i : i + rows] for i in range(0, v.shape[0], rows)], axis=1
             )
 
+        end = cut + share * ((wide + 2 * narrow) // tile)
         output_sum = untile(summed[0][:cut], wide // device_count)
-        pre_sum = untile(summed[0][cut:], share)
+        pre_sum = untile(summed[0][cut:end], share)
+        down_low.append(untile(summed[0][end:], hidden_ff // dp_count))
     else:
         output_sum, pre_sum = summed
+    down_grad = jnp.stack([v.astype(f32) for v in down_low])
 
     small = jnp.concatenate(
         [

time: 640 us -> 624 us (0.975)
  blocking collectives: 15.7 us -> 0 us
  waiting for transfers between devices: 47.3 us -> 61.9 us
  matrix products: 72.8 us -> 63.8 us
    reduce_scatter x1, waiting for transfers between devices: 6.6 us -> 58.2 us  [body(): lax.psum_scatter(v, 'dp', scatter_dimension=0, tiled=True).astype(f32)]
    pallas_call x1, Pallas kernels: 99.4 us -> 73.3 us  [weight_grads(): pl.pallas_call(weight_grad_kernel, out_shape=jax.ShapeDtypeStruct((elemen...]
    all_to_all x1 -> x0, waiting for transfers between devices: 17.9 us -> none  [owned(): return lax.all_to_all(v, plane, split_axis=0, concat_axis=0, tiled=True)]
    pallas_call x3, Pallas kernels: 127 us -> 143 us  [the longest x2 105 us: plane_sum(): pl.pallas_call(kernel, out_shape=[jax.ShapeDtypeStruct((count, wide), f32...]
    all_to_all x1 -> x0, blocking collectives: 15.7 us -> none  [owned(): return lax.all_to_all(v, plane, split_axis=0, concat_axis=0, tiled=True)]
    reduce_scatter x3 -> x2, waiting for transfers between devices: 15.2 us -> 2.32 us  [body(): lax.psum_scatter(v, 'dp', scatter_dimension=0, tiled=True)]
    dot_general x10 -> x9, matrix products: 68.1 us -> 58.5 us  [dot(): return jnp.dot(a, b, preferred_element_type=f32)]
  transfers between devices with their start and end apart: 9 -> 7, of which waited for: 5 -> 3; matrix products, arithmetic and copies ran while one was open for 16% -> 17% of each run, Pallas kernels for 40% -> 39%
where the time goes in v6:
time: 624 us; the launch traced here: 615 us
  Pallas kernels  414 us (66%)
  matrix products  63.8 us (10%)
  waiting for transfers between devices  61.9 us (10%)
  other arithmetic  29.5 us (5%)
  local copies, waits for them, and re-layouts  24.3 us (4%)
  between operations  15.1 us (2%)
  starting transfers between devices  7.26 us (1%)
    pallas_call x1, Pallas kernels, fetch_and_attend(): pl.pallas_call(fetch_kernel, out_shape=[jax.ShapeDtypeStruct((half, 2 * n...  125 us
    pallas_call x2, Pallas kernels, plane_sum(): pl.pallas_call(kernel, out_shape=[jax.ShapeDtypeStruct((count, wide), f32...  105 us
    pallas_call x1, Pallas kernels, weight_grads(): pl.pallas_call(weight_grad_kernel, out_shape=jax.ShapeDtypeStruct((elemen...  73.3 us
    dot_general x9, matrix products, dot(): return jnp.dot(a, b, preferred_element_type=f32)  58.5 us
    reduce_scatter x1, waiting for transfers between devices, body(): lax.psum_scatter(v, 'dp', scatter_dimension=0, tiled=True).astype(f32)  58.2 us
    pallas_call x1, Pallas kernels, gather_first_expert(): pl.pallas_call(first_expert_kernel, out_shape=[jax.ShapeDtypeStruct((tota...  48 us
    pallas_call x1, Pallas kernels, attention_back_gather(): pl.pallas_call(attention_back_gather_kernel, out_shape=[jax.ShapeDtypeStr...  38.1 us
    pallas_call x1, Pallas kernels, last_expert(): pl.pallas_call(kernel, grid=(4,), out_shape=[jax.ShapeDtypeStruct((total,...  23.6 us
  transfers between devices with their start and end apart: 7, of which 3 were waited for; matrix products, arithmetic and copies ran while one was open for 17% of the time, Pallas kernels for 39%

profile of v6, /device:TPU:0, one launch (start us, length us, event | category | flops | bytes accessed | tf_op | source)
XLA Modules:
  0.0 615.5 jit_solution(6701548283617770683)
XLA Ops:
  7.3 1.5 copy.59.routes_ref
  8.8 1.1 fusion.21
  10.0 125.4 %shard_map.237 = (bf16[1024,1024]{1,0:T(8,128)(2,1)}, bf16[1024,4096]{1,0:T(8,128)(2,1)}, bf16[2048,2048]{1,0:T(8,128)(2,1)}, bf16[1536,2048]{1,0:T(8,128)(2,1)}...) custom-call(bf16[192,2048]{1,0:T(8,128)(2,1)} %hidden_ref.1, ...), custom_call_target="tpu_custom_call" | custom-call | flops 14495514624 | bytes 62914560 | tf_op jit(solution)/shard_map/pallas_call | solution.py:490
  135.4 48.0 %shard_map.238 = (bf16[1536,2048]{1,0:T(8,128)(2,1)}, bf16[1536,768]{1,0:T(8,128)(2,1)}, bf16[1536,3072]{1,0:T(8,128)(2,1)}, f32[1536,128]{1,0:T(8,128)}, f32[15...) custom-call(bf16[192,2048]{1,0:T(8,128)(2,1)} %get-tuple-element.55.ffn_ref, s32[1536,8]{1,0:T(8,128)} %get-tuple-element.56.routes_ref, ...), custom_call_target="tpu_custom_call" | custom-call | flops 14495514624 | bytes 41943040 | tf_op jit(solution)/shard_map/pallas_call | solution.py:695
  183.4 23.6 %shard_map.239 = (bf16[1536,768]{1,0:T(8,128)(2,1)}, bf16[1536,3072]{1,0:T(8,128)(2,1)}, bf16[1536,128]{1,0:T(8,128)(2,1)}) custom-call(bf16[1536,2048]{1,0:T(8,128)(2,1)} %get-tuple-element.61.refs_0_, bf16[1536,2048]{1,0:T(8,128)(2,1)} %get-tuple-element.57.g_hbm.refs_1_, f32[1536,128]{1,0:T(8,128)} %get-tuple-element.62.refs_2_, ...), custom_call_target="tpu_custom_call", output_to_operand_aliasing={{1}: (6, {})} | custom-call | flops 1000000 | bytes 1000000 | tf_op jit(solution)/shard_map/pallas_call | solution.py:763
  207.0 24.3 %convolution_convert_fusion = bf16[2048,3072]{1,0:T(8,128)(2,1)} fusion(bf16[1536,2048]{1,0:T(8,128)(2,1)S(1)} %copy-done.12, bf16[1536,3072]{1,0:T(8,128)(2,1)} %get-tuple-element.73.refs_0_), kind=kOutput, calls=%fused_computation | convolution fusion | flops 19333644288 | bytes 28311552 | tf_op jit(solution)/shard_map/dot_general | solution.py:1305
  231.5 0.6 copy-done.26
  232.3 62.0 %shard_map.240 = (f32[192,2176]{1,0:T(8,128)}, bf16[8,192,512]{2,1,0:T(8,128)(2,1)}, bf16[8,192,256]{2,1,0:T(8,128)(2,1)}) custom-call(bf16[1536,3072]{1,0:T(8,128)(2,1)} %get-tuple-element.73.refs_0_, bf16[2,2048,1536]{2,1,0:T(8,128)(2,1)} %refs_1_.1, bf16[1536,128]{1,0:T(8,128)(2,1)} %get-tuple-element.74.refs_2_, ...), custom_call_target="tpu_custom_call" | custom-call | flops 1000000 | bytes 1000000 | tf_op jit(solution)/shard_map/pallas_call | solution.py:1047
  295.0 1.2 multiply_reduce_fusion.5
  296.4 3.5 multiply_reduce_fusion
  299.9 1.7 fusion.27
  301.6 6.5 %fusion.37 = bf16[192,2048]{1,0:T(8,128)(2,1)S(1)} fusion(bf16[192,2048]{1,0:T(8,128)(2,1)S(1)} %get-tuple-element.167.branch, bf16[2048,2048]{1,0:T(8,128)(2,1)} %get-tuple-element.78), kind=kOutput, calls=%fused_computation.116 | convolution fusion | flops 1610612736 | bytes 9961472 | tf_op jit(solution)/shard_map/dot_general | solution.py:1305
  308.1 2.9 select_convert_fusion.1
  311.1 1.3 pad_maximum_fusion.1.grad_ref
  312.9 38.1 %shard_map.241 = (bf16[192,4096]{1,0:T(8,128)(2,1)S(1)}, f32[576,512]{1,0:T(8,128)S(1)}, f32[576,512]{1,0:T(8,128)S(1)}, f32[4,1,128]{2,1,0:T(1,128)S(1)}, bf16[1536,2048]{1,0:T(8,128)(2,1)}) custom-call(f32[192,4096]{1,0:T(8,128)} %get-tuple-element.70.query_pre_ref, f32[1,128]{1,0:T(1,128)S(1)} %bitcast.83, f32[192,128]{1,0:T(8,128)S(1)} %copy-done.2, ...), custom_call_target="tpu_custom_call" | custom-call | flops 1000000 | bytes 1000000 | tf_op jit(solution)/shard_map/pallas_call | solution.py:1234
  351.0 1.2 copy-done
  352.1 0.9 convert.30
  353.0 1.2 fusion.11
  354.2 0.8 copy-done.7
  355.0 0.8 fusion.17
  356.3 1.4 collective-permute-done.1
  357.7 1.8 add_convert_fusion.1
  359.5 0.8 collective-permute-start.2
  360.4 9.3 %convolution_convert_fusion.1.down_part = bf16[768,2048]{1,0:T(8,128)(2,1)} fusion(bf16[1536,768]{1,0:T(8,128)(2,1)} %get-tuple-element.88.refs_1_, bf16[1536,2048]{1,0:T(8,128)(2,1)} %get-tuple-element.57.g_hbm.refs_1_), kind=kOutput, calls=%fused_computation.1 | convolution fusion | flops 4833411072 | bytes 11796480 | tf_op jit(solution)/shard_map/dot_general | solution.py:1305
  369.7 1.2 reshape.220
  370.8 0.7 concatenate.67
  371.5 1.2 convert_add_fusion
  372.7 0.7 slice_bitcast_fusion.3
  373.6 0.9 constant_dynamic-update-slice_fusion
  374.9 1.2 multiply_reduce_fusion.4
  376.1 1.0 copy.63
  377.2 0.8 copy.64
  378.0 0.8 copy.65
  378.8 1.2 mul.262
  380.6 2.0 fusion.14
  382.6 0.8 maximum_maximum_fusion.kv_grad
  383.4 73.3 %shard_map.242 = bf16[3840,1024]{1,0:T(8,128)(2,1)} custom-call(bf16[192,4096]{1,0:T(8,128)(2,1)} %copy-done, bf16[192,1024]{1,0:T(8,128)(2,1)} %maximum_maximum_fusion.kv_grad, bf16[1536,2048]{1,0:T(8,128)(2,1)} %get-tuple-element.83.branch, bf16[8,192,512]{2,1,0:T(8,128)(2,1)} %get-tuple-element.84.attended_owned, ...), custom_call_target="tpu_custom_call" | custom-call | flops 1000000 | bytes 1000000 | tf_op jit(solution)/shard_map/pallas_call | solution.py:882
  456.7 2.3 reduce-scatter.4.cloned.1.call-done
  459.1 0.7 reshape.223
  459.9 1.8 fusion.36
  461.7 0.6 reshape.225
  462.6 2.7 fusion.39
  465.4 0.8 broadcast_select_fusion.1
  466.8 8.6 %fusion.38 = f32[192,1024]{1,0:T(8,128)S(1)} fusion(bf16[192,4096]{1,0:T(8,128)(2,1)S(1)} %copy-done.1, bf16[1024,4096]{1,0:T(8,128)(2,1)} %get-tuple-element.90), kind=kOutput, calls=%fused_computation.117 | convolution fusion | flops 1610612736 | bytes 10747904 | tf_op jit(solution)/shard_map/dot_general | solution.py:1305
  475.4 2.9 broadcast_select_fusion.3
  478.4 0.6 fusion.10
  479.5 0.8 copy.69
  480.4 5.8 all-to-all-start
  486.2 43.3 %shard_map.243 = f32[192,2048]{1,0:T(8,128)} custom-call(bf16[1536,768]{1,0:T(8,128)(2,1)} %get-tuple-element.87.refs_0_, bf16[1536,768]{1,0:T(8,128)(2,1)} %get-tuple-element.88.refs_1_, bf16[2,768,2048]{2,1,0:T(8,128)(2,1)} %refs_2_.1), custom_call_target="tpu_custom_call" | custom-call | flops 1000000 | bytes 1000000 | tf_op jit(solution)/shard_map/pallas_call | solution.py:1047
  529.5 3.9 fusion.7
  533.4 1.1 add_convert_fusion
  534.7 0.7 copy.70
  535.4 0.6 fusion.33
  536.0 0.6 fusion.34
  536.6 1.3 bitcast_convert_fusion
  537.9 2.1 slice_bitcast_fusion.1
  540.0 3.1 maximum_convert_fusion
  543.1 58.2 %reduce-scatter.8.cloned.1.call-done = bf16[960,1024]{1,0:T(8,128)(2,1)} async-done(((bf16[3840,1024]{1,0:T(8,128)(2,1)}), bf16[960,1024]{1,0:T(8,128)(2,1)}) %reduce-scatter.8.cloned.1.call-update) | async-done | bytes 1966096 | tf_op jit(solution)/shard_map/reduce_scatter | solution.py:1582
  601.3 1.1 fusion.29
  602.4 1.1 pad_maximum_fusion.3
  603.5 0.8 copy-done.8
  604.6 1.9 pad_maximum_fusion
  606.7 1.0 pad_maximum_fusion.2
  607.7 0.7 fusion.30
  (132 shorter events, 5.7 us)
Async XLA Ops:
  7.2 449.5 %reduce-scatter.6.cloned.1.call-start = ((), (), s32[]{:S(2)}) async-start(), calls=%async_computation.5 | async-start | bytes 3932160 | tf_op jit(solution)/shard_map/reduce_scatter | solution.py:1478
  183.4 275.6 %reduce-scatter.4.cloned.1.call-start = ((), (), s32[]{:S(2)}) async-start(), calls=%async_computation.4 | async-start | bytes 15728640 | tf_op jit(solution)/shard_map/reduce_scatter | solution.py:1478
  183.4 23.6 %copy-start.12 = (bf16[1536,2048]{1,0:T(8,128)(2,1)S(1)}, bf16[1536,2048]{1,0:T(8,128)(2,1)}, u32[]{:S(2)}) copy-start(bf16[1536,2048]{1,0:T(8,128)(2,1)} %get-tuple-element.61.refs_0_) | copy-start | bytes 18874372
  231.4 0.7 copy-start.26
  231.4 369.8 %reduce-scatter.8.cloned.1.call-start = ((), (), s32[]{:S(2)}) async-start(), calls=%async_computation.6 | async-start | bytes 9830400 | tf_op jit(solution)/shard_map/reduce_scatter | solution.py:1582
  232.2 62.0 %copy-start.21 = (bf16[192,2048]{1,0:T(8,128)(2,1)S(1)}, bf16[192,2048]{1,0:T(8,128)(2,1)}, u32[]{:S(2)}) copy-start(bf16[192,2048]{1,0:T(8,128)(2,1)} %get-tuple-element.55.ffn_ref) | copy-start | bytes 2359300
  232.2 62.0 %copy-start.36 = (bf16[2048,16]{0,1:T(8,128)(2,1)S(1)}, bf16[2048,16]{0,1:T(8,128)(2,1)}, u32[]{:S(2)}) copy-start(bf16[2048,16]{0,1:T(8,128)(2,1)} %param.23) | copy-start | bytes 196612
  232.2 63.9 %copy-start.6 = (f32[192,2048]{1,0:T(8,128)S(1)}, f32[192,2048]{1,0:T(8,128)}, u32[]{:S(2)}) copy-start(f32[192,2048]{1,0:T(8,128)} %get-tuple-element.54) | copy-start | bytes 4718596
  294.3 2.1 copy-start.29
  294.7 5.1 copy-start.18
  294.9 4.9 copy-start.27
  296.2 3.7 copy-start.32
  296.4 3.5 copy-start.20
  299.9 8.2 %slice-start.3 = ((s8[8388608]{0:T(1024)(128)(4,1)}), s8[4194304]{0:T(1024)(128)(4,1)S(1)}, s32[]{:S(2)}) async-start(s8[8388608]{0:T(1024)(128)(4,1)} %bitcast.95), calls=%async_computation.10 | async-start | bytes 8388608
  301.6 6.5 %slice-start.4 = ((s8[8388608]{0:T(1024)(128)(4,1)}), s8[4194304]{0:T(1024)(128)(4,1)S(1)}, s32[]{:S(2)}) async-start(s8[8388608]{0:T(1024)(128)(4,1)} %bitcast.95), calls=%async_computation.11 | async-start | bytes 8388608
  311.0 1.3 copy-start.2
  311.0 1.8 copy-start.3
  311.0 1.8 copy-start.4
  311.1 1.8 copy-start.5
  351.0 1.2 copy-start
  354.2 0.8 copy-start.7
  355.8 1.9 collective-permute-start.1
  356.2 15.3 %collective-permute-start = (bf16[2,128,512]{2,1,0:T(8,128)(2,1)}, bf16[2,128,512]{2,1,0:T(8,128)(2,1)}, u32[]{:S(2)}, u32[]{:S(2)}) collective-permute-start(bf16[2,128,512]{2,1,0:T(8,128)(2,1)} %get-tuple-element.189), channel_id=1, source_target_pairs={{0,2},{2,0},{4,6},{6,4},{1,3},{3,1},{5,7},{7,5},{8,10},{10,8},{12,... | collective-permute-start | bytes 786440 | tf_op jit(solution)/shard_map/ppermute | solution.py:66
  359.5 12.0 %copy-start.33 = (f32[128]{0:T(128)S(1)}, f32[128]{0:T(128)}, u32[]{:S(2)}) copy-start(f32[128]{0:T(128)} %param.20) | copy-start | bytes 1540
  359.5 12.0 %collective-permute-start.2 = (bf16[2,128,512]{2,1,0:T(8,128)(2,1)}, bf16[2,128,512]{2,1,0:T(8,128)(2,1)}, u32[]{:S(2)}, u32[]{:S(2)}) collective-permute-start(bf16[2,128,512]{2,1,0:T(8,128)(2,1)} %add_convert_fusion.1), channel_id=1, source_target_pairs={{0,4},{2,6},{4,0},{6,2},{1,5},{3,7},{5,1},{7,3},{8,12},{10,14},{12... | collective-permute-start | bytes 786440 | tf_op jit(solution)/shard_map/ppermute | solution.py:66
  369.6 3.1 copy-start.17
  372.7 1.8 copy-start.22
  376.1 4.4 copy-start.16
  378.7 1.6 copy-start.23
  380.6 2.0 slice-start.2
  456.6 2.4 copy-start.30
  456.7 3.2 copy-start.19
  456.7 3.2 copy-start.28
  459.9 2.5 copy-start.9
  462.6 2.7 copy-start.13
  462.6 2.7 copy-start.34
  462.6 2.7 copy-start.35
  465.4 1.4 copy-start.1
  465.4 10.0 %slice-start = ((s8[8388608]{0:T(1024)(128)(4,1)}), s8[4194304]{0:T(1024)(128)(4,1)S(1)}, s32[]{:S(2)}) async-start(s8[8388608]{0:T(1024)(128)(4,1)} %bitcast.84), calls=%async_computation.7 | async-start | bytes 8388608
  466.2 12.1 %copy-start.14 = (f32[192,1024]{1,0:T(8,128)}, f32[192,1024]{1,0:T(8,128)S(1)}, u32[]{:S(2)}) copy-start(f32[192,1024]{1,0:T(8,128)S(1)} %get-tuple-element.185) | copy-start | bytes 2359300
  466.2 12.1 %copy-start.15 = (f32[192,1024]{1,0:T(8,128)}, f32[192,1024]{1,0:T(8,128)S(1)}, u32[]{:S(2)}) copy-start(f32[192,1024]{1,0:T(8,128)S(1)} %get-tuple-element.186) | copy-start | bytes 2359300
  466.8 8.6 %slice-start.1 = ((s8[8388608]{0:T(1024)(128)(4,1)}), s8[4194304]{0:T(1024)(128)(4,1)S(1)}, s32[]{:S(2)}) async-start(s8[8388608]{0:T(1024)(128)(4,1)} %bitcast.84), calls=%async_computation.8 | async-start | bytes 8388608
  475.4 2.9 copy-start.25
  478.3 0.9 copy-start.10
  478.4 0.9 copy-start.31
  478.4 1.0 copy-start.24
  480.4 54.1 %all-to-all-start = ((f32[32,1,1160]{2,1,0:T(1,128)}), f32[32,1,1160]{2,1,0:T(1,128)S(1)}, u32[]{:S(2)}, u32[]{:S(2)}) async-start(f32[32,1,1160]{2,1,0:T(1,128)} %copy.69), calls=%async_computation | async-start | bytes 327680 | tf_op jit(solution)/shard_map/all_to_all | solution.py:1615
  529.5 3.9 copy-start.11
  602.4 1.9 copy-start.8
Sparse Core Ops, SparseCore 0:
  183.5 61.1 reduce-scatter.5
  247.1 211.8 reduce-scatter.3
  461.3 139.8 reduce-scatter.7

commit v7 on v6

--- a/solution.py
+++ b/solution.py
@@ -281,13 +281,17 @@
     g_blocks,
     route_blocks,
     kv_all_out,
+    normed_out,
+    attended_out,
+    query_pre_out,
+    queries_out,
+    key_pre_ref,
+    residual_ref,
+    ffn_ref,
     normed_owned,
     attended_owned,
     query_pre_ref,
-    key_pre_ref,
     queries_ref,
-    residual_ref,
-    ffn_ref,
     normed_ref,
     attended_ref,
     kv_own,
@@ -324,6 +328,10 @@
         pltpu.make_async_copy(q_other, q_out, local_sem.at[5]),
         pltpu.make_async_copy(o_other, o_out, local_sem.at[6]),
         pltpu.make_async_copy(kv_all, kv_all_out, local_sem.at[7]),
+        pltpu.make_async_copy(normed_owned, normed_out, local_sem.at[11]),
+        pltpu.make_async_copy(attended_owned, attended_out, local_sem.at[12]),
+        pltpu.make_async_copy(query_pre_ref, query_pre_out, local_sem.at[13]),
+        pltpu.make_async_copy(queries_ref, queries_out, local_sem.at[14]),
     ]
 
     def part_of(size, which):
@@ -355,6 +363,7 @@
                 ],
                 axis=1,
             )
+        stores[4].start()
         for load in loads[:3]:
             load.wait()
         project(normed_ref, kv_own, kv_pre, 0, 0, 2 * narrow // tile, False)
@@ -398,6 +407,7 @@
             exchange[name].wait_recv()
         exchange["own"].wait()
         stores[3].start()
+        stores[6].start()
 
     group = 4
     pieces = 4
@@ -425,6 +435,8 @@
                 attended_owned[lax.rem(head, spread), :, pl.ds(at, HEAD_SIZE)] = attended
 
     def output_own():
+        stores[5].start()
+        stores[7].start()
         loads[3].wait()
         project(attended_ref, o_own, residual_ref, 0, 0, width // tile, False)
 
@@ -499,14 +511,18 @@
             jax.ShapeDtypeStruct((spread, rows, width // spread), bf16),
             jax.ShapeDtypeStruct((spread, rows, wide // spread), bf16),
             jax.ShapeDtypeStruct((rows, wide), f32),
+            jax.ShapeDtypeStruct((rows, wide), bf16),
             jax.ShapeDtypeStruct((rows, narrow), f32),
-            jax.ShapeDtypeStruct((rows, wide), bf16),
             jax.ShapeDtypeStruct((rows, width), f32),
             jax.ShapeDtypeStruct((rows, width), bf16),
         ],
         in_specs=[vmem] * 7 + [anywhere] * 6,
-        out_specs=[anywhere] * 6 + [vmem] * 7,
+        out_specs=[anywhere] * 10 + [vmem] * 3,
         scratch_shapes=[
+            pltpu.VMEM((spread, rows, width // spread), bf16),
+            pltpu.VMEM((spread, rows, wide // spread), bf16),
+            pltpu.VMEM((rows, wide), f32),
+            pltpu.VMEM((rows, wide), bf16),
             pltpu.VMEM((rows, width), bf16),
             pltpu.VMEM((rows, wide), bf16),
             pltpu.VMEM((half, 2 * narrow), bf16),
@@ -520,7 +536,7 @@
             pltpu.VMEM((keys, 2 * narrow), bf16),
             pltpu.SemaphoreType.DMA((copies,)),
             pltpu.SemaphoreType.DMA((copies,)),
-            pltpu.SemaphoreType.DMA((11,)),
+            pltpu.SemaphoreType.DMA((15,)),
         ],
         compiler_params=pltpu.CompilerParams(
             collective_id=1, has_side_effects=True, vmem_limit_bytes=60 * 2**20
@@ -702,7 +718,7 @@
             jax.ShapeDtypeStruct((total, 128), f32),
             jax.ShapeDtypeStruct((ff, width), bf16),
         ],
-        in_specs=[vmem] * 3 + [anywhere] * 3,
+        in_specs=[anywhere] + [vmem] * 2 + [anywhere] * 3,
         out_specs=[anywhere] * 3 + [vmem] * 3,
         scratch_shapes=[
             pltpu.VMEM((total, width), bf16),
@@ -898,6 +914,42 @@
         ),
         cost_estimate=pl.CostEstimate(flops=10**6, bytes_accessed=10**6, transcendentals=0),
     )(query_grad, kv_grad, branch, attended_owned, normed_owned, down_part)
+
+
+def untile_kernel(sums_ref, down_ref, output_ref, query_ref, key_ref, value_ref, downs_ref):
+    tile = sums_ref.shape[1]
+    at = 0
+
+    def take(rows):
+        nonlocal at
+        part = sums_ref[at : at + rows, :].astype(f32)
+        at = at + rows
+        return part
+
+    for out in (output_ref, query_ref):
+        for first in range(0, out.shape[1], tile):
+            out[:, first : first + tile] = take(out.shape[0])
+    both = take(key_ref.shape[0])
+    key_ref[...] = both[:, : key_ref.shape[1]]
+    value_ref[...] = both[:, key_ref.shape[1] :]
+    downs_ref[0] = down_ref[...].astype(f32)
+    for first in range(0, downs_ref.shape[2], tile):
+        downs_ref[1, :, first : first + tile] = take(downs_ref.shape[1])
+
+
+def untile(sums, down, output_rows, wide, share, narrow):
+    vmem = pl.BlockSpec(memory_space=pltpu.VMEM)
+    rows, width = down.shape
+    shapes = [
+        (output_rows, width), (share, wide), (share, narrow), (share, narrow), (2, rows, width)
+    ]
+    return pl.pallas_call(
+        untile_kernel,
+        out_shape=[jax.ShapeDtypeStruct(shape, f32) for shape in shapes],
+        in_specs=[vmem] * 2,
+        out_specs=[vmem] * 5,
+        compiler_params=pltpu.CompilerParams(vmem_limit_bytes=32 * 2**20),
+    )(sums, down)
 
 
 def arrive(got, name):
@@ -1369,8 +1421,8 @@
             normed_owned,
             attended_owned,
             query_pre,
+            queries,
             key_pre,
-            queries,
             residual,
             ffn_in,
         ) = fetch_and_attend(
@@ -1578,26 +1630,18 @@
         moe_sum = plane_sum(after(hiddens, local), down_proj, None, [], 4)[0]
     block_out = (residual + moe_sum).astype(bf16)
     local = lax.optimization_barrier((local, gate_up_low, down_low))[0]
-    summed = [
-        lax.psum_scatter(v, "dp", scatter_dimension=0, tiled=True).astype(f32) for v in local
-    ]
+    summed = [lax.psum_scatter(v, "dp", scatter_dimension=0, tiled=True) for v in local]
     share = MODEL_WIDTH // device_count
     if small_plane():
-        tile = summed[0].shape[1]
-        cut = wide // device_count * (MODEL_WIDTH // tile)
-
-        def untile(v, rows):
-            return jnp.concatenate(
-                [v[i : i + rows] for i in range(0, v.shape[0], rows)], axis=1
-            )
-
-        end = cut + share * ((wide + 2 * narrow) // tile)
-        output_sum = untile(summed[0][:cut], wide // device_count)
-        pre_sum = untile(summed[0][cut:end], share)
-        down_low.append(untile(summed[0][end:], hidden_ff // dp_count))
+        output_sum, query_sum, key_sum, value_sum, down_grad = untile(
+            summed[0], down_low[0], wide // device_count, wide, share, narrow
+        )
     else:
-        output_sum, pre_sum = summed
-    down_grad = jnp.stack([v.astype(f32) for v in down_low])
+        output_sum, pre_sum = [v.astype(f32) for v in summed]
+        query_sum = pre_sum[:, :wide]
+        key_sum = pre_sum[:, wide : wide + narrow]
+        value_sum = pre_sum[:, wide + narrow :]
+        down_grad = jnp.stack([v.astype(f32) for v in down_low])
 
     small = jnp.concatenate(
         [
@@ -1624,9 +1668,9 @@
         block_out,
         hidden_grad,
         a_grad,
-        pre_sum[:, :wide],
-        pre_sum[:, wide : wide + narrow],
-        pre_sum[:, wide + narrow :],
+        query_sum,
+        key_sum,
+        value_sum,
         q_grad,
         k_grad,
         output_sum,

time: 624 us -> 618 us (level)
    reduce_scatter x2 -> x3, waiting for transfers between devices: 2.32 us -> 61.7 us  [body(): lax.psum_scatter(v, 'dp', scatter_dimension=0, tiled=True)]
    reduce_scatter x1 -> x0, waiting for transfers between devices: 58.2 us -> none  [body(): lax.psum_scatter(v, 'dp', scatter_dimension=0, tiled=True).astype(f32)]
where the time goes in v7:
time: 618 us; the launch traced here: 610 us
  Pallas kernels  414 us (67%)
  matrix products  63.9 us (10%)
  waiting for transfers between devices  63.1 us (10%)
  other arithmetic  24 us (4%)
  local copies, waits for them, and re-layouts  22.9 us (4%)
  between operations  15 us (2%)
  starting transfers between devices  7.27 us (1%)
    pallas_call x1, Pallas kernels, fetch_and_attend(): pl.pallas_call(fetch_kernel, out_shape=[jax.ShapeDtypeStruct((half, 2 * n...  123 us
    pallas_call x2, Pallas kernels, plane_sum(): pl.pallas_call(kernel, out_shape=[jax.ShapeDtypeStruct((count, wide), f32...  105 us
    pallas_call x1, Pallas kernels, weight_grads(): pl.pallas_call(weight_grad_kernel, out_shape=jax.ShapeDtypeStruct((elemen...  73.3 us
    reduce_scatter x3, waiting for transfers between devices, body(): lax.psum_scatter(v, 'dp', scatter_dimension=0, tiled=True)  61.7 us
    dot_general x9, matrix products, dot(): return jnp.dot(a, b, preferred_element_type=f32)  58.6 us
    pallas_call x1, Pallas kernels, gather_first_expert(): pl.pallas_call(first_expert_kernel, out_shape=[jax.ShapeDtypeStruct((tota...  47.4 us
    pallas_call x1, Pallas kernels, attention_back_gather(): pl.pallas_call(attention_back_gather_kernel, out_shape=[jax.ShapeDtypeStr...  38 us
    pallas_call x1, Pallas kernels, last_expert(): pl.pallas_call(kernel, grid=(4,), out_shape=[jax.ShapeDtypeStruct((total,...  23.6 us
  transfers between devices with their start and end apart: 7, of which 3 were waited for; matrix products, arithmetic and copies ran while one was open for 17% of the time, Pallas kernels for 39%

profile of v7, /device:TPU:0, one launch (start us, length us, event | category | flops | bytes accessed | tf_op | source)
XLA Modules:
  0.0 609.8 jit_solution(7758532938195974080)
XLA Ops:
  7.3 1.5 copy.59.routes_ref
  8.8 1.1 fusion.21
  10.0 123.4 %shard_map.237 = (bf16[1024,1024]{1,0:T(8,128)(2,1)}, bf16[1024,4096]{1,0:T(8,128)(2,1)}, bf16[2048,2048]{1,0:T(8,128)(2,1)}, bf16[1536,2048]{1,0:T(8,128)(2,1)}...) custom-call(bf16[192,2048]{1,0:T(8,128)(2,1)} %hidden_ref.1, ...), custom_call_target="tpu_custom_call" | custom-call | flops 14495514624 | bytes 62914560 | tf_op jit(solution)/shard_map/pallas_call | solution.py:502
  133.4 47.4 %shard_map.238 = (bf16[1536,2048]{1,0:T(8,128)(2,1)}, bf16[1536,768]{1,0:T(8,128)(2,1)}, bf16[1536,3072]{1,0:T(8,128)(2,1)}, f32[1536,128]{1,0:T(8,128)}, f32[15...) custom-call(bf16[192,2048]{1,0:T(8,128)(2,1)} %get-tuple-element.60.ffn_ref, s32[1536,8]{1,0:T(8,128)} %get-tuple-element.61.routes_ref, ...), custom_call_target="tpu_custom_call" | custom-call | flops 14495514624 | bytes 41943040 | tf_op jit(solution)/shard_map/pallas_call | solution.py:711
  180.9 23.6 %shard_map.239 = (bf16[1536,768]{1,0:T(8,128)(2,1)}, bf16[1536,3072]{1,0:T(8,128)(2,1)}, bf16[1536,128]{1,0:T(8,128)(2,1)}) custom-call(bf16[1536,2048]{1,0:T(8,128)(2,1)} %get-tuple-element.66.refs_0_, bf16[1536,2048]{1,0:T(8,128)(2,1)} %get-tuple-element.62.g_hbm.refs_1_, f32[1536,128]{1,0:T(8,128)} %get-tuple-element.67.refs_2_, ...), custom_call_target="tpu_custom_call", output_to_operand_aliasing={{1}: (6, {})} | custom-call | flops 1000000 | bytes 1000000 | tf_op jit(solution)/shard_map/pallas_call | solution.py:779
  204.5 24.5 %convolution_convert_fusion = bf16[2048,3072]{1,0:T(8,128)(2,1)} fusion(bf16[1536,2048]{1,0:T(8,128)(2,1)S(1)} %copy-done.13, bf16[1536,3072]{1,0:T(8,128)(2,1)} %get-tuple-element.78.refs_0_), kind=kOutput, calls=%fused_computation | convolution fusion | flops 19333644288 | bytes 28311552 | tf_op jit(solution)/shard_map/dot_general | solution.py:1357
  229.0 0.6 copy-done.27
  229.8 62.0 %shard_map.240 = (f32[192,2176]{1,0:T(8,128)}, bf16[8,192,512]{2,1,0:T(8,128)(2,1)}, bf16[8,192,256]{2,1,0:T(8,128)(2,1)}) custom-call(bf16[1536,3072]{1,0:T(8,128)(2,1)} %get-tuple-element.78.refs_0_, bf16[2,2048,1536]{2,1,0:T(8,128)(2,1)} %refs_1_.1, bf16[1536,128]{1,0:T(8,128)(2,1)} %get-tuple-element.79.refs_2_, ...), custom_call_target="tpu_custom_call" | custom-call | flops 1000000 | bytes 1000000 | tf_op jit(solution)/shard_map/pallas_call | solution.py:1099
  291.9 0.4 fusion.31
  292.5 1.2 multiply_reduce_fusion.5
  294.0 3.5 multiply_reduce_fusion
  297.5 1.7 fusion.27
  299.2 6.5 %fusion.33 = bf16[192,2048]{1,0:T(8,128)(2,1)S(1)} fusion(bf16[192,2048]{1,0:T(8,128)(2,1)S(1)} %get-tuple-element.177.branch, bf16[2048,2048]{1,0:T(8,128)(2,1)} %get-tuple-element.83), kind=kOutput, calls=%fused_computation.107 | convolution fusion | flops 1610612736 | bytes 9961472 | tf_op jit(solution)/shard_map/dot_general | solution.py:1357
  305.7 2.9 select_convert_fusion.1
  308.7 1.3 pad_maximum_fusion.grad_ref
  310.0 0.4 copy-done.4
  310.5 38.0 %shard_map.241 = (bf16[192,4096]{1,0:T(8,128)(2,1)S(1)}, f32[576,512]{1,0:T(8,128)S(1)}, f32[576,512]{1,0:T(8,128)S(1)}, f32[4,1,128]{2,1,0:T(1,128)S(1)}, bf16[1536,2048]{1,0:T(8,128)(2,1)}) custom-call(f32[192,4096]{1,0:T(8,128)} %get-tuple-element.75.query_pre_ref, f32[1,128]{1,0:T(1,128)S(1)} %bitcast.78, f32[192,128]{1,0:T(8,128)S(1)} %copy-done.3, ...), custom_call_target="tpu_custom_call" | custom-call | flops 1000000 | bytes 1000000 | tf_op jit(solution)/shard_map/pallas_call | solution.py:1286
  348.5 1.2 copy-done
  349.7 0.9 convert.29
  350.6 1.2 fusion.11
  351.7 0.8 copy-done.9
  352.5 0.8 fusion.17
  353.3 0.4 collective-permute-start.1
  353.9 1.4 collective-permute-done.1
  355.2 1.8 add_convert_fusion.1
  357.0 0.8 collective-permute-start.2
  357.9 9.3 %convolution_convert_fusion.1.down_part = bf16[768,2048]{1,0:T(8,128)(2,1)} fusion(bf16[1536,768]{1,0:T(8,128)(2,1)} %get-tuple-element.93.refs_1_, bf16[1536,2048]{1,0:T(8,128)(2,1)} %get-tuple-element.62.g_hbm.refs_1_), kind=kOutput, calls=%fused_computation.1 | convolution fusion | flops 4833411072 | bytes 11796480 | tf_op jit(solution)/shard_map/dot_general | solution.py:1357
  367.2 1.2 reshape.220
  368.4 0.7 concatenate.58
  369.1 1.2 convert_add_fusion
  370.3 0.7 slice_bitcast_fusion.3
  371.1 0.9 constant_dynamic-update-slice_fusion
  372.2 0.3 fusion.28
  372.5 1.2 multiply_reduce_fusion.4
  373.7 1.0 copy.63
  374.7 0.8 copy.64
  375.5 0.8 copy.65
  376.3 1.2 mul.262
  378.1 2.0 fusion.14
  380.1 0.8 maximum_maximum_fusion.kv_grad
  380.9 73.3 %shard_map.242 = bf16[3840,1024]{1,0:T(8,128)(2,1)} custom-call(bf16[192,4096]{1,0:T(8,128)(2,1)} %copy-done, bf16[192,1024]{1,0:T(8,128)(2,1)} %maximum_maximum_fusion.kv_grad, bf16[1536,2048]{1,0:T(8,128)(2,1)} %get-tuple-element.88.branch, bf16[8,192,512]{2,1,0:T(8,128)(2,1)} %get-tuple-element.89.attended_owned, ...), custom_call_target="tpu_custom_call" | custom-call | flops 1000000 | bytes 1000000 | tf_op jit(solution)/shard_map/pallas_call | solution.py:898
  454.2 2.2 reduce-scatter.4.cloned.1.call-done
  456.5 0.7 reshape.223
  457.2 1.8 fusion.32
  459.1 0.6 reshape.225
  460.0 2.7 fusion.35
  462.8 0.8 broadcast_select_fusion.1
  463.6 0.5 copy-done.1
  464.2 8.6 %fusion.34 = f32[192,1024]{1,0:T(8,128)S(1)} fusion(bf16[192,4096]{1,0:T(8,128)(2,1)S(1)} %copy-done.1, bf16[1024,4096]{1,0:T(8,128)(2,1)} %get-tuple-element.95), kind=kOutput, calls=%fused_computation.108 | convolution fusion | flops 1610612736 | bytes 10747904 | tf_op jit(solution)/shard_map/dot_general | solution.py:1357
  472.8 2.9 broadcast_select_fusion.3
  475.8 0.6 fusion.10
  476.9 0.8 copy.69
  477.8 5.8 all-to-all-start
  483.6 43.3 %shard_map.243 = f32[192,2048]{1,0:T(8,128)} custom-call(bf16[1536,768]{1,0:T(8,128)(2,1)} %get-tuple-element.92.refs_0_, bf16[1536,768]{1,0:T(8,128)(2,1)} %get-tuple-element.93.refs_1_, bf16[2,768,2048]{2,1,0:T(8,128)(2,1)} %refs_2_.1), custom_call_target="tpu_custom_call" | custom-call | flops 1000000 | bytes 1000000 | tf_op jit(solution)/shard_map/pallas_call | solution.py:1099
  526.9 3.9 fusion.7
  530.8 1.1 add_convert_fusion
  532.1 0.7 copy.70
  532.8 0.6 fusion.29
  533.4 0.6 fusion.30
  534.0 2.1 slice_bitcast_fusion.1
  536.1 3.1 maximum_convert_fusion
  539.2 59.5 %reduce-scatter.8.cloned.1.call-done.sums_ref = bf16[960,1024]{1,0:T(8,128)(2,1)} async-done(((bf16[3840,1024]{1,0:T(8,128)(2,1)}), bf16[960,1024]{1,0:T(8,128)(2,1)}) %reduce-scatter.8.cloned.1.call-update) | async-done | bytes 1966096 | tf_op jit(solution)/shard_map/reduce_scatter | solution.py:1633
  598.7 1.5 copy-done.2
  600.2 2.5 shard_map.244
  (126 shorter events, 3.2 us)
Async XLA Ops:
  7.2 447.0 %reduce-scatter.6.cloned.1.call-start = ((), (), s32[]{:S(2)}) async-start(), calls=%async_computation.5 | async-start | bytes 3932160 | tf_op jit(solution)/shard_map/reduce_scatter | solution.py:1530
  180.8 275.6 %reduce-scatter.4.cloned.1.call-start = ((), (), s32[]{:S(2)}) async-start(), calls=%async_computation.4 | async-start | bytes 15728640 | tf_op jit(solution)/shard_map/reduce_scatter | solution.py:1530
  180.9 23.6 %copy-start.13 = (bf16[1536,2048]{1,0:T(8,128)(2,1)S(1)}, bf16[1536,2048]{1,0:T(8,128)(2,1)}, u32[]{:S(2)}) copy-start(bf16[1536,2048]{1,0:T(8,128)(2,1)} %get-tuple-element.66.refs_0_) | copy-start | bytes 18874372
  228.9 0.7 copy-start.27
  229.0 369.7 %reduce-scatter.8.cloned.1.call-start = ((), (), s32[]{:S(2)}) async-start(), calls=%async_computation.6 | async-start | bytes 9830400 | tf_op jit(solution)/shard_map/reduce_scatter | solution.py:1633
  229.8 62.1 %copy-start.22 = (bf16[192,2048]{1,0:T(8,128)(2,1)S(1)}, bf16[192,2048]{1,0:T(8,128)(2,1)}, u32[]{:S(2)}) copy-start(bf16[192,2048]{1,0:T(8,128)(2,1)} %get-tuple-element.60.ffn_ref) | copy-start | bytes 2359300
  229.8 62.1 %copy-start.37 = (bf16[2048,16]{0,1:T(8,128)(2,1)S(1)}, bf16[2048,16]{0,1:T(8,128)(2,1)}, u32[]{:S(2)}) copy-start(bf16[2048,16]{0,1:T(8,128)(2,1)} %param.23) | copy-start | bytes 196612
  229.8 63.9 %copy-start.8 = (f32[192,2048]{1,0:T(8,128)S(1)}, f32[192,2048]{1,0:T(8,128)}, u32[]{:S(2)}) copy-start(f32[192,2048]{1,0:T(8,128)} %get-tuple-element.59) | copy-start | bytes 4718596
  291.9 2.1 copy-start.30
  292.3 5.1 copy-start.19
  292.5 4.9 copy-start.28
  293.7 3.7 copy-start.33
  294.0 3.5 copy-start.21
  297.5 8.2 %slice-start.3 = ((s8[8388608]{0:T(1024)(128)(4,1)}), s8[4194304]{0:T(1024)(128)(4,1)S(1)}, s32[]{:S(2)}) async-start(s8[8388608]{0:T(1024)(128)(4,1)} %bitcast.90), calls=%async_computation.10 | async-start | bytes 8388608
  299.2 6.5 %slice-start.4 = ((s8[8388608]{0:T(1024)(128)(4,1)}), s8[4194304]{0:T(1024)(128)(4,1)S(1)}, s32[]{:S(2)}) async-start(s8[8388608]{0:T(1024)(128)(4,1)} %bitcast.90), calls=%async_computation.11 | async-start | bytes 8388608
  308.6 1.3 copy-start.3
  308.6 1.8 copy-start.4
  308.6 1.8 copy-start.6
  308.7 1.8 copy-start.7
  348.5 1.2 copy-start
  351.7 0.8 copy-start.9
  353.3 1.9 collective-permute-start.1
  353.7 15.3 %collective-permute-start = (bf16[2,128,512]{2,1,0:T(8,128)(2,1)}, bf16[2,128,512]{2,1,0:T(8,128)(2,1)}, u32[]{:S(2)}, u32[]{:S(2)}) collective-permute-start(bf16[2,128,512]{2,1,0:T(8,128)(2,1)} %get-tuple-element.189), channel_id=1, source_target_pairs={{0,2},{2,0},{4,6},{6,4},{1,3},{3,1},{5,7},{7,5},{8,10},{10,8},{12,... | collective-permute-start | bytes 786440 | tf_op jit(solution)/shard_map/ppermute | solution.py:66
  357.0 12.0 %copy-start.34 = (f32[128]{0:T(128)S(1)}, f32[128]{0:T(128)}, u32[]{:S(2)}) copy-start(f32[128]{0:T(128)} %param.20) | copy-start | bytes 1540
  357.0 12.0 %collective-permute-start.2 = (bf16[2,128,512]{2,1,0:T(8,128)(2,1)}, bf16[2,128,512]{2,1,0:T(8,128)(2,1)}, u32[]{:S(2)}, u32[]{:S(2)}) collective-permute-start(bf16[2,128,512]{2,1,0:T(8,128)(2,1)} %add_convert_fusion.1), channel_id=1, source_target_pairs={{0,4},{2,6},{4,0},{6,2},{1,5},{3,7},{5,1},{7,3},{8,12},{10,14},{12... | collective-permute-start | bytes 786440 | tf_op jit(solution)/shard_map/ppermute | solution.py:66
  367.2 3.1 copy-start.18
  370.2 1.8 copy-start.23
  373.7 4.4 copy-start.17
  376.2 1.6 copy-start.24
  378.1 2.0 slice-start.2
  454.1 2.3 copy-start.31
  454.2 3.1 copy-start.20
  454.2 3.1 copy-start.29
  457.2 2.5 copy-start.10
  460.0 2.7 copy-start.14
  460.0 2.7 copy-start.35
  460.0 2.7 copy-start.36
  462.7 1.4 copy-start.1
  462.8 10.0 %slice-start = ((s8[8388608]{0:T(1024)(128)(4,1)}), s8[4194304]{0:T(1024)(128)(4,1)S(1)}, s32[]{:S(2)}) async-start(s8[8388608]{0:T(1024)(128)(4,1)} %bitcast.79), calls=%async_computation.7 | async-start | bytes 8388608
  463.6 12.1 %copy-start.15 = (f32[192,1024]{1,0:T(8,128)}, f32[192,1024]{1,0:T(8,128)S(1)}, u32[]{:S(2)}) copy-start(f32[192,1024]{1,0:T(8,128)S(1)} %get-tuple-element.185) | copy-start | bytes 2359300
  463.6 12.1 %copy-start.16 = (f32[192,1024]{1,0:T(8,128)}, f32[192,1024]{1,0:T(8,128)S(1)}, u32[]{:S(2)}) copy-start(f32[192,1024]{1,0:T(8,128)S(1)} %get-tuple-element.186) | copy-start | bytes 2359300
  464.2 8.6 %slice-start.1 = ((s8[8388608]{0:T(1024)(128)(4,1)}), s8[4194304]{0:T(1024)(128)(4,1)S(1)}, s32[]{:S(2)}) async-start(s8[8388608]{0:T(1024)(128)(4,1)} %bitcast.79), calls=%async_computation.8 | async-start | bytes 8388608
  472.8 2.9 copy-start.26
  475.7 0.9 copy-start.11
  475.7 0.9 copy-start.32
  475.8 1.0 copy-start.25
  477.8 54.1 %all-to-all-start = ((f32[32,1,1160]{2,1,0:T(1,128)}), f32[32,1,1160]{2,1,0:T(1,128)S(1)}, u32[]{:S(2)}, u32[]{:S(2)}) async-start(f32[32,1,1160]{2,1,0:T(1,128)} %copy.69), calls=%async_computation | async-start | bytes 327680 | tf_op jit(solution)/shard_map/all_to_all | solution.py:1659
  526.9 3.9 copy-start.12
  536.0 62.6 %copy-start.5 = (bf16[192,2048]{1,0:T(8,128)(2,1)S(1)}, bf16[192,2048]{1,0:T(8,128)(2,1)}, u32[]{:S(2)}) copy-start(bf16[192,2048]{1,0:T(8,128)(2,1)} %reduce-scatter.6.cloned.1.call-done.down_ref) | copy-start | bytes 2359300
  598.7 1.5 copy-start.2
Sparse Core Ops, SparseCore 0:
  180.9 61.1 reduce-scatter.5
  244.5 211.8 reduce-scatter.3
  458.7 139.9 reduce-scatter.7

commit v8 on v7

--- a/solution.py
+++ b/solution.py
@@ -274,7 +274,7 @@
     query_ref,
     output_ref,
     grad_ref,
-    routes_ref,
+    routes_across,
     kv_out,
     q_out,
     o_out,
@@ -303,6 +303,7 @@
     kv_pre,
     kv_low,
     kv_all,
+    routes_ref,
     send_sem,
     recv_sem,
     local_sem,
@@ -350,6 +351,7 @@
     def start():
         for load in loads:
             load.start()
+        routes_ref[...] = routes_across[...].T
         inputs = hidden_ref[...].astype(f32)
         normed_ref[...] = (inputs * head_norm(inputs) * attn_gain_ref[...]).astype(bf16)
 
@@ -516,7 +518,7 @@
             jax.ShapeDtypeStruct((rows, width), f32),
             jax.ShapeDtypeStruct((rows, width), bf16),
         ],
-        in_specs=[vmem] * 7 + [anywhere] * 6,
+        in_specs=[vmem] * 7 + [anywhere] * 5 + [vmem],
         out_specs=[anywhere] * 10 + [vmem] * 3,
         scratch_shapes=[
             pltpu.VMEM((spread, rows, width // spread), bf16),
@@ -534,6 +536,7 @@
             pltpu.VMEM((rows, 2 * narrow), f32),
             pltpu.VMEM((rows, 2 * narrow), bf16),
             pltpu.VMEM((keys, 2 * narrow), bf16),
+            pltpu.VMEM(routes.shape, jnp.int32),
             pltpu.SemaphoreType.DMA((copies,)),
             pltpu.SemaphoreType.DMA((copies,)),
             pltpu.SemaphoreType.DMA((15,)),
@@ -549,7 +552,7 @@
     )(
         hidden_in, attn_gain.reshape(1, width), query_gain.reshape(1, HEAD_SIZE),
         key_gain.reshape(1, HEAD_SIZE), ffn_gain.reshape(1, width), cosine, sine,
-        key_matrix, value_matrix, query_weight, output_weight, out_grad, routes,
+        key_matrix, value_matrix, query_weight, output_weight, out_grad, routes.T,
     )
 
 
@@ -558,7 +561,13 @@
     return pl.ds(pl.multiple_of(first, rows), 2 * rows)
 
 
-def expert_chunk(some, first, rows_v, g_v, gate_up_v, down_v, hidden_v, grad_v, total_v, gate, mark):
+def across_down(rows, down_rows):
+    return lax.dot_general(rows, down_rows, (((1,), (1,)), ((), ())), preferred_element_type=f32)
+
+
+def expert_chunk(
+    some, rows_v, g_v, gate_up_v, down_v, hidden_v, grad_v, total_v, gate, mark, q_v=None
+):
     ff = down_v.shape[0]
     tile = 256
 
@@ -567,12 +576,10 @@
         at = pl.multiple_of(f * tile, tile)
         a = dot(rows_v[some, :], gate_up_v[:, pl.ds(at, tile)])
         b = dot(rows_v[some, :], gate_up_v[:, pl.ds(ff + at, tile)])
-        q = lax.dot_general(
-            g_v[some, :],
-            down_v[pl.ds(at, tile), :],
-            (((1,), (1,)), ((), ())),
-            preferred_element_type=f32,
-        )
+        if q_v is None:
+            q = across_down(g_v[some, :], down_v[pl.ds(at, tile), :])
+        else:
+            q = q_v[some, pl.ds(at, tile)]
         s = 1.0 / (1.0 + jnp.exp(-a))
         raised_a = a * s
         hidden = raised_a * b
@@ -606,6 +613,7 @@
     grad_v,
     total_v,
     down_total,
+    q_v,
     send_sem,
     recv_sem,
     local_sem,
@@ -619,9 +627,9 @@
     stages, got = block_gather(here, send, ffn_ref, local_sem.at[0], rows_v)
     stages[0]()
     loads = [
-        pltpu.make_async_copy(gate_up_hbm.at[0], gate_up_v, local_sem.at[1]),
         pltpu.make_async_copy(down_hbm.at[0], down_v, local_sem.at[2]),
         pltpu.make_async_copy(g_hbm, g_v, local_sem.at[3]),
+        pltpu.make_async_copy(gate_up_hbm.at[0], gate_up_v, local_sem.at[1]),
     ]
     for load in loads:
         load.start()
@@ -657,7 +665,7 @@
         gates_ref[some, :] = spread
         mark = (lane == first_expert) | (lane == first_expert + experts)
         expert_chunk(
-            some, 0, rows_v, g_v, gate_up_v, down_v, hidden_v, grad_v, total_v, columns[0], mark
+            some, rows_v, g_v, gate_up_v, down_v, hidden_v, grad_v, total_v, columns[0], mark, q_v
         )
         gate_grad_ref[some, :] = total_v[...]
         for source, target in ((hidden_v, hidden_out), (grad_v, grad_out), (rows_v, rows_out)):
@@ -684,10 +692,18 @@
                 down_total[:, cols] = part
 
     x, y = here.x, here.y
+    for load in loads[:2]:
+        load.wait()
+
+    @pl.loop(0, rows_v.shape[0] // (2 * count))
+    def _(i):
+        some = pl.ds(pl.multiple_of(i * 2 * count, 2 * count), 2 * count)
+        for at in range(0, down_v.shape[0], 256):
+            q_v[some, at : at + 256] = across_down(g_v[some, :], down_v[at : at + 256, :])
+
     for name in ("c", "own"):
         arrive(got, name)
-    for load in loads:
-        load.wait()
+    loads[2].wait()
     chunk(x, y)
     stages[1]()
     arrive(got, "yc")
@@ -729,6 +745,7 @@
             pltpu.VMEM((total, 2 * ff), bf16),
             pltpu.VMEM((2 * ffn_in.shape[0], 128), f32),
             pltpu.VMEM((ff, width), f32),
+            pltpu.VMEM((total, ff), f32),
             pltpu.SemaphoreType.DMA((9,)),
             pltpu.SemaphoreType.DMA((9,)),
             pltpu.SemaphoreType.DMA((16,)),
@@ -755,7 +772,7 @@
     gate = jnp.sum(jnp.where(lane == which, gates_ref[...], 0.0), axis=-1, keepdims=True)
     some = pl.ds(0, rows_v.shape[0])
     expert_chunk(
-        some, 0, rows_v, g_v, gate_up_v.at[0], down_v.at[0], hidden_v, grad_v, total_v, gate, mark
+        some, rows_v, g_v, gate_up_v.at[0], down_v.at[0], hidden_v, grad_v, total_v, gate, mark
     )
     total = total_v[...]
     high = total.astype(bf16).astype(f32)

time: 618 us -> 616 us (level)
  transfers between devices with their start and end apart: 7 -> 7, of which waited for: 3 -> 3; matrix products, arithmetic and copies ran while one was open for 17% -> 17% of each run, Pallas kernels for 39% -> 40%
where the time goes in v8:
time: 616 us; the launch traced here: 606 us
  Pallas kernels  412 us (67%)
  matrix products  64.1 us (10%)
  waiting for transfers between devices  63.1 us (10%)
  other arithmetic  24 us (4%)
  local copies, waits for them, and re-layouts  21.5 us (3%)
  between operations  14.7 us (2%)
  starting transfers between devices  7.1 us (1%)
    pallas_call x1, Pallas kernels, fetch_and_attend(): pl.pallas_call(fetch_kernel, out_shape=[jax.ShapeDtypeStruct((half, 2 * n...  123 us
    pallas_call x2, Pallas kernels, plane_sum(): pl.pallas_call(kernel, out_shape=[jax.ShapeDtypeStruct((count, wide), f32...  106 us
    pallas_call x1, Pallas kernels, weight_grads(): pl.pallas_call(weight_grad_kernel, out_shape=jax.ShapeDtypeStruct((elemen...  73.2 us
    reduce_scatter x3, waiting for transfers between devices, body(): lax.psum_scatter(v, 'dp', scatter_dimension=0, tiled=True)  61.7 us
    dot_general x9, matrix products, dot(): return jnp.dot(a, b, preferred_element_type=f32)  58.8 us
    pallas_call x1, Pallas kernels, gather_first_expert(): pl.pallas_call(first_expert_kernel, out_shape=[jax.ShapeDtypeStruct((tota...  45 us
    pallas_call x1, Pallas kernels, attention_back_gather(): pl.pallas_call(attention_back_gather_kernel, out_shape=[jax.ShapeDtypeStr...  38 us
    pallas_call x1, Pallas kernels, last_expert(): pl.pallas_call(kernel, grid=(4,), out_shape=[jax.ShapeDtypeStruct((total,...  23.9 us
  transfers between devices with their start and end apart: 7, of which 3 were waited for; matrix products, arithmetic and copies ran while one was open for 17% of the time, Pallas kernels for 40%

profile of v8, /device:TPU:0, one launch (start us, length us, event | category | flops | bytes accessed | tf_op | source)
XLA Modules:
  0.0 606.2 jit_solution(2808838920986867162)
XLA Ops:
  7.4 1.1 fusion.21
  8.5 123.4 %shard_map.237 = (bf16[1024,1024]{1,0:T(8,128)(2,1)}, bf16[1024,4096]{1,0:T(8,128)(2,1)}, bf16[2048,2048]{1,0:T(8,128)(2,1)}, bf16[1536,2048]{1,0:T(8,128)(2,1)}...) custom-call(bf16[192,2048]{1,0:T(8,128)(2,1)} %hidden_ref.1, ...), custom_call_target="tpu_custom_call" | custom-call | flops 14495514624 | bytes 62914560 | tf_op jit(solution)/shard_map/pallas_call | solution.py:504
  131.9 45.0 %shard_map.238 = (bf16[1536,2048]{1,0:T(8,128)(2,1)}, bf16[1536,768]{1,0:T(8,128)(2,1)}, bf16[1536,3072]{1,0:T(8,128)(2,1)}, f32[1536,128]{1,0:T(8,128)}, f32[15...) custom-call(bf16[192,2048]{1,0:T(8,128)(2,1)} %get-tuple-element.60.ffn_ref, s32[1536,8]{1,0:T(8,128)} %get-tuple-element.61.routes_ref, ...), custom_call_target="tpu_custom_call" | custom-call | flops 14495514624 | bytes 41943040 | tf_op jit(solution)/shard_map/pallas_call | solution.py:727
  176.9 23.9 %shard_map.239 = (bf16[1536,768]{1,0:T(8,128)(2,1)}, bf16[1536,3072]{1,0:T(8,128)(2,1)}, bf16[1536,128]{1,0:T(8,128)(2,1)}) custom-call(bf16[1536,2048]{1,0:T(8,128)(2,1)} %get-tuple-element.66.refs_0_, bf16[1536,2048]{1,0:T(8,128)(2,1)} %get-tuple-element.62.g_hbm.refs_1_, f32[1536,128]{1,0:T(8,128)} %get-tuple-element.67.refs_2_, ...), custom_call_target="tpu_custom_call", output_to_operand_aliasing={{1}: (6, {})} | custom-call | flops 1000000 | bytes 1000000 | tf_op jit(solution)/shard_map/pallas_call | solution.py:796
  200.8 24.5 %convolution_convert_fusion = bf16[2048,3072]{1,0:T(8,128)(2,1)} fusion(bf16[1536,2048]{1,0:T(8,128)(2,1)S(1)} %copy-done.13, bf16[1536,3072]{1,0:T(8,128)(2,1)} %get-tuple-element.78.refs_0_), kind=kOutput, calls=%fused_computation | convolution fusion | flops 19333644288 | bytes 28311552 | tf_op jit(solution)/shard_map/dot_general | solution.py:1374
  225.4 0.6 copy-done.31
  226.1 62.5 %shard_map.240 = (f32[192,2176]{1,0:T(8,128)}, bf16[8,192,512]{2,1,0:T(8,128)(2,1)}, bf16[8,192,256]{2,1,0:T(8,128)(2,1)}) custom-call(bf16[1536,3072]{1,0:T(8,128)(2,1)} %get-tuple-element.78.refs_0_, bf16[2,2048,1536]{2,1,0:T(8,128)(2,1)} %refs_1_.1, bf16[1536,128]{1,0:T(8,128)(2,1)} %get-tuple-element.79.refs_2_, ...), custom_call_target="tpu_custom_call" | custom-call | flops 1000000 | bytes 1000000 | tf_op jit(solution)/shard_map/pallas_call | solution.py:1116
  288.7 0.4 fusion.31
  289.3 1.2 multiply_reduce_fusion.5
  290.8 3.5 multiply_reduce_fusion
  294.3 1.7 fusion.27
  296.0 6.5 %fusion.33 = bf16[192,2048]{1,0:T(8,128)(2,1)S(1)} fusion(bf16[192,2048]{1,0:T(8,128)(2,1)S(1)} %get-tuple-element.177.branch, bf16[2048,2048]{1,0:T(8,128)(2,1)} %get-tuple-element.83), kind=kOutput, calls=%fused_computation.107 | convolution fusion | flops 1610612736 | bytes 9961472 | tf_op jit(solution)/shard_map/dot_general | solution.py:1374
  302.6 2.9 select_convert_fusion.1
  305.5 1.3 pad_maximum_fusion.grad_ref
  306.8 0.4 copy-done.4
  307.3 38.0 %shard_map.241 = (bf16[192,4096]{1,0:T(8,128)(2,1)S(1)}, f32[576,512]{1,0:T(8,128)S(1)}, f32[576,512]{1,0:T(8,128)S(1)}, f32[4,1,128]{2,1,0:T(1,128)S(1)}, bf16[1536,2048]{1,0:T(8,128)(2,1)}) custom-call(f32[192,4096]{1,0:T(8,128)} %get-tuple-element.75.query_pre_ref, f32[1,128]{1,0:T(1,128)S(1)} %bitcast.79, f32[192,128]{1,0:T(8,128)S(1)} %copy-done.3, ...), custom_call_target="tpu_custom_call" | custom-call | flops 1000000 | bytes 1000000 | tf_op jit(solution)/shard_map/pallas_call | solution.py:1303
  345.3 1.2 copy-done
  346.5 0.9 convert.29
  347.4 1.2 fusion.11
  348.5 0.8 copy-done.9
  349.3 0.8 fusion.17
  350.1 0.4 collective-permute-start.1
  350.6 1.4 collective-permute-done.1
  352.0 1.8 add_convert_fusion.1
  353.8 0.7 collective-permute-start.2
  354.5 9.5 %convolution_convert_fusion.1.down_part = bf16[768,2048]{1,0:T(8,128)(2,1)} fusion(bf16[1536,768]{1,0:T(8,128)(2,1)} %get-tuple-element.93.refs_1_, bf16[1536,2048]{1,0:T(8,128)(2,1)} %get-tuple-element.62.g_hbm.refs_1_), kind=kOutput, calls=%fused_computation.1 | convolution fusion | flops 4833411072 | bytes 11796480 | tf_op jit(solution)/shard_map/dot_general | solution.py:1374
  364.0 1.2 reshape.220
  365.2 0.7 concatenate.58
  365.9 1.2 convert_add_fusion
  367.1 0.7 slice_bitcast_fusion.3
  368.0 0.9 constant_dynamic-update-slice_fusion
  369.0 0.3 fusion.28
  369.3 1.2 multiply_reduce_fusion.4
  370.5 1.0 copy.57
  371.6 0.8 copy.58
  372.3 0.8 copy.59
  373.1 1.2 mul.262
  374.4 0.3 mul.284
  375.0 2.0 fusion.14
  377.0 0.8 maximum_maximum_fusion.kv_grad
  377.7 73.2 %shard_map.242 = bf16[3840,1024]{1,0:T(8,128)(2,1)} custom-call(bf16[192,4096]{1,0:T(8,128)(2,1)} %copy-done, bf16[192,1024]{1,0:T(8,128)(2,1)} %maximum_maximum_fusion.kv_grad, bf16[1536,2048]{1,0:T(8,128)(2,1)} %get-tuple-element.88.branch, bf16[8,192,512]{2,1,0:T(8,128)(2,1)} %get-tuple-element.89.attended_owned, ...), custom_call_target="tpu_custom_call" | custom-call | flops 1000000 | bytes 1000000 | tf_op jit(solution)/shard_map/pallas_call | solution.py:915
  451.0 2.1 reduce-scatter.4.cloned.1.call-done
  453.2 0.7 reshape.223
  453.9 1.8 fusion.32
  455.8 0.6 reshape.225
  456.7 2.7 fusion.35
  459.5 0.8 broadcast_select_fusion.1
  460.3 0.5 copy-done.1
  460.8 8.6 %fusion.34 = f32[192,1024]{1,0:T(8,128)S(1)} fusion(bf16[192,4096]{1,0:T(8,128)(2,1)S(1)} %copy-done.1, bf16[1024,4096]{1,0:T(8,128)(2,1)} %get-tuple-element.95), kind=kOutput, calls=%fused_computation.108 | convolution fusion | flops 1610612736 | bytes 10747904 | tf_op jit(solution)/shard_map/dot_general | solution.py:1374
  469.5 2.9 broadcast_select_fusion.3
  472.5 0.6 fusion.10
  473.6 0.8 copy.63
  474.5 5.8 all-to-all-start
  480.2 43.3 %shard_map.243 = f32[192,2048]{1,0:T(8,128)} custom-call(bf16[1536,768]{1,0:T(8,128)(2,1)} %get-tuple-element.92.refs_0_, bf16[1536,768]{1,0:T(8,128)(2,1)} %get-tuple-element.93.refs_1_, bf16[2,768,2048]{2,1,0:T(8,128)(2,1)} %refs_2_.1), custom_call_target="tpu_custom_call" | custom-call | flops 1000000 | bytes 1000000 | tf_op jit(solution)/shard_map/pallas_call | solution.py:1116
  523.5 3.9 fusion.7
  527.4 1.1 add_convert_fusion
  528.7 0.7 copy.64
  529.4 0.6 fusion.29
  530.0 0.6 fusion.30
  530.6 2.1 slice_bitcast_fusion.1
  532.7 3.1 maximum_convert_fusion
  535.8 59.6 %reduce-scatter.8.cloned.1.call-done.sums_ref = bf16[960,1024]{1,0:T(8,128)(2,1)} async-done(((bf16[3840,1024]{1,0:T(8,128)(2,1)}), bf16[960,1024]{1,0:T(8,128)(2,1)}) %reduce-scatter.8.cloned.1.call-update) | async-done | bytes 1966096 | tf_op jit(solution)/shard_map/reduce_scatter | solution.py:1650
  595.4 1.5 copy-done.2
  596.9 2.5 shard_map.244
  (125 shorter events, 3.0 us)
Async XLA Ops:
  7.2 443.8 %reduce-scatter.6.cloned.1.call-start = ((), (), s32[]{:S(2)}) async-start(), calls=%async_computation.5 | async-start | bytes 3932160 | tf_op jit(solution)/shard_map/reduce_scatter | solution.py:1547
  176.9 276.2 %reduce-scatter.4.cloned.1.call-start = ((), (), s32[]{:S(2)}) async-start(), calls=%async_computation.4 | async-start | bytes 15728640 | tf_op jit(solution)/shard_map/reduce_scatter | solution.py:1547
  176.9 23.9 %copy-start.13 = (bf16[1536,2048]{1,0:T(8,128)(2,1)S(1)}, bf16[1536,2048]{1,0:T(8,128)(2,1)}, u32[]{:S(2)}) copy-start(bf16[1536,2048]{1,0:T(8,128)(2,1)} %get-tuple-element.66.refs_0_) | copy-start | bytes 18874372
  225.3 0.7 copy-start.31
  225.3 370.1 %reduce-scatter.8.cloned.1.call-start = ((), (), s32[]{:S(2)}) async-start(), calls=%async_computation.6 | async-start | bytes 9830400 | tf_op jit(solution)/shard_map/reduce_scatter | solution.py:1650
  226.1 62.6 %copy-start.22 = (bf16[192,2048]{1,0:T(8,128)(2,1)S(1)}, bf16[192,2048]{1,0:T(8,128)(2,1)}, u32[]{:S(2)}) copy-start(bf16[192,2048]{1,0:T(8,128)(2,1)} %get-tuple-element.60.ffn_ref) | copy-start | bytes 2359300
  226.1 62.6 %copy-start.37 = (bf16[2048,16]{0,1:T(8,128)(2,1)S(1)}, bf16[2048,16]{0,1:T(8,128)(2,1)}, u32[]{:S(2)}) copy-start(bf16[2048,16]{0,1:T(8,128)(2,1)} %param.23) | copy-start | bytes 196612
  226.1 64.4 %copy-start.8 = (f32[192,2048]{1,0:T(8,128)S(1)}, f32[192,2048]{1,0:T(8,128)}, u32[]{:S(2)}) copy-start(f32[192,2048]{1,0:T(8,128)} %get-tuple-element.59) | copy-start | bytes 4718596
  288.7 2.1 copy-start.29
  289.1 5.1 copy-start.19
  289.3 4.9 copy-start.27
  290.6 3.7 copy-start.33
  290.8 3.5 copy-start.21
  294.3 8.2 %slice-start.3 = ((s8[8388608]{0:T(1024)(128)(4,1)}), s8[4194304]{0:T(1024)(128)(4,1)S(1)}, s32[]{:S(2)}) async-start(s8[8388608]{0:T(1024)(128)(4,1)} %bitcast.92), calls=%async_computation.10 | async-start | bytes 8388608
  296.0 6.5 %slice-start.4 = ((s8[8388608]{0:T(1024)(128)(4,1)}), s8[4194304]{0:T(1024)(128)(4,1)S(1)}, s32[]{:S(2)}) async-start(s8[8388608]{0:T(1024)(128)(4,1)} %bitcast.92), calls=%async_computation.11 | async-start | bytes 8388608
  305.4 1.3 copy-start.3
  305.5 1.8 copy-start.4
  305.5 1.8 copy-start.6
  305.5 1.8 copy-start.7
  345.3 1.2 copy-start
  348.5 0.8 copy-start.9
  350.1 1.9 collective-permute-start.1
  350.5 15.4 %collective-permute-start = (bf16[2,128,512]{2,1,0:T(8,128)(2,1)}, bf16[2,128,512]{2,1,0:T(8,128)(2,1)}, u32[]{:S(2)}, u32[]{:S(2)}) collective-permute-start(bf16[2,128,512]{2,1,0:T(8,128)(2,1)} %get-tuple-element.189), channel_id=1, source_target_pairs={{0,2},{2,0},{4,6},{6,4},{1,3},{3,1},{5,7},{7,5},{8,10},{10,8},{12,... | collective-permute-start | bytes 786440 | tf_op jit(solution)/shard_map/ppermute | solution.py:66
  353.8 12.1 %copy-start.34 = (f32[128]{0:T(128)S(1)}, f32[128]{0:T(128)}, u32[]{:S(2)}) copy-start(f32[128]{0:T(128)} %param.20) | copy-start | bytes 1540
  353.8 12.1 %collective-permute-start.2 = (bf16[2,128,512]{2,1,0:T(8,128)(2,1)}, bf16[2,128,512]{2,1,0:T(8,128)(2,1)}, u32[]{:S(2)}, u32[]{:S(2)}) collective-permute-start(bf16[2,128,512]{2,1,0:T(8,128)(2,1)} %add_convert_fusion.1), channel_id=1, source_target_pairs={{0,4},{2,6},{4,0},{6,2},{1,5},{3,7},{5,1},{7,3},{8,12},{10,14},{12... | collective-permute-start | bytes 786440 | tf_op jit(solution)/shard_map/ppermute | solution.py:66
  364.0 3.1 copy-start.18
  367.1 1.8 copy-start.23
  370.5 4.4 copy-start.17
  373.1 1.6 copy-start.24
  374.9 2.0 slice-start.2
  451.0 2.2 copy-start.30
  451.0 3.0 copy-start.20
  451.0 3.0 copy-start.28
  453.9 2.5 copy-start.10
  456.7 2.7 copy-start.14
  456.7 2.7 copy-start.35
  456.7 2.7 copy-start.36
  459.4 1.4 copy-start.1
  459.4 10.0 %slice-start = ((s8[8388608]{0:T(1024)(128)(4,1)}), s8[4194304]{0:T(1024)(128)(4,1)S(1)}, s32[]{:S(2)}) async-start(s8[8388608]{0:T(1024)(128)(4,1)} %bitcast.80), calls=%async_computation.7 | async-start | bytes 8388608
  460.3 12.1 %copy-start.15 = (f32[192,1024]{1,0:T(8,128)}, f32[192,1024]{1,0:T(8,128)S(1)}, u32[]{:S(2)}) copy-start(f32[192,1024]{1,0:T(8,128)S(1)} %get-tuple-element.185) | copy-start | bytes 2359300
  460.3 12.1 %copy-start.16 = (f32[192,1024]{1,0:T(8,128)}, f32[192,1024]{1,0:T(8,128)S(1)}, u32[]{:S(2)}) copy-start(f32[192,1024]{1,0:T(8,128)S(1)} %get-tuple-element.186) | copy-start | bytes 2359300
  460.8 8.6 %slice-start.1 = ((s8[8388608]{0:T(1024)(128)(4,1)}), s8[4194304]{0:T(1024)(128)(4,1)S(1)}, s32[]{:S(2)}) async-start(s8[8388608]{0:T(1024)(128)(4,1)} %bitcast.80), calls=%async_computation.8 | async-start | bytes 8388608
  469.5 2.9 copy-start.26
  472.4 0.9 copy-start.11
  472.4 0.9 copy-start.32
  472.4 1.0 copy-start.25
  474.5 54.0 %all-to-all-start = ((f32[32,1,1160]{2,1,0:T(1,128)}), f32[32,1,1160]{2,1,0:T(1,128)S(1)}, u32[]{:S(2)}, u32[]{:S(2)}) async-start(f32[32,1,1160]{2,1,0:T(1,128)} %copy.63), calls=%async_computation | async-start | bytes 327680 | tf_op jit(solution)/shard_map/all_to_all | solution.py:1676
  523.5 3.9 copy-start.12
  532.7 62.7 %copy-start.5 = (bf16[192,2048]{1,0:T(8,128)(2,1)S(1)}, bf16[192,2048]{1,0:T(8,128)(2,1)}, u32[]{:S(2)}) copy-start(bf16[192,2048]{1,0:T(8,128)(2,1)} %reduce-scatter.6.cloned.1.call-done.down_ref) | copy-start | bytes 2359300
  595.4 1.5 copy-start.2
Sparse Core Ops, SparseCore 0:
  177.0 61.7 reduce-scatter.5
  241.2 211.8 reduce-scatter.3
  455.4 139.9 reduce-scatter.7

commit v9 on v8

--- a/solution.py
+++ b/solution.py
@@ -678,7 +678,7 @@
         add_down(some, len(stores) == 3, len(stores) == 12)
 
     def add_down(some, is_first, is_last):
-        tile = 512
+        tile = 1024
 
         @pl.loop(0, down_total.shape[1] // tile)
         def _(i):

time: 616 us -> 625 us (1.015)
  Pallas kernels: 412 us -> 421 us
    pallas_call x1, Pallas kernels: 45 us -> 54.1 us  [gather_first_expert(): pl.pallas_call(first_expert_kernel, out_shape=[jax.ShapeDtypeStruct((tota...]
  transfers between devices with their start and end apart: 7 -> 7, of which waited for: 3 -> 3; matrix products, arithmetic and copies ran while one was open for 17% -> 17% of each run, Pallas kernels for 40% -> 39%
where the time goes in v9:
time: 625 us; the launch traced here: 616 us
  Pallas kernels  421 us (67%)
  matrix products  63.9 us (10%)
  waiting for transfers between devices  63.3 us (10%)
  other arithmetic  24 us (4%)
  local copies, waits for them, and re-layouts  21.5 us (3%)
  between operations  15 us (2%)
  starting transfers between devices  7.24 us (1%)
    pallas_call x1, Pallas kernels, fetch_and_attend(): pl.pallas_call(fetch_kernel, out_shape=[jax.ShapeDtypeStruct((half, 2 * n...  123 us
    pallas_call x2, Pallas kernels, plane_sum(): pl.pallas_call(kernel, out_shape=[jax.ShapeDtypeStruct((count, wide), f32...  106 us
    pallas_call x1, Pallas kernels, weight_grads(): pl.pallas_call(weight_grad_kernel, out_shape=jax.ShapeDtypeStruct((elemen...  73.3 us
    reduce_scatter x3, waiting for transfers between devices, body(): lax.psum_scatter(v, 'dp', scatter_dimension=0, tiled=True)  61.8 us
    dot_general x9, matrix products, dot(): return jnp.dot(a, b, preferred_element_type=f32)  58.6 us
    pallas_call x1, Pallas kernels, gather_first_expert(): pl.pallas_call(first_expert_kernel, out_shape=[jax.ShapeDtypeStruct((tota...  54.1 us
    pallas_call x1, Pallas kernels, attention_back_gather(): pl.pallas_call(attention_back_gather_kernel, out_shape=[jax.ShapeDtypeStr...  38.1 us
    pallas_call x1, Pallas kernels, last_expert(): pl.pallas_call(kernel, grid=(4,), out_shape=[jax.ShapeDtypeStruct((total,...  23.4 us
  transfers between devices with their start and end apart: 7, of which 3 were waited for; matrix products, arithmetic and copies ran while one was open for 17% of the time, Pallas kernels for 39%

profile of v9, /device:TPU:0, one launch (start us, length us, event | category | flops | bytes accessed | tf_op | source)
XLA Modules:
  0.0 615.5 jit_solution(9173406660927580094)
XLA Ops:
  7.4 1.1 fusion.21
  8.5 123.4 %shard_map.237 = (bf16[1024,1024]{1,0:T(8,128)(2,1)}, bf16[1024,4096]{1,0:T(8,128)(2,1)}, bf16[2048,2048]{1,0:T(8,128)(2,1)}, bf16[1536,2048]{1,0:T(8,128)(2,1)}...) custom-call(bf16[192,2048]{1,0:T(8,128)(2,1)} %hidden_ref.1, ...), custom_call_target="tpu_custom_call" | custom-call | flops 14495514624 | bytes 62914560 | tf_op jit(solution)/shard_map/pallas_call | solution.py:504
  131.9 54.1 %shard_map.238 = (bf16[1536,2048]{1,0:T(8,128)(2,1)}, bf16[1536,768]{1,0:T(8,128)(2,1)}, bf16[1536,3072]{1,0:T(8,128)(2,1)}, f32[1536,128]{1,0:T(8,128)}, f32[15...) custom-call(bf16[192,2048]{1,0:T(8,128)(2,1)} %get-tuple-element.60.ffn_ref, s32[1536,8]{1,0:T(8,128)} %get-tuple-element.61.routes_ref, ...), custom_call_target="tpu_custom_call" | custom-call | flops 14495514624 | bytes 41943040 | tf_op jit(solution)/shard_map/pallas_call | solution.py:727
  186.0 23.4 %shard_map.239 = (bf16[1536,768]{1,0:T(8,128)(2,1)}, bf16[1536,3072]{1,0:T(8,128)(2,1)}, bf16[1536,128]{1,0:T(8,128)(2,1)}) custom-call(bf16[1536,2048]{1,0:T(8,128)(2,1)} %get-tuple-element.66.refs_0_, bf16[1536,2048]{1,0:T(8,128)(2,1)} %get-tuple-element.62.g_hbm.refs_1_, f32[1536,128]{1,0:T(8,128)} %get-tuple-element.67.refs_2_, ...), custom_call_target="tpu_custom_call", output_to_operand_aliasing={{1}: (6, {})} | custom-call | flops 1000000 | bytes 1000000 | tf_op jit(solution)/shard_map/pallas_call | solution.py:796
  209.4 24.5 %convolution_convert_fusion = bf16[2048,3072]{1,0:T(8,128)(2,1)} fusion(bf16[1536,2048]{1,0:T(8,128)(2,1)S(1)} %copy-done.13, bf16[1536,3072]{1,0:T(8,128)(2,1)} %get-tuple-element.78.refs_0_), kind=kOutput, calls=%fused_computation | convolution fusion | flops 19333644288 | bytes 28311552 | tf_op jit(solution)/shard_map/dot_general | solution.py:1374
  234.0 0.6 copy-done.31
  234.8 62.6 %shard_map.240 = (f32[192,2176]{1,0:T(8,128)}, bf16[8,192,512]{2,1,0:T(8,128)(2,1)}, bf16[8,192,256]{2,1,0:T(8,128)(2,1)}) custom-call(bf16[1536,3072]{1,0:T(8,128)(2,1)} %get-tuple-element.78.refs_0_, bf16[2,2048,1536]{2,1,0:T(8,128)(2,1)} %refs_1_.1, bf16[1536,128]{1,0:T(8,128)(2,1)} %get-tuple-element.79.refs_2_, ...), custom_call_target="tpu_custom_call" | custom-call | flops 1000000 | bytes 1000000 | tf_op jit(solution)/shard_map/pallas_call | solution.py:1116
  297.4 0.4 fusion.31
  298.1 1.2 multiply_reduce_fusion.5
  299.5 3.5 multiply_reduce_fusion
  303.0 1.7 fusion.27
  304.7 6.5 %fusion.33 = bf16[192,2048]{1,0:T(8,128)(2,1)S(1)} fusion(bf16[192,2048]{1,0:T(8,128)(2,1)S(1)} %get-tuple-element.177.branch, bf16[2048,2048]{1,0:T(8,128)(2,1)} %get-tuple-element.83), kind=kOutput, calls=%fused_computation.107 | convolution fusion | flops 1610612736 | bytes 9961472 | tf_op jit(solution)/shard_map/dot_general | solution.py:1374
  311.2 2.9 select_convert_fusion.1
  314.2 1.3 pad_maximum_fusion.grad_ref
  315.5 0.4 copy-done.4
  316.0 38.1 %shard_map.241 = (bf16[192,4096]{1,0:T(8,128)(2,1)S(1)}, f32[576,512]{1,0:T(8,128)S(1)}, f32[576,512]{1,0:T(8,128)S(1)}, f32[4,1,128]{2,1,0:T(1,128)S(1)}, bf16[1536,2048]{1,0:T(8,128)(2,1)}) custom-call(f32[192,4096]{1,0:T(8,128)} %get-tuple-element.75.query_pre_ref, f32[1,128]{1,0:T(1,128)S(1)} %bitcast.79, f32[192,128]{1,0:T(8,128)S(1)} %copy-done.3, ...), custom_call_target="tpu_custom_call" | custom-call | flops 1000000 | bytes 1000000 | tf_op jit(solution)/shard_map/pallas_call | solution.py:1303
  354.1 1.2 copy-done
  355.2 0.9 convert.29
  356.1 1.2 fusion.11
  357.3 0.8 copy-done.9
  358.1 0.8 fusion.17
  358.9 0.4 collective-permute-start.1
  359.4 1.4 collective-permute-done.1
  360.8 1.8 add_convert_fusion.1
  362.6 0.8 collective-permute-start.2
  363.4 9.3 %convolution_convert_fusion.1.down_part = bf16[768,2048]{1,0:T(8,128)(2,1)} fusion(bf16[1536,768]{1,0:T(8,128)(2,1)} %get-tuple-element.93.refs_1_, bf16[1536,2048]{1,0:T(8,128)(2,1)} %get-tuple-element.62.g_hbm.refs_1_), kind=kOutput, calls=%fused_computation.1 | convolution fusion | flops 4833411072 | bytes 11796480 | tf_op jit(solution)/shard_map/dot_general | solution.py:1374
  372.8 1.2 reshape.220
  373.9 0.7 concatenate.58
  374.6 1.2 convert_add_fusion
  375.8 0.7 slice_bitcast_fusion.3
  376.7 0.9 constant_dynamic-update-slice_fusion
  377.7 0.3 fusion.28
  378.0 1.2 multiply_reduce_fusion.4
  379.2 1.0 copy.57
  380.3 0.8 copy.58
  381.0 0.8 copy.59
  381.9 1.2 mul.262
  383.4 0.3 mul.277
  383.7 2.0 fusion.14
  385.7 0.8 maximum_maximum_fusion.kv_grad
  386.5 73.3 %shard_map.242 = bf16[3840,1024]{1,0:T(8,128)(2,1)} custom-call(bf16[192,4096]{1,0:T(8,128)(2,1)} %copy-done, bf16[192,1024]{1,0:T(8,128)(2,1)} %maximum_maximum_fusion.kv_grad, bf16[1536,2048]{1,0:T(8,128)(2,1)} %get-tuple-element.88.branch, bf16[8,192,512]{2,1,0:T(8,128)(2,1)} %get-tuple-element.89.attended_owned, ...), custom_call_target="tpu_custom_call" | custom-call | flops 1000000 | bytes 1000000 | tf_op jit(solution)/shard_map/pallas_call | solution.py:915
  459.9 2.3 reduce-scatter.4.cloned.1.call-done
  462.3 0.7 reshape.223
  463.0 1.8 fusion.32
  464.9 0.6 reshape.225
  465.8 2.7 fusion.35
  468.5 0.8 broadcast_select_fusion.1
  469.4 0.5 copy-done.1
  469.9 8.6 %fusion.34 = f32[192,1024]{1,0:T(8,128)S(1)} fusion(bf16[192,4096]{1,0:T(8,128)(2,1)S(1)} %copy-done.1, bf16[1024,4096]{1,0:T(8,128)(2,1)} %get-tuple-element.95), kind=kOutput, calls=%fused_computation.108 | convolution fusion | flops 1610612736 | bytes 10747904 | tf_op jit(solution)/shard_map/dot_general | solution.py:1374
  478.6 2.9 broadcast_select_fusion.3
  481.5 0.6 fusion.10
  482.7 0.8 copy.63
  483.5 5.8 all-to-all-start
  489.3 43.3 %shard_map.243 = f32[192,2048]{1,0:T(8,128)} custom-call(bf16[1536,768]{1,0:T(8,128)(2,1)} %get-tuple-element.92.refs_0_, bf16[1536,768]{1,0:T(8,128)(2,1)} %get-tuple-element.93.refs_1_, bf16[2,768,2048]{2,1,0:T(8,128)(2,1)} %refs_2_.1), custom_call_target="tpu_custom_call" | custom-call | flops 1000000 | bytes 1000000 | tf_op jit(solution)/shard_map/pallas_call | solution.py:1116
  532.7 3.9 fusion.7
  536.5 1.1 add_convert_fusion
  537.9 0.7 copy.64
  538.6 0.6 fusion.29
  539.1 0.6 fusion.30
  539.7 2.1 slice_bitcast_fusion.1
  541.8 3.1 maximum_convert_fusion
  544.9 59.5 %reduce-scatter.8.cloned.1.call-done.sums_ref = bf16[960,1024]{1,0:T(8,128)(2,1)} async-done(((bf16[3840,1024]{1,0:T(8,128)(2,1)}), bf16[960,1024]{1,0:T(8,128)(2,1)}) %reduce-scatter.8.cloned.1.call-update) | async-done | bytes 1966096 | tf_op jit(solution)/shard_map/reduce_scatter | solution.py:1650
  604.4 1.5 copy-done.2
  606.0 2.5 shard_map.244
  (125 shorter events, 3.0 us)
Async XLA Ops:
  7.2 452.7 %reduce-scatter.6.cloned.1.call-start = ((), (), s32[]{:S(2)}) async-start(), calls=%async_computation.5 | async-start | bytes 3932160 | tf_op jit(solution)/shard_map/reduce_scatter | solution.py:1547
  186.0 276.2 %reduce-scatter.4.cloned.1.call-start = ((), (), s32[]{:S(2)}) async-start(), calls=%async_computation.4 | async-start | bytes 15728640 | tf_op jit(solution)/shard_map/reduce_scatter | solution.py:1547
  186.0 23.4 %copy-start.13 = (bf16[1536,2048]{1,0:T(8,128)(2,1)S(1)}, bf16[1536,2048]{1,0:T(8,128)(2,1)}, u32[]{:S(2)}) copy-start(bf16[1536,2048]{1,0:T(8,128)(2,1)} %get-tuple-element.66.refs_0_) | copy-start | bytes 18874372
  233.9 0.7 copy-start.31
  234.0 370.5 %reduce-scatter.8.cloned.1.call-start = ((), (), s32[]{:S(2)}) async-start(), calls=%async_computation.6 | async-start | bytes 9830400 | tf_op jit(solution)/shard_map/reduce_scatter | solution.py:1650
  234.8 62.6 %copy-start.22 = (bf16[192,2048]{1,0:T(8,128)(2,1)S(1)}, bf16[192,2048]{1,0:T(8,128)(2,1)}, u32[]{:S(2)}) copy-start(bf16[192,2048]{1,0:T(8,128)(2,1)} %get-tuple-element.60.ffn_ref) | copy-start | bytes 2359300
  234.8 62.6 %copy-start.37 = (bf16[2048,16]{0,1:T(8,128)(2,1)S(1)}, bf16[2048,16]{0,1:T(8,128)(2,1)}, u32[]{:S(2)}) copy-start(bf16[2048,16]{0,1:T(8,128)(2,1)} %param.23) | copy-start | bytes 196612
  234.8 64.5 %copy-start.8 = (f32[192,2048]{1,0:T(8,128)S(1)}, f32[192,2048]{1,0:T(8,128)}, u32[]{:S(2)}) copy-start(f32[192,2048]{1,0:T(8,128)} %get-tuple-element.59) | copy-start | bytes 4718596
  297.4 2.1 copy-start.29
  297.9 5.1 copy-start.19
  298.1 4.9 copy-start.27
  299.3 3.7 copy-start.33
  299.5 3.5 copy-start.21
  303.0 8.2 %slice-start.3 = ((s8[8388608]{0:T(1024)(128)(4,1)}), s8[4194304]{0:T(1024)(128)(4,1)S(1)}, s32[]{:S(2)}) async-start(s8[8388608]{0:T(1024)(128)(4,1)} %bitcast.92), calls=%async_computation.10 | async-start | bytes 8388608
  304.7 6.5 %slice-start.4 = ((s8[8388608]{0:T(1024)(128)(4,1)}), s8[4194304]{0:T(1024)(128)(4,1)S(1)}, s32[]{:S(2)}) async-start(s8[8388608]{0:T(1024)(128)(4,1)} %bitcast.92), calls=%async_computation.11 | async-start | bytes 8388608
  314.1 1.3 copy-start.3
  314.1 1.8 copy-start.4
  314.2 1.8 copy-start.6
  314.2 1.8 copy-start.7
  354.1 1.2 copy-start
  357.3 0.8 copy-start.9
  358.9 1.9 collective-permute-start.1
  359.3 15.3 %collective-permute-start = (bf16[2,128,512]{2,1,0:T(8,128)(2,1)}, bf16[2,128,512]{2,1,0:T(8,128)(2,1)}, u32[]{:S(2)}, u32[]{:S(2)}) collective-permute-start(bf16[2,128,512]{2,1,0:T(8,128)(2,1)} %get-tuple-element.189), channel_id=1, source_target_pairs={{0,2},{2,0},{4,6},{6,4},{1,3},{3,1},{5,7},{7,5},{8,10},{10,8},{12,... | collective-permute-start | bytes 786440 | tf_op jit(solution)/shard_map/ppermute | solution.py:66
  362.6 12.0 %copy-start.34 = (f32[128]{0:T(128)S(1)}, f32[128]{0:T(128)}, u32[]{:S(2)}) copy-start(f32[128]{0:T(128)} %param.20) | copy-start | bytes 1540
  362.6 12.0 %collective-permute-start.2 = (bf16[2,128,512]{2,1,0:T(8,128)(2,1)}, bf16[2,128,512]{2,1,0:T(8,128)(2,1)}, u32[]{:S(2)}, u32[]{:S(2)}) collective-permute-start(bf16[2,128,512]{2,1,0:T(8,128)(2,1)} %add_convert_fusion.1), channel_id=1, source_target_pairs={{0,4},{2,6},{4,0},{6,2},{1,5},{3,7},{5,1},{7,3},{8,12},{10,14},{12... | collective-permute-start | bytes 786440 | tf_op jit(solution)/shard_map/ppermute | solution.py:66
  372.7 3.1 copy-start.18
  375.8 1.8 copy-start.23
  379.2 4.4 copy-start.17
  381.8 1.6 copy-start.24
  383.7 2.0 slice-start.2
  459.8 2.4 copy-start.30
  459.8 3.2 copy-start.20
  459.8 3.2 copy-start.28
  463.0 2.5 copy-start.10
  465.7 2.7 copy-start.14
  465.8 2.7 copy-start.35
  465.8 2.7 copy-start.36
  468.5 1.4 copy-start.1
  468.5 10.0 %slice-start = ((s8[8388608]{0:T(1024)(128)(4,1)}), s8[4194304]{0:T(1024)(128)(4,1)S(1)}, s32[]{:S(2)}) async-start(s8[8388608]{0:T(1024)(128)(4,1)} %bitcast.80), calls=%async_computation.7 | async-start | bytes 8388608
  469.4 12.1 %copy-start.15 = (f32[192,1024]{1,0:T(8,128)}, f32[192,1024]{1,0:T(8,128)S(1)}, u32[]{:S(2)}) copy-start(f32[192,1024]{1,0:T(8,128)S(1)} %get-tuple-element.185) | copy-start | bytes 2359300
  469.4 12.1 %copy-start.16 = (f32[192,1024]{1,0:T(8,128)}, f32[192,1024]{1,0:T(8,128)S(1)}, u32[]{:S(2)}) copy-start(f32[192,1024]{1,0:T(8,128)S(1)} %get-tuple-element.186) | copy-start | bytes 2359300
  469.9 8.6 %slice-start.1 = ((s8[8388608]{0:T(1024)(128)(4,1)}), s8[4194304]{0:T(1024)(128)(4,1)S(1)}, s32[]{:S(2)}) async-start(s8[8388608]{0:T(1024)(128)(4,1)} %bitcast.80), calls=%async_computation.8 | async-start | bytes 8388608
  478.6 2.9 copy-start.26
  481.5 0.9 copy-start.11
  481.5 0.9 copy-start.32
  481.5 1.0 copy-start.25
  483.5 54.1 %all-to-all-start = ((f32[32,1,1160]{2,1,0:T(1,128)}), f32[32,1,1160]{2,1,0:T(1,128)S(1)}, u32[]{:S(2)}, u32[]{:S(2)}) async-start(f32[32,1,1160]{2,1,0:T(1,128)} %copy.63), calls=%async_computation | async-start | bytes 327680 | tf_op jit(solution)/shard_map/all_to_all | solution.py:1676
  532.7 3.9 copy-start.12
  541.8 62.6 %copy-start.5 = (bf16[192,2048]{1,0:T(8,128)(2,1)S(1)}, bf16[192,2048]{1,0:T(8,128)(2,1)}, u32[]{:S(2)}) copy-start(bf16[192,2048]{1,0:T(8,128)(2,1)} %reduce-scatter.6.cloned.1.call-done.down_ref) | copy-start | bytes 2359300
  604.4 1.5 copy-start.2
Sparse Core Ops, SparseCore 0:
  186.1 61.7 reduce-scatter.5
  250.3 211.8 reduce-scatter.3
  464.5 139.9 reduce-scatter.7
